TPU v7x, 32 devices: a whole 2x2x4 slice. The times are simulated.
32 devices in a mesh: dp: 4 (over y, x), tensor: 8 (over z, core).
Axes of the slice: x: 2, y: 2, z: 4, core: 2. Of those that a mesh axis runs over, the one named last changes fastest.
Arguments:
- tokens: bfloat16 [8192, 2048], P(('dp', 'tensor')), may hold values from -6 to 6
- out_grad: bfloat16 [8192, 2048], P(('dp', 'tensor')), may hold values from -6 to 6
- query_two: bfloat16 [8192, 2048], P('dp', 'tensor'), may hold values from -6 to 6
- grad_two: bfloat16 [8192, 2048], P('dp', 'tensor'), may hold values from -6 to 6
- doc_split: int32 [4], P('dp'), may hold values from 0 to 1, as said below
- attn_gain: float32 [2048], replicated, may hold values from 0.5 to 1.5
- mlp_gain: float32 [2048], replicated, may hold values from 0.5 to 1.5
- w_query: bfloat16 [2048, 2048], P(None, 'tensor'), may hold values from -0.125 to 0.125
- w_kv: bfloat16 [2048, 256], replicated, may hold values from -0.125 to 0.125
- w_out: bfloat16 [2048, 2048], P('tensor'), may hold values from -1.5 to 1.5
- w_gate: bfloat16 [2048, 5632], P(None, 'tensor'), may hold values from -0.125 to 0.125
- w_up: bfloat16 [2048, 5632], P(None, 'tensor'), may hold values from -0.125 to 0.125
- w_down: bfloat16 [5632, 2048], P('tensor'), may hold values from -0.078125 to 0.078125
Outputs:
- block_output: bfloat16 [8192, 2048], P(('dp', 'tensor'))
- tokens_grad: bfloat16 [8192, 2048], P(('dp', 'tensor'))
- attn_gain_grad: float32 [2048], replicated
- mlp_gain_grad: float32 [2048], replicated
- query_w_grad: float32 [2048, 2048], P(None, 'tensor')
- kv_w_grad: float32 [2048, 256], replicated
- out_w_grad: float32 [2048, 2048], P('tensor')
- gate_w_grad: float32 [2048, 5632], P(None, 'tensor')
- up_w_grad: float32 [2048, 5632], P(None, 'tensor')
- down_w_grad: float32 [5632, 2048], P('tensor')
Inputs may be any that keep to these rules, and one draw needn't show every extreme that they name: `doc_split`: each entry is 0 or 1; every draw has a shard of each kind.
All inputs are finite; a program needn't handle non-finite values.
Results may differ from a plain program's by a relative error of at most 0.024.
Values may be sent and summed in bfloat16 or wider, within the bound.
A program may use at most 256 MiB of HBM per device.

v0:
```python
import jax
import jax.numpy as jnp
from jax import lax
from jax.sharding import PartitionSpec as P

HD = 128
SEQ_LONG = 2048
SEQ_SHORT = 1024


EPSILON = 1e-05
MASKED = -1e30


def rotate(values, cosine, sine):
    middle = values.shape[-1] // 2
    leading = values[..., :middle]
    trailing = values[..., middle:]
    return jnp.concatenate(
        [leading * cosine - trailing * sine, trailing * cosine + leading * sine], axis=-1
    )


def unrotate(gradient, cosine, sine):
    middle = gradient.shape[-1] // 2
    leading = gradient[..., :middle]
    trailing = gradient[..., middle:]
    return jnp.concatenate(
        [leading * cosine + trailing * sine, trailing * cosine - leading * sine], axis=-1
    )


def phase_tables(two_docs):
    position = jnp.arange(SEQ_LONG, dtype=jnp.int32)
    in_sequence = jnp.where(two_docs > 0, position % SEQ_SHORT, position)
    frequency = 10000.0 ** (-jnp.arange(HD // 2, dtype=jnp.float32) * 2.0 / HD)
    phases = in_sequence.astype(jnp.float32)[:, None] * frequency[None, :]
    return (jnp.cos(phases), jnp.sin(phases))


def block_mask(two_docs, first_row, last_row):
    row_ids = jnp.arange(first_row, last_row, dtype=jnp.int32)
    col_ids = jnp.arange(last_row, dtype=jnp.int32)
    doc_rows = jnp.where(two_docs > 0, row_ids // SEQ_SHORT, 0)
    doc_cols = jnp.where(two_docs > 0, col_ids // SEQ_SHORT, 0)
    return (row_ids[:, None] >= col_ids[None, :]) & (doc_rows[:, None] == doc_cols[None, :])


def block_scores(queries, key_rows, allowed, score_scale):
    scores = (
        jnp.einsum("bhd,kd->hbk", queries, key_rows, preferred_element_type=jnp.float32)
        * score_scale
    )
    return jnp.where(allowed[None], scores, MASKED)


def attend(queries, key_rows, value_rows, two_docs, block_rows, score_scale):
    outputs, row_maxes, row_sums = ([], [], [])
    for first_row in range(0, SEQ_LONG, block_rows):
        last_row = first_row + block_rows
        allowed = block_mask(two_docs, first_row, last_row)
        scores = block_scores(
            queries[first_row:last_row], key_rows[:last_row], allowed, score_scale
        )
        row_max = jnp.max(scores, axis=-1, keepdims=True)
        lifted = jnp.exp(scores - row_max)
        row_sum = jnp.sum(lifted, axis=-1, keepdims=True)
        weights = (lifted / row_sum).astype(jnp.bfloat16)
        outputs.append(
            jnp.einsum(
                "hbk,kd->bhd", weights, value_rows[:last_row], preferred_element_type=jnp.float32
            )
        )
        row_maxes.append(row_max)
        row_sums.append(row_sum)
    return (jnp.concatenate(outputs, axis=0), row_maxes, row_sums)


def attend_back(
    queries,
    key_rows,
    value_rows,
    grad_context,
    query_two,
    grad_two,
    two_docs,
    row_maxes,
    row_sums,
    block_rows,
    score_scale,
):
    key_grads = jnp.zeros(key_rows.shape, jnp.float32)
    value_grads = jnp.zeros(value_rows.shape, jnp.float32)
    query_parts = []
    for block_no, first_row in enumerate(range(0, SEQ_LONG, block_rows)):
        last_row = first_row + block_rows
        allowed = block_mask(two_docs, first_row, last_row)
        near_keys = key_rows[:last_row]
        near_values = value_rows[:last_row]
        padding = ((0, SEQ_LONG - last_row), (0, 0))
        block_queries = queries[first_row:last_row]
        scores = block_scores(block_queries, near_keys, allowed, score_scale)
        weights = jnp.exp(scores - row_maxes[block_no]) / row_sums[block_no]
        block_grad = grad_context[first_row:last_row]
        grad_weights = jnp.einsum(
            "bhd,kd->hbk", block_grad, near_values, preferred_element_type=jnp.float32
        )
        row_dot = jnp.sum(weights * grad_weights, axis=-1, keepdims=True)
        grad_scores = (weights * (grad_weights - row_dot)).astype(jnp.bfloat16)
        query_parts.append(
            jnp.einsum("hbk,kd->bhd", grad_scores, near_keys, preferred_element_type=jnp.float32)
            * score_scale
        )
        key_part = (
            jnp.einsum(
                "hbk,bhd->kd", grad_scores, block_queries, preferred_element_type=jnp.float32
            )
            * score_scale
        )
        value_part = jnp.einsum(
            "hbk,bhd->kd",
            weights.astype(jnp.bfloat16),
            block_grad,
            preferred_element_type=jnp.float32,
        )
        other_queries = query_two[first_row:last_row]
        other_grad = grad_two[first_row:last_row]
        scores_two = block_scores(other_queries, near_keys, allowed, score_scale)
        lifted_two = jnp.exp(scores_two - jnp.max(scores_two, axis=-1, keepdims=True))
        weights_two = lifted_two / jnp.sum(lifted_two, axis=-1, keepdims=True)
        grad_weights_two = jnp.einsum(
            "bhd,kd->hbk", other_grad, near_values, preferred_element_type=jnp.float32
        )
        row_dot_two = jnp.sum(weights_two * grad_weights_two, axis=-1, keepdims=True)
        grad_scores_two = (weights_two * (grad_weights_two - row_dot_two)).astype(jnp.bfloat16)
        key_part = (
            key_part
            + jnp.einsum(
                "hbk,bhd->kd", grad_scores_two, other_queries, preferred_element_type=jnp.float32
            )
            * score_scale
        )
        value_part = value_part + jnp.einsum(
            "hbk,bhd->kd",
            weights_two.astype(jnp.bfloat16),
            other_grad,
            preferred_element_type=jnp.float32,
        )
        key_grads = key_grads + jnp.pad(key_part, padding)
        value_grads = value_grads + jnp.pad(value_part, padding)
    return (jnp.concatenate(query_parts, axis=0), key_grads, value_grads)


def local(
    tokens,
    out_grad,
    query_two,
    grad_two,
    doc_split,
    attn_gain,
    mlp_gain,
    w_query,
    w_kv,
    w_out,
    w_gate,
    w_up,
    w_down,
):
    own_rows = tokens.shape[0]
    heads_here = w_query.shape[1] // HD
    block_rows = min(512, SEQ_LONG)
    score_scale = HD ** (-0.5)
    two_docs = doc_split[0]
    offset = lax.axis_index("tensor") * own_rows
    cosine, sine = phase_tables(two_docs)
    residual = tokens.astype(jnp.float32)
    attn_scale = lax.rsqrt(jnp.mean(residual * residual, axis=-1, keepdims=True) + EPSILON)
    attn_pre = residual * attn_scale
    normed_own = (attn_pre * attn_gain).astype(jnp.bfloat16)
    normed = lax.all_gather(normed_own, "tensor", axis=0, tiled=True)
    query_lin = jnp.dot(normed, w_query, preferred_element_type=jnp.float32)
    kv_lin = jnp.dot(normed, w_kv, preferred_element_type=jnp.float32)
    queries = rotate(
        query_lin.reshape(SEQ_LONG, heads_here, HD), cosine[:, None, :], sine[:, None, :]
    ).astype(jnp.bfloat16)
    key_rows = rotate(kv_lin[:, :HD], cosine, sine).astype(jnp.bfloat16)
    value_rows = kv_lin[:, HD:].astype(jnp.bfloat16)
    context, row_maxes, row_sums = attend(
        queries, key_rows, value_rows, two_docs, block_rows, score_scale
    )
    context = context.reshape(SEQ_LONG, heads_here * HD).astype(jnp.bfloat16)
    branch = lax.psum_scatter(
        jnp.dot(context, w_out, preferred_element_type=jnp.float32).astype(jnp.bfloat16),
        "tensor",
        scatter_dimension=0,
        tiled=True,
    ).astype(jnp.float32)
    hidden = residual + branch
    mlp_scale = lax.rsqrt(jnp.mean(hidden * hidden, axis=-1, keepdims=True) + EPSILON)
    mlp_pre = hidden * mlp_scale
    hidden_own = (mlp_pre * mlp_gain).astype(jnp.bfloat16)
    hidden_normed = lax.all_gather(hidden_own, "tensor", axis=0, tiled=True)
    gate = jnp.dot(hidden_normed, w_gate, preferred_element_type=jnp.float32)
    upward = jnp.dot(hidden_normed, w_up, preferred_element_type=jnp.float32)
    sigma = jax.nn.sigmoid(gate)
    swish = gate * sigma
    activated = (swish * upward).astype(jnp.bfloat16)
    mlp_out = lax.psum_scatter(
        jnp.dot(activated, w_down, preferred_element_type=jnp.float32).astype(jnp.bfloat16),
        "tensor",
        scatter_dimension=0,
        tiled=True,
    ).astype(jnp.float32)
    block_output = (hidden + mlp_out).astype(jnp.bfloat16)
    grad_full = lax.all_gather(out_grad, "tensor", axis=0, tiled=True)
    down_w_grad = jnp.einsum("tf,td->fd", activated, grad_full, preferred_element_type=jnp.float32)
    grad_act = jnp.einsum("td,fd->tf", grad_full, w_down, preferred_element_type=jnp.float32)
    grad_gate = (grad_act * upward * sigma * (1.0 + gate * (1.0 - sigma))).astype(jnp.bfloat16)
    grad_up = (grad_act * swish).astype(jnp.bfloat16)
    gate_w_grad = jnp.einsum(
        "td,tf->df", hidden_normed, grad_gate, preferred_element_type=jnp.float32
    )
    up_w_grad = jnp.einsum("td,tf->df", hidden_normed, grad_up, preferred_element_type=jnp.float32)
    grad_hn = lax.psum_scatter(
        (
            jnp.einsum("tf,df->td", grad_gate, w_gate, preferred_element_type=jnp.float32)
            + jnp.einsum("tf,df->td", grad_up, w_up, preferred_element_type=jnp.float32)
        ).astype(jnp.bfloat16),
        "tensor",
        scatter_dimension=0,
        tiled=True,
    ).astype(jnp.float32)
    mlp_gain_part = jnp.sum(grad_hn * mlp_pre, axis=0)
    scaled_mlp = grad_hn * mlp_gain
    grad_hidden = out_grad.astype(jnp.float32) + mlp_scale * (
        scaled_mlp - mlp_pre * jnp.mean(scaled_mlp * mlp_pre, axis=-1, keepdims=True)
    )
    branch_own = grad_hidden.astype(jnp.bfloat16)
    branch_full = lax.all_gather(branch_own, "tensor", axis=0, tiled=True)
    out_w_grad = jnp.einsum("tc,td->cd", context, branch_full, preferred_element_type=jnp.float32)
    grad_context = jnp.einsum(
        "td,cd->tc", branch_full, w_out, preferred_element_type=jnp.float32
    ).astype(jnp.bfloat16)
    grad_context = grad_context.reshape(SEQ_LONG, heads_here, HD)
    other_queries = query_two.reshape(SEQ_LONG, heads_here, HD)
    other_grads = grad_two.reshape(SEQ_LONG, heads_here, HD)
    grad_rot_q, grad_rot_k, grad_values = attend_back(
        queries,
        key_rows,
        value_rows,
        grad_context,
        other_queries,
        other_grads,
        two_docs,
        row_maxes,
        row_sums,
        block_rows,
        score_scale,
    )
    grad_rot_k, grad_values = (
        lax.psum(grad_rot_k.astype(jnp.bfloat16), "tensor").astype(jnp.float32),
        lax.psum(grad_values.astype(jnp.bfloat16), "tensor").astype(jnp.float32),
    )
    kv_grad_lin = jnp.concatenate([unrotate(grad_rot_k, cosine, sine), grad_values], axis=1).astype(
        jnp.bfloat16
    )
    query_grad_lin = (
        unrotate(grad_rot_q, cosine[:, None, :], sine[:, None, :])
        .reshape(SEQ_LONG, heads_here * HD)
        .astype(jnp.bfloat16)
    )
    query_w_grad = jnp.einsum(
        "td,tc->dc", normed, query_grad_lin, preferred_element_type=jnp.float32
    )
    grad_normed = lax.psum_scatter(
        jnp.einsum("tc,dc->td", query_grad_lin, w_query, preferred_element_type=jnp.float32).astype(
            jnp.bfloat16
        ),
        "tensor",
        scatter_dimension=0,
        tiled=True,
    ).astype(jnp.float32)
    kv_own = lax.dynamic_slice_in_dim(kv_grad_lin, offset, own_rows, 0)
    grad_normed = grad_normed + jnp.einsum(
        "tc,dc->td", kv_own, w_kv, preferred_element_type=jnp.float32
    )
    kv_w_part = jnp.einsum("td,tc->dc", normed_own, kv_own, preferred_element_type=jnp.float32)
    attn_gain_part = jnp.sum(grad_normed * attn_pre, axis=0)
    scaled_attn = grad_normed * attn_gain
    tokens_grad = (
        grad_hidden
        + attn_scale
        * (scaled_attn - attn_pre * jnp.mean(scaled_attn * attn_pre, axis=-1, keepdims=True))
    ).astype(jnp.bfloat16)
    query_w_grad, out_w_grad, gate_w_grad, up_w_grad, down_w_grad = (
        lax.psum(query_w_grad.astype(jnp.bfloat16), "dp").astype(jnp.float32),
        lax.psum(out_w_grad.astype(jnp.bfloat16), "dp").astype(jnp.float32),
        lax.psum(gate_w_grad.astype(jnp.bfloat16), "dp").astype(jnp.float32),
        lax.psum(up_w_grad.astype(jnp.bfloat16), "dp").astype(jnp.float32),
        lax.psum(down_w_grad.astype(jnp.bfloat16), "dp").astype(jnp.float32),
    )
    kv_w_grad, attn_gain_grad, mlp_gain_grad = lax.psum(
        (kv_w_part, attn_gain_part, mlp_gain_part), ("dp", "tensor")
    )
    return (
        block_output,
        tokens_grad,
        attn_gain_grad,
        mlp_gain_grad,
        query_w_grad,
        kv_w_grad,
        out_w_grad,
        gate_w_grad,
        up_w_grad,
        down_w_grad,
    )


def solution(mesh):
    return jax.shard_map(
        local,
        mesh=mesh,
        in_specs=(
            P(("dp", "tensor"), None),
            P(("dp", "tensor"), None),
            P("dp", "tensor"),
            P("dp", "tensor"),
            P("dp"),
            P(),
            P(),
            P(None, "tensor"),
            P(),
            P("tensor", None),
            P(None, "tensor"),
            P(None, "tensor"),
            P("tensor", None),
        ),
        out_specs=(
            P(("dp", "tensor"), None),
            P(("dp", "tensor"), None),
            P(),
            P(),
            P(None, "tensor"),
            P(),
            P("tensor", None),
            P(None, "tensor"),
            P(None, "tensor"),
            P("tensor", None),
        ),
        check_vma=False,
    )
```

profile of v0, /device:TPU:0, one launch (start us, length us, event | category | flops | bytes accessed | tf_op | source)
XLA Modules:
  0.0 1366.6 jit_solution(2029983769829980237)
XLA Ops:
  18.4 78.5 %all-gather.5.cloned.1.call-done = bf16[2048,2048]{1,0:T(8,128)(2,1)} async-done(((bf16[256,2048]{1,0:T(8,128)(2,1)}), bf16[2048,2048]{1,0:T(8,128)(2,1)}) %all-gather.5.cloned.1.call-update) | async-done | bytes 8388624 | tf_op jit(solution)/shard_map/all_gather | solution.py:180
  96.9 7.0 fusion.316
  103.9 3.6 fusion.198
  113.8 6.0 fusion.339
  121.2 3.2 copy.232
  127.5 3.3 subtract_convert_fusion.1
  132.9 3.3 fusion.330
  139.2 6.8 fusion.322
  146.0 5.6 fusion.161
  151.6 5.1 fusion.325
  156.7 3.4 fusion.157
  160.1 8.1 fusion.317
  168.2 4.4 fusion.158
  173.9 5.7 convolution_convert_fusion.2
  179.6 88.3 %reduce-scatter.5.cloned.1.call-done = bf16[256,2048]{1,0:T(8,128)(2,1)} async-done(((bf16[2048,2048]{1,0:T(8,128)(2,1)}), bf16[256,2048]{1,0:T(8,128)(2,1)}) %reduce-scatter.5.cloned.1.call-update) | async-done | bytes 1048592 | tf_op jit(solution)/shard_map/reduce_scatter | solution.py:192
  273.4 79.9 %all-gather.7.cloned.1.call-done = bf16[2048,2048]{1,0:T(8,128)(2,1)} async-done(((bf16[256,2048]{1,0:T(8,128)(2,1)}), bf16[2048,2048]{1,0:T(8,128)(2,1)}) %all-gather.7.cloned.1.call-update) | async-done | bytes 8388624 | tf_op jit(solution)/shard_map/all_gather | solution.py:202
  353.3 11.4 fusion.340
  364.7 8.0 fusion.341
  372.7 62.7 %all-gather.9.cloned.1.call-done = bf16[2048,2048]{1,0:T(8,128)(2,1)} async-done(((bf16[256,2048]{1,0:T(8,128)(2,1)}), bf16[2048,2048]{1,0:T(8,128)(2,1)}) %all-gather.9.cloned.1.call-update) | async-done | bytes 8388624 | tf_op jit(solution)/shard_map/all_gather | solution.py:215
  435.4 14.6 %multiply_convert_fusion = (bf16[2048,704]{0,1:T(8,128)(2,1)S(1)}, bf16[2048,704]{0,1:T(8,128)(2,1)S(1)}, bf16[2048,704]{0,1:T(8,128)(2,1)}) fusion(f32[2048,704]{0,1:T(8,128)} %fusion.340, f32[2048,704]{0,1:T(8,128)} %fusion.341, bf16[2048,2048]{1,0:T(8,128)(2,1)} %all-gather.9.cloned.1.call-done, bf16[704,2048]{1,0:T(8,128)(2,1)S(1)} %copy-done), kind=kOutput, calls=%fused_computation.42 | convolution fusion | flops 5927206912 | bytes 31457280 | tf_op jit(solution)/shard_map/td,fd->tf/dot_general | solution.py:217
  450.0 10.7 fusion.342
  460.7 12.5 add_convert_fusion
  473.4 88.3 %reduce-scatter.9.cloned.1.call-done = bf16[256,2048]{1,0:T(8,128)(2,1)} async-done(((bf16[2048,2048]{1,0:T(8,128)(2,1)}), bf16[256,2048]{1,0:T(8,128)(2,1)}) %reduce-scatter.9.cloned.1.call-update) | async-done | bytes 1048592 | tf_op jit(solution)/shard_map/reduce_scatter | solution.py:224
  561.6 3.5 fusion.102
  565.8 3.3 fusion.291
  588.2 3.3 fusion.338
  594.5 3.6 fusion.113
  598.1 3.9 convolution_bitcast_fusion.8
  601.9 5.0 fusion.337
  606.9 6.5 fusion.336
  613.4 8.2 fusion.331
  621.6 4.0 fusion.140
  629.1 4.2 fusion.16
  635.6 5.6 fusion.8
  641.3 7.5 convolution_convert_fusion.3
  648.7 7.4 convolution_convert_fusion.4
  656.2 7.8 convolution_convert_fusion.5
  664.0 6.1 convolution_convert_fusion.8
  671.0 6.7 fusion.19
  677.7 6.5 fusion.21
  697.5 5.5 convolution_bitcast_fusion.1
  720.6 3.6 fusion.149
  727.2 3.9 fusion.150
  731.2 5.7 fusion.75
  736.8 8.0 fusion.81
  744.9 6.2 fusion.95
  751.2 8.8 fusion.96
  760.0 7.1 convolution_convert_fusion.6
  767.2 6.9 convolution_convert_fusion.7
  774.2 7.2 convolution_convert_fusion
  781.5 10.9 convolution_convert_fusion.1
  792.5 24.8 %all-reduce.15.cloned.1.call-done = (bf16[2048,128]{1,0:T(8,128)(2,1)}, bf16[2048,128]{0,1:T(8,128)(2,1)}) async-done(((bf16[2048,128]{1,0:T(8,128)(2,1)}, bf16[2048,128]{0,1:T(8,128)(2,1)}), (bf16[2048,128]{1,0:T(8,128)(2,1)}, bf16[2048,128]{0,1:T(8,128)(2,1)})) %all-reduce.15.cloned.1.call-update) | async-done | bytes 1048592 | tf_op jit(solution)/shard_map/psum | solution.py:262
  818.5 3.2 fusion.202
  824.9 3.2 fusion.293
  828.1 206.4 %all-reduce.17.cloned.1.call-done = (bf16[2048,256]{1,0:T(8,128)(2,1)}, bf16[256,2048]{1,0:T(8,128)(2,1)}, bf16[2048,704]{0,1:T(8,128)(2,1)}, bf16[2048,704]{0,1:T(8,128)(2,1)}, bf16[704,2048]{1,0:T(8,128)(2,1)}) async-done(((bf16[2048,256]{1,0:T(8,128)(2,1)}, bf16[256,2048]{1,0:T(8,128)(2,1)}, bf16[2048,704]{0,1:T(8,128)(2,1)}, bf16[2048,704]{0,1:T(8,128)(2,1)}, bf16[704,2048]{1,0:T(8,128)(2,1)}), ...) | async-done | bytes 10747920 | tf_op jit(solution)/shard_map/psum | solution.py:296
  1034.4 5.3 convert_element_type.223
  1039.7 3.3 convert_element_type.225
  1043.0 3.3 convert_element_type.227
  1049.4 77.7 %reduce-scatter.11.cloned.1.call-done = bf16[256,2048]{1,0:T(8,128)(2,1)} async-done(((bf16[2048,2048]{1,0:T(8,128)(2,1)}), bf16[256,2048]{1,0:T(8,128)(2,1)}) %reduce-scatter.11.cloned.1.call-update) | async-done | bytes 1048592 | tf_op jit(solution)/shard_map/reduce_scatter | solution.py:275
  1127.2 4.1 fusion.109
  1131.3 39.6 %all-reduce.6 = (f32[2048]{0:T(1024)}, f32[2048]{0:T(1024)}) all-reduce(f32[2048]{0:T(1024)S(1)} %get-tuple-element.12, f32[2048]{0:T(1024)S(1)} %copy-done.53), channel_id=1, replica_groups=mesh['dp'=4,'tensor'=8] {'dp','tensor'}, use_global_device_ids=true, to_apply=%region_35.36 | all-reduce | flops 4096 | bytes 32768 | tf_op jit(solution)/shard_map/psum | solution.py:302
  1170.9 47.6 %reduce-scatter.7.cloned.1.call-done = bf16[256,2048]{1,0:T(8,128)(2,1)} async-done(((bf16[2048,2048]{1,0:T(8,128)(2,1)}), bf16[256,2048]{1,0:T(8,128)(2,1)}) %reduce-scatter.7.cloned.1.call-update) | async-done | bytes 1048592 | tf_op jit(solution)/shard_map/reduce_scatter | solution.py:208
  1218.5 6.1 fusion.108
  1224.6 132.2 %all-reduce.13.cloned.1.call-done = f32[2048,256]{1,0:T(8,128)} async-done(((f32[2048,256]{1,0:T(8,128)}), f32[2048,256]{1,0:T(8,128)}) %all-reduce.13.cloned.1.call-update) | async-done | bytes 2097168 | tf_op jit(solution)/shard_map/psum | solution.py:302
  (293 shorter events, 107.1 us)
Async XLA Ops:
  7.2 428.2 %copy-start = (bf16[704,2048]{1,0:T(8,128)(2,1)S(1)}, bf16[704,2048]{1,0:T(8,128)(2,1)}, u32[]{:S(2)}) copy-start(bf16[704,2048]{1,0:T(8,128)(2,1)} %param.25) | copy-start | bytes 8650756
  7.2 89.7 %all-gather.5.cloned.1.call-start = ((), (), s32[]{:S(2)}) async-start(), calls=%async_computation.4 | async-start | bytes 9437184 | tf_op jit(solution)/shard_map/all_gather | solution.py:180
  12.0 255.9 %reduce-scatter.5.cloned.1.call-start = ((), (), s32[]{:S(2)}) async-start(), calls=%async_computation.5 | async-start | bytes 9437184 | tf_op jit(solution)/shard_map/reduce_scatter | solution.py:192
  12.7 91.2 %copy-start.68 = (f32[64]{0:T(128)}, f32[64]{0:T(128)S(1)}, u32[]{:S(2)}) copy-start(f32[64]{0:T(128)S(1)} %multiply_power_fusion) | copy-start | bytes 772
  12.8 91.1 %copy-start.50 = (f32[2048]{0:T(1024)}, f32[2048]{0:T(1024)S(1)}, u32[]{:S(2)}) copy-start(f32[2048]{0:T(1024)S(1)} %fusion.235) | copy-start | bytes 24580
  146.0 5.7 copy-start.66
  168.2 4.4 copy-start.45
  168.2 4.5 copy-start.46
  168.2 4.5 copy-start.47
  168.2 5.6 copy-start.21
  179.5 90.3 %copy-start.48 = (f32[2048]{0:T(1024)S(1)}, f32[2048]{0:T(1024)}, u32[]{:S(2)}) copy-start(f32[2048]{0:T(1024)} %param.19) | copy-start | bytes 24580
  179.6 173.8 %all-gather.7.cloned.1.call-start = ((), (), s32[]{:S(2)}) async-start(), calls=%async_computation.6 | async-start | bytes 9437184 | tf_op jit(solution)/shard_map/all_gather | solution.py:202
  269.9 295.3 %copy-start.54 = (f32[256]{0:T(256)}, f32[256]{0:T(256)S(1)}, u32[]{:S(2)}) copy-start(f32[256]{0:T(256)S(1)} %add_rsqrt_fusion) | copy-start | bytes 3076
  272.8 162.6 %all-gather.9.cloned.1.call-start = ((), (), s32[]{:S(2)}) async-start(), calls=%async_computation.8 | async-start | bytes 9437184 | tf_op jit(solution)/shard_map/all_gather | solution.py:215
  273.4 288.2 %reduce-scatter.9.cloned.1.call-start = ((), (), s32[]{:S(2)}) async-start(), calls=%async_computation.9 | async-start | bytes 9437184 | tf_op jit(solution)/shard_map/reduce_scatter | solution.py:224
  353.3 11.4 copy-start.70
  353.3 11.4 copy-start.72
  435.4 14.6 %copy-start.71 = (bf16[2048,704]{0,1:T(8,128)(2,1)S(1)}, bf16[2048,704]{0,1:T(8,128)(2,1)}, u32[]{:S(2)}) copy-start(bf16[2048,704]{0,1:T(8,128)(2,1)} %param.23) | copy-start | bytes 8650756
  450.0 10.7 copy-start.77
  450.0 10.7 copy-start.79
  450.0 10.7 copy-start.73
  473.3 190.7 %all-gather.11.cloned.1.call-start = ((), (), s32[]{:S(2)}) async-start(), calls=%async_computation.10 | async-start | bytes 9437184 | tf_op jit(solution)/shard_map/all_gather | solution.py:239
  569.1 248.2 %all-reduce.15.cloned.1.call-start = ((), (), s32[]{:S(2)}) async-start(), calls=%async_computation.13 | async-start | bytes 2097152 | tf_op jit(solution)/shard_map/psum | solution.py:262
  621.6 14.0 %copy-start.83 = (f32[2,512]{1,0:T(2,128)}, f32[2,512]{1,0:T(2,128)S(1)}, u32[]{:S(2)}) copy-start(f32[2,512]{1,0:T(2,128)S(1)} %get-tuple-element.72) | copy-start | bytes 12292
  626.5 6.8 slice-start.8
  633.4 7.9 slice-start.2
  635.6 5.6 slice-start.3
  635.6 5.6 copy-start.80
  641.2 7.5 copy-start.78
  641.3 14.9 %slice-start.4 = ((s8[8388608]{0:T(1024)(128)(4,1)}), s8[4194304]{0:T(1024)(128)(4,1)S(1)}, s32[]{:S(2)}) async-start(s8[8388608]{0:T(1024)(128)(4,1)} %bitcast.504), calls=%async_computation.19 | async-start | bytes 8388608
  648.7 7.4 slice-start.5
  648.7 7.4 copy-start.81
  664.0 7.0 copy-start.67
  664.0 7.0 copy-start.76
  671.0 6.8 copy-start.43
  671.0 17.5 %copy-start.38 = (bf16[512,256]{0,1:T(8,128)(2,1)}, bf16[512,256]{0,1:T(8,128)(2,1)S(1)}, u32[]{:S(2)}) copy-start(bf16[512,256]{0,1:T(8,128)(2,1)S(1)} %get-tuple-element.49) | copy-start | bytes 786436
  671.0 17.5 %slice-start = ((s8[8388608]{0:T(1024)(128)(4,1)}), s8[4194304]{0:T(1024)(128)(4,1)S(1)}, s32[]{:S(2)}) async-start(s8[8388608]{0:T(1024)(128)(4,1)} %bitcast.469), calls=%async_computation.15 | async-start | bytes 8388608
  677.7 6.5 copy-start.20
  677.7 10.8 slice-start.1
  697.5 5.5 copy-start.41
  697.5 5.5 copy-start.63
  731.2 5.7 copy-start.85
  736.8 8.0 copy-start.39
  744.8 6.3 copy-start.25
  744.8 6.3 copy-start.28
  744.8 6.3 copy-start.30
  744.8 6.3 copy-start.31
  744.8 6.3 copy-start.82
  744.9 6.3 copy-start.84
  744.9 6.3 copy-start.86
  760.0 274.5 %all-reduce.17.cloned.1.call-start = ((), (), s32[]{:S(2)}) async-start(), calls=%async_computation.14 | async-start | bytes 21495808 | tf_op jit(solution)/shard_map/psum | solution.py:296
  760.0 7.1 copy-start.12
  774.1 353.1 %reduce-scatter.11.cloned.1.call-start = ((), (), s32[]{:S(2)}) async-start(), calls=%async_computation.11 | async-start | bytes 9437184 | tf_op jit(solution)/shard_map/reduce_scatter | solution.py:275
  781.4 437.1 %reduce-scatter.7.cloned.1.call-start = ((), (), s32[]{:S(2)}) async-start(), calls=%async_computation.7 | async-start | bytes 9437184 | tf_op jit(solution)/shard_map/reduce_scatter | solution.py:208
  792.4 26.0 %copy-start.51 = (f32[2048]{0:T(1024)S(1)}, f32[2048]{0:T(1024)}, u32[]{:S(2)}) copy-start(f32[2048]{0:T(1024)} %copy-done.50) | copy-start | bytes 24580
  792.4 26.0 %copy-start.69 = (f32[64]{0:T(128)S(1)}, f32[64]{0:T(128)}, u32[]{:S(2)}) copy-start(f32[64]{0:T(128)} %copy-done.68) | copy-start | bytes 772
  792.4 564.4 %all-reduce.13.cloned.1.call-start = ((), (), s32[]{:S(2)}) async-start(), calls=%async_computation.12 | async-start | bytes 4194304 | tf_op jit(solution)/shard_map/psum | solution.py:302
  1034.4 5.3 copy-start.16
  1046.3 80.8 %copy-start.52 = (f32[2048]{0:T(1024)S(1)}, f32[2048]{0:T(1024)}, u32[]{:S(2)}) copy-start(f32[2048]{0:T(1024)} %param.18) | copy-start | bytes 24580
  1046.3 80.8 %copy-start.57 = (f32[256]{0:T(256)S(1)}, f32[256]{0:T(256)}, u32[]{:S(2)}) copy-start(f32[256]{0:T(256)} %copy-done.56) | copy-start | bytes 3076
  1049.4 81.9 %copy-start.53 = (f32[2048]{0:T(1024)S(1)}, f32[2048]{0:T(1024)}, u32[]{:S(2)}) copy-start(f32[2048]{0:T(1024)} %get-tuple-element.10) | copy-start | bytes 24580
  1049.4 169.1 %copy-start.49 = (f32[2048]{0:T(1024)S(1)}, f32[2048]{0:T(1024)}, u32[]{:S(2)}) copy-start(f32[2048]{0:T(1024)} %param.19) | copy-start | bytes 24580
  1049.4 169.1 %copy-start.55 = (f32[256]{0:T(256)S(1)}, f32[256]{0:T(256)}, u32[]{:S(2)}) copy-start(f32[256]{0:T(256)} %copy-done.54) | copy-start | bytes 3076
  1049.4 169.1 %copy-start.59 = (f32[256]{0:T(256)S(1)}, f32[256]{0:T(256)}, u32[]{:S(2)}) copy-start(f32[256]{0:T(256)} %copy-done.58) | copy-start | bytes 3076
  (44 other events, 121.0 us)
Sparse Core Ops, SparseCore 0:
  12.1 84.7 all-gather.4
  179.7 88.1 reduce-scatter.4
  272.9 80.3 all-gather.6
  354.8 80.5 all-gather.8
  473.4 88.1 reduce-scatter.8
  569.2 80.3 all-gather.10
  760.1 57.1 all-reduce.14
  822.8 211.6 all-reduce.16
  1036.8 90.2 reduce-scatter.10
  1129.4 89.0 reduce-scatter.6
  1224.7 132.1 all-reduce.12
where the time goes:
time: 1370 us
  waiting for transfers between devices  887 us (65%)
  matrix products  306 us (22%)
  other arithmetic  69.8 us (5%)
  local copies, waits for them, and re-layouts  48.2 us (4%)
  blocking collectives  39.6 us (3%)
  between operations  15.6 us (1%)
    psum x1, waiting for transfers between devices, local(): lax.psum(query_w_grad.astype(jnp.bfloat16), 'dp').astype(jnp.float32)  206 us
    psum x1, waiting for transfers between devices, local(): lax.psum((kv_w_part, attn_gain_part, mlp_gain_part), ('dp', 'tensor'))  132 us
    reduce_scatter x1, waiting for transfers between devices, local(): lax.psum_scatter(jnp.dot(context, w_out, preferred_element_type=jnp.float...  88.3 us
    reduce_scatter x1, waiting for transfers between devices, local(): lax.psum_scatter((jnp.einsum('tf,df->td', grad_gate, w_gate, preferred_el...  88.3 us
    all_gather x1, waiting for transfers between devices, local(): hidden_normed = lax.all_gather(hidden_own, 'tensor', axis=0, tiled=True)  79.9 us
    all_gather x1, waiting for transfers between devices, local(): normed = lax.all_gather(normed_own, 'tensor', axis=0, tiled=True)  78.5 us
    reduce_scatter x1, waiting for transfers between devices, local(): lax.psum_scatter(jnp.einsum('tc,dc->td', query_grad_lin, w_query, preferr...  77.7 us
    all_gather x1, waiting for transfers between devices, local(): grad_full = lax.all_gather(out_grad, 'tensor', axis=0, tiled=True)  62.7 us
  transfers between devices with their start and end apart: 11, of which 10 were waited for; matrix products, arithmetic and copies ran while one was open for 14% of the time, Pallas kernels for 0%

commit v1 on v0

v1 whole, which is shorter than its diff:
```python
import functools

import jax
import jax.numpy as jnp
from jax import lax
from jax.experimental import pallas as pl
from jax.experimental.pallas import tpu as pltpu
from jax.sharding import PartitionSpec as P

HD = 128
SEQ_SHORT = 1024
EPSILON = 1e-05
MASKED = -1e30
SCALE = HD ** (-0.5)
SCALE2 = SCALE * 1.4426950408889634
F32 = jnp.float32
BF16 = jnp.bfloat16
VMEM_LIMIT = 56 * 2**20


def mm(left, right, dims):
    return lax.dot_general(left, right, (dims, ((), ())), preferred_element_type=F32)


NN = ((1,), (0,))
NT = ((1,), (1,))
TN = ((0,), (0,))


class Links:
    def __init__(self, n_tensor, n_dp):
        self.n_tensor, self.n_dp = n_tensor, n_dp
        self.chips = n_tensor // 2
        odd = list(range(1, self.chips, 2))
        even = list(range(2, self.chips, 2))
        self.order = [0] + odd + even[::-1]
        nxt = {c: self.order[(i + 1) % self.chips] for i, c in enumerate(self.order)}
        self.place = [self.order.index(c) for c in range(self.chips)]
        self.ring_pairs = [(2 * c + k, 2 * nxt[c] + k) for c in range(self.chips) for k in (0, 1)]
        self.swap_pairs = [(i, i ^ 1) for i in range(n_tensor)]
        self.bits = [1 << b for b in range(n_dp.bit_length() - 1)]

    def ring(self, x):
        return lax.ppermute(x, "tensor", self.ring_pairs)

    def swap(self, x):
        return lax.ppermute(x, "tensor", self.swap_pairs)

    def across(self, x, bit):
        return lax.ppermute(x, "dp", [(i, i ^ bit) for i in range(self.n_dp)])

    def across_tensor(self, x, bit):
        return lax.ppermute(x, "tensor", [(i, i ^ bit) for i in range(self.n_tensor)])

    def orders(self, rows, unit):
        ways = len(self.bits)
        if ways < 2 or rows % (ways * unit):
            return [self.bits]
        return [self.bits[i:] + self.bits[:i] for i in range(ways)]


def take_rows(x, index, size):
    return lax.dynamic_slice_in_dim(x, index * size, size, 0)


def gather_dp(links, piece, me):
    orders = links.orders(piece.shape[0], 8)
    part_rows = piece.shape[0] // len(orders)
    parts = []
    for number, bits in enumerate(orders):
        stack = lax.slice_in_dim(piece, number * part_rows, (number + 1) * part_rows, axis=0)
        held = [0]
        for bit in bits:
            stack = jnp.concatenate([stack, links.across(stack, bit)], axis=0)
            held = held + [h ^ bit for h in held]
        where = jnp.array([held.index(rel) for rel in range(links.n_dp)], jnp.int32)
        parts.append((stack, where))
    out = []
    for j in range(links.n_dp):
        for stack, where in parts:
            out.append(take_rows(stack, where[me ^ j], part_rows))
    return jnp.concatenate(out, axis=0)


def gather_weight(links, block, me):
    rows = block.shape[0] // links.n_dp
    blocks = [block]
    piece = take_rows(block, me, rows)
    for _ in range(links.chips - 1):
        piece = links.ring(piece)
        blocks.append(gather_dp(links, piece, me))
    return blocks


def sum_dp(links, x, me):
    orders = links.orders(x.shape[0], 8 * links.n_dp)
    part_rows = x.shape[0] // len(orders)
    size = part_rows // links.n_dp
    outs = []
    for number, bits in enumerate(orders):
        held = lax.slice_in_dim(x, number * part_rows, (number + 1) * part_rows, axis=0)
        pieces = [held.reshape((links.n_dp, size) + x.shape[1:])]
        array = pieces[0]
        axes = [links.n_dp]
        nbits = len(links.bits)
        array = array.reshape((2,) * nbits + (size,) + x.shape[1:])
        left = list(reversed(links.bits))
        for bit in bits:
            axis = left.index(bit)
            mine = jnp.minimum(me & bit, 1)
            keep = lax.dynamic_index_in_dim(array, mine, axis, keepdims=False)
            send = lax.dynamic_index_in_dim(array, 1 - mine, axis, keepdims=False)
            got = links.across(send, bit)
            array = (keep.astype(F32) + got.astype(F32)).astype(BF16)
            left.remove(bit)
        stack = array.reshape((size,) + x.shape[1:])
        rel = [0]
        for bit in reversed(bits):
            stack = jnp.concatenate([stack, links.across(stack, bit)], axis=0)
            rel = rel + [r ^ bit for r in rel]
        where = jnp.array([rel.index(r) for r in range(links.n_dp)], jnp.int32)
        for j in range(links.n_dp):
            outs.append(take_rows(stack, where[me ^ j], size))
    return jnp.concatenate(outs, axis=0).astype(F32)


def ring_gather(links, own):
    out = [own]
    for _ in range(links.chips - 1):
        out.append(links.ring(out[-1]))
    return out


def ring_scatter(links, terms):
    got = None
    for term in terms[1:] + terms[:1]:
        total = term if got is None else term.astype(F32) + got.astype(F32)
        if term is terms[0]:
            return total.astype(F32)
        got = links.ring(total.astype(BF16))
    return got


def both(links, own):
    return jnp.concatenate([own, links.swap(own)], axis=0)


def pair_sum(links, part):
    rows = part.shape[0] // 2
    return part[:rows].astype(F32) + links.swap(part[rows:].astype(BF16)).astype(F32)


def sum_all(links, x):
    bit = 1
    while bit < links.n_tensor:
        x = x + links.across_tensor(x, bit)
        bit *= 2
    for bit in links.bits:
        x = x + links.across(x, bit)
    return x


def diagonal(shape, row_axis, shift):
    size = shape[row_axis]
    row = lax.broadcasted_iota(jnp.int32, shape, row_axis) + shift
    row = jnp.where(row >= size, row - size, row)
    return lax.broadcasted_iota(jnp.int32, shape, 1 - row_axis) <= row


def span(block, two_docs, rows):
    per_doc = SEQ_SHORT // rows
    inner = jnp.where(two_docs > 0, lax.rem(block, per_doc), block)
    return inner + 1, pl.multiple_of((block - inner) * rows, rows)


def fwd_kernel(blocks, sp_ref, q_ref, c_ref, s_ref, k_ref, v_ref, qo_ref, ctx_ref, lse_ref):
    rows = q_ref.shape[0]
    chip, two_docs, core = sp_ref[0], sp_ref[1], sp_ref[2]
    x = q_ref[...]
    q = (x * c_ref[...] + pltpu.roll(x, HD // 2, 1) * s_ref[...]).astype(BF16)
    qo_ref[...] = q
    count, low = span(chip, two_docs, rows)
    mask = diagonal((rows, rows), 0, core * (rows // 2))
    for n in range(1, blocks + 1):

        @pl.when(count == n)
        def _(n=n):
            near = (n - 1) * rows
            diag = pl.ds(low + near, rows)
            s_diag = jnp.where(mask, mm(q, k_ref[diag, :], NT) * SCALE2, MASKED)
            top = jnp.max(s_diag, axis=1, keepdims=True)
            if n > 1:
                main = pl.ds(low, near)
                s_main = mm(q, k_ref[main, :], NT) * SCALE2
                top = jnp.maximum(top, jnp.max(s_main, axis=1, keepdims=True))
            p_diag = jnp.exp2(s_diag - top)
            total = jnp.sum(p_diag, axis=1, keepdims=True)
            out = mm(p_diag.astype(BF16), v_ref[diag, :], NN)
            if n > 1:
                p_main = jnp.exp2(s_main - top)
                total = total + jnp.sum(p_main, axis=1, keepdims=True)
                out = out + mm(p_main.astype(BF16), v_ref[main, :], NN)
            ctx_ref[...] = (out / total).astype(BF16)
            lse = jnp.broadcast_to(top + jnp.log2(total), (rows, HD))
            lse_ref[0] = lse.T[:8]


def bwd_kernel(
    blocks, sp_ref, q_ref, do_ref, ctx_ref, lse_ref, c_ref, s_ref, k_ref, kt_ref, v_ref, dk0_ref, dv0_ref,
    dq_ref, dk_ref, dv_ref,
):
    rows = q_ref.shape[0]
    chip, two_docs, core = sp_ref[0], sp_ref[1], sp_ref[2]

    @pl.when(pl.program_id(0) == 0)
    def _():
        dk_ref[...] = dk0_ref[...]
        dv_ref[...] = dv0_ref[...]

    q, do = q_ref[...], do_ref[...]
    dot = jnp.sum(do.astype(F32) * ctx_ref[...].astype(F32), axis=1, keepdims=True)
    dot = jnp.broadcast_to(dot, (rows, HD)).T[:1]
    lse = lse_ref[0, :1]
    count, low = span(chip, two_docs, rows)
    mask = diagonal((rows, rows), 1, core * (rows // 2))
    for n in range(1, blocks + 1):

        @pl.when(count == n)
        def _(n=n):
            near = (n - 1) * rows
            dqt = jnp.zeros((HD, rows), F32)
            for keys, masked in ((pl.ds(low, near), False), (pl.ds(low + near, rows), True)):
                if not masked and n == 1:
                    continue
                p = jnp.exp2(mm(k_ref[keys, :], q, NT) * SCALE2 - lse)
                if masked:
                    p = jnp.where(mask, p, 0.0)
                ds = (p * (mm(v_ref[keys, :], do, NT) - dot)).astype(BF16)
                dv_ref[keys, :] += mm(p.astype(BF16), do, NN)
                dk_ref[keys, :] += mm(ds, q, NN)
                dqt = dqt + mm(kt_ref[:, keys], ds, NN)
            g = dqt.T * SCALE
            dq_ref[...] = (g * c_ref[...] - pltpu.roll(g, HD // 2, 1) * s_ref[...]).astype(BF16)


def second_kernel(blocks, sp_ref, q_ref, do_ref, k_ref, v_ref, dk_ref, dv_ref):
    rows = q_ref.shape[0]
    block, two_docs = pl.program_id(0), sp_ref[1]

    @pl.when((block == 0) & (pl.program_id(1) == 0))
    def _():
        dk_ref[...] = jnp.zeros_like(dk_ref)
        dv_ref[...] = jnp.zeros_like(dv_ref)

    q, do = q_ref[...], do_ref[...]
    count, low = span(block, two_docs, rows)
    mask = diagonal((rows, rows), 1, 0)
    for n in range(1, blocks + 1):

        @pl.when(count == n)
        def _(n=n):
            near = (n - 1) * rows
            parts = [pl.ds(low + near, rows)] + ([pl.ds(low, near)] if n > 1 else [])
            scores = [mm(k_ref[keys, :], q, NT) * SCALE2 for keys in parts]
            scores[0] = jnp.where(mask, scores[0], MASKED)
            top = functools.reduce(jnp.maximum, [jnp.max(s, axis=0, keepdims=True) for s in scores])
            lifted = [jnp.exp2(s - top) for s in scores]
            total = sum(jnp.sum(p, axis=0, keepdims=True) for p in lifted)
            inverse = 1.0 / total
            back = [mm(v_ref[keys, :], do, NT) for keys in parts]
            dot = sum(jnp.sum(p * b, axis=0, keepdims=True) for p, b in zip(lifted, back)) * inverse
            for keys, p, b in zip(parts, lifted, back):
                p = p * inverse
                dv_ref[keys, :] += mm(p.astype(BF16), do, NN)
                dk_ref[keys, :] += mm((p * (b - dot)).astype(BF16), q, NN)


def whole(shape):
    return pl.BlockSpec(shape, lambda *_: (0,) * len(shape))


def attend(sp, q_lin, cosine, sine, key_rows, value_rows):
    rows, width = q_lin.shape
    seq = key_rows.shape[0]
    heads = width // HD
    column = pl.BlockSpec((rows, HD), lambda h, *_: (0, h))
    return pl.pallas_call(
        functools.partial(fwd_kernel, seq // rows),
        grid_spec=pltpu.PrefetchScalarGridSpec(
            num_scalar_prefetch=1,
            grid=(heads,),
            in_specs=[column, whole((rows, HD)), whole((rows, HD)), whole((seq, HD)), whole((seq, HD))],
            out_specs=[column, column, pl.BlockSpec((1, 8, rows), lambda h, *_: (h, 0, 0))],
        ),
        out_shape=[
            jax.ShapeDtypeStruct((rows, width), BF16),
            jax.ShapeDtypeStruct((rows, width), BF16),
            jax.ShapeDtypeStruct((heads, 8, rows), F32),
        ],
        compiler_params=pltpu.CompilerParams(vmem_limit_bytes=VMEM_LIMIT),
        cost_estimate=pl.CostEstimate(
            flops=8 * heads * rows * seq * HD, bytes_accessed=16 * rows * width, transcendentals=heads * rows * seq
        ),
        name="attend",
    )(sp, q_lin, cosine, sine, key_rows, value_rows)


def attend_back(sp, queries, grad_context, context, lse, cosine, sine, key_rows, value_rows, dk0, dv0):
    rows, width = queries.shape
    seq = key_rows.shape[0]
    heads = width // HD
    column = pl.BlockSpec((rows, HD), lambda h, *_: (0, h))
    return pl.pallas_call(
        functools.partial(bwd_kernel, seq // rows),
        grid_spec=pltpu.PrefetchScalarGridSpec(
            num_scalar_prefetch=1,
            grid=(heads,),
            in_specs=[
                column, column, column, pl.BlockSpec((1, 8, rows), lambda h, *_: (h, 0, 0)),
                whole((rows, HD)), whole((rows, HD)), whole((seq, HD)), whole((HD, seq)), whole((seq, HD)),
                whole((seq, HD)), whole((seq, HD)),
            ],
            out_specs=[column, whole((seq, HD)), whole((seq, HD))],
        ),
        out_shape=[
            jax.ShapeDtypeStruct((rows, width), BF16),
            jax.ShapeDtypeStruct((seq, HD), F32),
            jax.ShapeDtypeStruct((seq, HD), F32),
        ],
        compiler_params=pltpu.CompilerParams(vmem_limit_bytes=VMEM_LIMIT),
        cost_estimate=pl.CostEstimate(
            flops=20 * heads * rows * seq * HD, bytes_accessed=16 * rows * width, transcendentals=heads * rows * seq
        ),
        name="attend_back",
    )(sp, queries, grad_context, context, lse, cosine, sine, key_rows, key_rows.T, value_rows, dk0, dv0)


def second_back(sp, query_two, grad_two, key_rows, value_rows):
    seq, width = query_two.shape
    rows = min(512, SEQ_SHORT)
    heads = width // HD
    column = pl.BlockSpec((rows, HD), lambda i, h, *_: (i, h))
    return pl.pallas_call(
        functools.partial(second_kernel, seq // rows),
        grid_spec=pltpu.PrefetchScalarGridSpec(
            num_scalar_prefetch=1,
            grid=(seq // rows, heads),
            in_specs=[column, column, whole((seq, HD)), whole((seq, HD))],
            out_specs=[whole((seq, HD)), whole((seq, HD))],
        ),
        out_shape=[jax.ShapeDtypeStruct((seq, HD), F32), jax.ShapeDtypeStruct((seq, HD), F32)],
        compiler_params=pltpu.CompilerParams(vmem_limit_bytes=VMEM_LIMIT),
        cost_estimate=pl.CostEstimate(
            flops=8 * heads * seq * seq * HD, bytes_accessed=4 * seq * width, transcendentals=heads * seq * seq // 2
        ),
        name="second_back",
    )(sp, query_two, grad_two, key_rows, value_rows)


def rms_factor(values):
    return lax.rsqrt(jnp.mean(values * values, axis=-1, keepdims=True) + EPSILON)


def local(
    n_tensor, n_dp,
    tokens, out_grad, query_two, grad_two, doc_split, attn_gain, mlp_gain, w_query, w_kv, w_out, w_gate, w_up, w_down,
):
    links = Links(n_tensor, n_dp)
    chips = links.chips
    own = tokens.shape[0]
    rows = 2 * own
    seq = own * n_tensor
    width = w_query.shape[1]
    me_dp = lax.axis_index("dp")
    me_t = lax.axis_index("tensor")
    chip, core = me_t // 2, me_t % 2
    two_docs = doc_split[0]
    sp = jnp.stack([chip, two_docs, core]).astype(jnp.int32)
    place = jnp.array(links.place, jnp.int32)
    order = jnp.array(links.order, jnp.int32)

    spot = jnp.arange(rows, dtype=jnp.int32) + core * own
    spot = chip * rows + jnp.where(spot >= rows, spot - rows, spot)
    position = jnp.where(two_docs > 0, spot % SEQ_SHORT, spot)
    frequency = 10000.0 ** (-jnp.arange(HD // 2, dtype=F32) * 2.0 / HD)
    phases = position.astype(F32)[:, None] * frequency[None, :]
    cos, sin = jnp.cos(phases), jnp.sin(phases)
    cosine = jnp.concatenate([cos, cos], axis=1)
    sine = jnp.concatenate([-sin, sin], axis=1)

    residual = tokens.astype(F32)
    attn_scale = rms_factor(residual)
    attn_pre = residual * attn_scale
    normed_own = (attn_pre * attn_gain).astype(BF16)

    kv_lin = mm(normed_own, w_kv, NN)
    half = HD // 2
    key_lin = kv_lin[:, :HD]
    key_own = key_lin * cosine[:own] + jnp.concatenate([key_lin[:, half:], key_lin[:, :half]], axis=1) * sine[:own]
    kv_own = jnp.concatenate([key_own, kv_lin[:, HD:]], axis=1).astype(BF16)
    kv_mine = jnp.stack(ring_gather(links, kv_own))
    kv_other = links.swap(kv_mine)
    kv_first = jnp.where(core == 0, kv_mine, kv_other)
    kv_second = jnp.where(core == 0, kv_other, kv_mine)
    kv_rel = jnp.concatenate([kv_first, kv_second], axis=1)
    kv_all = jnp.concatenate(
        [
            lax.dynamic_index_in_dim(kv_rel, (place[chip] - links.place[j] + chips) % chips, 0, keepdims=False)
            for j in range(chips)
        ],
        axis=0,
    )
    key_rows, value_rows = kv_all[:, :HD], kv_all[:, HD:]

    wq_blocks = gather_weight(links, w_query, me_dp)
    wo_blocks = gather_weight(links, w_out, me_dp)
    wq = jnp.concatenate(wq_blocks, axis=1)
    wo = jnp.concatenate(wo_blocks, axis=0)
    grad_chunks = [both(links, piece) for piece in ring_gather(links, out_grad)]

    dk2, dv2 = second_back(sp, query_two, grad_two, key_rows, value_rows)

    normed = both(links, normed_own)
    q_lin = mm(normed, wq, NN)
    queries, context, lse = attend(sp, q_lin, cosine, sine, key_rows, value_rows)
    branch = pair_sum(links, mm(context, wo, NN))
    hidden = residual + branch
    mlp_scale = rms_factor(hidden)
    mlp_pre = hidden * mlp_scale
    hidden_own = (mlp_pre * mlp_gain).astype(BF16)

    hidden_chunks, act_chunks, gate_chunks, up_chunks = [], [], [], []
    mlp_parts, back_parts = [], []
    for piece, grad in zip(ring_gather(links, hidden_own), grad_chunks):
        chunk = both(links, piece)
        gate = mm(chunk, w_gate, NN)
        upward = mm(chunk, w_up, NN)
        grad_act = mm(grad, w_down, NT)
        sigma = jax.nn.sigmoid(gate)
        swish = gate * sigma
        activated = (swish * upward).astype(BF16)
        grad_gate = (grad_act * upward * sigma * (1.0 + gate * (1.0 - sigma))).astype(BF16)
        grad_up = (grad_act * swish).astype(BF16)
        back_parts.append((mm(grad_gate, w_gate, NT) + mm(grad_up, w_up, NT)).astype(BF16))
        mlp_parts.append(mm(activated, w_down, NN).astype(BF16))
        hidden_chunks.append(chunk)
        act_chunks.append(activated)
        gate_chunks.append(grad_gate)
        up_chunks.append(grad_up)

    grad_hn = ring_scatter(links, [pair_sum(links, part) for part in back_parts])
    mlp_out = ring_scatter(links, [pair_sum(links, part) for part in mlp_parts])
    block_output = (hidden + mlp_out).astype(BF16)

    hidden_all = jnp.concatenate(hidden_chunks, axis=0)
    act_all = jnp.concatenate(act_chunks, axis=0)
    gate_all = jnp.concatenate(gate_chunks, axis=0)
    up_all = jnp.concatenate(up_chunks, axis=0)
    grad_all = jnp.concatenate(grad_chunks, axis=0)
    gate_w_grad = sum_dp(links, mm(gate_all, hidden_all, TN).astype(BF16), me_dp).T
    up_w_grad = sum_dp(links, mm(up_all, hidden_all, TN).astype(BF16), me_dp).T
    down_w_grad = sum_dp(links, mm(act_all, grad_all, TN).astype(BF16), me_dp)

    mlp_gain_part = jnp.sum(grad_hn * mlp_pre, axis=0)
    scaled_mlp = grad_hn * mlp_gain
    grad_hidden = out_grad.astype(F32) + mlp_scale * (
        scaled_mlp - mlp_pre * jnp.mean(scaled_mlp * mlp_pre, axis=-1, keepdims=True)
    )

    grad_branch = both(links, grad_hidden.astype(BF16))
    grad_context = mm(grad_branch, wo, NT).astype(BF16)
    query_grad, dk, dv = attend_back(
        sp, queries, grad_context, context, lse, cosine, sine, key_rows, value_rows, dk2, dv2
    )
    out_w_parts = [
        mm(context[:, k * width : (k + 1) * width], grad_branch, TN).astype(BF16) for k in range(chips)
    ]
    out_w_grad = sum_dp(links, ring_scatter(links, out_w_parts).astype(BF16), me_dp)

    kv_part = jnp.concatenate([dk * SCALE, dv], axis=1).astype(BF16).reshape(chips, 2, own, 2 * HD)
    kv_keep = lax.dynamic_index_in_dim(kv_part, core, 1, keepdims=False)
    kv_send = lax.dynamic_index_in_dim(kv_part, 1 - core, 1, keepdims=False)
    kv_sum = kv_keep.astype(F32) + links.swap(kv_send).astype(F32)
    kv_terms = [
        lax.dynamic_index_in_dim(kv_sum, order[(place[chip] - k + chips) % chips], 0, keepdims=False)
        for k in range(chips)
    ]
    kv_grad = ring_scatter(links, kv_terms)
    key_grad = kv_grad[:, :HD]
    key_grad = key_grad * cosine[:own] - jnp.concatenate([key_grad[:, half:], key_grad[:, :half]], axis=1) * sine[:own]
    kv_grad_lin = jnp.concatenate([key_grad, kv_grad[:, HD:]], axis=1).astype(BF16)

    query_w_parts = [
        mm(normed, query_grad[:, k * width : (k + 1) * width], TN).astype(BF16) for k in range(chips)
    ]
    query_w_grad = sum_dp(links, ring_scatter(links, query_w_parts).astype(BF16), me_dp)

    grad_normed = pair_sum(links, mm(query_grad, wq, NT)) + mm(kv_grad_lin, w_kv, NT)
    attn_gain_part = jnp.sum(grad_normed * attn_pre, axis=0)
    scaled_attn = grad_normed * attn_gain
    tokens_grad = (
        grad_hidden
        + attn_scale * (scaled_attn - attn_pre * jnp.mean(scaled_attn * attn_pre, axis=-1, keepdims=True))
    ).astype(BF16)

    kv_w = mm(kv_grad_lin, normed_own, TN).astype(BF16).reshape(chips, 2, HD // chips, -1)
    kv_w_keep = lax.dynamic_index_in_dim(kv_w, core, 1, keepdims=False)
    kv_w_send = lax.dynamic_index_in_dim(kv_w, 1 - core, 1, keepdims=False)
    kv_w_sum = kv_w_keep.astype(F32) + links.swap(kv_w_send).astype(F32)
    kv_w_terms = [
        lax.dynamic_index_in_dim(kv_w_sum, order[(place[chip] - k + chips) % chips], 0, keepdims=False)
        for k in range(chips)
    ]
    kv_w_own = sum_dp(links, ring_scatter(links, kv_w_terms).astype(BF16), me_dp)
    kv_w_mine = jnp.stack(ring_gather(links, kv_w_own.astype(BF16)))
    kv_w_other = links.swap(kv_w_mine)
    kv_w_pair = jnp.stack(
        [jnp.where(core == 0, kv_w_mine, kv_w_other), jnp.where(core == 0, kv_w_other, kv_w_mine)], axis=1
    )
    kv_w_grad = (
        jnp.concatenate(
            [
                lax.dynamic_index_in_dim(kv_w_pair, (place[chip] - links.place[j] + chips) % chips, 0, keepdims=False)
                for j in range(chips)
            ],
            axis=0,
        )
        .reshape(2 * HD, -1)
        .astype(F32)
        .T
    )

    attn_gain_grad = sum_all(links, attn_gain_part)
    mlp_gain_grad = sum_all(links, mlp_gain_part)
    return (
        block_output,
        tokens_grad,
        attn_gain_grad,
        mlp_gain_grad,
        query_w_grad,
        kv_w_grad,
        out_w_grad,
        gate_w_grad,
        up_w_grad,
        down_w_grad,
    )


def solution(mesh):
    both_axes = P(("dp", "tensor"), None)
    return jax.shard_map(
        functools.partial(local, mesh.shape["tensor"], mesh.shape["dp"]),
        mesh=mesh,
        in_specs=(
            both_axes,
            both_axes,
            P("dp", "tensor"),
            P("dp", "tensor"),
            P("dp"),
            P(),
            P(),
            P(None, "tensor"),
            P(),
            P("tensor", None),
            P(None, "tensor"),
            P(None, "tensor"),
            P("tensor", None),
        ),
        out_specs=(
            both_axes,
            both_axes,
            P(),
            P(),
            P(None, "tensor"),
            P(),
            P("tensor", None),
            P(None, "tensor"),
            P(None, "tensor"),
            P("tensor", None),
        ),
        check_vma=False,
    )
```

time: 1370 us -> 897 us (0.65)
  waiting for transfers between devices: 887 us -> 341 us
  starting transfers between devices: 0.62 us -> 234 us
  matrix products: 306 us -> 116 us
  Pallas kernels: 0 us -> 43.7 us
  blocking collectives: 39.6 us -> 0 us
  local copies, waits for them, and re-layouts: 48.2 us -> 71.4 us
    psum x3 -> x0, waiting for transfers between devices: 363 us -> none  [the longest x1 206 us: local(): lax.psum(query_w_grad.astype(jnp.bfloat16), 'dp').astype(jnp.float32)]
    ppermute x0 -> x138, waiting for transfers between devices: none -> 341 us  [the longest x72 162 us: across(): return lax.ppermute(x, 'dp', [(i, i ^ bit) for i in range(self.n_dp)])]
    reduce_scatter x4 -> x0, waiting for transfers between devices: 302 us -> none  [the longest x1 88.3 us: local(): lax.psum_scatter(jnp.dot(context, w_out, preferred_element_type=jnp.float...]
    ppermute x0 -> x138, starting transfers between devices: none -> 234 us  [the longest x72 146 us: across(): return lax.ppermute(x, 'dp', [(i, i ^ bit) for i in range(self.n_dp)])]
    all_gather x4 -> x0, waiting for transfers between devices: 221 us -> none  [the longest x1 79.9 us: local(): hidden_normed = lax.all_gather(hidden_own, 'tensor', axis=0, tiled=True)]
    dot_general x50 -> x42, matrix products: 260 us -> 116 us  [mm(): lax.dot_general(left, right, (dims, ((), ())), preferred_element_type=F32)]
    sub x8 -> x0, matrix products: 46.1 us -> none  [the longest x4 23.2 us: attend(): lifted = jnp.exp(scores - row_max)]
    pallas_call x0 -> x3, Pallas kernels: none -> 43.7 us  [the longest x1 16.3 us: attend_back(): pl.pallas_call(functools.partial(bwd_kernel, seq // rows), grid_spec=pltp...]
  transfers between devices with their start and end apart: 11 -> 138, of which waited for: 10 -> 63; matrix products, arithmetic and copies ran while one was open for 14% -> 25% of each run, Pallas kernels for 0% -> 3%
where the time goes in v1:
time: 897 us; the launch traced here: 888 us
  waiting for transfers between devices  341 us (38%)
  starting transfers between devices  234 us (26%)
  matrix products  116 us (13%)
  local copies, waits for them, and re-layouts  71.4 us (8%)
  other arithmetic  56.4 us (6%)
  Pallas kernels  43.7 us (5%)
  between operations  25.7 us (3%)
    ppermute x72, waiting for transfers between devices, across(): return lax.ppermute(x, 'dp', [(i, i ^ bit) for i in range(self.n_dp)])  162 us
    ppermute x72, starting transfers between devices, across(): return lax.ppermute(x, 'dp', [(i, i ^ bit) for i in range(self.n_dp)])  146 us
    ppermute x36, waiting for transfers between devices, ring(): return lax.ppermute(x, 'tensor', self.ring_pairs)  130 us
    dot_general x42, matrix products, mm(): lax.dot_general(left, right, (dims, ((), ())), preferred_element_type=F32)  116 us
    ppermute x36, starting transfers between devices, ring(): return lax.ppermute(x, 'tensor', self.ring_pairs)  83.1 us
    unnamed x249, local copies, waits for them, and re-layouts  51.1 us
    ppermute x6, waiting for transfers between devices, across_tensor(): lax.ppermute(x, 'tensor', [(i, i ^ bit) for i in range(self.n_tensor)])  49.4 us
  transfers between devices with their start and end apart: 138, of which 63 were waited for; matrix products, arithmetic and copies ran while one was open for 25% of the time, Pallas kernels for 3%

profile of v1, /device:TPU:0, one launch (start us, length us, event | category | flops | bytes accessed | tf_op | source)
XLA Modules:
  0.0 888.4 jit_solution(15303042085988563217)
XLA Ops:
  75.8 6.6 collective-permute-done.25
  84.5 4.2 collective-permute-done.22
  90.9 4.6 collective-permute-done.24
  114.3 3.6 collective-permute-done.30
  124.5 3.4 collective-permute-done.33
  135.0 4.3 collective-permute-done.10
  140.5 5.2 collective-permute-done.27
  147.7 4.4 collective-permute-done.29
  178.2 5.2 fusion.87.q_ref
  183.4 11.5 %attend.1 = (bf16[512,1024]{1,0:T(8,128)(2,1)}, bf16[512,1024]{1,0:T(8,128)(2,1)}, f32[8,8,512]{2,1,0:T(8,128)}) custom-call(s32[3]{0:T(128)} %pad_add_fusion.sp_ref, f32[512,1024]{1,0:T(8,128)} %fusion.87.q_ref, f32[512,128]{1,0:T(8,128)} %get-tuple-element.132.c_ref, f32[512,128]{1,0:T(8,128)} %get-tuple-element.133.s_ref, ...), custom_call_target="tpu_custom_call" | custom-call | flops 8589934592 | bytes 8388608 | tf_op jit(solution)/shard_map/attend/pallas_call | solution.py:287
  195.0 4.8 fusion.178
  200.9 15.8 %second_back.1 = (f32[2048,128]{1,0:T(8,128)}, f32[2048,128]{1,0:T(8,128)}) custom-call(s32[3]{0:T(128)} %pad_add_fusion.sp_ref, bf16[2048,256]{1,0:T(8,128)(2,1)} %q_ref.1, bf16[2048,256]{1,0:T(8,128)(2,1)} %do_ref.1, bf16[2048,128]{1,0:T(8,128)(2,1)} %get-tuple-element.89.k_ref, bf16[2048,128]{1,0:T(8,128)(2,1)} %get-tuple-element.88.v_ref), custom_call_target="tpu_custom_call" | custom-call | flops 8589934592 | bytes 2097152 | tf_op jit(solution)/shard_map/second_back/pallas_call | solution.py:343
  219.6 5.8 collective-permute-start.54
  234.5 3.6 collective-permute-start.38
  238.0 11.2 %collective-permute-done.54 = bf16[256,2048]{1,0:T(8,128)(2,1)S(1)} collective-permute-done((bf16[256,2048]{1,0:T(8,128)(2,1)}, bf16[256,2048]{1,0:T(8,128)(2,1)S(1)}, u32[]{:S(2)}, u32[]{:S(2)}) %collective-permute-start.54) | collective-permute-done | bytes 1048608 | tf_op jit(solution)/shard_map/ppermute | solution.py:44
  254.9 3.8 multiply_convert_fusion.7
  264.0 7.1 collective-permute-done.38
  273.0 3.8 collective-permute-start.39
  284.7 3.5 multiply_convert_fusion.1
  290.0 11.4 %collective-permute-done.39 = bf16[256,2048]{1,0:T(8,128)(2,1)S(1)} collective-permute-done((bf16[256,2048]{1,0:T(8,128)(2,1)S(1)}, bf16[256,2048]{1,0:T(8,128)(2,1)S(1)}, u32[]{:S(2)}, u32[]{:S(2)}) %collective-permute-start.39) | collective-permute-done | bytes 1048608 | tf_op jit(solution)/shard_map/ppermute | solution.py:44
  315.5 3.4 collective-permute-start.61
  318.9 3.5 multiply_convert_fusion.3
  327.1 6.0 collective-permute-done.40
  344.5 11.1 %collective-permute-done.61 = bf16[256,2048]{1,0:T(8,128)(2,1)S(1)} collective-permute-done((bf16[256,2048]{1,0:T(8,128)(2,1)S(1)}, bf16[256,2048]{1,0:T(8,128)(2,1)S(1)}, u32[]{:S(2)}, u32[]{:S(2)}) %collective-permute-start.61) | collective-permute-done | bytes 1048608 | tf_op jit(solution)/shard_map/ppermute | solution.py:44
  364.3 9.0 %convolution_convert_fusion.2 = bf16[704,2048]{1,0:T(8,128)(2,1)S(1)} fusion(bf16[2048,2048]{1,0:T(8,128)(2,1)} %get-tuple-element.65, bf16[512,704]{0,1:T(8,128)(2,1)S(1)} %get-tuple-element.56, bf16[512,704]{0,1:T(8,128)(2,1)S(1)} %copy-done.28, bf16[512,704]{0,1:T(8,128)(2,1)S(1)} %get-tuple-element.62, bf16[512,704]{0,1:T(8,128)(2,1)S(1)} %get-tuple-element.53), kind=kOutput, calls=%fused_computation.9 | convolution fusion | flops 5918556160 | bytes 14155776 | tf_op jit(solution)/shard_map/dot_general | solution.py:22
  373.3 10.2 %convolution_convert_fusion.1 = bf16[704,2048]{1,0:T(8,128)(2,1)S(1)} fusion(bf16[2048,2048]{1,0:T(8,128)(2,1)} %get-tuple-element.65, bf16[512,704]{0,1:T(8,128)(2,1)} %get-tuple-element.55, bf16[512,704]{0,1:T(8,128)(2,1)} %copy-done.74, bf16[512,704]{0,1:T(8,128)(2,1)S(1)} %copy-done.73, bf16[512,704]{0,1:T(8,128)(2,1)S(1)} %copy-done.71), kind=kOutput, calls=%fused_computation.8 | convolution fusion | flops 5918556160 | bytes 14155776 | tf_op jit(solution)/shard_map/dot_general | solution.py:22
  390.0 9.1 %convolution_convert_fusion = bf16[704,2048]{1,0:T(8,128)(2,1)S(1)} fusion(bf16[2048,2048]{1,0:T(8,128)(2,1)} %constant_dynamic-update-slice_fusion.79, bf16[512,704]{0,1:T(8,128)(2,1)S(1)} %copy-done.68, bf16[512,704]{0,1:T(8,128)(2,1)S(1)} %copy-done.66, bf16[512,704]{0,1:T(8,128)(2,1)S(1)} %copy-done.64, bf16[512,704]{0,1:T(8,128)(2,1)S(1)} %copy-done.62), kind=kOutput, calls=%fused_computation.7 | convolution fusion | flops 5918556160 | bytes 14155776 | tf_op jit(solution)/shard_map/dot_general | solution.py:22
  403.9 14.8 %collective-permute-done.114 = bf16[2,88,2048]{2,1,0:T(8,128)(2,1)S(1)} collective-permute-done((bf16[2,88,2048]{2,1,0:T(8,128)(2,1)S(1)}, bf16[2,88,2048]{2,1,0:T(8,128)(2,1)S(1)}, u32[]{:S(2)}, u32[]{:S(2)}) %collective-permute-start.114) | collective-permute-done | bytes 720928 | tf_op jit(solution)/shard_map/ppermute | solution.py:50
  418.6 19.5 %collective-permute-start.118 = (bf16[2,88,2048]{2,1,0:T(8,128)(2,1)S(1)}, bf16[2,88,2048]{2,1,0:T(8,128)(2,1)S(1)}, u32[]{:S(2)}, u32[]{:S(2)}) collective-permute-start(bf16[2,88,2048]{2,1,0:T(8,128)(2,1)S(1)} %dynamic-slice_bitcast_fusion.4), channel_id=1, source_target_pairs={{0,16},{8,24},{16,0},{24,8},{1,17},{9,25},{17,1},{25,9},{2,18},{10... | collective-permute-start | bytes 2162696 | tf_op jit(solution)/shard_map/ppermute | solution.py:50
  438.4 14.8 %collective-permute-start.126 = (bf16[2,88,2048]{2,1,0:T(8,128)(2,1)S(1)}, bf16[2,88,2048]{2,1,0:T(8,128)(2,1)S(1)}, u32[]{:S(2)}, u32[]{:S(2)}) collective-permute-start(bf16[2,88,2048]{2,1,0:T(8,128)(2,1)S(1)} %dynamic-slice_bitcast_fusion.2), channel_id=1, source_target_pairs={{0,16},{8,24},{16,0},{24,8},{1,17},{9,25},{17,1},{25,9},{2,18},{10... | collective-permute-start | bytes 2162696 | tf_op jit(solution)/shard_map/ppermute | solution.py:50
  454.8 14.4 %collective-permute-done.126 = bf16[2,88,2048]{2,1,0:T(8,128)(2,1)S(1)} collective-permute-done((bf16[2,88,2048]{2,1,0:T(8,128)(2,1)S(1)}, bf16[2,88,2048]{2,1,0:T(8,128)(2,1)S(1)}, u32[]{:S(2)}, u32[]{:S(2)}) %collective-permute-start.126) | collective-permute-done | bytes 720928 | tf_op jit(solution)/shard_map/ppermute | solution.py:50
  471.3 3.4 collective-permute-start.48
  474.9 11.5 %collective-permute-done.134 = bf16[2,88,2048]{2,1,0:T(8,128)(2,1)S(1)} collective-permute-done((bf16[2,88,2048]{2,1,0:T(8,128)(2,1)S(1)}, bf16[2,88,2048]{2,1,0:T(8,128)(2,1)S(1)}, u32[]{:S(2)}, u32[]{:S(2)}) %collective-permute-start.134) | collective-permute-done | bytes 720928 | tf_op jit(solution)/shard_map/ppermute | solution.py:50
  490.9 4.9 collective-permute-done.48
  499.5 7.7 collective-permute-done.119
  508.9 6.0 collective-permute-done.127
  520.7 7.5 collective-permute-done.116
  529.7 9.7 %collective-permute-done.124 = bf16[88,2048]{1,0:T(8,128)(2,1)S(1)} collective-permute-done((bf16[88,2048]{1,0:T(8,128)(2,1)S(1)}, bf16[88,2048]{1,0:T(8,128)(2,1)S(1)}, u32[]{:S(2)}, u32[]{:S(2)}) %collective-permute-start.124) | collective-permute-done | bytes 360480 | tf_op jit(solution)/shard_map/ppermute | solution.py:50
  543.1 3.8 collective-permute-done.128
  548.5 8.4 collective-permute-done.76
  563.1 3.3 collective-permute-done.78
  568.8 4.2 fusion.161
  573.0 12.5 %collective-permute-done.79 = f32[2048]{0:T(1024)S(1)} collective-permute-done((f32[2048]{0:T(1024)S(1)}, f32[2048]{0:T(1024)S(1)}, u32[]{:S(2)}, u32[]{:S(2)}) %collective-permute-start.79) | collective-permute-done | bytes 8224 | tf_op jit(solution)/shard_map/ppermute | solution.py:50
  589.5 12.8 %collective-permute-done.133 = bf16[176,2048]{1,0:T(8,128)(2,1)S(1)} collective-permute-done((bf16[176,2048]{1,0:T(8,128)(2,1)S(1)}, bf16[176,2048]{1,0:T(8,128)(2,1)S(1)}, u32[]{:S(2)}, u32[]{:S(2)}) %collective-permute-start.133) | collective-permute-done | bytes 720928 | tf_op jit(solution)/shard_map/ppermute | solution.py:50
  606.7 3.4 convolution_convert_fusion.16.do_ref
  610.0 16.3 %attend_back.1 = (bf16[512,1024]{1,0:T(8,128)(2,1)}, f32[2048,128]{1,0:T(8,128)}, f32[2048,128]{1,0:T(8,128)}) custom-call(s32[3]{0:T(128)} %pad_add_fusion.sp_ref, bf16[512,1024]{1,0:T(8,128)(2,1)} %get-tuple-element.19.q_ref, bf16[512,1024]{1,0:T(8,128)(2,1)} %convolution_convert_fusion.16.do_ref, bf16[512,1024]{1,0:T(8,128)(2,1)} %get-tuple-element.18.ctx_ref, ...), custom_call_target="tpu_custom_call" | custom-call | flops 21474836480 | bytes 8388608 | tf_op jit(solution)/shard_map/attend_back/pallas_call | solution.py:313
  632.8 5.7 collective-permute-start.67
  638.5 3.4 collective-permute-done.67
  645.1 4.3 collective-permute-done.68
  651.2 4.1 collective-permute-done.69
  662.8 5.0 collective-permute-done.92
  669.7 3.6 convert_element_type.829
  686.5 10.4 %collective-permute-start.96 = (bf16[8,2048]{1,0:T(8,128)(2,1)S(1)}, bf16[8,2048]{1,0:T(8,128)(2,1)S(1)}, u32[]{:S(2)}, u32[]{:S(2)}) collective-permute-start(bf16[8,2048]{1,0:T(8,128)(2,1)S(1)} %fusion.142), channel_id=1, source_target_pairs={{0,16},{8,24},{16,0},{24,8},{1,17},{9,25},{17,1},{25,9},{2,18},{10... | collective-permute-start | bytes 98312 | tf_op jit(solution)/shard_map/ppermute | solution.py:50
  706.4 4.7 collective-permute-done.80
  715.2 36.7 %collective-permute-done.71 = f32[2048]{0:T(1024)S(1)} collective-permute-done((f32[2048]{0:T(1024)S(1)}, f32[2048]{0:T(1024)S(1)}, u32[]{:S(2)}, u32[]{:S(2)}) %collective-permute-start.71) | collective-permute-done | bytes 8224 | tf_op jit(solution)/shard_map/ppermute | solution.py:53
  752.0 7.2 collective-permute-start.99
  766.6 10.3 %collective-permute-start.74 = (f32[2048]{0:T(1024)S(1)}, f32[2048]{0:T(1024)S(1)}, u32[]{:S(2)}, u32[]{:S(2)}) collective-permute-start(f32[2048]{0:T(1024)S(1)} %add.1011), channel_id=1, source_target_pairs={{0,16},{8,24},{16,0},{24,8},{1,17},{9,25},{17,1},{25,9},{2,18},{10... | collective-permute-start | bytes 24584 | tf_op jit(solution)/shard_map/ppermute | solution.py:50
  779.2 9.7 %collective-permute-done.101 = bf16[32,2048]{1,0:T(8,128)(2,1)S(1)} collective-permute-done((bf16[32,2048]{1,0:T(8,128)(2,1)S(1)}, bf16[32,2048]{1,0:T(8,128)(2,1)S(1)}, u32[]{:S(2)}, u32[]{:S(2)}) %collective-permute-start.101) | collective-permute-done | bytes 131104 | tf_op jit(solution)/shard_map/ppermute | solution.py:44
  799.5 20.0 %collective-permute-done.82 = bf16[2048,256]{1,0:T(8,128)(2,1)} collective-permute-done((bf16[2048,256]{1,0:T(8,128)(2,1)}, bf16[2048,256]{1,0:T(8,128)(2,1)}, u32[]{:S(2)}, u32[]{:S(2)}) %collective-permute-start.82) | collective-permute-done | bytes 1048608 | tf_op jit(solution)/shard_map/ppermute | solution.py:44
  822.9 10.4 %collective-permute-start.87 = (bf16[2,256,256]{2,1,0:T(8,128)(2,1)S(1)}, bf16[2,256,256]{2,1,0:T(8,128)(2,1)S(1)}, u32[]{:S(2)}, u32[]{:S(2)}) collective-permute-start(bf16[2,256,256]{2,1,0:T(8,128)(2,1)S(1)} %dynamic-slice_bitcast_fusion.15), channel_id=1, source_target_pairs={{0,16},{8,24},{16,0},{24,8},{1,17},{9,25},{17,1},{25,9},{2,18},{10... | collective-permute-start | bytes 786440 | tf_op jit(solution)/shard_map/ppermute | solution.py:50
  833.3 8.2 collective-permute-done.105
  844.4 10.4 %collective-permute-start.110 = (bf16[2,32,2048]{2,1,0:T(8,128)(2,1)S(1)}, bf16[2,32,2048]{2,1,0:T(8,128)(2,1)S(1)}, u32[]{:S(2)}, u32[]{:S(2)}) collective-permute-start(bf16[2,32,2048]{2,1,0:T(8,128)(2,1)S(1)} %dynamic-slice_bitcast_fusion.13), channel_id=1, source_target_pairs={{0,16},{8,24},{16,0},{24,8},{1,17},{9,25},{17,1},{25,9},{2,18},{10... | collective-permute-start | bytes 786440 | tf_op jit(solution)/shard_map/ppermute | solution.py:50
  856.7 6.8 collective-permute-start.107
  877.7 4.1 collective-permute-done.86
  (705 shorter events, 342.6 us)
Async XLA Ops:
  2.5 56.0 %collective-permute-start.1 = (bf16[512,256]{1,0:T(8,128)(2,1)}, bf16[512,256]{1,0:T(8,128)(2,1)}, u32[]{:S(2)}, u32[]{:S(2)}) collective-permute-start(bf16[512,256]{1,0:T(8,128)(2,1)} %constant_dynamic-slice_fusion.7), channel_id=1, source_target_pairs={{0,2},{1,3},{2,6},{3,7},{4,0},{5,1},{6,4},{7,5},{8,10},{9,11},{10,... | collective-permute-start | bytes 786440 | tf_op jit(solution)/shard_map/ppermute | solution.py:44
  10.1 168.1 %collective-permute-start = (bf16[256,2048]{1,0:T(8,128)(2,1)}, bf16[256,2048]{1,0:T(8,128)(2,1)}, u32[]{:S(2)}, u32[]{:S(2)}) collective-permute-start(bf16[256,2048]{1,0:T(8,128)(2,1)} %fusion.43), channel_id=1, source_target_pairs={{0,1},{1,0},{2,3},{3,2},{4,5},{5,4},{6,7},{7,6},{8,9},{9,8},{10,11... | collective-permute-start | bytes 3145736 | tf_op jit(solution)/shard_map/ppermute | solution.py:47
  17.9 36.1 %collective-permute-start.16 = (bf16[256,256]{1,0:T(8,128)(2,1)}, bf16[256,256]{1,0:T(8,128)(2,1)}, u32[]{:S(2)}, u32[]{:S(2)}) collective-permute-start(bf16[256,256]{1,0:T(8,128)(2,1)} %pad_maximum_fusion.58), channel_id=1, source_target_pairs={{0,2},{1,3},{2,6},{3,7},{4,0},{5,1},{6,4},{7,5},{8,10},{9,11},{10,... | collective-permute-start | bytes 393224 | tf_op jit(solution)/shard_map/ppermute | solution.py:44
  22.2 33.7 %collective-permute-start.20 = (bf16[64,2048]{1,0:T(8,128)(2,1)}, bf16[64,2048]{1,0:T(8,128)(2,1)}, u32[]{:S(2)}, u32[]{:S(2)}) collective-permute-start(bf16[64,2048]{1,0:T(8,128)(2,1)} %constant_dynamic-slice_fusion.6), channel_id=1, source_target_pairs={{0,2},{1,3},{2,6},{3,7},{4,0},{5,1},{6,4},{7,5},{8,10},{9,11},{10,... | collective-permute-start | bytes 786440 | tf_op jit(solution)/shard_map/ppermute | solution.py:44
  22.6 144.1 %collective-permute-start.52 = (bf16[256,2048]{1,0:T(8,128)(2,1)}, bf16[256,2048]{1,0:T(8,128)(2,1)}, u32[]{:S(2)}, u32[]{:S(2)}) collective-permute-start(bf16[256,2048]{1,0:T(8,128)(2,1)} %param.39), channel_id=1, source_target_pairs={{0,2},{1,3},{2,6},{3,7},{4,0},{5,1},{6,4},{7,5},{8,10},{9,11},{10,... | collective-permute-start | bytes 3145736 | tf_op jit(solution)/shard_map/ppermute | solution.py:44
  60.5 12.3 %collective-permute-start.4 = (bf16[256,256]{1,0:T(8,128)(2,1)S(1)}, bf16[256,256]{1,0:T(8,128)(2,1)S(1)}, u32[]{:S(2)}, u32[]{:S(2)}) collective-permute-start(bf16[256,256]{1,0:T(8,128)(2,1)S(1)} %get-tuple-element.106), channel_id=1, source_target_pairs={{0,16},{8,24},{16,0},{24,8},{1,17},{9,25},{17,1},{25,9},{2,18},{10... | collective-permute-start | bytes 393224 | tf_op jit(solution)/shard_map/ppermute | solution.py:50
  74.3 30.3 %collective-permute-start.3 = (bf16[512,256]{1,0:T(8,128)(2,1)S(1)}, bf16[512,256]{1,0:T(8,128)(2,1)S(1)}, u32[]{:S(2)}, u32[]{:S(2)}) collective-permute-start(bf16[512,256]{1,0:T(8,128)(2,1)S(1)} %pad_maximum_fusion.40), channel_id=1, source_target_pairs={{0,16},{8,24},{16,0},{24,8},{1,17},{9,25},{17,1},{25,9},{2,18},{10... | collective-permute-start | bytes 786440 | tf_op jit(solution)/shard_map/ppermute | solution.py:50
  83.0 24.0 %collective-permute-start.5 = (bf16[512,256]{1,0:T(8,128)(2,1)S(1)}, bf16[512,256]{1,0:T(8,128)(2,1)S(1)}, u32[]{:S(2)}, u32[]{:S(2)}) collective-permute-start(bf16[512,256]{1,0:T(8,128)(2,1)S(1)} %pad_maximum_fusion.41), channel_id=1, source_target_pairs={{0,8},{8,0},{16,24},{24,16},{1,9},{9,1},{17,25},{25,17},{2,10},{10... | collective-permute-start | bytes 786440 | tf_op jit(solution)/shard_map/ppermute | solution.py:50
  113.5 21.4 %collective-permute-start.8 = (bf16[512,256]{1,0:T(8,128)(2,1)S(1)}, bf16[512,256]{1,0:T(8,128)(2,1)S(1)}, u32[]{:S(2)}, u32[]{:S(2)}) collective-permute-start(bf16[512,256]{1,0:T(8,128)(2,1)S(1)} %pad_maximum_fusion.42), channel_id=1, source_target_pairs={{0,16},{8,24},{16,0},{24,8},{1,17},{9,25},{17,1},{25,9},{2,18},{10... | collective-permute-start | bytes 786440 | tf_op jit(solution)/shard_map/ppermute | solution.py:50
  129.5 87.7 %collective-permute-start.50 = (bf16[256,2048]{1,0:T(8,128)(2,1)}, bf16[256,2048]{1,0:T(8,128)(2,1)}, u32[]{:S(2)}, u32[]{:S(2)}) collective-permute-start(bf16[256,2048]{1,0:T(8,128)(2,1)} %param.39), channel_id=1, source_target_pairs={{0,1},{1,0},{2,3},{3,2},{4,5},{5,4},{6,7},{7,6},{8,9},{9,8},{10,11... | collective-permute-start | bytes 3145736 | tf_op jit(solution)/shard_map/ppermute | solution.py:47
  134.9 22.7 %collective-permute-start.19 = (bf16[4,256,256]{2,1,0:T(8,128)(2,1)S(1)}, bf16[4,256,256]{2,1,0:T(8,128)(2,1)S(1)}, u32[]{:S(2)}, u32[]{:S(2)}) collective-permute-start(bf16[4,256,256]{2,1,0:T(8,128)(2,1)S(1)} %pad_maximum_fusion.28), channel_id=1, source_target_pairs={{0,1},{1,0},{2,3},{3,2},{4,5},{5,4},{6,7},{7,6},{8,9},{9,8},{10,11... | collective-permute-start | bytes 1572872 | tf_op jit(solution)/shard_map/ppermute | solution.py:47
  152.0 12.7 %collective-permute-start.13 = (bf16[512,256]{1,0:T(8,128)(2,1)}, bf16[512,256]{1,0:T(8,128)(2,1)}, u32[]{:S(2)}, u32[]{:S(2)}) collective-permute-start(bf16[512,256]{1,0:T(8,128)(2,1)} %pad_maximum_fusion.44), channel_id=1, source_target_pairs={{0,16},{8,24},{16,0},{24,8},{1,17},{9,25},{17,1},{25,9},{2,18},{10... | collective-permute-start | bytes 786440 | tf_op jit(solution)/shard_map/ppermute | solution.py:50
  167.6 51.9 %collective-permute-start.53 = (bf16[256,2048]{1,0:T(8,128)(2,1)}, bf16[256,2048]{1,0:T(8,128)(2,1)}, u32[]{:S(2)}, u32[]{:S(2)}) collective-permute-start(bf16[256,2048]{1,0:T(8,128)(2,1)} %collective-permute-done.52), channel_id=1, source_target_pairs={{0,2},{1,3},{2,6},{3,7},{4,0},{5,1},{6,4},{7,5},{8,10},{9,11},{10,... | collective-permute-start | bytes 3145736 | tf_op jit(solution)/shard_map/ppermute | solution.py:44
  200.9 24.5 %collective-permute-start.35 = (bf16[256,2048]{1,0:T(8,128)(2,1)}, bf16[256,2048]{1,0:T(8,128)(2,1)}, u32[]{:S(2)}, u32[]{:S(2)}) collective-permute-start(bf16[256,2048]{1,0:T(8,128)(2,1)} %slice.393), channel_id=1, source_target_pairs={{0,1},{1,0},{2,3},{3,2},{4,5},{5,4},{6,7},{7,6},{8,9},{9,8},{10,11... | collective-permute-start | bytes 3145736 | tf_op jit(solution)/shard_map/ppermute | solution.py:47
  216.8 14.1 %collective-permute-start.59 = (bf16[256,2048]{1,0:T(8,128)(2,1)}, bf16[256,2048]{1,0:T(8,128)(2,1)S(1)}, u32[]{:S(2)}, u32[]{:S(2)}) collective-permute-start(bf16[256,2048]{1,0:T(8,128)(2,1)} %collective-permute-done.52), channel_id=1, source_target_pairs={{0,1},{1,0},{2,3},{3,2},{4,5},{5,4},{6,7},{7,6},{8,9},{9,8},{10,11... | collective-permute-start | bytes 3145736 | tf_op jit(solution)/shard_map/ppermute | solution.py:47
  219.5 29.8 %collective-permute-start.57 = (bf16[256,2048]{1,0:T(8,128)(2,1)}, bf16[256,2048]{1,0:T(8,128)(2,1)S(1)}, u32[]{:S(2)}, u32[]{:S(2)}) collective-permute-start(bf16[256,2048]{1,0:T(8,128)(2,1)} %collective-permute-done.53), channel_id=1, source_target_pairs={{0,1},{1,0},{2,3},{3,2},{4,5},{5,4},{6,7},{7,6},{8,9},{9,8},{10,11... | collective-permute-start | bytes 3145736 | tf_op jit(solution)/shard_map/ppermute | solution.py:47
  219.6 29.6 %collective-permute-start.54 = (bf16[256,2048]{1,0:T(8,128)(2,1)}, bf16[256,2048]{1,0:T(8,128)(2,1)S(1)}, u32[]{:S(2)}, u32[]{:S(2)}) collective-permute-start(bf16[256,2048]{1,0:T(8,128)(2,1)} %collective-permute-done.53), channel_id=1, source_target_pairs={{0,2},{1,3},{2,6},{3,7},{4,0},{5,1},{6,4},{7,5},{8,10},{9,11},{10,... | collective-permute-start | bytes 3145736 | tf_op jit(solution)/shard_map/ppermute | solution.py:44
  228.5 22.8 %collective-permute-start.36 = (bf16[256,2048]{1,0:T(8,128)(2,1)S(1)}, bf16[256,2048]{1,0:T(8,128)(2,1)S(1)}, u32[]{:S(2)}, u32[]{:S(2)}) collective-permute-start(bf16[256,2048]{1,0:T(8,128)(2,1)S(1)} %get-tuple-element.41), channel_id=1, source_target_pairs={{0,1},{1,0},{2,3},{3,2},{4,5},{5,4},{6,7},{7,6},{8,9},{9,8},{10,11... | collective-permute-start | bytes 3145736 | tf_op jit(solution)/shard_map/ppermute | solution.py:47
  234.5 36.6 %collective-permute-start.38 = (bf16[256,2048]{1,0:T(8,128)(2,1)S(1)}, bf16[256,2048]{1,0:T(8,128)(2,1)S(1)}, u32[]{:S(2)}, u32[]{:S(2)}) collective-permute-start(bf16[256,2048]{1,0:T(8,128)(2,1)S(1)} %get-tuple-element.41), channel_id=1, source_target_pairs={{0,2},{1,3},{2,6},{3,7},{4,0},{5,1},{6,4},{7,5},{8,10},{9,11},{10,... | collective-permute-start | bytes 3145736 | tf_op jit(solution)/shard_map/ppermute | solution.py:44
  249.3 29.8 %collective-permute-start.55 = (bf16[256,2048]{1,0:T(8,128)(2,1)S(1)}, bf16[256,2048]{1,0:T(8,128)(2,1)S(1)}, u32[]{:S(2)}, u32[]{:S(2)}) collective-permute-start(bf16[256,2048]{1,0:T(8,128)(2,1)S(1)} %collective-permute-done.54), channel_id=1, source_target_pairs={{0,1},{1,0},{2,3},{3,2},{4,5},{5,4},{6,7},{7,6},{8,9},{9,8},{10,11... | collective-permute-start | bytes 3145736 | tf_op jit(solution)/shard_map/ppermute | solution.py:47
  263.5 276.4 %collective-permute-start.51 = (bf16[256,2048]{1,0:T(8,128)(2,1)}, bf16[256,2048]{1,0:T(8,128)(2,1)S(1)}, u32[]{:S(2)}, u32[]{:S(2)}) collective-permute-start(bf16[256,2048]{1,0:T(8,128)(2,1)} %slice.290), channel_id=1, source_target_pairs={{0,1},{1,0},{2,3},{3,2},{4,5},{5,4},{6,7},{7,6},{8,9},{9,8},{10,11... | collective-permute-start | bytes 3145736 | tf_op jit(solution)/shard_map/ppermute | solution.py:47
  273.0 28.4 %collective-permute-start.39 = (bf16[256,2048]{1,0:T(8,128)(2,1)S(1)}, bf16[256,2048]{1,0:T(8,128)(2,1)S(1)}, u32[]{:S(2)}, u32[]{:S(2)}) collective-permute-start(bf16[256,2048]{1,0:T(8,128)(2,1)S(1)} %collective-permute-done.38), channel_id=1, source_target_pairs={{0,2},{1,3},{2,6},{3,7},{4,0},{5,1},{6,4},{7,5},{8,10},{9,11},{10,... | collective-permute-start | bytes 3145736 | tf_op jit(solution)/shard_map/ppermute | solution.py:44
  306.0 27.2 %collective-permute-start.46 = (bf16[256,2048]{1,0:T(8,128)(2,1)S(1)}, bf16[256,2048]{1,0:T(8,128)(2,1)S(1)}, u32[]{:S(2)}, u32[]{:S(2)}) collective-permute-start(bf16[256,2048]{1,0:T(8,128)(2,1)S(1)} %slice.288), channel_id=1, source_target_pairs={{0,1},{1,0},{2,3},{3,2},{4,5},{5,4},{6,7},{7,6},{8,9},{9,8},{10,11... | collective-permute-start | bytes 3145736 | tf_op jit(solution)/shard_map/ppermute | solution.py:47
  306.1 27.1 %collective-permute-start.40 = (bf16[256,2048]{1,0:T(8,128)(2,1)S(1)}, bf16[256,2048]{1,0:T(8,128)(2,1)S(1)}, u32[]{:S(2)}, u32[]{:S(2)}) collective-permute-start(bf16[256,2048]{1,0:T(8,128)(2,1)S(1)} %collective-permute-done.39), channel_id=1, source_target_pairs={{0,2},{1,3},{2,6},{3,7},{4,0},{5,1},{6,4},{7,5},{8,10},{9,11},{10,... | collective-permute-start | bytes 3145736 | tf_op jit(solution)/shard_map/ppermute | solution.py:44
  315.5 40.1 %collective-permute-start.61 = (bf16[256,2048]{1,0:T(8,128)(2,1)S(1)}, bf16[256,2048]{1,0:T(8,128)(2,1)S(1)}, u32[]{:S(2)}, u32[]{:S(2)}) collective-permute-start(bf16[256,2048]{1,0:T(8,128)(2,1)S(1)} %add_convert_fusion.6), channel_id=1, source_target_pairs={{0,2},{1,3},{2,6},{3,7},{4,0},{5,1},{6,4},{7,5},{8,10},{9,11},{10,... | collective-permute-start | bytes 3145736 | tf_op jit(solution)/shard_map/ppermute | solution.py:44
  327.0 28.6 %collective-permute-start.58 = (bf16[256,2048]{1,0:T(8,128)(2,1)S(1)}, bf16[256,2048]{1,0:T(8,128)(2,1)S(1)}, u32[]{:S(2)}, u32[]{:S(2)}) collective-permute-start(bf16[256,2048]{1,0:T(8,128)(2,1)S(1)} %slice.294), channel_id=1, source_target_pairs={{0,1},{1,0},{2,3},{3,2},{4,5},{5,4},{6,7},{7,6},{8,9},{9,8},{10,11... | collective-permute-start | bytes 3145736 | tf_op jit(solution)/shard_map/ppermute | solution.py:47
  333.6 66.1 %collective-permute-start.47 = (bf16[256,2048]{1,0:T(8,128)(2,1)S(1)}, bf16[256,2048]{1,0:T(8,128)(2,1)}, u32[]{:S(2)}, u32[]{:S(2)}) collective-permute-start(bf16[256,2048]{1,0:T(8,128)(2,1)S(1)} %add_convert_fusion.10), channel_id=1, source_target_pairs={{0,2},{1,3},{2,6},{3,7},{4,0},{5,1},{6,4},{7,5},{8,10},{9,11},{10,... | collective-permute-start | bytes 3145736 | tf_op jit(solution)/shard_map/ppermute | solution.py:44
  339.8 60.4 %collective-permute-start.44 = (bf16[256,2048]{1,0:T(8,128)(2,1)}, bf16[256,2048]{1,0:T(8,128)(2,1)}, u32[]{:S(2)}, u32[]{:S(2)}) collective-permute-start(bf16[256,2048]{1,0:T(8,128)(2,1)} %slice.286), channel_id=1, source_target_pairs={{0,1},{1,0},{2,3},{3,2},{4,5},{5,4},{6,7},{7,6},{8,9},{9,8},{10,11... | collective-permute-start | bytes 3145736 | tf_op jit(solution)/shard_map/ppermute | solution.py:47
  357.1 129.7 %collective-permute-start.62 = (bf16[256,2048]{1,0:T(8,128)(2,1)}, bf16[256,2048]{1,0:T(8,128)(2,1)}, u32[]{:S(2)}, u32[]{:S(2)}) collective-permute-start(bf16[256,2048]{1,0:T(8,128)(2,1)} %add_convert_fusion.5), channel_id=1, source_target_pairs={{0,2},{1,3},{2,6},{3,7},{4,0},{5,1},{6,4},{7,5},{8,10},{9,11},{10,... | collective-permute-start | bytes 3145736 | tf_op jit(solution)/shard_map/ppermute | solution.py:44
  385.7 101.8 %collective-permute-start.56 = (bf16[256,2048]{1,0:T(8,128)(2,1)S(1)}, bf16[256,2048]{1,0:T(8,128)(2,1)}, u32[]{:S(2)}, u32[]{:S(2)}) collective-permute-start(bf16[256,2048]{1,0:T(8,128)(2,1)S(1)} %slice.292), channel_id=1, source_target_pairs={{0,1},{1,0},{2,3},{3,2},{4,5},{5,4},{6,7},{7,6},{8,9},{9,8},{10,11... | collective-permute-start | bytes 3145736 | tf_op jit(solution)/shard_map/ppermute | solution.py:47
  399.6 19.0 %collective-permute-start.114 = (bf16[2,88,2048]{2,1,0:T(8,128)(2,1)S(1)}, bf16[2,88,2048]{2,1,0:T(8,128)(2,1)S(1)}, u32[]{:S(2)}, u32[]{:S(2)}) collective-permute-start(bf16[2,88,2048]{2,1,0:T(8,128)(2,1)S(1)} %dynamic-slice_bitcast_fusion.5), channel_id=1, source_target_pairs={{0,8},{8,0},{16,24},{24,16},{1,9},{9,1},{17,25},{25,17},{2,10},{10... | collective-permute-start | bytes 2162696 | tf_op jit(solution)/shard_map/ppermute | solution.py:50
  400.2 38.2 %collective-permute-start.122 = (bf16[2,88,2048]{2,1,0:T(8,128)(2,1)S(1)}, bf16[2,88,2048]{2,1,0:T(8,128)(2,1)S(1)}, u32[]{:S(2)}, u32[]{:S(2)}) collective-permute-start(bf16[2,88,2048]{2,1,0:T(8,128)(2,1)S(1)} %dynamic-slice_bitcast_fusion.3), channel_id=1, source_target_pairs={{0,8},{8,0},{16,24},{24,16},{1,9},{9,1},{17,25},{25,17},{2,10},{10... | collective-permute-start | bytes 2162696 | tf_op jit(solution)/shard_map/ppermute | solution.py:50
  418.6 35.2 %collective-permute-start.118 = (bf16[2,88,2048]{2,1,0:T(8,128)(2,1)S(1)}, bf16[2,88,2048]{2,1,0:T(8,128)(2,1)S(1)}, u32[]{:S(2)}, u32[]{:S(2)}) collective-permute-start(bf16[2,88,2048]{2,1,0:T(8,128)(2,1)S(1)} %dynamic-slice_bitcast_fusion.4), channel_id=1, source_target_pairs={{0,16},{8,24},{16,0},{24,8},{1,17},{9,25},{17,1},{25,9},{2,18},{10... | collective-permute-start | bytes 2162696 | tf_op jit(solution)/shard_map/ppermute | solution.py:50
  438.4 30.8 %collective-permute-start.126 = (bf16[2,88,2048]{2,1,0:T(8,128)(2,1)S(1)}, bf16[2,88,2048]{2,1,0:T(8,128)(2,1)S(1)}, u32[]{:S(2)}, u32[]{:S(2)}) collective-permute-start(bf16[2,88,2048]{2,1,0:T(8,128)(2,1)S(1)} %dynamic-slice_bitcast_fusion.2), channel_id=1, source_target_pairs={{0,16},{8,24},{16,0},{24,8},{1,17},{9,25},{17,1},{25,9},{2,18},{10... | collective-permute-start | bytes 2162696 | tf_op jit(solution)/shard_map/ppermute | solution.py:50
  453.8 17.5 %collective-permute-start.130 = (bf16[2,88,2048]{2,1,0:T(8,128)(2,1)S(1)}, bf16[2,88,2048]{2,1,0:T(8,128)(2,1)S(1)}, u32[]{:S(2)}, u32[]{:S(2)}) collective-permute-start(bf16[2,88,2048]{2,1,0:T(8,128)(2,1)S(1)} %dynamic-slice_bitcast_fusion.1), channel_id=1, source_target_pairs={{0,8},{8,0},{16,24},{24,16},{1,9},{9,1},{17,25},{25,17},{2,10},{10... | collective-permute-start | bytes 2162696 | tf_op jit(solution)/shard_map/ppermute | solution.py:50
  469.2 17.2 %collective-permute-start.134 = (bf16[2,88,2048]{2,1,0:T(8,128)(2,1)S(1)}, bf16[2,88,2048]{2,1,0:T(8,128)(2,1)S(1)}, u32[]{:S(2)}, u32[]{:S(2)}) collective-permute-start(bf16[2,88,2048]{2,1,0:T(8,128)(2,1)S(1)} %dynamic-slice_bitcast_fusion), channel_id=1, source_target_pairs={{0,16},{8,24},{16,0},{24,8},{1,17},{9,25},{17,1},{25,9},{2,18},{10... | collective-permute-start | bytes 2162696 | tf_op jit(solution)/shard_map/ppermute | solution.py:50
  471.3 24.6 %collective-permute-start.48 = (bf16[256,2048]{1,0:T(8,128)(2,1)S(1)}, bf16[256,2048]{1,0:T(8,128)(2,1)S(1)}, u32[]{:S(2)}, u32[]{:S(2)}) collective-permute-start(bf16[256,2048]{1,0:T(8,128)(2,1)S(1)} %add_convert_fusion.9), channel_id=1, source_target_pairs={{0,2},{1,3},{2,6},{3,7},{4,0},{5,1},{6,4},{7,5},{8,10},{9,11},{10,... | collective-permute-start | bytes 3145736 | tf_op jit(solution)/shard_map/ppermute | solution.py:44
  486.9 79.9 %collective-permute-start.37 = (bf16[256,2048]{1,0:T(8,128)(2,1)S(1)}, bf16[256,2048]{1,0:T(8,128)(2,1)S(1)}, u32[]{:S(2)}, u32[]{:S(2)}) collective-permute-start(bf16[256,2048]{1,0:T(8,128)(2,1)S(1)} %slice.282), channel_id=1, source_target_pairs={{0,1},{1,0},{2,3},{3,2},{4,5},{5,4},{6,7},{7,6},{8,9},{9,8},{10,11... | collective-permute-start | bytes 3145736 | tf_op jit(solution)/shard_map/ppermute | solution.py:47
  498.7 16.2 %collective-permute-start.127 = (bf16[88,2048]{1,0:T(8,128)(2,1)S(1)}, bf16[88,2048]{1,0:T(8,128)(2,1)S(1)}, u32[]{:S(2)}, u32[]{:S(2)}) collective-permute-start(bf16[88,2048]{1,0:T(8,128)(2,1)S(1)} %dynamic-slice_bitcast_fusion.9), channel_id=1, source_target_pairs={{0,8},{8,0},{16,24},{24,16},{1,9},{9,1},{17,25},{25,17},{2,10},{10... | collective-permute-start | bytes 1081352 | tf_op jit(solution)/shard_map/ppermute | solution.py:50
  514.9 26.5 %collective-permute-start.63 = (bf16[256,2048]{1,0:T(8,128)(2,1)S(1)}, bf16[256,2048]{1,0:T(8,128)(2,1)S(1)}, u32[]{:S(2)}, u32[]{:S(2)}) collective-permute-start(bf16[256,2048]{1,0:T(8,128)(2,1)S(1)} %add_convert_fusion.4), channel_id=1, source_target_pairs={{0,2},{1,3},{2,6},{3,7},{4,0},{5,1},{6,4},{7,5},{8,10},{9,11},{10,... | collective-permute-start | bytes 3145736 | tf_op jit(solution)/shard_map/ppermute | solution.py:44
  528.3 39.6 %collective-permute-start.49 = (bf16[256,2048]{1,0:T(8,128)(2,1)S(1)}, bf16[256,2048]{1,0:T(8,128)(2,1)S(1)}, u32[]{:S(2)}, u32[]{:S(2)}) collective-permute-start(bf16[256,2048]{1,0:T(8,128)(2,1)S(1)} %add_convert_fusion.8), channel_id=1, source_target_pairs={{0,2},{1,3},{2,6},{3,7},{4,0},{5,1},{6,4},{7,5},{8,10},{9,11},{10,... | collective-permute-start | bytes 3145736 | tf_op jit(solution)/shard_map/ppermute | solution.py:44
  541.4 16.3 %collective-permute-start.136 = (bf16[88,2048]{1,0:T(8,128)(2,1)S(1)}, bf16[88,2048]{1,0:T(8,128)(2,1)S(1)}, u32[]{:S(2)}, u32[]{:S(2)}) collective-permute-start(bf16[88,2048]{1,0:T(8,128)(2,1)S(1)} %fusion.80), channel_id=1, source_target_pairs={{0,8},{8,0},{16,24},{24,16},{1,9},{9,1},{17,25},{25,17},{2,10},{10... | collective-permute-start | bytes 1081352 | tf_op jit(solution)/shard_map/ppermute | solution.py:50
  548.0 39.8 %collective-permute-start.117 = (bf16[176,2048]{1,0:T(8,128)(2,1)S(1)}, bf16[176,2048]{1,0:T(8,128)(2,1)S(1)}, u32[]{:S(2)}, u32[]{:S(2)}) collective-permute-start(bf16[176,2048]{1,0:T(8,128)(2,1)S(1)} %pad_maximum_fusion.14), channel_id=1, source_target_pairs={{0,8},{8,0},{16,24},{24,16},{1,9},{9,1},{17,25},{25,17},{2,10},{10... | collective-permute-start | bytes 2162696 | tf_op jit(solution)/shard_map/ppermute | solution.py:50
  556.9 31.9 %collective-permute-start.121 = (bf16[176,2048]{1,0:T(8,128)(2,1)S(1)}, bf16[176,2048]{1,0:T(8,128)(2,1)S(1)}, u32[]{:S(2)}, u32[]{:S(2)}) collective-permute-start(bf16[176,2048]{1,0:T(8,128)(2,1)S(1)} %pad_maximum_fusion.15), channel_id=1, source_target_pairs={{0,16},{8,24},{16,0},{24,8},{1,17},{9,25},{17,1},{25,9},{2,18},{10... | collective-permute-start | bytes 2162696 | tf_op jit(solution)/shard_map/ppermute | solution.py:50
  566.4 21.9 %collective-permute-start.125 = (bf16[176,2048]{1,0:T(8,128)(2,1)S(1)}, bf16[176,2048]{1,0:T(8,128)(2,1)S(1)}, u32[]{:S(2)}, u32[]{:S(2)}) collective-permute-start(bf16[176,2048]{1,0:T(8,128)(2,1)S(1)} %pad_maximum_fusion.16), channel_id=1, source_target_pairs={{0,8},{8,0},{16,24},{24,16},{1,9},{9,1},{17,25},{25,17},{2,10},{10... | collective-permute-start | bytes 2162696 | tf_op jit(solution)/shard_map/ppermute | solution.py:50
  566.8 22.3 %collective-permute-start.129 = (bf16[176,2048]{1,0:T(8,128)(2,1)S(1)}, bf16[176,2048]{1,0:T(8,128)(2,1)S(1)}, u32[]{:S(2)}, u32[]{:S(2)}) collective-permute-start(bf16[176,2048]{1,0:T(8,128)(2,1)S(1)} %pad_maximum_fusion.17), channel_id=1, source_target_pairs={{0,16},{8,24},{16,0},{24,8},{1,17},{9,25},{17,1},{25,9},{2,18},{10... | collective-permute-start | bytes 2162696 | tf_op jit(solution)/shard_map/ppermute | solution.py:50
  567.9 17.6 %collective-permute-start.79 = (f32[2048]{0:T(1024)S(1)}, f32[2048]{0:T(1024)S(1)}, u32[]{:S(2)}, u32[]{:S(2)}) collective-permute-start(f32[2048]{0:T(1024)S(1)} %add.1016), channel_id=1, source_target_pairs={{0,16},{8,24},{16,0},{24,8},{1,17},{9,25},{17,1},{25,9},{2,18},{10... | collective-permute-start | bytes 24584 | tf_op jit(solution)/shard_map/ppermute | solution.py:50
  585.6 16.7 %collective-permute-start.133 = (bf16[176,2048]{1,0:T(8,128)(2,1)S(1)}, bf16[176,2048]{1,0:T(8,128)(2,1)S(1)}, u32[]{:S(2)}, u32[]{:S(2)}) collective-permute-start(bf16[176,2048]{1,0:T(8,128)(2,1)S(1)} %pad_maximum_fusion.18), channel_id=1, source_target_pairs={{0,8},{8,0},{16,24},{24,16},{1,9},{9,1},{17,25},{25,17},{2,10},{10... | collective-permute-start | bytes 2162696 | tf_op jit(solution)/shard_map/ppermute | solution.py:50
  587.8 16.5 %collective-permute-start.137 = (bf16[176,2048]{1,0:T(8,128)(2,1)S(1)}, bf16[176,2048]{1,0:T(8,128)(2,1)S(1)}, u32[]{:S(2)}, u32[]{:S(2)}) collective-permute-start(bf16[176,2048]{1,0:T(8,128)(2,1)S(1)} %pad_maximum_fusion.19), channel_id=1, source_target_pairs={{0,16},{8,24},{16,0},{24,8},{1,17},{9,25},{17,1},{25,9},{2,18},{10... | collective-permute-start | bytes 2162696 | tf_op jit(solution)/shard_map/ppermute | solution.py:50
  588.3 17.2 %collective-permute-start.64 = (bf16[256,2048]{1,0:T(8,128)(2,1)S(1)}, bf16[256,2048]{1,0:T(8,128)(2,1)S(1)}, u32[]{:S(2)}, u32[]{:S(2)}) collective-permute-start(bf16[256,2048]{1,0:T(8,128)(2,1)S(1)} %get-tuple-element.42), channel_id=1, source_target_pairs={{0,1},{1,0},{2,3},{3,2},{4,5},{5,4},{6,7},{7,6},{8,9},{9,8},{10,11... | collective-permute-start | bytes 3145736 | tf_op jit(solution)/shard_map/ppermute | solution.py:47
  679.8 17.0 %collective-permute-start.65 = (bf16[256,2048]{1,0:T(8,128)(2,1)S(1)}, bf16[256,2048]{1,0:T(8,128)(2,1)S(1)}, u32[]{:S(2)}, u32[]{:S(2)}) collective-permute-start(bf16[256,2048]{1,0:T(8,128)(2,1)S(1)} %slice.392), channel_id=1, source_target_pairs={{0,1},{1,0},{2,3},{3,2},{4,5},{5,4},{6,7},{7,6},{8,9},{9,8},{10,11... | collective-permute-start | bytes 3145736 | tf_op jit(solution)/shard_map/ppermute | solution.py:47
  684.0 27.0 %collective-permute-start.80 = (bf16[2048,256]{1,0:T(8,128)(2,1)S(1)}, bf16[2048,256]{1,0:T(8,128)(2,1)S(1)}, u32[]{:S(2)}, u32[]{:S(2)}) collective-permute-start(bf16[2048,256]{1,0:T(8,128)(2,1)S(1)} %convolution_convert_fusion.11), channel_id=1, source_target_pairs={{0,2},{1,3},{2,6},{3,7},{4,0},{5,1},{6,4},{7,5},{8,10},{9,11},{10,... | collective-permute-start | bytes 3145736 | tf_op jit(solution)/shard_map/ppermute | solution.py:44
  701.6 57.6 %collective-permute-start.103 = (bf16[256,2048]{1,0:T(8,128)(2,1)S(1)}, bf16[256,2048]{1,0:T(8,128)(2,1)S(1)}, u32[]{:S(2)}, u32[]{:S(2)}) collective-permute-start(bf16[256,2048]{1,0:T(8,128)(2,1)S(1)} %convolution_convert_fusion.7), channel_id=1, source_target_pairs={{0,2},{1,3},{2,6},{3,7},{4,0},{5,1},{6,4},{7,5},{8,10},{9,11},{10,... | collective-permute-start | bytes 3145736 | tf_op jit(solution)/shard_map/ppermute | solution.py:44
  704.4 47.5 %collective-permute-start.71 = (f32[2048]{0:T(1024)S(1)}, f32[2048]{0:T(1024)S(1)}, u32[]{:S(2)}, u32[]{:S(2)}) collective-permute-start(f32[2048]{0:T(1024)S(1)} %add.1008), channel_id=1, source_target_pairs={{0,2},{1,3},{2,0},{3,1},{4,6},{5,7},{6,4},{7,5},{8,10},{9,11},{10,... | collective-permute-start | bytes 24584 | tf_op jit(solution)/shard_map/ppermute | solution.py:53
  704.7 47.3 %collective-permute-start.98 = (bf16[16,2048]{1,0:T(8,128)(2,1)S(1)}, bf16[16,2048]{1,0:T(8,128)(2,1)S(1)}, u32[]{:S(2)}, u32[]{:S(2)}) collective-permute-start(bf16[16,2048]{1,0:T(8,128)(2,1)S(1)} %pad_maximum_fusion.66), channel_id=1, source_target_pairs={{0,8},{8,0},{16,24},{24,16},{1,9},{9,1},{17,25},{25,17},{2,10},{10... | collective-permute-start | bytes 196616 | tf_op jit(solution)/shard_map/ppermute | solution.py:50
  713.4 75.6 %collective-permute-start.81 = (bf16[2048,256]{1,0:T(8,128)(2,1)S(1)}, bf16[2048,256]{1,0:T(8,128)(2,1)S(1)}, u32[]{:S(2)}, u32[]{:S(2)}) collective-permute-start(bf16[2048,256]{1,0:T(8,128)(2,1)S(1)} %fusion.33), channel_id=1, source_target_pairs={{0,2},{1,3},{2,6},{3,7},{4,0},{5,1},{6,4},{7,5},{8,10},{9,11},{10,... | collective-permute-start | bytes 3145736 | tf_op jit(solution)/shard_map/ppermute | solution.py:44
  763.1 13.7 %collective-permute-start.100 = (bf16[32,2048]{1,0:T(8,128)(2,1)S(1)}, bf16[32,2048]{1,0:T(8,128)(2,1)S(1)}, u32[]{:S(2)}, u32[]{:S(2)}) collective-permute-start(bf16[32,2048]{1,0:T(8,128)(2,1)S(1)} %collective-permute-done.99), channel_id=1, source_target_pairs={{0,2},{1,3},{2,6},{3,7},{4,0},{5,1},{6,4},{7,5},{8,10},{9,11},{10,... | collective-permute-start | bytes 393224 | tf_op jit(solution)/shard_map/ppermute | solution.py:44
  765.6 28.1 %collective-permute-start.104 = (bf16[256,2048]{1,0:T(8,128)(2,1)S(1)}, bf16[256,2048]{1,0:T(8,128)(2,1)S(1)}, u32[]{:S(2)}, u32[]{:S(2)}) collective-permute-start(bf16[256,2048]{1,0:T(8,128)(2,1)S(1)} %fusion.42), channel_id=1, source_target_pairs={{0,2},{1,3},{2,6},{3,7},{4,0},{5,1},{6,4},{7,5},{8,10},{9,11},{10,... | collective-permute-start | bytes 3145736 | tf_op jit(solution)/shard_map/ppermute | solution.py:44
  792.3 27.2 %collective-permute-start.82 = (bf16[2048,256]{1,0:T(8,128)(2,1)}, bf16[2048,256]{1,0:T(8,128)(2,1)}, u32[]{:S(2)}, u32[]{:S(2)}) collective-permute-start(bf16[2048,256]{1,0:T(8,128)(2,1)} %fusion.30), channel_id=1, source_target_pairs={{0,2},{1,3},{2,6},{3,7},{4,0},{5,1},{6,4},{7,5},{8,10},{9,11},{10,... | collective-permute-start | bytes 3145736 | tf_op jit(solution)/shard_map/ppermute | solution.py:44
  795.5 46.1 %collective-permute-start.105 = (bf16[256,2048]{1,0:T(8,128)(2,1)}, bf16[256,2048]{1,0:T(8,128)(2,1)}, u32[]{:S(2)}, u32[]{:S(2)}) collective-permute-start(bf16[256,2048]{1,0:T(8,128)(2,1)} %fusion.39), channel_id=1, source_target_pairs={{0,2},{1,3},{2,6},{3,7},{4,0},{5,1},{6,4},{7,5},{8,10},{9,11},{10,... | collective-permute-start | bytes 3145736 | tf_op jit(solution)/shard_map/ppermute | solution.py:44
  822.3 32.4 %collective-permute-start.83 = (bf16[2,256,256]{2,1,0:T(8,128)(2,1)S(1)}, bf16[2,256,256]{2,1,0:T(8,128)(2,1)S(1)}, u32[]{:S(2)}, u32[]{:S(2)}) collective-permute-start(bf16[2,256,256]{2,1,0:T(8,128)(2,1)S(1)} %dynamic-slice_bitcast_fusion.16), channel_id=1, source_target_pairs={{0,8},{8,0},{16,24},{24,16},{1,9},{9,1},{17,25},{25,17},{2,10},{10... | collective-permute-start | bytes 786440 | tf_op jit(solution)/shard_map/ppermute | solution.py:50
  822.9 32.0 %collective-permute-start.87 = (bf16[2,256,256]{2,1,0:T(8,128)(2,1)S(1)}, bf16[2,256,256]{2,1,0:T(8,128)(2,1)S(1)}, u32[]{:S(2)}, u32[]{:S(2)}) collective-permute-start(bf16[2,256,256]{2,1,0:T(8,128)(2,1)S(1)} %dynamic-slice_bitcast_fusion.15), channel_id=1, source_target_pairs={{0,16},{8,24},{16,0},{24,8},{1,17},{9,25},{17,1},{25,9},{2,18},{10... | collective-permute-start | bytes 786440 | tf_op jit(solution)/shard_map/ppermute | solution.py:50
  843.7 12.8 %collective-permute-start.106 = (bf16[2,32,2048]{2,1,0:T(8,128)(2,1)S(1)}, bf16[2,32,2048]{2,1,0:T(8,128)(2,1)S(1)}, u32[]{:S(2)}, u32[]{:S(2)}) collective-permute-start(bf16[2,32,2048]{2,1,0:T(8,128)(2,1)S(1)} %dynamic-slice_bitcast_fusion.14), channel_id=1, source_target_pairs={{0,8},{8,0},{16,24},{24,16},{1,9},{9,1},{17,25},{25,17},{2,10},{10... | collective-permute-start | bytes 786440 | tf_op jit(solution)/shard_map/ppermute | solution.py:50
  844.4 19.1 %collective-permute-start.110 = (bf16[2,32,2048]{2,1,0:T(8,128)(2,1)S(1)}, bf16[2,32,2048]{2,1,0:T(8,128)(2,1)S(1)}, u32[]{:S(2)}, u32[]{:S(2)}) collective-permute-start(bf16[2,32,2048]{2,1,0:T(8,128)(2,1)S(1)} %dynamic-slice_bitcast_fusion.13), channel_id=1, source_target_pairs={{0,16},{8,24},{16,0},{24,8},{1,17},{9,25},{17,1},{25,9},{2,18},{10... | collective-permute-start | bytes 786440 | tf_op jit(solution)/shard_map/ppermute | solution.py:50
  (152 other events, 1914.9 us)

commit v2 on v1

--- a/solution.py
+++ b/solution.py
@@ -51,6 +51,13 @@
 
     def across_tensor(self, x, bit):
         return lax.ppermute(x, "tensor", [(i, i ^ bit) for i in range(self.n_tensor)])
+
+    def neighbours(self, chip):
+        ahead, behind = chip * 0, chip * 0
+        for i, c in enumerate(self.order):
+            ahead = jnp.where(chip == c, self.order[(i + 1) % self.chips], ahead)
+            behind = jnp.where(chip == c, self.order[i - 1], behind)
+        return ahead, behind
 
     def orders(self, rows, unit):
         ways = len(self.bits)
@@ -357,6 +364,220 @@
     )(sp, query_two, grad_two, key_rows, value_rows)
 
 
+def mlp_kernel(
+    links, h_hbm, g_hbm, wg_hbm, wu_hbm, wd_hbm, ghn_ref, mlp_hbm, gw_hbm, uw_hbm, dw_hbm,
+    h_all, g_all, wg, wu, wd, act_t, gg_t, gu_t, keep, stage, pair_out, pair_in, ring_out, ring_in,
+    load_sem, ring_s, ring_r, swap_s, swap_r, pair_s, pair_r, rs_s, rs_r, stage_sem, store_sem,
+):
+    chips = links.chips
+    own, depth = h_hbm.shape
+    seq = chips * 2 * own
+    me = lax.axis_index("tensor")
+    chip, core = me // 2, lax.rem(me, 2)
+    ahead, behind = links.neighbours(chip)
+    right = {"tensor": ahead * 2 + core}
+    left = {"tensor": behind * 2 + core}
+    sibling = {"tensor": chip * 2 + 1 - core}
+
+    loads = [
+        pltpu.make_async_copy(h_hbm, h_all.at[0, 0], load_sem.at[0]),
+        pltpu.make_async_copy(wg_hbm, wg, load_sem.at[1]),
+        pltpu.make_async_copy(wu_hbm, wu, load_sem.at[2]),
+        pltpu.make_async_copy(wd_hbm, wd, load_sem.at[3]),
+        pltpu.make_async_copy(g_hbm, g_all, load_sem.at[4]),
+    ]
+    for load in loads:
+        load.start()
+    barrier = pltpu.get_barrier_semaphore()
+    for peer in (right, left, sibling):
+        pl.semaphore_signal(barrier, inc=1, device_id=peer, device_id_type=pl.DeviceIdType.MESH)
+    pl.semaphore_wait(barrier, 3)
+
+    def remote(src, dst, send, recv, peer):
+        return pltpu.make_async_remote_copy(
+            src_ref=src, dst_ref=dst, send_sem=send, recv_sem=recv, device_id=peer,
+            device_id_type=pl.DeviceIdType.MESH,
+        )
+
+    def ring(k):
+        return remote(h_all.at[k, 0], h_all.at[k + 1, 0], ring_s.at[k], ring_r.at[k], right)
+
+    def swap(k):
+        return remote(h_all.at[k, 0], h_all.at[k, 1], swap_s.at[k], swap_r.at[k], sibling)
+
+    def pair(k):
+        slot = lax.rem(k, 2)
+        return remote(pair_out.at[slot], pair_in.at[slot], pair_s.at[slot], pair_r.at[slot], sibling)
+
+    def scatter(k):
+        slot = lax.rem(k, 2)
+        return remote(ring_out.at[slot], ring_in.at[k], rs_s.at[k], rs_r.at[k], right)
+
+    def store(k, half):
+        return pltpu.make_async_copy(stage.at[half], mlp_hbm.at[k, half], stage_sem.at[half])
+
+    loads[0].wait()
+    ring(0).start()
+    swap(0).start()
+    for load in loads[1:]:
+        load.wait()
+
+    def half_chunk(k, half):
+        h, g = h_all[k, half], g_all[k, half]
+        gate = mm(h, wg[...], NT)
+        upward = mm(h, wu[...], NT)
+        grad_act = mm(g, wd[...], NT)
+        sigma = jax.nn.sigmoid(gate)
+        swish = gate * sigma
+        act = (swish * upward).astype(BF16)
+        gg = (grad_act * upward * sigma * (1.0 + gate * (1.0 - sigma))).astype(BF16)
+        gu = (grad_act * swish).astype(BF16)
+        columns = pl.ds(pl.multiple_of((2 * k + half) * own, own), own)
+        act_t[:, columns] = act.T
+        gg_t[:, columns] = gg.T
+        gu_t[:, columns] = gu.T
+        if half == 1:
+
+            @pl.when(k >= 2)
+            def _():
+                pair(k - 2).wait_send()
+
+        part = mm(gg, wg[...], NN) + mm(gu, wu[...], NN)
+        if half == 1:
+            pair_out[lax.rem(k, 2)] = part.astype(BF16)
+            pair(k).start()
+        else:
+            keep[...] = part
+
+        @pl.when(k >= 1)
+        def _():
+            store(k - 1, half).wait()
+
+        stage[half] = mm(act, wd[...], NN).astype(BF16)
+        store(k, half).start()
+
+    def chunk(k, _):
+        @pl.when(k >= 1)
+        def _():
+            ring(k - 1).wait_recv()
+
+            @pl.when(k < chips - 1)
+            def _():
+                ring(k).start()
+
+            swap(k).start()
+
+        swap(k).wait_recv()
+        half_chunk(k, 1)
+        half_chunk(k, 0)
+        pair(k).wait_recv()
+        total = keep[...] + pair_in[lax.rem(k, 2)].astype(F32)
+
+        @pl.when(k == 0)
+        def _():
+            ghn_ref[...] = total
+
+        @pl.when(k == 1)
+        def _():
+            ring_out[1] = total.astype(BF16)
+            scatter(k).start()
+
+        @pl.when(k >= 2)
+        def _():
+            scatter(k - 1).wait_recv()
+
+            @pl.when(k >= 3)
+            def _():
+                scatter(k - 2).wait_send()
+
+            ring_out[lax.rem(k, 2)] = (total + ring_in[k - 1].astype(F32)).astype(BF16)
+            scatter(k).start()
+
+        return 0
+
+    lax.fori_loop(0, chips, chunk, 0)
+
+    tile = 512
+
+    def columns_of(j, _):
+        at = pl.ds(pl.multiple_of(j * tile, tile), tile)
+        h = h_all[:, :, :, at].reshape(seq, tile)
+        g = g_all[:, :, :, at].reshape(seq, tile)
+        wg[:, at] = mm(gg_t[...], h, NN).astype(BF16)
+        wu[:, at] = mm(gu_t[...], h, NN).astype(BF16)
+        wd[:, at] = mm(act_t[...], g, NN).astype(BF16)
+        return 0
+
+    lax.fori_loop(0, depth // tile, columns_of, 0)
+    stores = [
+        pltpu.make_async_copy(wg, gw_hbm, store_sem.at[0]),
+        pltpu.make_async_copy(wu, uw_hbm, store_sem.at[1]),
+        pltpu.make_async_copy(wd, dw_hbm, store_sem.at[2]),
+    ]
+    for copy in stores:
+        copy.start()
+    scatter(chips - 1).wait_recv()
+    ghn_ref[...] += ring_in[chips - 1].astype(F32)
+
+    for copy in stores:
+        copy.wait()
+    for half in (0, 1):
+        store(chips - 1, half).wait()
+    for k in (chips - 2, chips - 1):
+        pair(k).wait_send()
+        scatter(k).wait_send()
+    for k in range(chips):
+        swap(k).wait_send()
+    for k in range(chips - 1):
+        ring(k).wait_send()
+
+
+def feed_forward(links, hidden_own, grad_chunks, gate_t, up_t, down):
+    own, depth = hidden_own.shape
+    chips, units = links.chips, down.shape[0]
+    seq = chips * 2 * own
+    anywhere = pl.BlockSpec(memory_space=pl.ANY)
+    dma = pltpu.SemaphoreType.DMA
+    return pl.pallas_call(
+        functools.partial(mlp_kernel, links),
+        in_specs=[anywhere] * 5,
+        out_specs=[pl.BlockSpec(memory_space=pltpu.VMEM)] + [anywhere] * 4,
+        out_shape=[
+            jax.ShapeDtypeStruct((own, depth), F32),
+            jax.ShapeDtypeStruct((chips, 2, own, depth), BF16),
+            jax.ShapeDtypeStruct((units, depth), BF16),
+            jax.ShapeDtypeStruct((units, depth), BF16),
+            jax.ShapeDtypeStruct((units, depth), BF16),
+        ],
+        scratch_shapes=[
+            pltpu.VMEM((chips, 2, own, depth), BF16),
+            pltpu.VMEM((chips, 2, own, depth), BF16),
+            pltpu.VMEM((units, depth), BF16),
+            pltpu.VMEM((units, depth), BF16),
+            pltpu.VMEM((units, depth), BF16),
+            pltpu.VMEM((units, seq), BF16),
+            pltpu.VMEM((units, seq), BF16),
+            pltpu.VMEM((units, seq), BF16),
+            pltpu.VMEM((own, depth), F32),
+            pltpu.VMEM((2, own, depth), BF16),
+            pltpu.VMEM((2, own, depth), BF16),
+            pltpu.VMEM((2, own, depth), BF16),
+            pltpu.VMEM((2, own, depth), BF16),
+            pltpu.VMEM((chips, own, depth), BF16),
+            dma((5,)),
+            dma((chips,)), dma((chips,)), dma((chips,)), dma((chips,)), dma((2,)), dma((2,)),
+            dma((chips,)), dma((chips,)), dma((2,)), dma((3,)),
+        ],
+        compiler_params=pltpu.CompilerParams(
+            collective_id=1, has_side_effects=True, vmem_limit_bytes=60 * 2**20
+        ),
+        cost_estimate=pl.CostEstimate(
+            flops=18 * seq * depth * units, bytes_accessed=64 * 2**20, transcendentals=seq * units
+        ),
+        name="feed_forward",
+    )(hidden_own, grad_chunks, gate_t, up_t, down)
+
+
 def rms_factor(values):
     return lax.rsqrt(jnp.mean(values * values, axis=-1, keepdims=True) + EPSILON)
 
@@ -429,37 +650,17 @@
     mlp_pre = hidden * mlp_scale
     hidden_own = (mlp_pre * mlp_gain).astype(BF16)
 
-    hidden_chunks, act_chunks, gate_chunks, up_chunks = [], [], [], []
-    mlp_parts, back_parts = [], []
-    for piece, grad in zip(ring_gather(links, hidden_own), grad_chunks):
-        chunk = both(links, piece)
-        gate = mm(chunk, w_gate, NN)
-        upward = mm(chunk, w_up, NN)
-        grad_act = mm(grad, w_down, NT)
-        sigma = jax.nn.sigmoid(gate)
-        swish = gate * sigma
-        activated = (swish * upward).astype(BF16)
-        grad_gate = (grad_act * upward * sigma * (1.0 + gate * (1.0 - sigma))).astype(BF16)
-        grad_up = (grad_act * swish).astype(BF16)
-        back_parts.append((mm(grad_gate, w_gate, NT) + mm(grad_up, w_up, NT)).astype(BF16))
-        mlp_parts.append(mm(activated, w_down, NN).astype(BF16))
-        hidden_chunks.append(chunk)
-        act_chunks.append(activated)
-        gate_chunks.append(grad_gate)
-        up_chunks.append(grad_up)
-
-    grad_hn = ring_scatter(links, [pair_sum(links, part) for part in back_parts])
-    mlp_out = ring_scatter(links, [pair_sum(links, part) for part in mlp_parts])
+    grad_stack = jnp.stack(grad_chunks).reshape(chips, 2, own, -1)
+    grad_hn, mlp_parts, gate_w, up_w, down_w = feed_forward(
+        links, hidden_own, grad_stack, w_gate.T, w_up.T, w_down
+    )
+    gate_w, up_w, down_w = lax.psum((gate_w, up_w, down_w), "dp")
+    gate_w_grad = gate_w.astype(F32).T
+    up_w_grad = up_w.astype(F32).T
+    down_w_grad = down_w.astype(F32)
+    mlp_sums = mlp_parts[:, 0].astype(F32) + links.swap(mlp_parts[:, 1]).astype(F32)
+    mlp_out = ring_scatter(links, [mlp_sums[k] for k in range(chips)])
     block_output = (hidden + mlp_out).astype(BF16)
-
-    hidden_all = jnp.concatenate(hidden_chunks, axis=0)
-    act_all = jnp.concatenate(act_chunks, axis=0)
-    gate_all = jnp.concatenate(gate_chunks, axis=0)
-    up_all = jnp.concatenate(up_chunks, axis=0)
-    grad_all = jnp.concatenate(grad_chunks, axis=0)
-    gate_w_grad = sum_dp(links, mm(gate_all, hidden_all, TN).astype(BF16), me_dp).T
-    up_w_grad = sum_dp(links, mm(up_all, hidden_all, TN).astype(BF16), me_dp).T
-    down_w_grad = sum_dp(links, mm(act_all, grad_all, TN).astype(BF16), me_dp)
 
     mlp_gain_part = jnp.sum(grad_hn * mlp_pre, axis=0)
     scaled_mlp = grad_hn * mlp_gain

time: 897 us -> 861 us (0.960)
  Pallas kernels: 43.7 us -> 202 us
  starting transfers between devices: 234 us -> 103 us
  matrix products: 116 us -> 46.3 us
  local copies, waits for them, and re-layouts: 71.4 us -> 44.3 us
  waiting for transfers between devices: 341 us -> 358 us
  other arithmetic: 56.4 us -> 65.9 us
    pallas_call x0 -> x1, Pallas kernels: none -> 151 us  [feed_forward(): pl.pallas_call(functools.partial(mlp_kernel, links), in_specs=[anywhere]...]
    ppermute x72 -> x48, starting transfers between devices: 146 us -> 53.7 us  [across(): return lax.ppermute(x, 'dp', [(i, i ^ bit) for i in range(self.n_dp)])]
    ppermute x36 -> x30, waiting for transfers between devices: 130 us -> 202 us  [ring(): return lax.ppermute(x, 'tensor', self.ring_pairs)]
    dot_general x42 -> x15, matrix products: 116 us -> 46.3 us  [mm(): lax.dot_general(left, right, (dims, ((), ())), preferred_element_type=F32)]
    ppermute x72 -> x48, waiting for transfers between devices: 162 us -> 94.6 us  [across(): return lax.ppermute(x, 'dp', [(i, i ^ bit) for i in range(self.n_dp)])]
    ppermute x36 -> x30, starting transfers between devices: 83.1 us -> 40.7 us  [ring(): return lax.ppermute(x, 'tensor', self.ring_pairs)]
    psum x0 -> x1, waiting for transfers between devices: none -> 31.9 us  [local(): gate_w, up_w, down_w = lax.psum((gate_w, up_w, down_w), 'dp')]
    unnamed x249 -> x151, local copies, waits for them, and re-layouts: 51.1 us -> 24.6 us
  transfers between devices with their start and end apart: 138 -> 98, of which waited for: 63 -> 55; matrix products, arithmetic and copies ran while one was open for 25% -> 13% of each run, Pallas kernels for 3% -> 4%
where the time goes in v2:
time: 861 us; the launch traced here: 853 us
  waiting for transfers between devices  358 us (42%)
  Pallas kernels  202 us (23%)
  starting transfers between devices  103 us (12%)
  other arithmetic  65.9 us (8%)
  matrix products  46.3 us (5%)
  local copies, waits for them, and re-layouts  44.3 us (5%)
  between operations  34.4 us (4%)
    ppermute x30, waiting for transfers between devices, ring(): return lax.ppermute(x, 'tensor', self.ring_pairs)  202 us
    pallas_call x1, Pallas kernels, feed_forward(): pl.pallas_call(functools.partial(mlp_kernel, links), in_specs=[anywhere]...  151 us
    ppermute x48, waiting for transfers between devices, across(): return lax.ppermute(x, 'dp', [(i, i ^ bit) for i in range(self.n_dp)])  94.6 us
    ppermute x48, starting transfers between devices, across(): return lax.ppermute(x, 'dp', [(i, i ^ bit) for i in range(self.n_dp)])  53.7 us
    dot_general x15, matrix products, mm(): lax.dot_general(left, right, (dims, ((), ())), preferred_element_type=F32)  46.3 us
    ppermute x30, starting transfers between devices, ring(): return lax.ppermute(x, 'tensor', self.ring_pairs)  40.7 us
    psum x1, waiting for transfers between devices, local(): gate_w, up_w, down_w = lax.psum((gate_w, up_w, down_w), 'dp')  31.9 us
    ppermute x6, waiting for transfers between devices, across_tensor(): lax.ppermute(x, 'tensor', [(i, i ^ bit) for i in range(self.n_tensor)])  26.8 us
  transfers between devices with their start and end apart: 98, of which 55 were waited for; matrix products, arithmetic and copies ran while one was open for 13% of the time, Pallas kernels for 4%

profile of v2, /device:TPU:0, one launch (start us, length us, event | category | flops | bytes accessed | tf_op | source)
XLA Modules:
  0.0 853.0 jit_solution(15360064526123928210)
XLA Ops:
  9.0 3.0 collective-permute-start.1
  47.6 13.5 %collective-permute-done.17 = bf16[256,256]{1,0:T(8,128)(2,1)S(1)} collective-permute-done((bf16[256,256]{1,0:T(8,128)(2,1)}, bf16[256,256]{1,0:T(8,128)(2,1)S(1)}, u32[]{:S(2)}, u32[]{:S(2)}) %collective-permute-start.17) | collective-permute-done | bytes 131104 | tf_op jit(solution)/shard_map/ppermute | solution.py:44
  63.1 5.3 collective-permute-done.18
  74.3 8.2 collective-permute-done.25
  85.7 3.2 collective-permute-done.22
  91.1 5.0 collective-permute-done.24
  111.2 2.8 collective-permute-done.28
  115.0 3.7 collective-permute-done.30
  120.9 2.9 collective-permute-done.31
  124.5 4.3 collective-permute-done.33
  129.6 4.1 collective-permute-done.14
  135.2 4.9 collective-permute-done.10
  141.1 5.4 collective-permute-done.27
  148.6 4.3 collective-permute-done.29
  165.0 3.8 collective-permute-done.32
  173.7 4.9 fusion.40.q_ref
  178.6 11.5 %attend.1 = (bf16[512,1024]{1,0:T(8,128)(2,1)}, bf16[512,1024]{1,0:T(8,128)(2,1)}, f32[8,8,512]{2,1,0:T(8,128)}) custom-call(s32[3]{0:T(128)} %pad_add_fusion.sp_ref, f32[512,1024]{1,0:T(8,128)} %fusion.40.q_ref, f32[512,128]{1,0:T(8,128)} %get-tuple-element.112.c_ref, f32[512,128]{1,0:T(8,128)} %get-tuple-element.113.s_ref, ...), custom_call_target="tpu_custom_call" | custom-call | flops 8589934592 | bytes 8388608 | tf_op jit(solution)/shard_map/attend/pallas_call | solution.py:294
  191.4 4.8 fusion.117
  196.3 4.5 collective-permute-start.41
  203.5 26.5 %collective-permute-done.41 = bf16[256,2048]{1,0:T(8,128)(2,1)S(1)} collective-permute-done((bf16[256,2048]{1,0:T(8,128)(2,1)S(1)}, bf16[256,2048]{1,0:T(8,128)(2,1)S(1)}, u32[]{:S(2)}, u32[]{:S(2)}) %collective-permute-start.41) | collective-permute-done | bytes 1048608 | tf_op jit(solution)/shard_map/ppermute | solution.py:44
  232.9 4.4 pad_maximum_fusion.g_hbm
  237.4 151.3 %feed_forward.1 = (f32[256,2048]{1,0:T(8,128)}, bf16[4,2,256,2048]{3,2,1,0:T(8,128)(2,1)}, bf16[704,2048]{1,0:T(8,128)(2,1)}, bf16[704,2048]{1,0:T(8,128)(2,1)}, bf16[704,2048]{1,0:T(8,128)(2,1)}) custom-call(bf16[256,2048]{1,0:T(8,128)(2,1)} %multiply_convert_fusion.h_hbm, bf16[4,2,256,2048]{3,2,1,0:T(8,128)(2,1)} %pad_maximum_fusion.g_hbm, ...), custom_call_target="tpu_custom_call" | custom-call | flops 53150220288 | bytes 67108864 | tf_op jit(solution)/shard_map/feed_forward/pallas_call | solution.py:541
  394.9 22.5 %second_back.1 = (f32[2048,128]{1,0:T(8,128)}, f32[2048,128]{1,0:T(8,128)}) custom-call(s32[3]{0:T(128)} %pad_add_fusion.sp_ref, bf16[2048,256]{1,0:T(8,128)(2,1)} %q_ref.1, bf16[2048,256]{1,0:T(8,128)(2,1)} %do_ref.1, bf16[2048,128]{1,0:T(8,128)(2,1)} %get-tuple-element.69.k_ref, bf16[2048,128]{1,0:T(8,128)(2,1)} %get-tuple-element.68.v_ref), custom_call_target="tpu_custom_call" | custom-call | flops 8589934592 | bytes 2097152 | tf_op jit(solution)/shard_map/second_back/pallas_call | solution.py:350
  417.3 6.2 convolution_convert_fusion.9.do_ref
  423.5 16.5 %attend_back.1 = (bf16[512,1024]{1,0:T(8,128)(2,1)}, f32[2048,128]{1,0:T(8,128)}, f32[2048,128]{1,0:T(8,128)}) custom-call(s32[3]{0:T(128)} %pad_add_fusion.sp_ref, bf16[512,1024]{1,0:T(8,128)(2,1)} %get-tuple-element.26.q_ref, bf16[512,1024]{1,0:T(8,128)(2,1)} %convolution_convert_fusion.9.do_ref, bf16[512,1024]{1,0:T(8,128)(2,1)} %get-tuple-element.23.ctx_ref, ...), custom_call_target="tpu_custom_call" | custom-call | flops 21474836480 | bytes 8388608 | tf_op jit(solution)/shard_map/attend_back/pallas_call | solution.py:320
  449.8 6.7 collective-permute-start.50
  458.4 6.1 collective-permute-done.50
  466.1 6.1 collective-permute-start.51
  490.4 4.5 collective-permute-done.75
  503.9 4.9 slice_bitcast_fusion
  509.1 3.2 collective-permute-start.59
  517.8 2.8 fusion.39
  525.8 17.0 %collective-permute-done.63 = bf16[2048,256]{1,0:T(8,128)(2,1)S(1)} collective-permute-done((bf16[2048,256]{1,0:T(8,128)(2,1)S(1)}, bf16[2048,256]{1,0:T(8,128)(2,1)S(1)}, u32[]{:S(2)}, u32[]{:S(2)}) %collective-permute-start.63) | collective-permute-done | bytes 1048608 | tf_op jit(solution)/shard_map/ppermute | solution.py:44
  544.5 3.0 fusion.12
  547.6 17.7 %collective-permute-done.86 = bf16[256,2048]{1,0:T(8,128)(2,1)S(1)} collective-permute-done((bf16[256,2048]{1,0:T(8,128)(2,1)S(1)}, bf16[256,2048]{1,0:T(8,128)(2,1)S(1)}, u32[]{:S(2)}, u32[]{:S(2)}) %collective-permute-start.86) | collective-permute-done | bytes 1048608 | tf_op jit(solution)/shard_map/ppermute | solution.py:44
  565.3 3.3 fusion.21
  569.5 21.1 %collective-permute-done.82 = bf16[32,2048]{1,0:T(8,128)(2,1)S(1)} collective-permute-done((bf16[32,2048]{1,0:T(8,128)(2,1)S(1)}, bf16[32,2048]{1,0:T(8,128)(2,1)S(1)}, u32[]{:S(2)}, u32[]{:S(2)}) %collective-permute-start.82) | collective-permute-done | bytes 131104 | tf_op jit(solution)/shard_map/ppermute | solution.py:44
  590.6 2.8 fusion.28
  594.7 2.9 collective-permute-start.60
  597.6 17.6 %collective-permute-done.60 = f32[2048]{0:T(1024)S(1)} collective-permute-done((f32[2048]{0:T(1024)S(1)}, f32[2048]{0:T(1024)S(1)}, u32[]{:S(2)}, u32[]{:S(2)}) %collective-permute-start.60) | collective-permute-done | bytes 8224 | tf_op jit(solution)/shard_map/ppermute | solution.py:53
  615.2 3.6 collective-permute-done.54
  622.6 4.4 collective-permute-done.55
  627.0 3.6 collective-permute-done.62
  634.4 3.6 collective-permute-done.57
  641.5 3.8 fusion.9
  645.3 3.8 fusion.18
  652.4 3.1 copy.68
  655.5 5.8 convert_add_fusion
  662.6 9.9 %collective-permute-done.65 = bf16[2048,256]{1,0:T(8,128)(2,1)} collective-permute-done((bf16[2048,256]{1,0:T(8,128)(2,1)}, bf16[2048,256]{1,0:T(8,128)(2,1)}, u32[]{:S(2)}, u32[]{:S(2)}) %collective-permute-start.65) | collective-permute-done | bytes 1048608 | tf_op jit(solution)/shard_map/ppermute | solution.py:44
  678.7 16.3 %collective-permute-done.88 = bf16[256,2048]{1,0:T(8,128)(2,1)} collective-permute-done((bf16[256,2048]{1,0:T(8,128)(2,1)}, bf16[256,2048]{1,0:T(8,128)(2,1)}, u32[]{:S(2)}, u32[]{:S(2)}) %collective-permute-start.88) | collective-permute-done | bytes 1048608 | tf_op jit(solution)/shard_map/ppermute | solution.py:44
  695.0 3.1 fusion.15
  702.8 10.3 %collective-permute-done.89 = bf16[2,32,2048]{2,1,0:T(8,128)(2,1)S(1)} collective-permute-done((bf16[2,32,2048]{2,1,0:T(8,128)(2,1)S(1)}, bf16[2,32,2048]{2,1,0:T(8,128)(2,1)S(1)}, u32[]{:S(2)}, u32[]{:S(2)}) %collective-permute-start.89) | collective-permute-done | bytes 262176 | tf_op jit(solution)/shard_map/ppermute | solution.py:50
  716.8 3.8 collective-permute-done.67
  722.9 3.3 collective-permute-done.90
  728.5 3.3 collective-permute-done.68
  734.1 3.3 collective-permute-done.91
  739.7 4.2 collective-permute-done.69
  744.2 4.6 collective-permute-done.92
  752.4 22.2 %collective-permute-done.45 = bf16[256,2048]{1,0:T(8,128)(2,1)S(1)} collective-permute-done((bf16[256,2048]{1,0:T(8,128)(2,1)S(1)}, bf16[256,2048]{1,0:T(8,128)(2,1)S(1)}, u32[]{:S(2)}, u32[]{:S(2)}) %collective-permute-start.45) | collective-permute-done | bytes 1048608 | tf_op jit(solution)/shard_map/ppermute | solution.py:44
  777.3 22.2 %collective-permute-done.46 = bf16[256,2048]{1,0:T(8,128)(2,1)S(1)} collective-permute-done((bf16[256,2048]{1,0:T(8,128)(2,1)S(1)}, bf16[256,2048]{1,0:T(8,128)(2,1)S(1)}, u32[]{:S(2)}, u32[]{:S(2)}) %collective-permute-start.46) | collective-permute-done | bytes 1048608 | tf_op jit(solution)/shard_map/ppermute | solution.py:44
  802.1 31.9 %all-reduce.3.cloned.1.call-done = (bf16[2048,704]{0,1:T(8,128)(2,1)}, bf16[2048,704]{0,1:T(8,128)(2,1)}, bf16[704,2048]{1,0:T(8,128)(2,1)}) async-done(((bf16[2048,704]{0,1:T(8,128)(2,1)}, bf16[2048,704]{0,1:T(8,128)(2,1)}, bf16[704,2048]{1,0:T(8,128)(2,1)}), (bf16[2048,704]{0,1:T(8,128)(2,1)}, bf16[2048,704]{0,1:T(8,128)(2,1)}, bf16[704,2048]{1,0:T(8,128)(2,1)})) %all-reduce.3.cloned.1.call-update) | async-done | bytes 8650768 | tf_op jit(solution)/shard_map/psum | solution.py:657
  834.0 5.3 transpose.47
  839.3 3.3 transpose.49
  842.6 3.3 convert_element_type.470
  (454 shorter events, 189.1 us)
Async XLA Ops:
  7.2 826.8 %all-reduce.3.cloned.1.call-start = ((), (), s32[]{:S(2)}) async-start(), calls=%async_computation | async-start | bytes 17301504 | tf_op jit(solution)/shard_map/psum | solution.py:657
  9.0 37.0 %collective-permute-start.1 = (bf16[512,256]{1,0:T(8,128)(2,1)}, bf16[512,256]{1,0:T(8,128)(2,1)}, u32[]{:S(2)}, u32[]{:S(2)}) collective-permute-start(bf16[512,256]{1,0:T(8,128)(2,1)} %constant_dynamic-slice_fusion.5), channel_id=1, source_target_pairs={{0,2},{1,3},{2,6},{3,7},{4,0},{5,1},{6,4},{7,5},{8,10},{9,11},{10,... | collective-permute-start | bytes 786440 | tf_op jit(solution)/shard_map/ppermute | solution.py:44
  15.7 158.0 %collective-permute-start = (bf16[256,2048]{1,0:T(8,128)(2,1)S(1)}, bf16[256,2048]{1,0:T(8,128)(2,1)}, u32[]{:S(2)}, u32[]{:S(2)}) collective-permute-start(bf16[256,2048]{1,0:T(8,128)(2,1)S(1)} %fusion.22), channel_id=1, source_target_pairs={{0,1},{1,0},{2,3},{3,2},{4,5},{5,4},{6,7},{7,6},{8,9},{9,8},{10,11... | collective-permute-start | bytes 3145736 | tf_op jit(solution)/shard_map/ppermute | solution.py:47
  22.0 19.6 %collective-permute-start.16 = (bf16[256,256]{1,0:T(8,128)(2,1)}, bf16[256,256]{1,0:T(8,128)(2,1)}, u32[]{:S(2)}, u32[]{:S(2)}) collective-permute-start(bf16[256,256]{1,0:T(8,128)(2,1)} %pad_maximum_fusion.48), channel_id=1, source_target_pairs={{0,2},{1,3},{2,6},{3,7},{4,0},{5,1},{6,4},{7,5},{8,10},{9,11},{10,... | collective-permute-start | bytes 393224 | tf_op jit(solution)/shard_map/ppermute | solution.py:44
  26.3 17.2 %collective-permute-start.20 = (bf16[64,2048]{1,0:T(8,128)(2,1)}, bf16[64,2048]{1,0:T(8,128)(2,1)}, u32[]{:S(2)}, u32[]{:S(2)}) collective-permute-start(bf16[64,2048]{1,0:T(8,128)(2,1)} %constant_dynamic-slice_fusion.4), channel_id=1, source_target_pairs={{0,2},{1,3},{2,6},{3,7},{4,0},{5,1},{6,4},{7,5},{8,10},{9,11},{10,... | collective-permute-start | bytes 786440 | tf_op jit(solution)/shard_map/ppermute | solution.py:44
  26.7 137.0 %collective-permute-start.37 = (bf16[256,2048]{1,0:T(8,128)(2,1)S(1)}, bf16[256,2048]{1,0:T(8,128)(2,1)}, u32[]{:S(2)}, u32[]{:S(2)}) collective-permute-start(bf16[256,2048]{1,0:T(8,128)(2,1)S(1)} %copy-done.6), channel_id=1, source_target_pairs={{0,2},{1,3},{2,6},{3,7},{4,0},{5,1},{6,4},{7,5},{8,10},{9,11},{10,... | collective-permute-start | bytes 3145736 | tf_op jit(solution)/shard_map/ppermute | solution.py:44
  41.6 19.5 %collective-permute-start.17 = (bf16[256,256]{1,0:T(8,128)(2,1)}, bf16[256,256]{1,0:T(8,128)(2,1)S(1)}, u32[]{:S(2)}, u32[]{:S(2)}) collective-permute-start(bf16[256,256]{1,0:T(8,128)(2,1)} %collective-permute-done.16), channel_id=1, source_target_pairs={{0,2},{1,3},{2,6},{3,7},{4,0},{5,1},{6,4},{7,5},{8,10},{9,11},{10,... | collective-permute-start | bytes 393224 | tf_op jit(solution)/shard_map/ppermute | solution.py:44
  44.4 18.1 %collective-permute-start.21 = (bf16[32,2048]{1,0:T(8,128)(2,1)S(1)}, bf16[32,2048]{1,0:T(8,128)(2,1)S(1)}, u32[]{:S(2)}, u32[]{:S(2)}) collective-permute-start(bf16[32,2048]{1,0:T(8,128)(2,1)S(1)} %get-tuple-element.83), channel_id=1, source_target_pairs={{0,8},{8,0},{16,24},{24,16},{1,9},{9,1},{17,25},{25,17},{2,10},{10... | collective-permute-start | bytes 393224 | tf_op jit(solution)/shard_map/ppermute | solution.py:50
  47.0 22.9 %collective-permute-start.2 = (bf16[256,256]{1,0:T(8,128)(2,1)S(1)}, bf16[256,256]{1,0:T(8,128)(2,1)S(1)}, u32[]{:S(2)}, u32[]{:S(2)}) collective-permute-start(bf16[256,256]{1,0:T(8,128)(2,1)S(1)} %get-tuple-element.87), channel_id=1, source_target_pairs={{0,8},{8,0},{16,24},{24,16},{1,9},{9,1},{17,25},{25,17},{2,10},{10... | collective-permute-start | bytes 393224 | tf_op jit(solution)/shard_map/ppermute | solution.py:50
  61.1 9.0 %collective-permute-start.4 = (bf16[256,256]{1,0:T(8,128)(2,1)S(1)}, bf16[256,256]{1,0:T(8,128)(2,1)S(1)}, u32[]{:S(2)}, u32[]{:S(2)}) collective-permute-start(bf16[256,256]{1,0:T(8,128)(2,1)S(1)} %get-tuple-element.86), channel_id=1, source_target_pairs={{0,16},{8,24},{16,0},{24,8},{1,17},{9,25},{17,1},{25,9},{2,18},{10... | collective-permute-start | bytes 393224 | tf_op jit(solution)/shard_map/ppermute | solution.py:50
  69.9 14.2 %collective-permute-start.6 = (bf16[512,256]{1,0:T(8,128)(2,1)}, bf16[512,256]{1,0:T(8,128)(2,1)S(1)}, u32[]{:S(2)}, u32[]{:S(2)}) collective-permute-start(bf16[512,256]{1,0:T(8,128)(2,1)} %collective-permute-done.1), channel_id=1, source_target_pairs={{0,2},{1,3},{2,6},{3,7},{4,0},{5,1},{6,4},{7,5},{8,10},{9,11},{10,... | collective-permute-start | bytes 786440 | tf_op jit(solution)/shard_map/ppermute | solution.py:44
  70.0 12.5 %collective-permute-start.25 = (bf16[64,2048]{1,0:T(8,128)(2,1)}, bf16[64,2048]{1,0:T(8,128)(2,1)S(1)}, u32[]{:S(2)}, u32[]{:S(2)}) collective-permute-start(bf16[64,2048]{1,0:T(8,128)(2,1)} %collective-permute-done.20), channel_id=1, source_target_pairs={{0,2},{1,3},{2,6},{3,7},{4,0},{5,1},{6,4},{7,5},{8,10},{9,11},{10,... | collective-permute-start | bytes 786440 | tf_op jit(solution)/shard_map/ppermute | solution.py:44
  74.1 30.9 %collective-permute-start.3 = (bf16[512,256]{1,0:T(8,128)(2,1)S(1)}, bf16[512,256]{1,0:T(8,128)(2,1)S(1)}, u32[]{:S(2)}, u32[]{:S(2)}) collective-permute-start(bf16[512,256]{1,0:T(8,128)(2,1)S(1)} %pad_maximum_fusion.30), channel_id=1, source_target_pairs={{0,16},{8,24},{16,0},{24,8},{1,17},{9,25},{17,1},{25,9},{2,18},{10... | collective-permute-start | bytes 786440 | tf_op jit(solution)/shard_map/ppermute | solution.py:50
  84.1 24.5 %collective-permute-start.5 = (bf16[512,256]{1,0:T(8,128)(2,1)S(1)}, bf16[512,256]{1,0:T(8,128)(2,1)S(1)}, u32[]{:S(2)}, u32[]{:S(2)}) collective-permute-start(bf16[512,256]{1,0:T(8,128)(2,1)S(1)} %pad_maximum_fusion.31), channel_id=1, source_target_pairs={{0,8},{8,0},{16,24},{24,16},{1,9},{9,1},{17,25},{25,17},{2,10},{10... | collective-permute-start | bytes 786440 | tf_op jit(solution)/shard_map/ppermute | solution.py:50
  88.9 7.2 collective-permute-start.24
  108.6 11.6 %collective-permute-start.11 = (bf16[512,256]{1,0:T(8,128)(2,1)S(1)}, bf16[512,256]{1,0:T(8,128)(2,1)S(1)}, u32[]{:S(2)}, u32[]{:S(2)}) collective-permute-start(bf16[512,256]{1,0:T(8,128)(2,1)S(1)} %collective-permute-done.6), channel_id=1, source_target_pairs={{0,2},{1,3},{2,6},{3,7},{4,0},{5,1},{6,4},{7,5},{8,10},{9,11},{10,... | collective-permute-start | bytes 786440 | tf_op jit(solution)/shard_map/ppermute | solution.py:44
  111.2 7.6 collective-permute-start.30
  114.0 21.1 %collective-permute-start.8 = (bf16[512,256]{1,0:T(8,128)(2,1)S(1)}, bf16[512,256]{1,0:T(8,128)(2,1)S(1)}, u32[]{:S(2)}, u32[]{:S(2)}) collective-permute-start(bf16[512,256]{1,0:T(8,128)(2,1)S(1)} %pad_maximum_fusion.32), channel_id=1, source_target_pairs={{0,16},{8,24},{16,0},{24,8},{1,17},{9,25},{17,1},{25,9},{2,18},{10... | collective-permute-start | bytes 786440 | tf_op jit(solution)/shard_map/ppermute | solution.py:50
  120.2 9.3 %collective-permute-start.12 = (bf16[256,256]{1,0:T(8,128)(2,1)S(1)}, bf16[256,256]{1,0:T(8,128)(2,1)S(1)}, u32[]{:S(2)}, u32[]{:S(2)}) collective-permute-start(bf16[256,256]{1,0:T(8,128)(2,1)S(1)} %get-tuple-element.91), channel_id=1, source_target_pairs={{0,8},{8,0},{16,24},{24,16},{1,9},{9,1},{17,25},{25,17},{2,10},{10... | collective-permute-start | bytes 393224 | tf_op jit(solution)/shard_map/ppermute | solution.py:50
  129.5 71.5 %collective-permute-start.36 = (bf16[256,2048]{1,0:T(8,128)(2,1)S(1)}, bf16[256,2048]{1,0:T(8,128)(2,1)S(1)}, u32[]{:S(2)}, u32[]{:S(2)}) collective-permute-start(bf16[256,2048]{1,0:T(8,128)(2,1)S(1)} %copy-done.6), channel_id=1, source_target_pairs={{0,1},{1,0},{2,3},{3,2},{4,5},{5,4},{6,7},{7,6},{8,9},{9,8},{10,11... | collective-permute-start | bytes 3145736 | tf_op jit(solution)/shard_map/ppermute | solution.py:47
  135.1 23.2 %collective-permute-start.19 = (bf16[4,256,256]{2,1,0:T(8,128)(2,1)S(1)}, bf16[4,256,256]{2,1,0:T(8,128)(2,1)S(1)}, u32[]{:S(2)}, u32[]{:S(2)}) collective-permute-start(bf16[4,256,256]{2,1,0:T(8,128)(2,1)S(1)} %pad_maximum_fusion.18), channel_id=1, source_target_pairs={{0,1},{1,0},{2,3},{3,2},{4,5},{5,4},{6,7},{7,6},{8,9},{9,8},{10,11... | collective-permute-start | bytes 1572872 | tf_op jit(solution)/shard_map/ppermute | solution.py:47
  152.8 9.4 %collective-permute-start.13 = (bf16[512,256]{1,0:T(8,128)(2,1)S(1)}, bf16[512,256]{1,0:T(8,128)(2,1)S(1)}, u32[]{:S(2)}, u32[]{:S(2)}) collective-permute-start(bf16[512,256]{1,0:T(8,128)(2,1)S(1)} %pad_maximum_fusion.34), channel_id=1, source_target_pairs={{0,16},{8,24},{16,0},{24,8},{1,17},{9,25},{17,1},{25,9},{2,18},{10... | collective-permute-start | bytes 786440 | tf_op jit(solution)/shard_map/ppermute | solution.py:50
  164.6 31.6 %collective-permute-start.39 = (bf16[256,2048]{1,0:T(8,128)(2,1)}, bf16[256,2048]{1,0:T(8,128)(2,1)S(1)}, u32[]{:S(2)}, u32[]{:S(2)}) collective-permute-start(bf16[256,2048]{1,0:T(8,128)(2,1)} %collective-permute-done.37), channel_id=1, source_target_pairs={{0,2},{1,3},{2,6},{3,7},{4,0},{5,1},{6,4},{7,5},{8,10},{9,11},{10,... | collective-permute-start | bytes 3145736 | tf_op jit(solution)/shard_map/ppermute | solution.py:44
  168.7 33.0 %collective-permute-start.38 = (bf16[256,2048]{1,0:T(8,128)(2,1)}, bf16[256,2048]{1,0:T(8,128)(2,1)}, u32[]{:S(2)}, u32[]{:S(2)}) collective-permute-start(bf16[256,2048]{1,0:T(8,128)(2,1)} %collective-permute-done.37), channel_id=1, source_target_pairs={{0,1},{1,0},{2,3},{3,2},{4,5},{5,4},{6,7},{7,6},{8,9},{9,8},{10,11... | collective-permute-start | bytes 3145736 | tf_op jit(solution)/shard_map/ppermute | solution.py:47
  196.3 33.8 %collective-permute-start.41 = (bf16[256,2048]{1,0:T(8,128)(2,1)S(1)}, bf16[256,2048]{1,0:T(8,128)(2,1)S(1)}, u32[]{:S(2)}, u32[]{:S(2)}) collective-permute-start(bf16[256,2048]{1,0:T(8,128)(2,1)S(1)} %collective-permute-done.39), channel_id=1, source_target_pairs={{0,2},{1,3},{2,6},{3,7},{4,0},{5,1},{6,4},{7,5},{8,10},{9,11},{10,... | collective-permute-start | bytes 3145736 | tf_op jit(solution)/shard_map/ppermute | solution.py:44
  200.9 29.2 %collective-permute-start.35 = (bf16[256,2048]{1,0:T(8,128)(2,1)S(1)}, bf16[256,2048]{1,0:T(8,128)(2,1)S(1)}, u32[]{:S(2)}, u32[]{:S(2)}) collective-permute-start(bf16[256,2048]{1,0:T(8,128)(2,1)S(1)} %slice.324), channel_id=1, source_target_pairs={{0,1},{1,0},{2,3},{3,2},{4,5},{5,4},{6,7},{7,6},{8,9},{9,8},{10,11... | collective-permute-start | bytes 3145736 | tf_op jit(solution)/shard_map/ppermute | solution.py:47
  201.2 30.7 %collective-permute-start.40 = (bf16[256,2048]{1,0:T(8,128)(2,1)S(1)}, bf16[256,2048]{1,0:T(8,128)(2,1)S(1)}, u32[]{:S(2)}, u32[]{:S(2)}) collective-permute-start(bf16[256,2048]{1,0:T(8,128)(2,1)S(1)} %collective-permute-done.39), channel_id=1, source_target_pairs={{0,1},{1,0},{2,3},{3,2},{4,5},{5,4},{6,7},{7,6},{8,9},{9,8},{10,11... | collective-permute-start | bytes 3145736 | tf_op jit(solution)/shard_map/ppermute | solution.py:47
  392.8 24.5 %collective-permute-start.47 = (bf16[256,2048]{1,0:T(8,128)(2,1)}, bf16[256,2048]{1,0:T(8,128)(2,1)}, u32[]{:S(2)}, u32[]{:S(2)}) collective-permute-start(bf16[256,2048]{1,0:T(8,128)(2,1)} %fusion.103), channel_id=1, source_target_pairs={{0,1},{1,0},{2,3},{3,2},{4,5},{5,4},{6,7},{7,6},{8,9},{9,8},{10,11... | collective-permute-start | bytes 3145736 | tf_op jit(solution)/shard_map/ppermute | solution.py:47
  449.8 14.6 %collective-permute-start.50 = (bf16[256,256]{1,0:T(8,128)(2,1)}, bf16[256,256]{1,0:T(8,128)(2,1)S(1)}, u32[]{:S(2)}, u32[]{:S(2)}) collective-permute-start(bf16[256,256]{1,0:T(8,128)(2,1)} %fusion.84), channel_id=1, source_target_pairs={{0,2},{1,3},{2,6},{3,7},{4,0},{5,1},{6,4},{7,5},{8,10},{9,11},{10,... | collective-permute-start | bytes 393224 | tf_op jit(solution)/shard_map/ppermute | solution.py:44
  466.1 10.2 %collective-permute-start.51 = (bf16[256,256]{1,0:T(8,128)(2,1)}, bf16[256,256]{1,0:T(8,128)(2,1)}, u32[]{:S(2)}, u32[]{:S(2)}) collective-permute-start(bf16[256,256]{1,0:T(8,128)(2,1)} %fusion.72), channel_id=1, source_target_pairs={{0,2},{1,3},{2,6},{3,7},{4,0},{5,1},{6,4},{7,5},{8,10},{9,11},{10,... | collective-permute-start | bytes 393224 | tf_op jit(solution)/shard_map/ppermute | solution.py:44
  499.4 9.7 %collective-permute-start.58 = (f32[2048]{0:T(1024)S(1)}, f32[2048]{0:T(1024)S(1)}, u32[]{:S(2)}, u32[]{:S(2)}) collective-permute-start(f32[2048]{0:T(1024)S(1)} %get-tuple-element.46), channel_id=1, source_target_pairs={{0,1},{1,0},{2,3},{3,2},{4,5},{5,4},{6,7},{7,6},{8,9},{9,8},{10,11... | collective-permute-start | bytes 24584 | tf_op jit(solution)/shard_map/ppermute | solution.py:53
  502.0 10.3 %collective-permute-start.77 = (bf16[32,2048]{1,0:T(8,128)(2,1)S(1)}, bf16[32,2048]{1,0:T(8,128)(2,1)S(1)}, u32[]{:S(2)}, u32[]{:S(2)}) collective-permute-start(bf16[32,2048]{1,0:T(8,128)(2,1)S(1)} %fusion.70), channel_id=1, source_target_pairs={{0,2},{1,3},{2,6},{3,7},{4,0},{5,1},{6,4},{7,5},{8,10},{9,11},{10,... | collective-permute-start | bytes 393224 | tf_op jit(solution)/shard_map/ppermute | solution.py:44
  508.8 146.6 %collective-permute-start.43 = (bf16[4,256,2048]{2,1,0:T(8,128)(2,1)}, bf16[4,256,2048]{2,1,0:T(8,128)(2,1)}, u32[]{:S(2)}, u32[]{:S(2)}) collective-permute-start(bf16[4,256,2048]{2,1,0:T(8,128)(2,1)} %slice_bitcast_fusion), channel_id=1, source_target_pairs={{0,1},{1,0},{2,3},{3,2},{4,5},{5,4},{6,7},{7,6},{8,9},{9,8},{10,11... | collective-permute-start | bytes 12582920 | tf_op jit(solution)/shard_map/ppermute | solution.py:47
  509.1 84.4 %collective-permute-start.59 = (f32[2048]{0:T(1024)S(1)}, f32[2048]{0:T(1024)S(1)}, u32[]{:S(2)}, u32[]{:S(2)}) collective-permute-start(f32[2048]{0:T(1024)S(1)} %add.772), channel_id=1, source_target_pairs={{0,2},{1,3},{2,0},{3,1},{4,6},{5,7},{6,4},{7,5},{8,10},{9,11},{10,... | collective-permute-start | bytes 24584 | tf_op jit(solution)/shard_map/ppermute | solution.py:53
  515.9 27.0 %collective-permute-start.63 = (bf16[2048,256]{1,0:T(8,128)(2,1)S(1)}, bf16[2048,256]{1,0:T(8,128)(2,1)S(1)}, u32[]{:S(2)}, u32[]{:S(2)}) collective-permute-start(bf16[2048,256]{1,0:T(8,128)(2,1)S(1)} %convolution_convert_fusion.4), channel_id=1, source_target_pairs={{0,2},{1,3},{2,6},{3,7},{4,0},{5,1},{6,4},{7,5},{8,10},{9,11},{10,... | collective-permute-start | bytes 3145736 | tf_op jit(solution)/shard_map/ppermute | solution.py:44
  520.7 47.9 %collective-permute-start.48 = (bf16[256,2048]{1,0:T(8,128)(2,1)S(1)}, bf16[256,2048]{1,0:T(8,128)(2,1)S(1)}, u32[]{:S(2)}, u32[]{:S(2)}) collective-permute-start(bf16[256,2048]{1,0:T(8,128)(2,1)S(1)} %slice.323), channel_id=1, source_target_pairs={{0,1},{1,0},{2,3},{3,2},{4,5},{5,4},{6,7},{7,6},{8,9},{9,8},{10,11... | collective-permute-start | bytes 3145736 | tf_op jit(solution)/shard_map/ppermute | solution.py:47
  525.6 39.7 %collective-permute-start.86 = (bf16[256,2048]{1,0:T(8,128)(2,1)S(1)}, bf16[256,2048]{1,0:T(8,128)(2,1)S(1)}, u32[]{:S(2)}, u32[]{:S(2)}) collective-permute-start(bf16[256,2048]{1,0:T(8,128)(2,1)S(1)} %convolution_convert_fusion), channel_id=1, source_target_pairs={{0,2},{1,3},{2,6},{3,7},{4,0},{5,1},{6,4},{7,5},{8,10},{9,11},{10,... | collective-permute-start | bytes 3145736 | tf_op jit(solution)/shard_map/ppermute | solution.py:44
  547.5 94.0 %collective-permute-start.64 = (bf16[2048,256]{1,0:T(8,128)(2,1)}, bf16[2048,256]{1,0:T(8,128)(2,1)}, u32[]{:S(2)}, u32[]{:S(2)}) collective-permute-start(bf16[2048,256]{1,0:T(8,128)(2,1)} %fusion.12), channel_id=1, source_target_pairs={{0,2},{1,3},{2,6},{3,7},{4,0},{5,1},{6,4},{7,5},{8,10},{9,11},{10,... | collective-permute-start | bytes 3145736 | tf_op jit(solution)/shard_map/ppermute | solution.py:44
  565.3 25.3 %collective-permute-start.82 = (bf16[32,2048]{1,0:T(8,128)(2,1)S(1)}, bf16[32,2048]{1,0:T(8,128)(2,1)S(1)}, u32[]{:S(2)}, u32[]{:S(2)}) collective-permute-start(bf16[32,2048]{1,0:T(8,128)(2,1)S(1)} %get-tuple-element.93), channel_id=1, source_target_pairs={{0,2},{1,3},{2,6},{3,7},{4,0},{5,1},{6,4},{7,5},{8,10},{9,11},{10,... | collective-permute-start | bytes 393224 | tf_op jit(solution)/shard_map/ppermute | solution.py:44
  568.6 76.7 %collective-permute-start.87 = (bf16[256,2048]{1,0:T(8,128)(2,1)}, bf16[256,2048]{1,0:T(8,128)(2,1)}, u32[]{:S(2)}, u32[]{:S(2)}) collective-permute-start(bf16[256,2048]{1,0:T(8,128)(2,1)} %fusion.21), channel_id=1, source_target_pairs={{0,2},{1,3},{2,6},{3,7},{4,0},{5,1},{6,4},{7,5},{8,10},{9,11},{10,... | collective-permute-start | bytes 3145736 | tf_op jit(solution)/shard_map/ppermute | solution.py:44
  590.6 43.8 %collective-permute-start.83 = (bf16[32,2048]{1,0:T(8,128)(2,1)S(1)}, bf16[32,2048]{1,0:T(8,128)(2,1)}, u32[]{:S(2)}, u32[]{:S(2)}) collective-permute-start(bf16[32,2048]{1,0:T(8,128)(2,1)S(1)} %collective-permute-done.82), channel_id=1, source_target_pairs={{0,2},{1,3},{2,6},{3,7},{4,0},{5,1},{6,4},{7,5},{8,10},{9,11},{10,... | collective-permute-start | bytes 393224 | tf_op jit(solution)/shard_map/ppermute | solution.py:44
  594.7 20.5 %collective-permute-start.60 = (f32[2048]{0:T(1024)S(1)}, f32[2048]{0:T(1024)S(1)}, u32[]{:S(2)}, u32[]{:S(2)}) collective-permute-start(f32[2048]{0:T(1024)S(1)} %add.773), channel_id=1, source_target_pairs={{0,4},{1,5},{2,6},{3,7},{4,0},{5,1},{6,2},{7,3},{8,12},{9,13},{10,... | collective-permute-start | bytes 24584 | tf_op jit(solution)/shard_map/ppermute | solution.py:53
  641.4 8.0 collective-permute-start.85
  645.3 27.2 %collective-permute-start.65 = (bf16[2048,256]{1,0:T(8,128)(2,1)}, bf16[2048,256]{1,0:T(8,128)(2,1)}, u32[]{:S(2)}, u32[]{:S(2)}) collective-permute-start(bf16[2048,256]{1,0:T(8,128)(2,1)} %fusion.9), channel_id=1, source_target_pairs={{0,2},{1,3},{2,6},{3,7},{4,0},{5,1},{6,4},{7,5},{8,10},{9,11},{10,... | collective-permute-start | bytes 3145736 | tf_op jit(solution)/shard_map/ppermute | solution.py:44
  649.1 45.9 %collective-permute-start.88 = (bf16[256,2048]{1,0:T(8,128)(2,1)}, bf16[256,2048]{1,0:T(8,128)(2,1)}, u32[]{:S(2)}, u32[]{:S(2)}) collective-permute-start(bf16[256,2048]{1,0:T(8,128)(2,1)} %fusion.18), channel_id=1, source_target_pairs={{0,2},{1,3},{2,6},{3,7},{4,0},{5,1},{6,4},{7,5},{8,10},{9,11},{10,... | collective-permute-start | bytes 3145736 | tf_op jit(solution)/shard_map/ppermute | solution.py:44
  661.4 87.5 %collective-permute-start.44 = (bf16[256,2048]{1,0:T(8,128)(2,1)S(1)}, bf16[256,2048]{1,0:T(8,128)(2,1)S(1)}, u32[]{:S(2)}, u32[]{:S(2)}) collective-permute-start(bf16[256,2048]{1,0:T(8,128)(2,1)S(1)} %fusion.38), channel_id=1, source_target_pairs={{0,2},{1,3},{2,6},{3,7},{4,0},{5,1},{6,4},{7,5},{8,10},{9,11},{10,... | collective-permute-start | bytes 3145736 | tf_op jit(solution)/shard_map/ppermute | solution.py:44
  675.1 26.7 %collective-permute-start.66 = (bf16[2,256,256]{2,1,0:T(8,128)(2,1)S(1)}, bf16[2,256,256]{2,1,0:T(8,128)(2,1)S(1)}, u32[]{:S(2)}, u32[]{:S(2)}) collective-permute-start(bf16[2,256,256]{2,1,0:T(8,128)(2,1)S(1)} %dynamic-slice_bitcast_fusion.4), channel_id=1, source_target_pairs={{0,8},{8,0},{16,24},{24,16},{1,9},{9,1},{17,25},{25,17},{2,10},{10... | collective-permute-start | bytes 786440 | tf_op jit(solution)/shard_map/ppermute | solution.py:50
  676.8 25.6 %collective-permute-start.70 = (bf16[2,256,256]{2,1,0:T(8,128)(2,1)S(1)}, bf16[2,256,256]{2,1,0:T(8,128)(2,1)S(1)}, u32[]{:S(2)}, u32[]{:S(2)}) collective-permute-start(bf16[2,256,256]{2,1,0:T(8,128)(2,1)S(1)} %dynamic-slice_bitcast_fusion.3), channel_id=1, source_target_pairs={{0,16},{8,24},{16,0},{24,8},{1,17},{9,25},{17,1},{25,9},{2,18},{10... | collective-permute-start | bytes 786440 | tf_op jit(solution)/shard_map/ppermute | solution.py:50
  698.3 14.8 %collective-permute-start.89 = (bf16[2,32,2048]{2,1,0:T(8,128)(2,1)S(1)}, bf16[2,32,2048]{2,1,0:T(8,128)(2,1)S(1)}, u32[]{:S(2)}, u32[]{:S(2)}) collective-permute-start(bf16[2,32,2048]{2,1,0:T(8,128)(2,1)S(1)} %dynamic-slice_bitcast_fusion.2), channel_id=1, source_target_pairs={{0,8},{8,0},{16,24},{24,16},{1,9},{9,1},{17,25},{25,17},{2,10},{10... | collective-permute-start | bytes 786440 | tf_op jit(solution)/shard_map/ppermute | solution.py:50
  700.1 15.0 %collective-permute-start.93 = (bf16[2,32,2048]{2,1,0:T(8,128)(2,1)S(1)}, bf16[2,32,2048]{2,1,0:T(8,128)(2,1)S(1)}, u32[]{:S(2)}, u32[]{:S(2)}) collective-permute-start(bf16[2,32,2048]{2,1,0:T(8,128)(2,1)S(1)} %dynamic-slice_bitcast_fusion.1), channel_id=1, source_target_pairs={{0,16},{8,24},{16,0},{24,8},{1,17},{9,25},{17,1},{25,9},{2,18},{10... | collective-permute-start | bytes 786440 | tf_op jit(solution)/shard_map/ppermute | solution.py:50
  701.9 18.7 %collective-permute-start.67 = (bf16[256,256]{1,0:T(8,128)(2,1)S(1)}, bf16[256,256]{1,0:T(8,128)(2,1)S(1)}, u32[]{:S(2)}, u32[]{:S(2)}) collective-permute-start(bf16[256,256]{1,0:T(8,128)(2,1)S(1)} %dynamic-slice_bitcast_fusion.8), channel_id=1, source_target_pairs={{0,16},{8,24},{16,0},{24,8},{1,17},{9,25},{17,1},{25,9},{2,18},{10... | collective-permute-start | bytes 393224 | tf_op jit(solution)/shard_map/ppermute | solution.py:50
  702.5 19.8 %collective-permute-start.71 = (bf16[256,256]{1,0:T(8,128)(2,1)S(1)}, bf16[256,256]{1,0:T(8,128)(2,1)S(1)}, u32[]{:S(2)}, u32[]{:S(2)}) collective-permute-start(bf16[256,256]{1,0:T(8,128)(2,1)S(1)} %dynamic-slice_bitcast_fusion.7), channel_id=1, source_target_pairs={{0,8},{8,0},{16,24},{24,16},{1,9},{9,1},{17,25},{25,17},{2,10},{10... | collective-permute-start | bytes 393224 | tf_op jit(solution)/shard_map/ppermute | solution.py:50
  713.2 13.0 %collective-permute-start.90 = (bf16[32,2048]{1,0:T(8,128)(2,1)S(1)}, bf16[32,2048]{1,0:T(8,128)(2,1)S(1)}, u32[]{:S(2)}, u32[]{:S(2)}) collective-permute-start(bf16[32,2048]{1,0:T(8,128)(2,1)S(1)} %dynamic-slice_bitcast_fusion.6), channel_id=1, source_target_pairs={{0,16},{8,24},{16,0},{24,8},{1,17},{9,25},{17,1},{25,9},{2,18},{10... | collective-permute-start | bytes 393224 | tf_op jit(solution)/shard_map/ppermute | solution.py:50
  715.2 12.7 %collective-permute-start.94 = (bf16[32,2048]{1,0:T(8,128)(2,1)S(1)}, bf16[32,2048]{1,0:T(8,128)(2,1)S(1)}, u32[]{:S(2)}, u32[]{:S(2)}) collective-permute-start(bf16[32,2048]{1,0:T(8,128)(2,1)S(1)} %dynamic-slice_bitcast_fusion.5), channel_id=1, source_target_pairs={{0,8},{8,0},{16,24},{24,16},{1,9},{9,1},{17,25},{25,17},{2,10},{10... | collective-permute-start | bytes 393224 | tf_op jit(solution)/shard_map/ppermute | solution.py:50
  720.6 11.2 %collective-permute-start.68 = (bf16[256,256]{1,0:T(8,128)(2,1)S(1)}, bf16[256,256]{1,0:T(8,128)(2,1)S(1)}, u32[]{:S(2)}, u32[]{:S(2)}) collective-permute-start(bf16[256,256]{1,0:T(8,128)(2,1)S(1)} %fusion.68), channel_id=1, source_target_pairs={{0,16},{8,24},{16,0},{24,8},{1,17},{9,25},{17,1},{25,9},{2,18},{10... | collective-permute-start | bytes 393224 | tf_op jit(solution)/shard_map/ppermute | solution.py:50
  722.3 9.8 %collective-permute-start.72 = (bf16[256,256]{1,0:T(8,128)(2,1)S(1)}, bf16[256,256]{1,0:T(8,128)(2,1)S(1)}, u32[]{:S(2)}, u32[]{:S(2)}) collective-permute-start(bf16[256,256]{1,0:T(8,128)(2,1)S(1)} %fusion.67), channel_id=1, source_target_pairs={{0,8},{8,0},{16,24},{24,16},{1,9},{9,1},{17,25},{25,17},{2,10},{10... | collective-permute-start | bytes 393224 | tf_op jit(solution)/shard_map/ppermute | solution.py:50
  726.2 11.2 %collective-permute-start.91 = (bf16[32,2048]{1,0:T(8,128)(2,1)S(1)}, bf16[32,2048]{1,0:T(8,128)(2,1)S(1)}, u32[]{:S(2)}, u32[]{:S(2)}) collective-permute-start(bf16[32,2048]{1,0:T(8,128)(2,1)S(1)} %fusion.66), channel_id=1, source_target_pairs={{0,16},{8,24},{16,0},{24,8},{1,17},{9,25},{17,1},{25,9},{2,18},{10... | collective-permute-start | bytes 393224 | tf_op jit(solution)/shard_map/ppermute | solution.py:50
  727.9 9.9 %collective-permute-start.95 = (bf16[32,2048]{1,0:T(8,128)(2,1)S(1)}, bf16[32,2048]{1,0:T(8,128)(2,1)S(1)}, u32[]{:S(2)}, u32[]{:S(2)}) collective-permute-start(bf16[32,2048]{1,0:T(8,128)(2,1)S(1)} %fusion.65), channel_id=1, source_target_pairs={{0,8},{8,0},{16,24},{24,16},{1,9},{9,1},{17,25},{25,17},{2,10},{10... | collective-permute-start | bytes 393224 | tf_op jit(solution)/shard_map/ppermute | solution.py:50
  731.8 12.1 %collective-permute-start.69 = (bf16[512,256]{1,0:T(8,128)(2,1)S(1)}, bf16[512,256]{1,0:T(8,128)(2,1)S(1)}, u32[]{:S(2)}, u32[]{:S(2)}) collective-permute-start(bf16[512,256]{1,0:T(8,128)(2,1)S(1)} %pad_maximum_fusion.42), channel_id=1, source_target_pairs={{0,8},{8,0},{16,24},{24,16},{1,9},{9,1},{17,25},{25,17},{2,10},{10... | collective-permute-start | bytes 786440 | tf_op jit(solution)/shard_map/ppermute | solution.py:50
  732.2 11.9 %collective-permute-start.73 = (bf16[512,256]{1,0:T(8,128)(2,1)S(1)}, bf16[512,256]{1,0:T(8,128)(2,1)S(1)}, u32[]{:S(2)}, u32[]{:S(2)}) collective-permute-start(bf16[512,256]{1,0:T(8,128)(2,1)S(1)} %pad_maximum_fusion.43), channel_id=1, source_target_pairs={{0,16},{8,24},{16,0},{24,8},{1,17},{9,25},{17,1},{25,9},{2,18},{10... | collective-permute-start | bytes 786440 | tf_op jit(solution)/shard_map/ppermute | solution.py:50
  737.5 11.4 %collective-permute-start.92 = (bf16[64,2048]{1,0:T(8,128)(2,1)S(1)}, bf16[64,2048]{1,0:T(8,128)(2,1)S(1)}, u32[]{:S(2)}, u32[]{:S(2)}) collective-permute-start(bf16[64,2048]{1,0:T(8,128)(2,1)S(1)} %pad_maximum_fusion.44), channel_id=1, source_target_pairs={{0,8},{8,0},{16,24},{24,16},{1,9},{9,1},{17,25},{25,17},{2,10},{10... | collective-permute-start | bytes 786440 | tf_op jit(solution)/shard_map/ppermute | solution.py:50
  737.8 14.5 %collective-permute-start.96 = (bf16[64,2048]{1,0:T(8,128)(2,1)S(1)}, bf16[64,2048]{1,0:T(8,128)(2,1)S(1)}, u32[]{:S(2)}, u32[]{:S(2)}) collective-permute-start(bf16[64,2048]{1,0:T(8,128)(2,1)S(1)} %pad_maximum_fusion.45), channel_id=1, source_target_pairs={{0,16},{8,24},{16,0},{24,8},{1,17},{9,25},{17,1},{25,9},{2,18},{10... | collective-permute-start | bytes 786440 | tf_op jit(solution)/shard_map/ppermute | solution.py:50
  749.2 25.4 %collective-permute-start.45 = (bf16[256,2048]{1,0:T(8,128)(2,1)S(1)}, bf16[256,2048]{1,0:T(8,128)(2,1)S(1)}, u32[]{:S(2)}, u32[]{:S(2)}) collective-permute-start(bf16[256,2048]{1,0:T(8,128)(2,1)S(1)} %fusion.32), channel_id=1, source_target_pairs={{0,2},{1,3},{2,6},{3,7},{4,0},{5,1},{6,4},{7,5},{8,10},{9,11},{10,... | collective-permute-start | bytes 3145736 | tf_op jit(solution)/shard_map/ppermute | solution.py:44
  775.0 24.5 %collective-permute-start.46 = (bf16[256,2048]{1,0:T(8,128)(2,1)S(1)}, bf16[256,2048]{1,0:T(8,128)(2,1)S(1)}, u32[]{:S(2)}, u32[]{:S(2)}) collective-permute-start(bf16[256,2048]{1,0:T(8,128)(2,1)S(1)} %fusion.34), channel_id=1, source_target_pairs={{0,2},{1,3},{2,6},{3,7},{4,0},{5,1},{6,4},{7,5},{8,10},{9,11},{10,... | collective-permute-start | bytes 3145736 | tf_op jit(solution)/shard_map/ppermute | solution.py:44
  (80 other events, 1031.5 us)
Sparse Core Ops, SparseCore 0:
  632.5 201.5 all-reduce.2

commit v3 on v2

--- a/solution.py
+++ b/solution.py
@@ -250,45 +250,17 @@
             dq_ref[...] = (g * c_ref[...] - pltpu.roll(g, HD // 2, 1) * s_ref[...]).astype(BF16)
 
 
-def second_kernel(blocks, sp_ref, q_ref, do_ref, k_ref, v_ref, dk_ref, dv_ref):
-    rows = q_ref.shape[0]
-    block, two_docs = pl.program_id(0), sp_ref[1]
-
-    @pl.when((block == 0) & (pl.program_id(1) == 0))
-    def _():
-        dk_ref[...] = jnp.zeros_like(dk_ref)
-        dv_ref[...] = jnp.zeros_like(dv_ref)
-
-    q, do = q_ref[...], do_ref[...]
-    count, low = span(block, two_docs, rows)
-    mask = diagonal((rows, rows), 1, 0)
-    for n in range(1, blocks + 1):
-
-        @pl.when(count == n)
-        def _(n=n):
-            near = (n - 1) * rows
-            parts = [pl.ds(low + near, rows)] + ([pl.ds(low, near)] if n > 1 else [])
-            scores = [mm(k_ref[keys, :], q, NT) * SCALE2 for keys in parts]
-            scores[0] = jnp.where(mask, scores[0], MASKED)
-            top = functools.reduce(jnp.maximum, [jnp.max(s, axis=0, keepdims=True) for s in scores])
-            lifted = [jnp.exp2(s - top) for s in scores]
-            total = sum(jnp.sum(p, axis=0, keepdims=True) for p in lifted)
-            inverse = 1.0 / total
-            back = [mm(v_ref[keys, :], do, NT) for keys in parts]
-            dot = sum(jnp.sum(p * b, axis=0, keepdims=True) for p, b in zip(lifted, back)) * inverse
-            for keys, p, b in zip(parts, lifted, back):
-                p = p * inverse
-                dv_ref[keys, :] += mm(p.astype(BF16), do, NN)
-                dk_ref[keys, :] += mm((p * (b - dot)).astype(BF16), q, NN)
-
-
 def whole(shape):
     return pl.BlockSpec(shape, lambda *_: (0,) * len(shape))
 
 
-def attend(sp, q_lin, cosine, sine, key_rows, value_rows):
+def second_half(seq):
+    return pl.BlockSpec((seq, HD), lambda *_: (0, 1))
+
+
+def attend(sp, q_lin, cosine, sine, kv_all):
     rows, width = q_lin.shape
-    seq = key_rows.shape[0]
+    seq = kv_all.shape[0]
     heads = width // HD
     column = pl.BlockSpec((rows, HD), lambda h, *_: (0, h))
     return pl.pallas_call(
@@ -296,7 +268,7 @@
         grid_spec=pltpu.PrefetchScalarGridSpec(
             num_scalar_prefetch=1,
             grid=(heads,),
-            in_specs=[column, whole((rows, HD)), whole((rows, HD)), whole((seq, HD)), whole((seq, HD))],
+            in_specs=[column, whole((rows, HD)), whole((rows, HD)), whole((seq, HD)), second_half(seq)],
             out_specs=[column, column, pl.BlockSpec((1, 8, rows), lambda h, *_: (h, 0, 0))],
         ),
         out_shape=[
@@ -309,12 +281,12 @@
             flops=8 * heads * rows * seq * HD, bytes_accessed=16 * rows * width, transcendentals=heads * rows * seq
         ),
         name="attend",
-    )(sp, q_lin, cosine, sine, key_rows, value_rows)
-
-
-def attend_back(sp, queries, grad_context, context, lse, cosine, sine, key_rows, value_rows, dk0, dv0):
+    )(sp, q_lin, cosine, sine, kv_all, kv_all)
+
+
+def attend_back(sp, queries, grad_context, context, lse, cosine, sine, kv_all, key_rows_t, dk0, dv0):
     rows, width = queries.shape
-    seq = key_rows.shape[0]
+    seq = kv_all.shape[0]
     heads = width // HD
     column = pl.BlockSpec((rows, HD), lambda h, *_: (0, h))
     return pl.pallas_call(
@@ -324,7 +296,7 @@
             grid=(heads,),
             in_specs=[
                 column, column, column, pl.BlockSpec((1, 8, rows), lambda h, *_: (h, 0, 0)),
-                whole((rows, HD)), whole((rows, HD)), whole((seq, HD)), whole((HD, seq)), whole((seq, HD)),
+                whole((rows, HD)), whole((rows, HD)), whole((seq, HD)), whole((HD, seq)), second_half(seq),
                 whole((seq, HD)), whole((seq, HD)),
             ],
             out_specs=[column, whole((seq, HD)), whole((seq, HD))],
@@ -339,36 +311,226 @@
             flops=20 * heads * rows * seq * HD, bytes_accessed=16 * rows * width, transcendentals=heads * rows * seq
         ),
         name="attend_back",
-    )(sp, queries, grad_context, context, lse, cosine, sine, key_rows, key_rows.T, value_rows, dk0, dv0)
-
-
-def second_back(sp, query_two, grad_two, key_rows, value_rows):
-    seq, width = query_two.shape
+    )(sp, queries, grad_context, context, lse, cosine, sine, kv_all, key_rows_t, kv_all, dk0, dv0)
+
+
+def second_unit(block, rows, q, do, kv, dk_ref, dv_ref, late):
+    mask = diagonal((rows, rows), 1, 0)
+    first = block * rows
+    parts = [(pl.ds(first, rows), True, False)]
+    middle = SEQ_SHORT * (first // SEQ_SHORT)
+    if first > middle:
+        parts.append((pl.ds(middle, first - middle), False, False))
+    if middle:
+        parts.append((pl.ds(0, middle), False, True))
+    scores = []
+    for keys, masked, far in parts:
+        score = mm(kv[keys, :HD], q, NT) * SCALE2
+        scores.append(jnp.where(mask, score, MASKED) if masked else score + late if far else score)
+    top = functools.reduce(jnp.maximum, [jnp.max(score, axis=0, keepdims=True) for score in scores])
+    lifted = [jnp.exp2(score - top) for score in scores]
+    inverse = 1.0 / sum(jnp.sum(p, axis=0, keepdims=True) for p in lifted)
+    back = [mm(kv[keys, HD:], do, NT) for keys, _, _ in parts]
+    dot = sum(jnp.sum(p * b, axis=0, keepdims=True) for p, b in zip(lifted, back)) * inverse
+    for (keys, _, _), p, b in zip(parts, lifted, back):
+        p = p * inverse
+        dv_ref[keys, :] += mm(p.astype(BF16), do, NN)
+        dk_ref[keys, :] += mm((p * (b - dot)).astype(BF16), q, NN)
+
+
+FRONT_ORDER = (
+    "kv q1 o1 kv", "q1 q2 o1 o2", "kv q1 q2 q3", "kv o1 o2 o3", "kv* s q2 q3", "s o2 o3 s", "q2 q3 s o2",
+    "o3 s q3 s", "g s o3 s",
+    "q1* o1* q2* o2*", "q3* o3* s* g*",
+)
+
+
+def front_kernel(
+    links, docs, tokens, gain, w_kv, cosine, sine, q_two, g_two, wq_hbm, wo_hbm, og_hbm,
+    normed, wq_out, wo_out, og_up, og_pair, og_up_pair, kv_out, kt_ref, dk_ref, dv_ref,
+    kv, ss, rs, ls,
+):
+    chips, bits, n_dp = links.chips, links.bits, links.n_dp
+    own, depth = tokens.shape
+    seq = own * links.n_tensor
+    width = wq_hbm.shape[1]
+    me = lax.axis_index("tensor")
+    me_dp = lax.axis_index("dp")
+    chip, core = me // 2, lax.rem(me, 2)
+    ahead, behind = links.neighbours(chip)
+    right = {"tensor": ahead * 2 + core}
+    left = {"tensor": behind * 2 + core}
+    sibling = {"tensor": me ^ 1}
+    barrier = pltpu.get_barrier_semaphore()
+    peers = [right, left, sibling] + [{"dp": me_dp ^ bit} for bit in bits]
+    for peer in peers:
+        pl.semaphore_signal(barrier, inc=1, device_id=peer, device_id_type=pl.DeviceIdType.MESH)
+
+    copies = []
+
+    def send(src, dst, peer):
+        number = len(copies)
+        copy = mesh_copy(src, dst, ss.at[number], rs.at[number], peer)
+        copy.start()
+        copies.append(copy)
+        return copy
+
+    def q_piece(ref, k, j, way, size=1):
+        rows = depth // n_dp // 2
+        at = pl.ds(pl.multiple_of((2 * j + way) * rows, rows), size * rows)
+        return ref.at[at, :] if k is None else ref.at[at, pl.ds(k * width, width)]
+
+    def o_piece(ref, k, j, way, size=1):
+        rows, half = width // n_dp, depth // 2
+        at = pl.ds(pl.multiple_of((k or 0) * width + j * rows, rows), rows)
+        return ref.at[at, pl.ds(way * half, size * half)]
+
+    pl.semaphore_wait(barrier, len(peers))
+    locals_ = [
+        pltpu.make_async_copy(wq_hbm, wq_out.at[:, pl.ds(0, width)], ls.at[0]),
+        pltpu.make_async_copy(wo_hbm, wo_out.at[pl.ds(0, width), :], ls.at[1]),
+    ]
+    for copy in locals_:
+        copy.start()
+    hops = {}
+    for name, piece, src, dst in (("q", q_piece, wq_hbm, wq_out), ("o", o_piece, wo_hbm, wo_out)):
+        hops[name, 1] = send(piece(src, None, me_dp, 0, 2), piece(dst, 1, me_dp, 0, 2), right)
+
+    x = tokens[...].astype(F32)
+    own_rows = pl.ds(0, own)
+    normed[own_rows] = (x * lax.rsqrt(jnp.mean(x * x, axis=1, keepdims=True) + EPSILON) * gain[...]).astype(BF16)
+    normed_swap = send(normed.at[own_rows], normed.at[pl.ds(own, own)], sibling)
+    lin = mm(normed[own_rows], w_kv[...], NN)
+    key = lin[:, :HD] * cosine[...] + pltpu.roll(lin[:, :HD], HD // 2, 1) * sine[...]
+
+    def chip_up(k):
+        found = chip * 0
+        for i, c in enumerate(links.order):
+            found = jnp.where(chip == c, links.order[(i - k) % chips], found)
+        return found
+
+    def kv_at(k):
+        return kv.at[pl.ds(pl.multiple_of((chip_up(k) * 2 + core) * own, own), own)]
+
+    kv_at(0)[...] = jnp.concatenate([key, lin[:, HD:]], axis=1).astype(BF16)
+    late = jnp.where(docs[0] > 0, MASKED, 0.0)
+    dk_ref[...] = jnp.zeros_like(dk_ref)
+    dv_ref[...] = jnp.zeros_like(dv_ref)
+
+    def kv_chain():
+        swaps = []
+        for k in range(chips):
+            copy = send(kv_at(k), kv_at(k), right) if k + 1 < chips else None
+            swaps.append(send(kv_at(k), kv_at(k), sibling))
+            yield
+            if copy is not None:
+                copy.wait_recv()
+        for copy in swaps:
+            copy.wait_recv()
+        store = pltpu.make_async_copy(kv, kv_out, ls.at[2])
+        store.start()
+        locals_.append(store)
+        kt_ref[...] = kv[:, :HD].T
+
+    def block_chain(name, piece, dst, k):
+        hops[name, k].wait_recv()
+        if k + 1 < chips:
+            hops[name, k + 1] = send(piece(dst, k, me_dp, 0, 2), piece(dst, k + 1, me_dp, 0, 2), right)
+        held = [[0], [0]]
+        for step in range(len(bits)):
+            sent = []
+            for rank in range(len(held[0])):
+                for way, order in enumerate((bits, bits[::-1])):
+                    bit, rel = order[step], held[way][rank]
+                    where = piece(dst, k, me_dp ^ rel, way)
+                    sent.append((send(where, where, {"dp": me_dp ^ bit}), way, rel ^ bit))
+            yield
+            for copy, way, rel in sent:
+                copy.wait_recv()
+                held[way].append(rel)
+
+    def grad_chain():
+        swap = send(og_hbm, og_pair, sibling)
+        hop = send(og_hbm, og_up, right)
+        yield
+        hop.wait_recv()
+        second = send(og_up, og_up_pair, sibling)
+        yield
+        swap.wait_recv()
+        second.wait_recv()
+
     rows = min(512, SEQ_SHORT)
-    heads = width // HD
-    column = pl.BlockSpec((rows, HD), lambda i, h, *_: (i, h))
+    heads = q_two.shape[1] // HD
+
+    def second_chain():
+        for block in reversed(range(seq // rows)):
+            for head in range(heads):
+                at = (pl.ds(block * rows, rows), pl.ds(head * HD, HD))
+                second_unit(block, rows, q_two[at], g_two[at], kv, dk_ref, dv_ref, late)
+                yield
+
+    chains = {"kv": kv_chain(), "s": second_chain(), "g": grad_chain()}
+    for k in range(1, chips):
+        chains["q%d" % k] = block_chain("q", q_piece, wq_out, k)
+        chains["o%d" % k] = block_chain("o", o_piece, wo_out, k)
+    take_turns(chains, FRONT_ORDER)
+    normed_swap.wait_recv()
+    for copy in copies:
+        copy.wait_send()
+    for copy in locals_:
+        copy.wait()
+
+
+def take_turns(chains, order):
+    def turn(name):
+        if name in chains and next(chains[name], chains) is chains:
+            del chains[name]
+
+    for name in " ".join(order).split():
+        turn(name.rstrip("*"))
+        while name.endswith("*") and name.rstrip("*") in chains:
+            turn(name.rstrip("*"))
+    while chains:
+        for name in list(chains):
+            turn(name)
+
+
+def front(links, docs, tokens, gain, w_kv, cosine, sine, q_two, g_two, w_query, w_out, out_grad):
+    chips = links.chips
+    own, depth = tokens.shape
+    seq = own * links.n_tensor
+    width = w_query.shape[1]
+    anywhere = pl.BlockSpec(memory_space=pl.ANY)
+    here = pl.BlockSpec(memory_space=pltpu.VMEM)
+    dma = pltpu.SemaphoreType.DMA
+    shape = jax.ShapeDtypeStruct
+    count = 2 * chips * (2 * links.n_dp) + 2 * chips + 8
     return pl.pallas_call(
-        functools.partial(second_kernel, seq // rows),
-        grid_spec=pltpu.PrefetchScalarGridSpec(
-            num_scalar_prefetch=1,
-            grid=(seq // rows, heads),
-            in_specs=[column, column, whole((seq, HD)), whole((seq, HD))],
-            out_specs=[whole((seq, HD)), whole((seq, HD))],
+        functools.partial(front_kernel, links),
+        in_specs=[pl.BlockSpec(memory_space=pltpu.SMEM)] + [here] * 7 + [anywhere] * 3,
+        out_specs=[here] + [anywhere] * 6 + [here] * 3,
+        out_shape=[
+            shape((2 * own, depth), BF16), shape((depth, chips * width), BF16), shape((chips * width, depth), BF16),
+            shape((own, depth), BF16), shape((own, depth), BF16), shape((own, depth), BF16),
+            shape((seq, 2 * HD), BF16), shape((HD, seq), BF16), shape((seq, HD), F32), shape((seq, HD), F32),
+        ],
+        scratch_shapes=[pltpu.VMEM((seq, 2 * HD), BF16), dma((count,)), dma((count,)), dma((3,))],
+        compiler_params=pltpu.CompilerParams(
+            collective_id=3, has_side_effects=True, vmem_limit_bytes=VMEM_LIMIT
         ),
-        out_shape=[jax.ShapeDtypeStruct((seq, HD), F32), jax.ShapeDtypeStruct((seq, HD), F32)],
-        compiler_params=pltpu.CompilerParams(vmem_limit_bytes=VMEM_LIMIT),
-        cost_estimate=pl.CostEstimate(
-            flops=8 * heads * seq * seq * HD, bytes_accessed=4 * seq * width, transcendentals=heads * seq * seq // 2
-        ),
-        name="second_back",
-    )(sp, query_two, grad_two, key_rows, value_rows)
+        cost_estimate=pl.CostEstimate(flops=10**10, bytes_accessed=64 * 2**20, transcendentals=0),
+        name="front",
+    )(docs, tokens, gain, w_kv, cosine, sine, q_two, g_two, w_query, w_out, out_grad)
 
 
 def mlp_kernel(
-    links, h_hbm, g_hbm, wg_hbm, wu_hbm, wd_hbm, ghn_ref, mlp_hbm, gw_hbm, uw_hbm, dw_hbm,
-    h_all, g_all, wg, wu, wd, act_t, gg_t, gu_t, keep, stage, pair_out, pair_in, ring_out, ring_in,
+    links, h_hbm, wg_hbm, wu_hbm, wd_hbm, *refs,
+):
+    g_hbm, refs = refs[: links.n_tensor], refs[links.n_tensor :]
+    (
+    ghn_ref, mlp_hbm, grads_hbm, h_all, g_all, wg, wu, wd, act_t, gg_t, gu_t, keep, stage, pair_out, pair_in, ring_out, ring_in,
     load_sem, ring_s, ring_r, swap_s, swap_r, pair_s, pair_r, rs_s, rs_r, stage_sem, store_sem,
-):
+    ) = refs
     chips = links.chips
     own, depth = h_hbm.shape
     seq = chips * 2 * own
@@ -384,7 +546,8 @@
         pltpu.make_async_copy(wg_hbm, wg, load_sem.at[1]),
         pltpu.make_async_copy(wu_hbm, wu, load_sem.at[2]),
         pltpu.make_async_copy(wd_hbm, wd, load_sem.at[3]),
-        pltpu.make_async_copy(g_hbm, g_all, load_sem.at[4]),
+    ] + [
+        pltpu.make_async_copy(ref, g_all.at[i // 2, i % 2], load_sem.at[4 + i]) for i, ref in enumerate(g_hbm)
     ]
     for load in loads:
         load.start()
@@ -509,10 +672,13 @@
         return 0
 
     lax.fori_loop(0, depth // tile, columns_of, 0)
+    units, (pieces, _, piece) = wg.shape[0], grads_hbm.shape
     stores = [
-        pltpu.make_async_copy(wg, gw_hbm, store_sem.at[0]),
-        pltpu.make_async_copy(wu, uw_hbm, store_sem.at[1]),
-        pltpu.make_async_copy(wd, dw_hbm, store_sem.at[2]),
+        pltpu.make_async_copy(
+            w.at[:, pl.ds(j * piece, piece)], grads_hbm.at[j, pl.ds(i * units, units)], store_sem.at[i, j]
+        )
+        for i, w in enumerate((wg, wu, wd))
+        for j in range(pieces)
     ]
     for copy in stores:
         copy.start()
@@ -536,18 +702,17 @@
     own, depth = hidden_own.shape
     chips, units = links.chips, down.shape[0]
     seq = chips * 2 * own
+    pieces = 2 * links.n_dp
     anywhere = pl.BlockSpec(memory_space=pl.ANY)
     dma = pltpu.SemaphoreType.DMA
     return pl.pallas_call(
         functools.partial(mlp_kernel, links),
-        in_specs=[anywhere] * 5,
-        out_specs=[pl.BlockSpec(memory_space=pltpu.VMEM)] + [anywhere] * 4,
+        in_specs=[anywhere] * (4 + links.n_tensor),
+        out_specs=[pl.BlockSpec(memory_space=pltpu.VMEM)] + [anywhere] * 2,
         out_shape=[
             jax.ShapeDtypeStruct((own, depth), F32),
             jax.ShapeDtypeStruct((chips, 2, own, depth), BF16),
-            jax.ShapeDtypeStruct((units, depth), BF16),
-            jax.ShapeDtypeStruct((units, depth), BF16),
-            jax.ShapeDtypeStruct((units, depth), BF16),
+            jax.ShapeDtypeStruct((pieces, 3 * units, depth // pieces), BF16),
         ],
         scratch_shapes=[
             pltpu.VMEM((chips, 2, own, depth), BF16),
@@ -564,9 +729,9 @@
             pltpu.VMEM((2, own, depth), BF16),
             pltpu.VMEM((2, own, depth), BF16),
             pltpu.VMEM((chips, own, depth), BF16),
-            dma((5,)),
+            dma((4 + links.n_tensor,)),
             dma((chips,)), dma((chips,)), dma((chips,)), dma((chips,)), dma((2,)), dma((2,)),
-            dma((chips,)), dma((chips,)), dma((2,)), dma((3,)),
+            dma((chips,)), dma((chips,)), dma((2,)), dma((3, pieces)),
         ],
         compiler_params=pltpu.CompilerParams(
             collective_id=1, has_side_effects=True, vmem_limit_bytes=60 * 2**20
@@ -575,7 +740,365 @@
             flops=18 * seq * depth * units, bytes_accessed=64 * 2**20, transcendentals=seq * units
         ),
         name="feed_forward",
-    )(hidden_own, grad_chunks, gate_t, up_t, down)
+    )(hidden_own, gate_t, up_t, down, *grad_chunks)
+
+
+def mesh_copy(src, dst, send, recv, peer):
+    return pltpu.make_async_remote_copy(
+        src_ref=src, dst_ref=dst, send_sem=send, recv_sem=recv, device_id=peer,
+        device_id_type=pl.DeviceIdType.MESH,
+    )
+
+
+def add_into(dst, src, rows):
+    band = max(b for b in range(16, 353, 16) if rows % b == 0)
+
+    def step(i, _):
+        at = pl.ds(pl.multiple_of(i * band, band), band)
+        dst[at, :] = (dst[at, :].astype(F32) + src[at, :].astype(F32)).astype(BF16)
+        return 0
+
+    lax.fori_loop(0, rows // band, step, 0)
+
+
+class DpSum:
+    def __init__(self, links, send, me, buf, got, free, first=0):
+        self.first = first
+        self.links, self.send, self.me, self.buf, self.got, self.free = links, send, me, buf, got, free
+        self.n = links.n_dp
+        self.ways = [links.bits, links.bits[::-1]]
+        self.pending = []
+
+    def at(self, way, rel):
+        return way * self.n + (self.me ^ rel)
+
+    def kept(self, way, step):
+        done = sum(self.ways[way][: step + 1])
+        return [r for r in range(self.n) if r & done == 0]
+
+    def first_slot(self, step):
+        return sum(self.n >> (i + 1) for i in range(self.first, step))
+
+    def peer(self, bit):
+        return {"dp": self.me ^ bit}
+
+    def start_halving(self, step):
+        self.pending = []
+        for rank in range(self.n >> (step + 1)):
+            for way in (0, 1):
+                bit = self.ways[way][step]
+                rel = self.kept(way, step)[rank]
+                slot = self.first_slot(step) + rank
+                copy = self.send(self.buf.at[self.at(way, rel ^ bit)], self.got.at[way, slot], self.peer(bit), False)
+                self.pending.append((copy, way, rel, slot))
+        self.step = step
+
+    def finish_halving(self):
+        for copy, way, rel, slot in self.pending:
+            copy.wait_recv()
+            add_into(self.buf.at[self.at(way, rel)], self.got.at[way, slot], self.buf.shape[1])
+        for copy, _, _, _ in self.pending:
+            copy.wait_send()
+        for way in (0, 1):
+            pl.semaphore_signal(
+                self.free.at[way, self.step], inc=1, device_id=self.peer(self.ways[way][self.step]),
+                device_id_type=pl.DeviceIdType.MESH,
+            )
+
+    def start_doubling(self, step):
+        self.pending = []
+        if step >= self.first:
+            for way in (0, 1):
+                pl.semaphore_wait(self.free.at[way, step], 1)
+        for rank in range(self.n >> (step + 1)):
+            for way in (0, 1):
+                bit = self.ways[way][step]
+                rel = self.kept(way, step)[rank]
+                where = self.buf.at[self.at(way, rel)]
+                self.pending.append((self.send(where, where, self.peer(bit)), way, rel ^ bit))
+
+    def finish_doubling(self):
+        for copy, _, _ in self.pending:
+            copy.wait_recv()
+        return [(way, rel) for _, way, rel in self.pending]
+
+    def chain(self, done):
+        rounds = len(self.links.bits)
+        for step in range(self.first, rounds):
+            self.start_halving(step)
+            yield
+            self.finish_halving()
+        for step in reversed(range(rounds)):
+            self.start_doubling(step)
+            if step == rounds - 1:
+                done(0, 0)
+                done(1, 0)
+            yield
+            for way, rel in self.finish_doubling():
+                done(way, rel)
+
+
+def first_halving(links, parts, me):
+    n = links.n_dp
+    out, names = [], []
+    for way, bits in enumerate((links.bits, links.bits[::-1])):
+        for rel in range(n):
+            if rel & bits[0] == 0:
+                mine = lax.dynamic_index_in_dim(parts, way * n + (me ^ rel), 0, keepdims=False)
+                other = lax.dynamic_index_in_dim(parts, way * n + (me ^ rel ^ bits[0]), 0, keepdims=False)
+                out.append((mine.astype(F32) + links.across(other, bits[0]).astype(F32)).astype(BF16))
+                names.append((way, rel))
+    return out, names
+
+
+def tail_kernel(
+    links, names, *refs,
+):
+    w_hbm, refs = refs[: len(names)], refs[len(names) :]
+    (
+        o_hbm, q_hbm, m_hbm, kv_keep, kv_send, gn_keep, gn_send, tokens, normed, w_kv, cosine, sine, gain_part,
+        ws_hbm, ow_hbm, qw_hbm, kvw_hbm, got_hbm, gn_ref, gains_ref,
+        o_buf, o_in, q_buf, q_in, w_buf, w_in, a_buf, a_in, b_buf, b_in,
+        kv_got, kv_ring, kv_in, gn_got, kvw_half, kvw_got, kvw_in, kvw_all, gains_in,
+        ss, rs, o_sem, q_sem, w_sem, out_sem, kvw_sem, w_free, a_free, b_free,
+    ) = refs
+    chips, bits = links.chips, links.bits
+    n_dp = links.n_dp
+    width = o_buf.shape[1]
+    piece = w_buf.shape[2]
+    me = lax.axis_index("tensor")
+    me_dp = lax.axis_index("dp")
+    chip, core = me // 2, lax.rem(me, 2)
+    ahead, behind = links.neighbours(chip)
+    right = {"tensor": ahead * 2 + core}
+    left = {"tensor": behind * 2 + core}
+    sibling = {"tensor": me ^ 1}
+    chip_bits = [2 << b for b in range(chips.bit_length() - 1)]
+    butterfly = [sibling] + [{"tensor": me ^ bit} for bit in chip_bits] + [{"dp": me_dp ^ bit} for bit in bits]
+
+    w_loads = [
+        pltpu.make_async_copy(ref, w_buf.at[way * n_dp + (me_dp ^ rel)], w_sem.at[i])
+        for i, (ref, (way, rel)) in enumerate(zip(w_hbm, names))
+    ]
+    loads = {}
+    for k in list(range(1, chips)) + [0]:
+        loads["o", k] = pltpu.make_async_copy(o_hbm.at[k], o_buf.at[k], o_sem.at[k])
+        loads["q", k] = pltpu.make_async_copy(q_hbm.at[k], q_buf.at[k], q_sem.at[k])
+    for load in w_loads + list(loads.values()):
+        load.start()
+    barrier = pltpu.get_barrier_semaphore()
+    peers = [right, left] + butterfly
+    for peer in peers:
+        pl.semaphore_signal(barrier, inc=1, device_id=peer, device_id_type=pl.DeviceIdType.MESH)
+    pl.semaphore_wait(barrier, len(peers))
+
+    copies, opened, locals_ = [], [], []
+
+    def send(src, dst, peer, later=True):
+        number = len(copies)
+        copy = mesh_copy(src, dst, ss.at[number], rs.at[number], peer)
+        copy.start()
+        copies.append(copy)
+        if later:
+            opened.append(copy)
+        return copy
+
+    def put(src, dst):
+        copy = pltpu.make_async_copy(src, dst, out_sem.at[len(locals_)])
+        copy.start()
+        locals_.append(copy)
+
+    def ring_chain(name, buf, got):
+        copy = None
+        for k in list(range(1, chips)) + [0]:
+            loads[name, k].wait()
+            if copy is not None:
+                copy.wait_recv()
+                add_into(buf.at[k], got.at[(k - 1) % chips - 1], buf.shape[1])
+            if k:
+                copy = send(buf.at[k], got.at[k - 1], right)
+            yield
+
+    kv_swap = send(kv_send, kv_got, sibling)
+    gn_swap = send(gn_send, gn_got, sibling)
+    held = {}
+
+    def kv_chain():
+        kv_swap.wait_recv()
+        copy = None
+        for k in list(range(1, chips)) + [0]:
+            total = kv_keep[k] + kv_got[k].astype(F32)
+            if copy is not None:
+                copy.wait_recv()
+                total = total + kv_in[(k - 1) % chips - 1].astype(F32)
+            if k:
+                kv_ring[k - 1] = total.astype(BF16)
+                copy = send(kv_ring.at[k - 1], kv_in.at[k - 1], right)
+                yield
+        key_grad = total[:, :HD]
+        key_grad = key_grad * cosine[...] - pltpu.roll(key_grad, HD // 2, 1) * sine[...]
+        kv_lin = jnp.concatenate([key_grad, total[:, HD:]], axis=1).astype(BF16)
+        kv_lin_t = kv_lin.T
+        for half in (0, 1):
+            kvw_half[half] = mm(kv_lin_t[half * HD : (half + 1) * HD], normed[...], NN).astype(BF16)
+        held["swap"] = send(kvw_half.at[1 - core], kvw_got, sibling)
+        yield
+        gn_swap.wait_recv()
+        grad = gn_keep[...] + gn_got[...].astype(F32) + mm(kv_lin, w_kv[...], NT)
+        gn_ref[...] = grad
+        x = tokens[...].astype(F32)
+        factor = lax.rsqrt(jnp.mean(x * x, axis=1, keepdims=True) + EPSILON)
+        part = jnp.sum(grad * (x * factor), axis=0, keepdims=True)
+        row = lax.broadcasted_iota(jnp.int32, gains_ref.shape, 0)
+        gains_ref[...] = jnp.where(row == 0, jnp.broadcast_to(part, gains_ref.shape), gain_part[...])
+
+    def gains_chain():
+        for number, peer in enumerate(butterfly):
+            copy = send(gains_ref, gains_in.at[number], peer, False)
+            yield
+            copy.wait_recv()
+            copy.wait_send()
+            gains_ref[...] += gains_in[number]
+
+    band = HD // chips
+
+    def chip_up(k):
+        found = chip * 0
+        for i, c in enumerate(links.order):
+            found = jnp.where(chip == c, links.order[(i - k) % chips], found)
+        return found
+
+    def rows_of(k):
+        return pl.ds(pl.multiple_of(chip_up(k) * band, band), band)
+
+    def kvw_chain():
+        held["swap"].wait_recv()
+        add_into(kvw_half.at[core], kvw_got, HD)
+        copy = None
+        for k in list(range(1, chips)) + [0]:
+            if copy is not None:
+                copy.wait_recv()
+                mine = kvw_half.at[core, rows_of(k)]
+                mine[...] = (mine[...].astype(F32) + kvw_in[(k - 1) % chips - 1].astype(F32)).astype(BF16)
+            if k:
+                copy = send(kvw_half.at[core, rows_of(k)], kvw_in.at[k - 1], right)
+                yield
+
+    sum_w = DpSum(links, send, me_dp, w_buf, w_in, w_free, 1)
+    sum_a = DpSum(links, send, me_dp, a_buf, a_in, a_free)
+    sum_b = DpSum(links, send, me_dp, b_buf, b_in, b_free)
+
+    def columns(ref, number):
+        return ref.at[:, pl.ds(pl.multiple_of(number * piece, piece), piece)]
+
+    def w_chain():
+        for load in w_loads:
+            load.wait()
+        yield from sum_w.chain(lambda way, rel: put(w_buf.at[sum_w.at(way, rel)], columns(ws_hbm, sum_w.at(way, rel))))
+
+    def a_chain():
+        for j in range(2 * n_dp):
+            a_buf[j, pl.ds(0, width)] = o_buf[0, :, pl.ds(j * piece, piece)]
+            a_buf[j, pl.ds(width, band)] = kvw_half[core, rows_of(0), pl.ds(j * piece, piece)]
+        yield from sum_a.chain(
+            lambda way, rel: put(
+                a_buf.at[sum_a.at(way, rel), pl.ds(0, width)], columns(ow_hbm, sum_a.at(way, rel))
+            )
+        )
+
+    def last_chain():
+        for j in range(2 * n_dp):
+            kvw_all[0, core, :, pl.ds(j * piece, piece)] = a_buf[j, pl.ds(width, band)]
+        for k in range(chips - 1):
+            copy = send(kvw_all.at[k, core], kvw_all.at[k + 1, core], right)
+            yield
+            copy.wait_recv()
+        copy = send(kvw_all.at[:, core], kvw_all.at[:, core], sibling)
+        yield
+        copy.wait_recv()
+        for k in range(chips):
+            for half in (0, 1):
+                to = pl.ds(pl.multiple_of(half * HD + chip_up(k) * band, band), band)
+                put(kvw_all.at[k, half], kvw_hbm.at[to])
+
+    def b_chain():
+        for j in range(2 * n_dp):
+            b_buf[j] = q_buf[0, :, pl.ds(j * piece, piece)]
+        yield from sum_b.chain(lambda way, rel: put(b_buf.at[sum_b.at(way, rel)], columns(qw_hbm, sum_b.at(way, rel))))
+
+    def m_chain():
+        copy = send(m_hbm, got_hbm, right)
+        yield
+        copy.wait_recv()
+
+    chains = {
+        "w": w_chain(), "o": ring_chain("o", o_buf, o_in), "q": ring_chain("q", q_buf, q_in), "kv": kv_chain(),
+        "g": gains_chain(), "kvw": kvw_chain(), "m": m_chain(), "a": a_chain(), "b": b_chain(), "l": last_chain(),
+    }
+
+    take_turns(chains, TAIL_ORDER)
+    for copy in opened:
+        copy.wait_send()
+    for copy in locals_:
+        copy.wait()
+
+
+TAIL_ORDER = (
+    "w o kv kv", "q kv kv o", "kv* kvw g w", "q kvw g w", "o kvw g kvw*", "g q g m", "o* a g* q*", "a b a b",
+    "a b a* l", "b l b l", "b* l* w* m*",
+)
+
+
+def tail(
+    links, o_parts, q_parts, m_part, w_pieces, names, kv_keep, kv_send, gn_keep, gn_send, tokens, normed, w_kv, cosine,
+    sine, gain_part,
+):
+    chips, width, depth = o_parts.shape
+    own = tokens.shape[0]
+    rows, piece = w_pieces[0].shape
+    band = HD // chips
+    n = links.n_dp
+    pieces = 2 * n
+    anywhere = pl.BlockSpec(memory_space=pl.ANY)
+    here = pl.BlockSpec(memory_space=pltpu.VMEM)
+    dma = pltpu.SemaphoreType.DMA
+    shape = jax.ShapeDtypeStruct
+    count = 16 * chips + 6 * n * 2 + 16
+    return pl.pallas_call(
+        functools.partial(tail_kernel, links, names),
+        in_specs=[anywhere] * (3 + len(names)) + [here] * 10,
+        out_specs=[anywhere] * 5 + [here] * 2,
+        out_shape=[
+            shape((rows, depth), BF16), shape((width, depth), BF16),
+            shape((width, depth), BF16), shape((2 * HD, depth), BF16), shape((own, depth), BF16),
+            shape((own, depth), F32), shape((8, depth), F32),
+        ],
+        scratch_shapes=[
+            pltpu.VMEM((chips, width, depth), BF16), pltpu.VMEM((chips - 1, width, depth), BF16),
+            pltpu.VMEM((chips, width, depth), BF16), pltpu.VMEM((chips - 1, width, depth), BF16),
+            pltpu.VMEM((pieces, rows, piece), BF16), pltpu.VMEM((2, max(1, n // 2 - 1), rows, piece), BF16),
+            pltpu.VMEM((pieces, width + band, piece), BF16), pltpu.VMEM((2, n - 1, width + band, piece), BF16),
+            pltpu.VMEM((pieces, width, piece), BF16), pltpu.VMEM((2, n - 1, width, piece), BF16),
+            pltpu.VMEM((chips, own, 2 * HD), BF16),
+            pltpu.VMEM((chips - 1, own, 2 * HD), BF16), pltpu.VMEM((chips - 1, own, 2 * HD), BF16),
+            pltpu.VMEM((own, depth), BF16),
+            pltpu.VMEM((2, HD, depth), BF16), pltpu.VMEM((HD, depth), BF16),
+            pltpu.VMEM((chips - 1, band, depth), BF16),
+            pltpu.VMEM((chips, 2, band, depth), BF16),
+            pltpu.VMEM((len(links.bits) + chips.bit_length(), 8, depth), F32),
+            dma((count,)), dma((count,)), dma((chips,)), dma((chips,)), dma((len(names),)),
+            dma((3 * pieces + 2 * chips,)), dma((chips, 2)),
+        ]
+        + [pltpu.SemaphoreType.REGULAR((2, len(links.bits)))] * 3,
+        compiler_params=pltpu.CompilerParams(
+            collective_id=2, has_side_effects=True, vmem_limit_bytes=60 * 2**20
+        ),
+        cost_estimate=pl.CostEstimate(flops=10**9, bytes_accessed=64 * 2**20, transcendentals=0),
+        name="tail",
+    )(
+        *w_pieces, o_parts, q_parts, m_part, kv_keep, kv_send, gn_keep, gn_send, tokens, normed, w_kv, cosine, sine,
+        gain_part,
+    )
 
 
 def rms_factor(values):
@@ -612,55 +1135,31 @@
     residual = tokens.astype(F32)
     attn_scale = rms_factor(residual)
     attn_pre = residual * attn_scale
-    normed_own = (attn_pre * attn_gain).astype(BF16)
-
-    kv_lin = mm(normed_own, w_kv, NN)
-    half = HD // 2
-    key_lin = kv_lin[:, :HD]
-    key_own = key_lin * cosine[:own] + jnp.concatenate([key_lin[:, half:], key_lin[:, :half]], axis=1) * sine[:own]
-    kv_own = jnp.concatenate([key_own, kv_lin[:, HD:]], axis=1).astype(BF16)
-    kv_mine = jnp.stack(ring_gather(links, kv_own))
-    kv_other = links.swap(kv_mine)
-    kv_first = jnp.where(core == 0, kv_mine, kv_other)
-    kv_second = jnp.where(core == 0, kv_other, kv_mine)
-    kv_rel = jnp.concatenate([kv_first, kv_second], axis=1)
-    kv_all = jnp.concatenate(
-        [
-            lax.dynamic_index_in_dim(kv_rel, (place[chip] - links.place[j] + chips) % chips, 0, keepdims=False)
-            for j in range(chips)
-        ],
-        axis=0,
+
+    normed, wq, wo, og_up, og_pair, og_up_pair, kv_all, key_rows_t, dk2, dv2 = front(
+        links, doc_split, tokens, attn_gain[None], w_kv, cosine[:own], sine[:own], query_two, grad_two, w_query, w_out,
+        out_grad,
     )
-    key_rows, value_rows = kv_all[:, :HD], kv_all[:, HD:]
-
-    wq_blocks = gather_weight(links, w_query, me_dp)
-    wo_blocks = gather_weight(links, w_out, me_dp)
-    wq = jnp.concatenate(wq_blocks, axis=1)
-    wo = jnp.concatenate(wo_blocks, axis=0)
-    grad_chunks = [both(links, piece) for piece in ring_gather(links, out_grad)]
-
-    dk2, dv2 = second_back(sp, query_two, grad_two, key_rows, value_rows)
-
-    normed = both(links, normed_own)
+    normed_own = normed[:own]
+    grad_chunks = [out_grad, og_pair, og_up, og_up_pair]
+    for _ in range(2, chips):
+        og_up = links.ring(og_up)
+        grad_chunks += [og_up, links.swap(og_up)]
+
     q_lin = mm(normed, wq, NN)
-    queries, context, lse = attend(sp, q_lin, cosine, sine, key_rows, value_rows)
+    queries, context, lse = attend(sp, q_lin, cosine, sine, kv_all)
     branch = pair_sum(links, mm(context, wo, NN))
     hidden = residual + branch
     mlp_scale = rms_factor(hidden)
     mlp_pre = hidden * mlp_scale
     hidden_own = (mlp_pre * mlp_gain).astype(BF16)
 
-    grad_stack = jnp.stack(grad_chunks).reshape(chips, 2, own, -1)
-    grad_hn, mlp_parts, gate_w, up_w, down_w = feed_forward(
-        links, hidden_own, grad_stack, w_gate.T, w_up.T, w_down
-    )
-    gate_w, up_w, down_w = lax.psum((gate_w, up_w, down_w), "dp")
-    gate_w_grad = gate_w.astype(F32).T
-    up_w_grad = up_w.astype(F32).T
-    down_w_grad = down_w.astype(F32)
-    mlp_sums = mlp_parts[:, 0].astype(F32) + links.swap(mlp_parts[:, 1]).astype(F32)
-    mlp_out = ring_scatter(links, [mlp_sums[k] for k in range(chips)])
-    block_output = (hidden + mlp_out).astype(BF16)
+    grad_hn, mlp_parts, ffn_parts = feed_forward(links, hidden_own, grad_chunks, w_gate.T, w_up.T, w_down)
+    ffn_pieces, ffn_names = first_halving(links, ffn_parts, me_dp)
+    mlp_terms = mlp_parts[:, 0].astype(F32) + links.swap(mlp_parts[:, 1]).astype(F32)
+    mlp_sent = mlp_terms[1].astype(BF16)
+    for k in range(2, chips):
+        mlp_sent = (mlp_terms[k] + links.ring(mlp_sent).astype(F32)).astype(BF16)
 
     mlp_gain_part = jnp.sum(grad_hn * mlp_pre, axis=0)
     scaled_mlp = grad_hn * mlp_gain
@@ -671,68 +1170,41 @@
     grad_branch = both(links, grad_hidden.astype(BF16))
     grad_context = mm(grad_branch, wo, NT).astype(BF16)
     query_grad, dk, dv = attend_back(
-        sp, queries, grad_context, context, lse, cosine, sine, key_rows, value_rows, dk2, dv2
+        sp, queries, grad_context, context, lse, cosine, sine, kv_all, key_rows_t, dk2, dv2
     )
-    out_w_parts = [
-        mm(context[:, k * width : (k + 1) * width], grad_branch, TN).astype(BF16) for k in range(chips)
-    ]
-    out_w_grad = sum_dp(links, ring_scatter(links, out_w_parts).astype(BF16), me_dp)
-
-    kv_part = jnp.concatenate([dk * SCALE, dv], axis=1).astype(BF16).reshape(chips, 2, own, 2 * HD)
+    out_parts = mm(context, grad_branch, TN).astype(BF16).reshape(chips, width, -1)
+    query_parts = mm(query_grad, normed, TN).astype(BF16).reshape(chips, width, -1)
+
+    kv_part = jnp.concatenate([dk * SCALE, dv], axis=1).reshape(chips, 2, own, 2 * HD)
+    kv_part = jnp.stack(
+        [
+            lax.dynamic_index_in_dim(kv_part, order[(place[chip] - k + chips) % chips], 0, keepdims=False)
+            for k in range(chips)
+        ]
+    )
     kv_keep = lax.dynamic_index_in_dim(kv_part, core, 1, keepdims=False)
-    kv_send = lax.dynamic_index_in_dim(kv_part, 1 - core, 1, keepdims=False)
-    kv_sum = kv_keep.astype(F32) + links.swap(kv_send).astype(F32)
-    kv_terms = [
-        lax.dynamic_index_in_dim(kv_sum, order[(place[chip] - k + chips) % chips], 0, keepdims=False)
-        for k in range(chips)
-    ]
-    kv_grad = ring_scatter(links, kv_terms)
-    key_grad = kv_grad[:, :HD]
-    key_grad = key_grad * cosine[:own] - jnp.concatenate([key_grad[:, half:], key_grad[:, :half]], axis=1) * sine[:own]
-    kv_grad_lin = jnp.concatenate([key_grad, kv_grad[:, HD:]], axis=1).astype(BF16)
-
-    query_w_parts = [
-        mm(normed, query_grad[:, k * width : (k + 1) * width], TN).astype(BF16) for k in range(chips)
-    ]
-    query_w_grad = sum_dp(links, ring_scatter(links, query_w_parts).astype(BF16), me_dp)
-
-    grad_normed = pair_sum(links, mm(query_grad, wq, NT)) + mm(kv_grad_lin, w_kv, NT)
-    attn_gain_part = jnp.sum(grad_normed * attn_pre, axis=0)
+    kv_send = lax.dynamic_index_in_dim(kv_part, 1 - core, 1, keepdims=False).astype(BF16)
+    gn_part = mm(query_grad, wq, NT)
+    gain_part = jnp.pad(mlp_gain_part[None], ((1, 6), (0, 0)))
+    ffn_w, out_w, query_w, kv_w, mlp_got, grad_normed, gains = tail(
+        links, out_parts, query_parts, mlp_sent, ffn_pieces, ffn_names, kv_keep, kv_send, gn_part[:own],
+        gn_part[own:].astype(BF16), tokens, normed_own, w_kv, cosine[:own], sine[:own], gain_part,
+    )
+    units = w_down.shape[0]
+
+    gate_w_grad = ffn_w[:units].astype(F32).T
+    up_w_grad = ffn_w[units : 2 * units].astype(F32).T
+    down_w_grad = ffn_w[2 * units :].astype(F32)
+    out_w_grad = out_w.astype(F32)
+    query_w_grad = query_w.astype(F32).T
+    kv_w_grad = kv_w.astype(F32).T
+    attn_gain_grad, mlp_gain_grad = gains[0], gains[1]
+    block_output = (hidden + (mlp_terms[0] + mlp_got.astype(F32))).astype(BF16)
     scaled_attn = grad_normed * attn_gain
     tokens_grad = (
         grad_hidden
         + attn_scale * (scaled_attn - attn_pre * jnp.mean(scaled_attn * attn_pre, axis=-1, keepdims=True))
     ).astype(BF16)
-
-    kv_w = mm(kv_grad_lin, normed_own, TN).astype(BF16).reshape(chips, 2, HD // chips, -1)
-    kv_w_keep = lax.dynamic_index_in_dim(kv_w, core, 1, keepdims=False)
-    kv_w_send = lax.dynamic_index_in_dim(kv_w, 1 - core, 1, keepdims=False)
-    kv_w_sum = kv_w_keep.astype(F32) + links.swap(kv_w_send).astype(F32)
-    kv_w_terms = [
-        lax.dynamic_index_in_dim(kv_w_sum, order[(place[chip] - k + chips) % chips], 0, keepdims=False)
-        for k in range(chips)
-    ]
-    kv_w_own = sum_dp(links, ring_scatter(links, kv_w_terms).astype(BF16), me_dp)
-    kv_w_mine = jnp.stack(ring_gather(links, kv_w_own.astype(BF16)))
-    kv_w_other = links.swap(kv_w_mine)
-    kv_w_pair = jnp.stack(
-        [jnp.where(core == 0, kv_w_mine, kv_w_other), jnp.where(core == 0, kv_w_other, kv_w_mine)], axis=1
-    )
-    kv_w_grad = (
-        jnp.concatenate(
-            [
-                lax.dynamic_index_in_dim(kv_w_pair, (place[chip] - links.place[j] + chips) % chips, 0, keepdims=False)
-                for j in range(chips)
-            ],
-            axis=0,
-        )
-        .reshape(2 * HD, -1)
-        .astype(F32)
-        .T
-    )
-
-    attn_gain_grad = sum_all(links, attn_gain_part)
-    mlp_gain_grad = sum_all(links, mlp_gain_part)
     return (
         block_output,
         tokens_grad,

time: 861 us -> 690 us (0.80)
  waiting for transfers between devices: 358 us -> 49.6 us
  Pallas kernels: 202 us -> 497 us
  starting transfers between devices: 103 us -> 22.6 us
  between operations: 34.4 us -> 12.5 us
  other arithmetic: 65.9 us -> 45.2 us
  matrix products: 46.3 us -> 26 us
  local copies, waits for them, and re-layouts: 44.3 us -> 26.3 us
    pallas_call x1 -> x2, Pallas kernels: 22.5 us -> 318 us  [the longest x1 213 us: tail(): pl.pallas_call(functools.partial(tail_kernel, links, names), in_specs=[an...]
    ppermute x30 -> x4, waiting for transfers between devices: 202 us -> 49.6 us  [ring(): return lax.ppermute(x, 'tensor', self.ring_pairs)]
    ppermute x48 -> x4, waiting for transfers between devices: 94.6 us -> 0.01 us  [across(): return lax.ppermute(x, 'dp', [(i, i ^ bit) for i in range(self.n_dp)])]
    ppermute x48 -> x4, starting transfers between devices: 53.7 us -> 4.05 us  [across(): return lax.ppermute(x, 'dp', [(i, i ^ bit) for i in range(self.n_dp)])]
    psum x1 -> x0, waiting for transfers between devices: 31.9 us -> none  [local(): gate_w, up_w, down_w = lax.psum((gate_w, up_w, down_w), 'dp')]
    ppermute x6 -> x0, waiting for transfers between devices: 26.8 us -> none  [across_tensor(): lax.ppermute(x, 'tensor', [(i, i ^ bit) for i in range(self.n_tensor)])]
    ppermute x30 -> x4, starting transfers between devices: 40.7 us -> 17.8 us  [ring(): return lax.ppermute(x, 'tensor', self.ring_pairs)]
    dot_general x15 -> x6, matrix products: 46.3 us -> 26 us  [mm(): lax.dot_general(left, right, (dims, ((), ())), preferred_element_type=F32)]
  transfers between devices with their start and end apart: 98 -> 13, of which waited for: 55 -> 4; matrix products, arithmetic and copies ran while one was open for 13% -> 9% of each run, Pallas kernels for 4% -> 4%
where the time goes in v3:
time: 690 us; the launch traced here: 680 us
  Pallas kernels  497 us (72%)
  waiting for transfers between devices  49.6 us (7%)
  other arithmetic  45.2 us (7%)
  local copies, waits for them, and re-layouts  26.3 us (4%)
  matrix products  26 us (4%)
  starting transfers between devices  22.6 us (3%)
  between operations  12.5 us (2%)
    pallas_call x1, Pallas kernels, tail(): pl.pallas_call(functools.partial(tail_kernel, links, names), in_specs=[an...  213 us
    pallas_call x1, Pallas kernels, feed_forward(): pl.pallas_call(functools.partial(mlp_kernel, links), in_specs=[anywhere]...  151 us
    pallas_call x1, Pallas kernels, front(): pl.pallas_call(functools.partial(front_kernel, links), in_specs=[pl.Block...  105 us
    ppermute x4, waiting for transfers between devices, ring(): return lax.ppermute(x, 'tensor', self.ring_pairs)  49.6 us
    dot_general x6, matrix products, mm(): lax.dot_general(left, right, (dims, ((), ())), preferred_element_type=F32)  26 us
    ppermute x4, starting transfers between devices, ring(): return lax.ppermute(x, 'tensor', self.ring_pairs)  17.8 us
    pallas_call x1, Pallas kernels, attend_back(): pl.pallas_call(functools.partial(bwd_kernel, seq // rows), grid_spec=pltp...  16.8 us
  transfers between devices with their start and end apart: 13, of which 4 were waited for; matrix products, arithmetic and copies ran while one was open for 9% of the time, Pallas kernels for 4%

profile of v3, /device:TPU:0, one launch (start us, length us, event | category | flops | bytes accessed | tf_op | source)
XLA Modules:
  0.0 679.7 jit_solution(2921549658758743023)
XLA Ops:
  1.4 1.0 multiply_sine_fusion
  2.4 0.8 fusion.21
  3.2 104.9 %front.1 = (bf16[512,2048]{1,0:T(8,128)(2,1)}, bf16[2048,1024]{1,0:T(8,128)(2,1)}, bf16[1024,2048]{1,0:T(8,128)(2,1)}, bf16[256,2048]{1,0:T(8,128)(2,1)}, bf16[2...) custom-call(s32[1]{0:T(128)S(6)} %copy.45.docs, ...), custom_call_target="tpu_custom_call" | custom-call | flops 10000000000 | bytes 67108864 | tf_op jit(solution)/shard_map/front/pallas_call | solution.py:508
  108.1 0.8 collective-permute-start.1
  108.9 1.0 pad_maximum_fusion.5
  109.9 6.5 fusion.33.q_ref
  116.3 0.6 pad_add_fusion.sp_ref
  116.9 12.0 %attend.1 = (bf16[512,1024]{1,0:T(8,128)(2,1)}, bf16[512,1024]{1,0:T(8,128)(2,1)}, f32[8,8,512]{2,1,0:T(8,128)}) custom-call(s32[3]{0:T(128)} %pad_add_fusion.sp_ref, f32[512,1024]{1,0:T(8,128)} %fusion.33.q_ref, f32[512,128]{1,0:T(8,128)} %get-tuple-element.113.c_ref, f32[512,128]{1,0:T(8,128)} %get-tuple-element.114.s_ref, ...), custom_call_target="tpu_custom_call" | custom-call | flops 8589934592 | bytes 8388608 | tf_op jit(solution)/shard_map/attend/pallas_call | solution.py:266
  129.0 3.6 fusion.34
  132.6 2.7 collective-permute-done.1.refs_4_
  135.3 4.2 collective-permute-start.3
  139.5 0.1 slice.136
  139.7 0.1 collective-permute-start
  139.8 0.6 dynamic_slice.71
  143.0 0.6 fusion.32
  148.8 2.3 slice.71.refs_12_
  153.8 0.5 collective-permute-start.2
  154.4 15.7 %collective-permute-done.3.refs_6_ = bf16[256,2048]{1,0:T(8,128)(2,1)} collective-permute-done((bf16[256,2048]{1,0:T(8,128)(2,1)}, bf16[256,2048]{1,0:T(8,128)(2,1)}, u32[]{:S(2)}, u32[]{:S(2)}) %collective-permute-start.3) | collective-permute-done | bytes 1048608 | tf_op jit(solution)/shard_map/ppermute | solution.py:44
  170.0 2.5 multiply_reduce_fusion.2
  172.6 1.2 multiply_convert_fusion.h_hbm
  173.8 150.7 %feed_forward.1 = (f32[256,2048]{1,0:T(8,128)}, bf16[4,2,256,2048]{3,2,1,0:T(8,128)(2,1)}, bf16[8,2112,256]{2,1,0:T(8,128)(2,1)}) custom-call(bf16[256,2048]{1,0:T(8,128)(2,1)} %multiply_convert_fusion.h_hbm, bf16[704,2048]{1,0:T(8,128)(2,1)} %bitcast.110, bf16[704,2048]{1,0:T(8,128)(2,1)} %bitcast.111, bf16[704,2048]{1,0:T(8,128)(2,1)} %wd_hbm.1, ...), custom_call_target="tpu_custom_call" | custom-call | flops 53150220288 | bytes 67108864 | tf_op jit(solution)/shard_map/feed_forward/pallas_call | solution.py:708
  324.5 2.3 multiply_reduce_fusion
  326.8 0.1 copy-done.7
  327.0 0.7 fusion.30
  327.7 5.5 slice_bitcast_fusion
  333.2 2.3 dynamic-slice_bitcast_fusion
  335.5 2.0 collective-permute-start.7
  337.6 0.6 pad.4.refs_16_
  338.2 2.0 collective-permute-start.9
  340.2 3.3 convolution_convert_fusion.2.do_ref
  343.6 16.8 %attend_back.1 = (bf16[512,1024]{1,0:T(8,128)(2,1)}, f32[2048,128]{1,0:T(8,128)}, f32[2048,128]{1,0:T(8,128)}) custom-call(s32[3]{0:T(128)} %pad_add_fusion.sp_ref, bf16[512,1024]{1,0:T(8,128)(2,1)} %get-tuple-element.47.q_ref, bf16[512,1024]{1,0:T(8,128)(2,1)} %convolution_convert_fusion.2.do_ref, bf16[512,1024]{1,0:T(8,128)(2,1)} %get-tuple-element.39.ctx_ref, ...), custom_call_target="tpu_custom_call" | custom-call | flops 21474836480 | bytes 8388608 | tf_op jit(solution)/shard_map/attend_back/pallas_call | solution.py:292
  360.4 1.4 broadcast_multiply_fusion
  361.8 0.1 copy-done.15
  361.9 0.1 pad_maximum_fusion.1
  362.1 0.2 dynamic-slice_bitcast_fusion.8
  362.3 0.1 pad_maximum_fusion.2
  362.4 1.2 copy-done.16
  363.7 0.3 copy-done.25
  363.9 4.4 convolution_convert_fusion
  368.4 4.0 convert_add_fusion
  372.4 0.1 fusion.19
  372.5 6.2 collective-permute-start.11
  378.7 1.1 dynamic-slice_bitcast_fusion.4.refs_7_
  379.8 3.8 fusion.35
  383.6 4.4 convolution_convert_fusion.1
  388.1 17.0 %collective-permute-done.11 = bf16[256,2048]{1,0:T(8,128)(2,1)S(1)} collective-permute-done((bf16[256,2048]{1,0:T(8,128)(2,1)S(1)}, bf16[256,2048]{1,0:T(8,128)(2,1)S(1)}, u32[]{:S(2)}, u32[]{:S(2)}) %collective-permute-start.11) | collective-permute-done | bytes 1048608 | tf_op jit(solution)/shard_map/ppermute | solution.py:44
  405.1 0.3 fusion.13
  405.4 6.7 collective-permute-start.12
  412.1 0.8 fusion.20.refs_8_
  412.9 1.5 slice.89.refs_9_
  414.4 1.1 slice.135.refs_10_
  415.5 5.1 fusion.2
  420.7 14.2 %collective-permute-done.12 = bf16[256,2048]{1,0:T(8,128)(2,1)S(1)} collective-permute-done((bf16[256,2048]{1,0:T(8,128)(2,1)S(1)}, bf16[256,2048]{1,0:T(8,128)(2,1)S(1)}, u32[]{:S(2)}, u32[]{:S(2)}) %collective-permute-start.12) | collective-permute-done | bytes 1048608 | tf_op jit(solution)/shard_map/ppermute | solution.py:44
  434.9 1.3 fusion.15.refs_6_
  436.2 213.1 %tail.1 = (bf16[2112,2048]{1,0:T(8,128)(2,1)}, bf16[256,2048]{1,0:T(8,128)(2,1)}, bf16[256,2048]{1,0:T(8,128)(2,1)}, bf16[256,2048]{1,0:T(8,128)(2,1)}, bf16[256...) custom-call(bf16[2112,256]{1,0:T(8,128)(2,1)} %get-tuple-element.92.refs_0_, ...), custom_call_target="tpu_custom_call" | custom-call | flops 1000000000 | bytes 67108864 | tf_op jit(solution)/shard_map/tail/pallas_call | solution.py:1067
  649.3 10.6 %slice_convert_fusion = (f32[704,2048]{1,0:T(8,128)}, f32[2048,704]{0,1:T(8,128)}, f32[2048,704]{0,1:T(8,128)}) fusion(bf16[2112,2048]{1,0:T(8,128)(2,1)} %get-tuple-element.61), kind=kLoop, calls=%fused_computation.10 | loop fusion | flops 4325376 | bytes 25952256 | tf_op jit(solution)/shard_map/convert_element_type | solution.py:1197
  659.8 1.6 convert_bitcast_fusion.3
  661.4 3.0 copy.35
  664.4 1.6 convert_bitcast_fusion.2
  665.9 3.0 copy.36
  668.9 2.2 fusion.6
  671.2 2.9 convert_element_type.170
  674.1 1.5 fusion.31
  675.7 3.8 fusion.10
  (82 shorter events, 0.3 us)
Async XLA Ops:
  108.1 27.2 %collective-permute-start.1 = (bf16[256,2048]{1,0:T(8,128)(2,1)}, bf16[256,2048]{1,0:T(8,128)(2,1)}, u32[]{:S(2)}, u32[]{:S(2)}) collective-permute-start(bf16[256,2048]{1,0:T(8,128)(2,1)} %get-tuple-element.42.refs_2_), channel_id=1, source_target_pairs={{0,2},{1,3},{2,6},{3,7},{4,0},{5,1},{6,4},{7,5},{8,10},{9,11},{10,... | collective-permute-start | bytes 3145736 | tf_op jit(solution)/shard_map/ppermute | solution.py:44
  116.9 12.0 %copy-start.23 = (bf16[1024,2048]{1,0:T(8,128)(2,1)S(1)}, bf16[1024,2048]{1,0:T(8,128)(2,1)}, u32[]{:S(2)}) copy-start(bf16[1024,2048]{1,0:T(8,128)(2,1)} %get-tuple-element.40) | copy-start | bytes 12582916
  132.5 7.0 %copy-start.9 = (f32[512,2048]{1,0:T(8,128)}, f32[512,2048]{1,0:T(8,128)S(1)}, u32[]{:S(2)}) copy-start(f32[512,2048]{1,0:T(8,128)S(1)} %fusion.34) | copy-start | bytes 12582916
  132.6 7.2 %copy-start.19 = (s32[4]{0:T(128)S(1)}, s32[4]{0:T(128)}, u32[]{:S(2)}) copy-start(s32[4]{0:T(128)} %constant.157.clone) | copy-start | bytes 52
  132.6 37.5 %copy-start.3 = (bf16[256,2048]{1,0:T(8,128)(2,1)S(1)}, bf16[256,2048]{1,0:T(8,128)(2,1)}, u32[]{:S(2)}) copy-start(bf16[256,2048]{1,0:T(8,128)(2,1)} %refs_11_.1) | copy-start | bytes 3145732
  135.3 34.7 %collective-permute-start.3 = (bf16[256,2048]{1,0:T(8,128)(2,1)}, bf16[256,2048]{1,0:T(8,128)(2,1)}, u32[]{:S(2)}, u32[]{:S(2)}) collective-permute-start(bf16[256,2048]{1,0:T(8,128)(2,1)} %collective-permute-done.1.refs_4_), channel_id=1, source_target_pairs={{0,2},{1,3},{2,6},{3,7},{4,0},{5,1},{6,4},{7,5},{8,10},{9,11},{10,... | collective-permute-start | bytes 3145736 | tf_op jit(solution)/shard_map/ppermute | solution.py:44
  139.7 30.4 %collective-permute-start = (bf16[256,2048]{1,0:T(8,128)(2,1)S(1)}, bf16[256,2048]{1,0:T(8,128)(2,1)}, u32[]{:S(2)}, u32[]{:S(2)}) collective-permute-start(bf16[256,2048]{1,0:T(8,128)(2,1)S(1)} %slice.136), channel_id=1, source_target_pairs={{0,1},{1,0},{2,3},{3,2},{4,5},{5,4},{6,7},{7,6},{8,9},{9,8},{10,11... | collective-permute-start | bytes 3145736 | tf_op jit(solution)/shard_map/ppermute | solution.py:47
  153.8 18.8 %copy-start.17 = (f32[2048]{0:T(1024)S(1)}, f32[2048]{0:T(1024)}, u32[]{:S(2)}) copy-start(f32[2048]{0:T(1024)} %param.21) | copy-start | bytes 24580
  153.8 20.0 %collective-permute-start.2 = (bf16[256,2048]{1,0:T(8,128)(2,1)}, bf16[256,2048]{1,0:T(8,128)(2,1)}, u32[]{:S(2)}, u32[]{:S(2)}) collective-permute-start(bf16[256,2048]{1,0:T(8,128)(2,1)} %collective-permute-done.1.refs_4_), channel_id=1, source_target_pairs={{0,1},{1,0},{2,3},{3,2},{4,5},{5,4},{6,7},{7,6},{8,9},{9,8},{10,11... | collective-permute-start | bytes 3145736 | tf_op jit(solution)/shard_map/ppermute | solution.py:47
  170.0 3.8 collective-permute-start.4
  324.5 2.3 copy-start.1
  324.5 2.5 copy-start.7
  327.0 6.3 copy-start.5
  327.7 12.6 %copy-start.13 = (bf16[256,2048]{1,0:T(8,128)(2,1)}, bf16[256,2048]{1,0:T(8,128)(2,1)S(1)}, u32[]{:S(2)}) copy-start(bf16[256,2048]{1,0:T(8,128)(2,1)S(1)} %fusion.30) | copy-start | bytes 3145732
  327.7 10.5 %collective-permute-start.10 = (bf16[256,2048]{1,0:T(8,128)(2,1)S(1)}, bf16[256,2048]{1,0:T(8,128)(2,1)S(1)}, u32[]{:S(2)}, u32[]{:S(2)}) collective-permute-start(bf16[256,2048]{1,0:T(8,128)(2,1)S(1)} %fusion.30), channel_id=1, source_target_pairs={{0,1},{1,0},{2,3},{3,2},{4,5},{5,4},{6,7},{7,6},{8,9},{9,8},{10,11... | collective-permute-start | bytes 3145736 | tf_op jit(solution)/shard_map/ppermute | solution.py:47
  333.2 35.1 %collective-permute-start.5 = (bf16[4,256,2048]{2,1,0:T(8,128)(2,1)}, bf16[4,256,2048]{2,1,0:T(8,128)(2,1)}, u32[]{:S(2)}, u32[]{:S(2)}) collective-permute-start(bf16[4,256,2048]{2,1,0:T(8,128)(2,1)} %slice_bitcast_fusion), channel_id=1, source_target_pairs={{0,1},{1,0},{2,3},{3,2},{4,5},{5,4},{6,7},{7,6},{8,9},{9,8},{10,11... | collective-permute-start | bytes 12582920 | tf_op jit(solution)/shard_map/ppermute | solution.py:47
  333.2 7.0 %copy-start.24 = (bf16[1024,2048]{1,0:T(8,128)(2,1)S(1)}, bf16[1024,2048]{1,0:T(8,128)(2,1)}, u32[]{:S(2)}) copy-start(bf16[1024,2048]{1,0:T(8,128)(2,1)} %get-tuple-element.40) | copy-start | bytes 12582916
  335.5 80.0 %collective-permute-start.6 = (bf16[2112,256]{1,0:T(8,128)(2,1)}, bf16[2112,256]{1,0:T(8,128)(2,1)}, u32[]{:S(2)}, u32[]{:S(2)}) collective-permute-start(bf16[2112,256]{1,0:T(8,128)(2,1)} %get-tuple-element.96), channel_id=1, source_target_pairs={{0,8},{8,0},{16,24},{24,16},{1,9},{9,1},{17,25},{25,17},{2,10},{10... | collective-permute-start | bytes 3244040 | tf_op jit(solution)/shard_map/ppermute | solution.py:50
  335.5 80.0 %collective-permute-start.7 = (bf16[2112,256]{1,0:T(8,128)(2,1)}, bf16[2112,256]{1,0:T(8,128)(2,1)}, u32[]{:S(2)}, u32[]{:S(2)}) collective-permute-start(bf16[2112,256]{1,0:T(8,128)(2,1)} %get-tuple-element.95), channel_id=1, source_target_pairs={{0,8},{8,0},{16,24},{24,16},{1,9},{9,1},{17,25},{25,17},{2,10},{10... | collective-permute-start | bytes 3244040 | tf_op jit(solution)/shard_map/ppermute | solution.py:50
  337.6 77.9 %collective-permute-start.8 = (bf16[2112,256]{1,0:T(8,128)(2,1)}, bf16[2112,256]{1,0:T(8,128)(2,1)}, u32[]{:S(2)}, u32[]{:S(2)}) collective-permute-start(bf16[2112,256]{1,0:T(8,128)(2,1)} %get-tuple-element.94), channel_id=1, source_target_pairs={{0,16},{8,24},{16,0},{24,8},{1,17},{9,25},{17,1},{25,9},{2,18},{10... | collective-permute-start | bytes 3244040 | tf_op jit(solution)/shard_map/ppermute | solution.py:50
  338.2 5.4 copy-start.20
  338.2 77.3 %collective-permute-start.9 = (bf16[2112,256]{1,0:T(8,128)(2,1)}, bf16[2112,256]{1,0:T(8,128)(2,1)}, u32[]{:S(2)}, u32[]{:S(2)}) collective-permute-start(bf16[2112,256]{1,0:T(8,128)(2,1)} %get-tuple-element.93), channel_id=1, source_target_pairs={{0,16},{8,24},{16,0},{24,8},{1,17},{9,25},{17,1},{25,9},{2,18},{10... | collective-permute-start | bytes 3244040 | tf_op jit(solution)/shard_map/ppermute | solution.py:50
  360.4 1.5 copy-start.15
  362.1 1.6 copy-start.16
  362.1 1.8 copy-start.25
  362.3 6.1 slice-start.3
  363.9 4.4 slice-start.4
  372.3 62.6 %copy-start = (f32[4,256,2048]{2,1,0:T(8,128)}, f32[4,256,2048]{2,1,0:T(8,128)S(1)}, u32[]{:S(2)}) copy-start(f32[4,256,2048]{2,1,0:T(8,128)S(1)} %convert_add_fusion) | copy-start | bytes 25165828
  372.3 7.4 %copy-start.22 = (bf16[2048,1024]{1,0:T(8,128)(2,1)S(1)}, bf16[2048,1024]{1,0:T(8,128)(2,1)}, u32[]{:S(2)}) copy-start(bf16[2048,1024]{1,0:T(8,128)(2,1)} %get-tuple-element.37) | copy-start | bytes 12582916
  372.5 32.6 %collective-permute-start.11 = (bf16[256,2048]{1,0:T(8,128)(2,1)S(1)}, bf16[256,2048]{1,0:T(8,128)(2,1)S(1)}, u32[]{:S(2)}, u32[]{:S(2)}) collective-permute-start(bf16[256,2048]{1,0:T(8,128)(2,1)S(1)} %fusion.19), channel_id=1, source_target_pairs={{0,2},{1,3},{2,6},{3,7},{4,0},{5,1},{6,4},{7,5},{8,10},{9,11},{10,... | collective-permute-start | bytes 3145736 | tf_op jit(solution)/shard_map/ppermute | solution.py:44
  379.8 3.8 copy-start.14
  379.8 3.8 copy-start.21
  379.8 3.8 copy-start.26
  383.6 31.9 %slice-start = ((s8[8650752]{0:T(1024)(128)(4,1)}), s8[4194304]{0:T(1024)(128)(4,1)S(1)}, s32[]{:S(2)}) async-start(s8[8650752]{0:T(1024)(128)(4,1)} %bitcast.99), calls=%async_computation | async-start | bytes 8388608
  383.6 31.9 %slice-start.1 = ((s8[8650752]{0:T(1024)(128)(4,1)}), s8[4194304]{0:T(1024)(128)(4,1)S(1)}, s32[]{:S(2)}) async-start(s8[8650752]{0:T(1024)(128)(4,1)} %bitcast.99), calls=%async_computation.1 | async-start | bytes 8388608
  388.1 27.5 %slice-start.2 = ((s8[8650752]{0:T(1024)(128)(4,1)}), s8[262144]{0:T(1024)(128)(4,1)S(1)}, s32[]{:S(2)}) async-start(s8[8650752]{0:T(1024)(128)(4,1)} %bitcast.99), calls=%async_computation.2 | async-start | bytes 524288
  405.4 29.5 %collective-permute-start.12 = (bf16[256,2048]{1,0:T(8,128)(2,1)S(1)}, bf16[256,2048]{1,0:T(8,128)(2,1)S(1)}, u32[]{:S(2)}, u32[]{:S(2)}) collective-permute-start(bf16[256,2048]{1,0:T(8,128)(2,1)S(1)} %fusion.13), channel_id=1, source_target_pairs={{0,2},{1,3},{2,6},{3,7},{4,0},{5,1},{6,4},{7,5},{8,10},{9,11},{10,... | collective-permute-start | bytes 3145736 | tf_op jit(solution)/shard_map/ppermute | solution.py:44
  649.3 10.6 %copy-start.12 = (bf16[256,2048]{1,0:T(8,128)(2,1)S(1)}, bf16[256,2048]{1,0:T(8,128)(2,1)}, u32[]{:S(2)}) copy-start(bf16[256,2048]{1,0:T(8,128)(2,1)} %get-tuple-element.58) | copy-start | bytes 3145732
  661.4 3.0 copy-start.11
  665.9 3.0 copy-start.4
  665.9 3.0 copy-start.18
  668.9 6.7 copy-start.6
  668.9 6.7 copy-start.10
  671.2 4.5 copy-start.2
  671.2 4.5 copy-start.8

commit v4 on v3

--- a/solution.py
+++ b/solution.py
@@ -338,18 +338,18 @@
         dk_ref[keys, :] += mm((p * (b - dot)).astype(BF16), q, NN)
 
 
+FRONT_HOPS = 1
 FRONT_ORDER = (
-    "kv q1 o1 kv", "q1 q2 o1 o2", "kv q1 q2 q3", "kv o1 o2 o3", "kv* s q2 q3", "s o2 o3 s", "q2 q3 s o2",
-    "o3 s q3 s", "g s o3 s",
-    "q1* o1* q2* o2*", "q3* o3* s* g*",
+    "kv q1 o1 kv", "q1 q2 o1 o2", "kv q1 q2 q3", "kv o1 o2 o3", "g kv* s q2", "q3 s o2 o3", "s g q2 q3",
+    "s o2 o3 s", "q3 s g s", "o3 s q1* o1*", "q2* o2* q3* o3*", "s* g*",
 )
 
 
 def front_kernel(
     links, docs, tokens, gain, w_kv, cosine, sine, q_two, g_two, wq_hbm, wo_hbm, og_hbm,
-    normed, wq_out, wo_out, og_up, og_pair, og_up_pair, kv_out, kt_ref, dk_ref, dv_ref,
-    kv, ss, rs, ls,
+    normed, wq_out, wo_out, kv_out, kt_ref, dk_ref, dv_ref, *refs,
 ):
+    og_outs, (kv, ss, rs, ls) = refs[:-4], refs[-4:]
     chips, bits, n_dp = links.chips, links.bits, links.n_dp
     own, depth = tokens.shape
     seq = own * links.n_tensor
@@ -450,14 +450,17 @@
                 held[way].append(rel)
 
     def grad_chain():
-        swap = send(og_hbm, og_pair, sibling)
-        hop = send(og_hbm, og_up, right)
+        source = og_hbm
+        swaps = [send(og_hbm, og_outs[0], sibling)]
+        for i in range(1, len(og_outs), 2):
+            hop = send(source, og_outs[i], right)
+            yield
+            hop.wait_recv()
+            source = og_outs[i]
+            swaps.append(send(source, og_outs[i + 1], sibling))
         yield
-        hop.wait_recv()
-        second = send(og_up, og_up_pair, sibling)
-        yield
-        swap.wait_recv()
-        second.wait_recv()
+        for copy in swaps:
+            copy.wait_recv()
 
     rows = min(512, SEQ_SHORT)
     heads = q_two.shape[1] // HD
@@ -504,16 +507,17 @@
     here = pl.BlockSpec(memory_space=pltpu.VMEM)
     dma = pltpu.SemaphoreType.DMA
     shape = jax.ShapeDtypeStruct
-    count = 2 * chips * (2 * links.n_dp) + 2 * chips + 8
+    count = 2 * chips * (2 * links.n_dp) + 4 * chips + 8
+    hops = min(FRONT_HOPS, chips - 1)
     return pl.pallas_call(
         functools.partial(front_kernel, links),
         in_specs=[pl.BlockSpec(memory_space=pltpu.SMEM)] + [here] * 7 + [anywhere] * 3,
-        out_specs=[here] + [anywhere] * 6 + [here] * 3,
+        out_specs=[here] + [anywhere] * 3 + [here] * 3 + [anywhere] * (1 + 2 * hops),
         out_shape=[
             shape((2 * own, depth), BF16), shape((depth, chips * width), BF16), shape((chips * width, depth), BF16),
-            shape((own, depth), BF16), shape((own, depth), BF16), shape((own, depth), BF16),
             shape((seq, 2 * HD), BF16), shape((HD, seq), BF16), shape((seq, HD), F32), shape((seq, HD), F32),
-        ],
+        ]
+        + [shape((own, depth), BF16)] * (1 + 2 * hops),
         scratch_shapes=[pltpu.VMEM((seq, 2 * HD), BF16), dma((count,)), dma((count,)), dma((3,))],
         compiler_params=pltpu.CompilerParams(
             collective_id=3, has_side_effects=True, vmem_limit_bytes=VMEM_LIMIT
@@ -528,8 +532,9 @@
 ):
     g_hbm, refs = refs[: links.n_tensor], refs[links.n_tensor :]
     (
-    ghn_ref, mlp_hbm, grads_hbm, h_all, g_all, wg, wu, wd, act_t, gg_t, gu_t, keep, stage, pair_out, pair_in, ring_out, ring_in,
-    load_sem, ring_s, ring_r, swap_s, swap_r, pair_s, pair_r, rs_s, rs_r, stage_sem, store_sem,
+    ghn_ref, mlp_hbm, grads_hbm, h_all, g_all, wg, wu, wd, act_t, gg_t, gu_t, mlp_in, stage, pair_out, pair_in, ring_out, ring_in,
+    load_sem, ring_s, ring_r, swap_s, swap_r, pair_s, pair_r, rs_s, rs_r, mlp_s, mlp_r,
+    stage_sem, store_sem,
     ) = refs
     chips = links.chips
     own, depth = h_hbm.shape
@@ -576,8 +581,12 @@
         slot = lax.rem(k, 2)
         return remote(ring_out.at[slot], ring_in.at[k], rs_s.at[k], rs_r.at[k], right)
 
-    def store(k, half):
-        return pltpu.make_async_copy(stage.at[half], mlp_hbm.at[k, half], stage_sem.at[half])
+    def mlp_pair(k):
+        slot = lax.rem(k, 2)
+        return remote(stage.at[1], mlp_in.at[slot], mlp_s.at[slot], mlp_r.at[slot], sibling)
+
+    def store(k):
+        return pltpu.make_async_copy(stage.at[0], mlp_hbm.at[k], stage_sem.at[0])
 
     loads[0].wait()
     ring(0).start()
@@ -585,7 +594,7 @@
     for load in loads[1:]:
         load.wait()
 
-    def half_chunk(k, half):
+    def hidden_units(k, half):
         h, g = h_all[k, half], g_all[k, half]
         gate = mm(h, wg[...], NT)
         upward = mm(h, wu[...], NT)
@@ -595,29 +604,13 @@
         act = (swish * upward).astype(BF16)
         gg = (grad_act * upward * sigma * (1.0 + gate * (1.0 - sigma))).astype(BF16)
         gu = (grad_act * swish).astype(BF16)
+        return act, gg, gu
+
+    def keep_units(k, half, act, gg, gu):
         columns = pl.ds(pl.multiple_of((2 * k + half) * own, own), own)
         act_t[:, columns] = act.T
         gg_t[:, columns] = gg.T
         gu_t[:, columns] = gu.T
-        if half == 1:
-
-            @pl.when(k >= 2)
-            def _():
-                pair(k - 2).wait_send()
-
-        part = mm(gg, wg[...], NN) + mm(gu, wu[...], NN)
-        if half == 1:
-            pair_out[lax.rem(k, 2)] = part.astype(BF16)
-            pair(k).start()
-        else:
-            keep[...] = part
-
-        @pl.when(k >= 1)
-        def _():
-            store(k - 1, half).wait()
-
-        stage[half] = mm(act, wd[...], NN).astype(BF16)
-        store(k, half).start()
 
     def chunk(k, _):
         @pl.when(k >= 1)
@@ -630,11 +623,19 @@
 
             swap(k).start()
 
+        act0, gg0, gu0 = hidden_units(k, 0)
         swap(k).wait_recv()
-        half_chunk(k, 1)
-        half_chunk(k, 0)
+        act1, gg1, gu1 = hidden_units(k, 1)
+
+        @pl.when(k >= 2)
+        def _():
+            pair(k - 2).wait_send()
+
+        pair_out[lax.rem(k, 2)] = (mm(gg1, wg[...], NN) + mm(gu1, wu[...], NN)).astype(BF16)
+        pair(k).start()
+        part = mm(gg0, wg[...], NN) + mm(gu0, wu[...], NN)
         pair(k).wait_recv()
-        total = keep[...] + pair_in[lax.rem(k, 2)].astype(F32)
+        total = part + pair_in[lax.rem(k, 2)].astype(F32)
 
         @pl.when(k == 0)
         def _():
@@ -656,6 +657,23 @@
             ring_out[lax.rem(k, 2)] = (total + ring_in[k - 1].astype(F32)).astype(BF16)
             scatter(k).start()
 
+        @pl.when(k >= 1)
+        def _():
+            mlp_pair(k - 1).wait_send()
+
+        stage[1] = mm(act1, wd[...], NN).astype(BF16)
+        mlp_pair(k).start()
+        keep_units(k, 0, act0, gg0, gu0)
+        keep_units(k, 1, act1, gg1, gu1)
+        mine = mm(act0, wd[...], NN)
+        mlp_pair(k).wait_recv()
+
+        @pl.when(k >= 1)
+        def _():
+            store(k - 1).wait()
+
+        stage[0] = (mine + mlp_in[lax.rem(k, 2)].astype(F32)).astype(BF16)
+        store(k).start()
         return 0
 
     lax.fori_loop(0, chips, chunk, 0)
@@ -687,8 +705,8 @@
 
     for copy in stores:
         copy.wait()
-    for half in (0, 1):
-        store(chips - 1, half).wait()
+    store(chips - 1).wait()
+    mlp_pair(chips - 1).wait_send()
     for k in (chips - 2, chips - 1):
         pair(k).wait_send()
         scatter(k).wait_send()
@@ -711,7 +729,7 @@
         out_specs=[pl.BlockSpec(memory_space=pltpu.VMEM)] + [anywhere] * 2,
         out_shape=[
             jax.ShapeDtypeStruct((own, depth), F32),
-            jax.ShapeDtypeStruct((chips, 2, own, depth), BF16),
+            jax.ShapeDtypeStruct((chips, own, depth), BF16),
             jax.ShapeDtypeStruct((pieces, 3 * units, depth // pieces), BF16),
         ],
         scratch_shapes=[
@@ -723,7 +741,7 @@
             pltpu.VMEM((units, seq), BF16),
             pltpu.VMEM((units, seq), BF16),
             pltpu.VMEM((units, seq), BF16),
-            pltpu.VMEM((own, depth), F32),
+            pltpu.VMEM((2, own, depth), BF16),
             pltpu.VMEM((2, own, depth), BF16),
             pltpu.VMEM((2, own, depth), BF16),
             pltpu.VMEM((2, own, depth), BF16),
@@ -731,7 +749,7 @@
             pltpu.VMEM((chips, own, depth), BF16),
             dma((4 + links.n_tensor,)),
             dma((chips,)), dma((chips,)), dma((chips,)), dma((chips,)), dma((2,)), dma((2,)),
-            dma((chips,)), dma((chips,)), dma((2,)), dma((3, pieces)),
+            dma((chips,)), dma((chips,)), dma((2,)), dma((2,)), dma((1,)), dma((3, pieces)),
         ],
         compiler_params=pltpu.CompilerParams(
             collective_id=1, has_side_effects=True, vmem_limit_bytes=60 * 2**20
@@ -762,8 +780,8 @@
 
 
 class DpSum:
-    def __init__(self, links, send, me, buf, got, free, first=0):
-        self.first = first
+    def __init__(self, links, send, me, buf, got, free, first=0, rows=None):
+        self.first, self.rows = first, rows or buf.shape[1]
         self.links, self.send, self.me, self.buf, self.got, self.free = links, send, me, buf, got, free
         self.n = links.n_dp
         self.ways = [links.bits, links.bits[::-1]]
@@ -771,6 +789,9 @@
 
     def at(self, way, rel):
         return way * self.n + (self.me ^ rel)
+
+    def view(self, way, rel):
+        return self.buf.at[self.at(way, rel), pl.ds(0, self.rows)]
 
     def kept(self, way, step):
         done = sum(self.ways[way][: step + 1])
@@ -814,7 +835,7 @@
             for way in (0, 1):
                 bit = self.ways[way][step]
                 rel = self.kept(way, step)[rank]
-                where = self.buf.at[self.at(way, rel)]
+                where = self.view(way, rel)
                 self.pending.append((self.send(where, where, self.peer(bit)), way, rel ^ bit))
 
     def finish_doubling(self):
@@ -822,12 +843,13 @@
             copy.wait_recv()
         return [(way, rel) for _, way, rel in self.pending]
 
-    def chain(self, done):
+    def chain(self, done, middle=()):
         rounds = len(self.links.bits)
         for step in range(self.first, rounds):
             self.start_halving(step)
             yield
             self.finish_halving()
+        yield from middle
         for step in reversed(range(rounds)):
             self.start_doubling(step)
             if step == rounds - 1:
@@ -858,13 +880,13 @@
     (
         o_hbm, q_hbm, m_hbm, kv_keep, kv_send, gn_keep, gn_send, tokens, normed, w_kv, cosine, sine, gain_part,
         ws_hbm, ow_hbm, qw_hbm, kvw_hbm, got_hbm, gn_ref, gains_ref,
-        o_buf, o_in, q_buf, q_in, w_buf, w_in, a_buf, a_in, b_buf, b_in,
+        o_buf, o_in, o_ring, q_buf, q_in, w_buf, w_in, c_buf, c_in, b_buf, b_in,
         kv_got, kv_ring, kv_in, gn_got, kvw_half, kvw_got, kvw_in, kvw_all, gains_in,
-        ss, rs, o_sem, q_sem, w_sem, out_sem, kvw_sem, w_free, a_free, b_free,
+        ss, rs, o_sem, q_sem, w_sem, out_sem, w_free, o_free, b_free,
     ) = refs
     chips, bits = links.chips, links.bits
     n_dp = links.n_dp
-    width = o_buf.shape[1]
+    width = q_buf.shape[1]
     piece = w_buf.shape[2]
     me = lax.axis_index("tensor")
     me_dp = lax.axis_index("dp")
@@ -873,8 +895,9 @@
     right = {"tensor": ahead * 2 + core}
     left = {"tensor": behind * 2 + core}
     sibling = {"tensor": me ^ 1}
-    chip_bits = [2 << b for b in range(chips.bit_length() - 1)]
-    butterfly = [sibling] + [{"tensor": me ^ bit} for bit in chip_bits] + [{"dp": me_dp ^ bit} for bit in bits]
+    column = [None] + [{"tensor": me ^ (2 * k)} for k in range(1, chips)]
+    group = [{"tensor": me ^ k} for k in range(1, links.n_tensor)]
+    replicas = [{"dp": me_dp ^ k} for k in range(1, n_dp)]
 
     w_loads = [
         pltpu.make_async_copy(ref, w_buf.at[way * n_dp + (me_dp ^ rel)], w_sem.at[i])
@@ -882,12 +905,14 @@
     ]
     loads = {}
     for k in list(range(1, chips)) + [0]:
-        loads["o", k] = pltpu.make_async_copy(o_hbm.at[k], o_buf.at[k], o_sem.at[k])
         loads["q", k] = pltpu.make_async_copy(q_hbm.at[k], q_buf.at[k], q_sem.at[k])
-    for load in w_loads + list(loads.values()):
+    o_loads = [
+        pltpu.make_async_copy(o_hbm.at[:, pl.ds(j * piece, piece)], o_buf.at[j], o_sem.at[j]) for j in range(2 * n_dp)
+    ]
+    for load in o_loads + list(loads.values()) + w_loads:
         load.start()
     barrier = pltpu.get_barrier_semaphore()
-    peers = [right, left] + butterfly
+    peers = [right, left] + group + replicas
     for peer in peers:
         pl.semaphore_signal(barrier, inc=1, device_id=peer, device_id_type=pl.DeviceIdType.MESH)
     pl.semaphore_wait(barrier, len(peers))
@@ -925,16 +950,15 @@
 
     def kv_chain():
         kv_swap.wait_recv()
-        copy = None
-        for k in list(range(1, chips)) + [0]:
-            total = kv_keep[k] + kv_got[k].astype(F32)
-            if copy is not None:
-                copy.wait_recv()
-                total = total + kv_in[(k - 1) % chips - 1].astype(F32)
-            if k:
-                kv_ring[k - 1] = total.astype(BF16)
-                copy = send(kv_ring.at[k - 1], kv_in.at[k - 1], right)
-                yield
+        sent = []
+        for k in range(1, chips):
+            kv_ring[k - 1] = (kv_keep[k] + kv_got[k].astype(F32)).astype(BF16)
+            sent.append(send(kv_ring.at[k - 1], kv_in.at[k - 1], column[k]))
+        yield
+        total = kv_keep[0] + kv_got[0].astype(F32)
+        for k, copy in enumerate(sent):
+            copy.wait_recv()
+            total = total + kv_in[k].astype(F32)
         key_grad = total[:, :HD]
         key_grad = key_grad * cosine[...] - pltpu.roll(key_grad, HD // 2, 1) * sine[...]
         kv_lin = jnp.concatenate([key_grad, total[:, HD:]], axis=1).astype(BF16)
@@ -949,43 +973,42 @@
         x = tokens[...].astype(F32)
         factor = lax.rsqrt(jnp.mean(x * x, axis=1, keepdims=True) + EPSILON)
         part = jnp.sum(grad * (x * factor), axis=0, keepdims=True)
-        row = lax.broadcasted_iota(jnp.int32, gains_ref.shape, 0)
-        gains_ref[...] = jnp.where(row == 0, jnp.broadcast_to(part, gains_ref.shape), gain_part[...])
+        lanes = gains_ref.shape[1]
+        gains_ref[...] = jnp.concatenate(
+            [v[:, i * lanes : (i + 1) * lanes] for v in (part, gain_part[...]) for i in range(4)], axis=0
+        )
 
     def gains_chain():
-        for number, peer in enumerate(butterfly):
-            copy = send(gains_ref, gains_in.at[number], peer, False)
+        done = 0
+        for stage in (group, replicas):
+            sent = [send(gains_ref, gains_in.at[done + i], peer, False) for i, peer in enumerate(stage)]
             yield
-            copy.wait_recv()
-            copy.wait_send()
-            gains_ref[...] += gains_in[number]
+            total = gains_ref[...]
+            for i, copy in enumerate(sent):
+                copy.wait_recv()
+                copy.wait_send()
+                total = total + gains_in[done + i]
+            gains_ref[...] = total
+            done += len(stage)
 
     band = HD // chips
 
-    def chip_up(k):
-        found = chip * 0
-        for i, c in enumerate(links.order):
-            found = jnp.where(chip == c, links.order[(i - k) % chips], found)
-        return found
-
     def rows_of(k):
-        return pl.ds(pl.multiple_of(chip_up(k) * band, band), band)
+        return pl.ds(pl.multiple_of((chip ^ k) * band, band), band)
 
     def kvw_chain():
         held["swap"].wait_recv()
         add_into(kvw_half.at[core], kvw_got, HD)
-        copy = None
-        for k in list(range(1, chips)) + [0]:
-            if copy is not None:
-                copy.wait_recv()
-                mine = kvw_half.at[core, rows_of(k)]
-                mine[...] = (mine[...].astype(F32) + kvw_in[(k - 1) % chips - 1].astype(F32)).astype(BF16)
-            if k:
-                copy = send(kvw_half.at[core, rows_of(k)], kvw_in.at[k - 1], right)
-                yield
+        sent = [send(kvw_half.at[core, rows_of(k)], kvw_in.at[k - 1], column[k]) for k in range(1, chips)]
+        yield
+        total = kvw_half[core, rows_of(0)].astype(F32)
+        for k, copy in enumerate(sent):
+            copy.wait_recv()
+            total = total + kvw_in[k].astype(F32)
+        c_buf[...] = total.astype(BF16)
 
     sum_w = DpSum(links, send, me_dp, w_buf, w_in, w_free, 1)
-    sum_a = DpSum(links, send, me_dp, a_buf, a_in, a_free)
+    sum_o = DpSum(links, send, me_dp, o_buf, o_in, o_free, 0, width)
     sum_b = DpSum(links, send, me_dp, b_buf, b_in, b_free)
 
     def columns(ref, number):
@@ -996,29 +1019,44 @@
             load.wait()
         yield from sum_w.chain(lambda way, rel: put(w_buf.at[sum_w.at(way, rel)], columns(ws_hbm, sum_w.at(way, rel))))
 
-    def a_chain():
-        for j in range(2 * n_dp):
-            a_buf[j, pl.ds(0, width)] = o_buf[0, :, pl.ds(j * piece, piece)]
-            a_buf[j, pl.ds(width, band)] = kvw_half[core, rows_of(0), pl.ds(j * piece, piece)]
-        yield from sum_a.chain(
-            lambda way, rel: put(
-                a_buf.at[sum_a.at(way, rel), pl.ds(0, width)], columns(ow_hbm, sum_a.at(way, rel))
-            )
+    def o_ring_chain():
+        sent = []
+        for k in list(range(1, chips)) + [0]:
+            rows = pl.ds(k * width, width)
+            for way, copy in enumerate(sent):
+                copy.wait_recv()
+                add_into(o_buf.at[sum_o.at(way, 0), rows], o_ring.at[(k - 1) % chips - 1, way], width)
+            if k:
+                sent = [
+                    send(o_buf.at[sum_o.at(way, 0), rows], o_ring.at[k - 1, way], right) for way in (0, 1)
+                ]
+                yield
+
+    def o_chain():
+        for load in o_loads:
+            load.wait()
+        yield from sum_o.chain(
+            lambda way, rel: put(sum_o.view(way, rel), columns(ow_hbm, sum_o.at(way, rel))), o_ring_chain()
         )
 
-    def last_chain():
-        for j in range(2 * n_dp):
-            kvw_all[0, core, :, pl.ds(j * piece, piece)] = a_buf[j, pl.ds(width, band)]
-        for k in range(chips - 1):
-            copy = send(kvw_all.at[k, core], kvw_all.at[k + 1, core], right)
-            yield
+    def c_chain():
+        sent = [send(c_buf, c_in.at[i], peer) for i, peer in enumerate(replicas)]
+        yield
+        total = c_buf[...].astype(F32)
+        for i, copy in enumerate(sent):
+            copy.wait_recv()
+            total = total + c_in[i].astype(F32)
+        kvw_all[0, core] = total.astype(BF16)
+        sent = [send(kvw_all.at[0, core], kvw_all.at[k, core], column[k]) for k in range(1, chips)]
+        yield
+        for copy in sent:
             copy.wait_recv()
         copy = send(kvw_all.at[:, core], kvw_all.at[:, core], sibling)
         yield
         copy.wait_recv()
         for k in range(chips):
             for half in (0, 1):
-                to = pl.ds(pl.multiple_of(half * HD + chip_up(k) * band, band), band)
+                to = pl.ds(pl.multiple_of(half * HD + (chip ^ k) * band, band), band)
                 put(kvw_all.at[k, half], kvw_hbm.at[to])
 
     def b_chain():
@@ -1032,8 +1070,8 @@
         copy.wait_recv()
 
     chains = {
-        "w": w_chain(), "o": ring_chain("o", o_buf, o_in), "q": ring_chain("q", q_buf, q_in), "kv": kv_chain(),
-        "g": gains_chain(), "kvw": kvw_chain(), "m": m_chain(), "a": a_chain(), "b": b_chain(), "l": last_chain(),
+        "w": w_chain(), "o": o_chain(), "q": ring_chain("q", q_buf, q_in), "kv": kv_chain(),
+        "g": gains_chain(), "kvw": kvw_chain(), "m": m_chain(), "c": c_chain(), "b": b_chain(),
     }
 
     take_turns(chains, TAIL_ORDER)
@@ -1044,8 +1082,7 @@
 
 
 TAIL_ORDER = (
-    "w o kv kv", "q kv kv o", "kv* kvw g w", "q kvw g w", "o kvw g kvw*", "g q g m", "o* a g* q*", "a b a b",
-    "a b a* l", "b l b l", "b* l* w* m*",
+    "o w kv q", "kv* kvw g kvw*", "c g* o c", "w q o c*", "o q w o", "q* b o m", "b o* b* m*", "w*",
 )
 
 
@@ -1053,7 +1090,7 @@
     links, o_parts, q_parts, m_part, w_pieces, names, kv_keep, kv_send, gn_keep, gn_send, tokens, normed, w_kv, cosine,
     sine, gain_part,
 ):
-    chips, width, depth = o_parts.shape
+    chips, width, depth = q_parts.shape
     own = tokens.shape[0]
     rows, piece = w_pieces[0].shape
     band = HD // chips
@@ -1063,7 +1100,7 @@
     here = pl.BlockSpec(memory_space=pltpu.VMEM)
     dma = pltpu.SemaphoreType.DMA
     shape = jax.ShapeDtypeStruct
-    count = 16 * chips + 6 * n * 2 + 16
+    count = 20 * chips + 20 * n + 16
     return pl.pallas_call(
         functools.partial(tail_kernel, links, names),
         in_specs=[anywhere] * (3 + len(names)) + [here] * 10,
@@ -1071,13 +1108,14 @@
         out_shape=[
             shape((rows, depth), BF16), shape((width, depth), BF16),
             shape((width, depth), BF16), shape((2 * HD, depth), BF16), shape((own, depth), BF16),
-            shape((own, depth), F32), shape((8, depth), F32),
+            shape((own, depth), F32), shape((8, depth // 4), F32),
         ],
         scratch_shapes=[
-            pltpu.VMEM((chips, width, depth), BF16), pltpu.VMEM((chips - 1, width, depth), BF16),
+            pltpu.VMEM((pieces, chips * width, piece), BF16), pltpu.VMEM((2, n - 1, chips * width, piece), BF16),
+            pltpu.VMEM((chips - 1, 2, width, piece), BF16),
             pltpu.VMEM((chips, width, depth), BF16), pltpu.VMEM((chips - 1, width, depth), BF16),
             pltpu.VMEM((pieces, rows, piece), BF16), pltpu.VMEM((2, max(1, n // 2 - 1), rows, piece), BF16),
-            pltpu.VMEM((pieces, width + band, piece), BF16), pltpu.VMEM((2, n - 1, width + band, piece), BF16),
+            pltpu.VMEM((band, depth), BF16), pltpu.VMEM((n - 1, band, depth), BF16),
             pltpu.VMEM((pieces, width, piece), BF16), pltpu.VMEM((2, n - 1, width, piece), BF16),
             pltpu.VMEM((chips, own, 2 * HD), BF16),
             pltpu.VMEM((chips - 1, own, 2 * HD), BF16), pltpu.VMEM((chips - 1, own, 2 * HD), BF16),
@@ -1085,9 +1123,9 @@
             pltpu.VMEM((2, HD, depth), BF16), pltpu.VMEM((HD, depth), BF16),
             pltpu.VMEM((chips - 1, band, depth), BF16),
             pltpu.VMEM((chips, 2, band, depth), BF16),
-            pltpu.VMEM((len(links.bits) + chips.bit_length(), 8, depth), F32),
-            dma((count,)), dma((count,)), dma((chips,)), dma((chips,)), dma((len(names),)),
-            dma((3 * pieces + 2 * chips,)), dma((chips, 2)),
+            pltpu.VMEM((links.n_tensor + n, 8, depth // 4), F32),
+            dma((count,)), dma((count,)), dma((pieces,)), dma((chips,)), dma((len(names),)),
+            dma((3 * pieces + 2 * chips,)),
         ]
         + [pltpu.SemaphoreType.REGULAR((2, len(links.bits)))] * 3,
         compiler_params=pltpu.CompilerParams(
@@ -1136,15 +1174,15 @@
     attn_scale = rms_factor(residual)
     attn_pre = residual * attn_scale
 
-    normed, wq, wo, og_up, og_pair, og_up_pair, kv_all, key_rows_t, dk2, dv2 = front(
+    normed, wq, wo, kv_all, key_rows_t, dk2, dv2, *grad_chunks = front(
         links, doc_split, tokens, attn_gain[None], w_kv, cosine[:own], sine[:own], query_two, grad_two, w_query, w_out,
         out_grad,
     )
     normed_own = normed[:own]
-    grad_chunks = [out_grad, og_pair, og_up, og_up_pair]
-    for _ in range(2, chips):
-        og_up = links.ring(og_up)
-        grad_chunks += [og_up, links.swap(og_up)]
+    grad_chunks = [out_grad] + grad_chunks
+    while len(grad_chunks) < n_tensor:
+        further = links.ring(grad_chunks[-2])
+        grad_chunks += [further, links.swap(further)]
 
     q_lin = mm(normed, wq, NN)
     queries, context, lse = attend(sp, q_lin, cosine, sine, kv_all)
@@ -1154,12 +1192,11 @@
     mlp_pre = hidden * mlp_scale
     hidden_own = (mlp_pre * mlp_gain).astype(BF16)
 
-    grad_hn, mlp_parts, ffn_parts = feed_forward(links, hidden_own, grad_chunks, w_gate.T, w_up.T, w_down)
+    grad_hn, mlp_terms, ffn_parts = feed_forward(links, hidden_own, grad_chunks, w_gate.T, w_up.T, w_down)
     ffn_pieces, ffn_names = first_halving(links, ffn_parts, me_dp)
-    mlp_terms = mlp_parts[:, 0].astype(F32) + links.swap(mlp_parts[:, 1]).astype(F32)
-    mlp_sent = mlp_terms[1].astype(BF16)
+    mlp_sent = mlp_terms[1]
     for k in range(2, chips):
-        mlp_sent = (mlp_terms[k] + links.ring(mlp_sent).astype(F32)).astype(BF16)
+        mlp_sent = (mlp_terms[k].astype(F32) + links.ring(mlp_sent).astype(F32)).astype(BF16)
 
     mlp_gain_part = jnp.sum(grad_hn * mlp_pre, axis=0)
     scaled_mlp = grad_hn * mlp_gain
@@ -1172,20 +1209,20 @@
     query_grad, dk, dv = attend_back(
         sp, queries, grad_context, context, lse, cosine, sine, kv_all, key_rows_t, dk2, dv2
     )
-    out_parts = mm(context, grad_branch, TN).astype(BF16).reshape(chips, width, -1)
+    out_parts = mm(context, grad_branch, TN).astype(BF16)
     query_parts = mm(query_grad, normed, TN).astype(BF16).reshape(chips, width, -1)
 
     kv_part = jnp.concatenate([dk * SCALE, dv], axis=1).reshape(chips, 2, own, 2 * HD)
     kv_part = jnp.stack(
         [
-            lax.dynamic_index_in_dim(kv_part, order[(place[chip] - k + chips) % chips], 0, keepdims=False)
+            lax.dynamic_index_in_dim(kv_part, chip ^ k, 0, keepdims=False)
             for k in range(chips)
         ]
     )
     kv_keep = lax.dynamic_index_in_dim(kv_part, core, 1, keepdims=False)
     kv_send = lax.dynamic_index_in_dim(kv_part, 1 - core, 1, keepdims=False).astype(BF16)
     gn_part = mm(query_grad, wq, NT)
-    gain_part = jnp.pad(mlp_gain_part[None], ((1, 6), (0, 0)))
+    gain_part = mlp_gain_part[None]
     ffn_w, out_w, query_w, kv_w, mlp_got, grad_normed, gains = tail(
         links, out_parts, query_parts, mlp_sent, ffn_pieces, ffn_names, kv_keep, kv_send, gn_part[:own],
         gn_part[own:].astype(BF16), tokens, normed_own, w_kv, cosine[:own], sine[:own], gain_part,
@@ -1198,8 +1235,8 @@
     out_w_grad = out_w.astype(F32)
     query_w_grad = query_w.astype(F32).T
     kv_w_grad = kv_w.astype(F32).T
-    attn_gain_grad, mlp_gain_grad = gains[0], gains[1]
-    block_output = (hidden + (mlp_terms[0] + mlp_got.astype(F32))).astype(BF16)
+    attn_gain_grad, mlp_gain_grad = gains[:4].reshape(-1), gains[4:].reshape(-1)
+    block_output = (hidden + (mlp_terms[0].astype(F32) + mlp_got.astype(F32))).astype(BF16)
     scaled_attn = grad_normed * attn_gain
     tokens_grad = (
         grad_hidden

time: 690 us -> 612 us (0.89)
  Pallas kernels: 497 us -> 463 us
  waiting for transfers between devices: 49.6 us -> 19.4 us
  between operations: 12.5 us -> 1.95 us
  starting transfers between devices: 22.6 us -> 30 us
    ppermute x4, waiting for transfers between devices: 49.6 us -> 18.6 us  [ring(): return lax.ppermute(x, 'tensor', self.ring_pairs)]
    pallas_call x1, Pallas kernels: 105 us -> 86.5 us  [front(): pl.pallas_call(functools.partial(front_kernel, links), in_specs=[pl.Block...]
    pallas_call x1, Pallas kernels: 213 us -> 200 us  [tail(): pl.pallas_call(functools.partial(tail_kernel, links, names), in_specs=[an...]
    ppermute x4, starting transfers between devices: 4.05 us -> 15.3 us  [across(): return lax.ppermute(x, 'dp', [(i, i ^ bit) for i in range(self.n_dp)])]
  transfers between devices with their start and end apart: 13 -> 12, of which waited for: 4 -> 3; matrix products, arithmetic and copies ran while one was open for 9% -> 8% of each run, Pallas kernels for 4% -> 5%
where the time goes in v4:
time: 612 us; the launch traced here: 603 us
  Pallas kernels  463 us (76%)
  other arithmetic  43.4 us (7%)
  starting transfers between devices  30 us (5%)
  matrix products  24.6 us (4%)
  local copies, waits for them, and re-layouts  20.9 us (3%)
  waiting for transfers between devices  19.4 us (3%)
    pallas_call x1, Pallas kernels, tail(): pl.pallas_call(functools.partial(tail_kernel, links, names), in_specs=[an...  200 us
    pallas_call x1, Pallas kernels, feed_forward(): pl.pallas_call(functools.partial(mlp_kernel, links), in_specs=[anywhere]...  147 us
    pallas_call x1, Pallas kernels, front(): pl.pallas_call(functools.partial(front_kernel, links), in_specs=[pl.Block...  86.5 us
    dot_general x6, matrix products, mm(): lax.dot_general(left, right, (dims, ((), ())), preferred_element_type=F32)  24.6 us
    ppermute x4, waiting for transfers between devices, ring(): return lax.ppermute(x, 'tensor', self.ring_pairs)  18.6 us
    pallas_call x1, Pallas kernels, attend_back(): pl.pallas_call(functools.partial(bwd_kernel, seq // rows), grid_spec=pltp...  16.7 us
    ppermute x4, starting transfers between devices, across(): return lax.ppermute(x, 'dp', [(i, i ^ bit) for i in range(self.n_dp)])  15.3 us
    ppermute x4, starting transfers between devices, ring(): return lax.ppermute(x, 'tensor', self.ring_pairs)  13.1 us
  transfers between devices with their start and end apart: 12, of which 3 were waited for; matrix products, arithmetic and copies ran while one was open for 8% of the time, Pallas kernels for 5%

profile of v4, /device:TPU:0, one launch (start us, length us, event | category | flops | bytes accessed | tf_op | source)
XLA Modules:
  0.0 603.0 jit_solution(17485308131993678531)
XLA Ops:
  1.4 1.0 multiply_sine_fusion
  2.4 0.9 fusion.17
  3.2 86.5 %front.1 = (bf16[512,2048]{1,0:T(8,128)(2,1)}, bf16[2048,1024]{1,0:T(8,128)(2,1)}, bf16[1024,2048]{1,0:T(8,128)(2,1)}, bf16[2048,256]{1,0:T(8,128)(2,1)}, bf16[1...) custom-call(s32[1]{0:T(128)S(6)} %copy.37.docs, ...), custom_call_target="tpu_custom_call" | custom-call | flops 10000000000 | bytes 67108864 | tf_op jit(solution)/shard_map/front/pallas_call | solution.py:512
  89.7 0.9 collective-permute-start.1
  90.6 1.0 pad_maximum_fusion.5
  91.6 6.5 %fusion.27.q_ref = f32[512,1024]{1,0:T(8,128)} fusion(bf16[512,2048]{1,0:T(8,128)(2,1)} %get-tuple-element.36, bf16[2048,1024]{1,0:T(8,128)(2,1)} %get-tuple-element.37), kind=kOutput, calls=%fused_computation.88 | convolution fusion | flops 2147483648 | bytes 8388608 | tf_op jit(solution)/shard_map/dot_general | solution.py:22
  98.1 0.6 pad_add_fusion.sp_ref
  98.7 12.0 %attend.1 = (bf16[512,1024]{1,0:T(8,128)(2,1)}, bf16[512,1024]{1,0:T(8,128)(2,1)}, f32[8,8,512]{2,1,0:T(8,128)}) custom-call(s32[3]{0:T(128)} %pad_add_fusion.sp_ref, f32[512,1024]{1,0:T(8,128)} %fusion.27.q_ref, f32[512,128]{1,0:T(8,128)} %get-tuple-element.109.c_ref, f32[512,128]{1,0:T(8,128)} %get-tuple-element.110.s_ref, ...), custom_call_target="tpu_custom_call" | custom-call | flops 8589934592 | bytes 8388608 | tf_op jit(solution)/shard_map/attend/pallas_call | solution.py:266
  110.7 3.6 fusion.28
  114.3 0.0 copy-start.2
  114.3 0.6 collective-permute-done.1.refs_4_
  114.9 6.4 %collective-permute-start.3 = (bf16[256,2048]{1,0:T(8,128)(2,1)}, bf16[256,2048]{1,0:T(8,128)(2,1)}, u32[]{:S(2)}, u32[]{:S(2)}) collective-permute-start(bf16[256,2048]{1,0:T(8,128)(2,1)} %collective-permute-done.1.refs_4_), channel_id=1, source_target_pairs={{0,2},{1,3},{2,6},{3,7},{4,0},{5,1},{6,4},{7,5},{8,10},{9,11},{10,... | collective-permute-start | bytes 3145736 | tf_op jit(solution)/shard_map/ppermute | solution.py:44
  121.3 0.1 slice.103
  121.5 0.1 collective-permute-start
  121.6 2.3 slice.62.refs_12_
  123.9 0.5 collective-permute-start.2
  124.4 18.0 %collective-permute-done.3.refs_6_ = bf16[256,2048]{1,0:T(8,128)(2,1)} collective-permute-done((bf16[256,2048]{1,0:T(8,128)(2,1)}, bf16[256,2048]{1,0:T(8,128)(2,1)}, u32[]{:S(2)}, u32[]{:S(2)}) %collective-permute-start.3) | collective-permute-done | bytes 1048608 | tf_op jit(solution)/shard_map/ppermute | solution.py:44
  142.4 2.5 multiply_reduce_fusion.2
  144.9 1.2 multiply_convert_fusion.h_hbm
  146.2 1.0 copy-done.22
  147.1 0.3 copy-done.23
  147.5 147.4 %feed_forward.1 = (f32[256,2048]{1,0:T(8,128)}, bf16[4,256,2048]{2,1,0:T(8,128)(2,1)}, bf16[8,2112,256]{2,1,0:T(8,128)(2,1)}) custom-call(bf16[256,2048]{1,0:T(8,128)(2,1)} %multiply_convert_fusion.h_hbm, bf16[704,2048]{1,0:T(8,128)(2,1)} %bitcast.84, bf16[704,2048]{1,0:T(8,128)(2,1)} %bitcast.85, bf16[704,2048]{1,0:T(8,128)(2,1)} %wd_hbm.1, ...), custom_call_target="tpu_custom_call" | custom-call | flops 53150220288 | bytes 67108864 | tf_op jit(solution)/shard_map/feed_forward/pallas_call | solution.py:726
  294.9 2.9 multiply_reduce_fusion
  297.8 0.7 fusion.26
  298.5 1.2 collective-permute-start.9
  299.7 2.4 slice_bitcast_fusion
  302.1 0.2 collective-permute-start.10
  302.3 1.8 dynamic-slice_bitcast_fusion
  304.1 1.5 collective-permute-start.5
  305.6 0.5 collective-permute-start.6
  306.1 13.2 %collective-permute-start.7 = (bf16[2112,256]{1,0:T(8,128)(2,1)}, bf16[2112,256]{1,0:T(8,128)(2,1)}, u32[]{:S(2)}, u32[]{:S(2)}) collective-permute-start(bf16[2112,256]{1,0:T(8,128)(2,1)} %get-tuple-element.94), channel_id=1, source_target_pairs={{0,16},{8,24},{16,0},{24,8},{1,17},{9,25},{17,1},{25,9},{2,18},{10... | collective-permute-start | bytes 3244040 | tf_op jit(solution)/shard_map/ppermute | solution.py:50
  319.3 0.1 collective-permute-start.8
  319.3 3.4 convolution_convert_fusion.2.do_ref
  322.7 16.7 %attend_back.1 = (bf16[512,1024]{1,0:T(8,128)(2,1)}, f32[2048,128]{1,0:T(8,128)}, f32[2048,128]{1,0:T(8,128)}) custom-call(s32[3]{0:T(128)} %pad_add_fusion.sp_ref, bf16[512,1024]{1,0:T(8,128)(2,1)} %get-tuple-element.47.q_ref, bf16[512,1024]{1,0:T(8,128)(2,1)} %convolution_convert_fusion.2.do_ref, bf16[512,1024]{1,0:T(8,128)(2,1)} %get-tuple-element.39.ctx_ref, ...), custom_call_target="tpu_custom_call" | custom-call | flops 21474836480 | bytes 8388608 | tf_op jit(solution)/shard_map/attend_back/pallas_call | solution.py:292
  339.4 1.3 broadcast_multiply_fusion
  340.7 1.8 fusion.12
  342.5 5.5 collective-permute-start.11
  348.1 4.4 convolution_convert_fusion
  352.5 0.3 pad_maximum_fusion.1
  352.8 0.2 dynamic-slice_bitcast_fusion.8
  353.0 0.0 copy-start.28
  353.0 0.1 pad_maximum_fusion.2
  353.1 1.1 dynamic-slice_bitcast_fusion.4.refs_7_
  354.3 0.6 copy-done.14
  354.9 0.3 copy-done.21
  355.2 4.4 convolution_convert_fusion.1.refs_4_
  359.7 2.4 fusion.29
  362.0 0.9 fusion.16.refs_8_
  363.0 1.5 slice.74.refs_9_
  364.4 1.1 slice.102.refs_10_
  365.5 0.9 collective-permute-done.8
  366.4 5.1 fusion.2
  371.5 1.4 fusion.13.refs_6_
  372.9 200.1 %tail.1 = (bf16[2112,2048]{1,0:T(8,128)(2,1)}, bf16[256,2048]{1,0:T(8,128)(2,1)}, bf16[256,2048]{1,0:T(8,128)(2,1)}, bf16[256,2048]{1,0:T(8,128)(2,1)}, bf16[256...) custom-call(bf16[2112,256]{1,0:T(8,128)(2,1)} %get-tuple-element.92.refs_0_, ...), custom_call_target="tpu_custom_call" | custom-call | flops 1000000000 | bytes 67108864 | tf_op jit(solution)/shard_map/tail/pallas_call | solution.py:1104
  572.9 10.6 %slice_convert_fusion = (f32[704,2048]{1,0:T(8,128)}, f32[2048,704]{0,1:T(8,128)}, f32[2048,704]{0,1:T(8,128)}) fusion(bf16[2112,2048]{1,0:T(8,128)(2,1)} %get-tuple-element.61), kind=kLoop, calls=%fused_computation.7 | loop fusion | flops 4325376 | bytes 25952256 | tf_op jit(solution)/shard_map/convert_element_type | solution.py:1234
  583.5 1.6 convert_bitcast_fusion.3
  585.1 3.0 copy.29
  588.0 1.6 convert_bitcast_fusion.2
  589.6 3.0 copy.30
  592.6 2.2 fusion.6
  594.8 2.9 convert_element_type.175
  597.8 0.6 copy.35
  598.4 0.6 copy.36
  599.0 3.8 fusion.10
  (76 shorter events, 0.2 us)
Async XLA Ops:
  89.7 25.2 %collective-permute-start.1 = (bf16[256,2048]{1,0:T(8,128)(2,1)}, bf16[256,2048]{1,0:T(8,128)(2,1)}, u32[]{:S(2)}, u32[]{:S(2)}) collective-permute-start(bf16[256,2048]{1,0:T(8,128)(2,1)} %get-tuple-element.42.refs_2_), channel_id=1, source_target_pairs={{0,2},{1,3},{2,6},{3,7},{4,0},{5,1},{6,4},{7,5},{8,10},{9,11},{10,... | collective-permute-start | bytes 3145736 | tf_op jit(solution)/shard_map/ppermute | solution.py:44
  98.7 12.0 %copy-start.25 = (bf16[1024,2048]{1,0:T(8,128)(2,1)S(1)}, bf16[1024,2048]{1,0:T(8,128)(2,1)}, u32[]{:S(2)}) copy-start(bf16[1024,2048]{1,0:T(8,128)(2,1)} %get-tuple-element.40) | copy-start | bytes 12582916
  114.3 7.0 %copy-start.9 = (f32[512,2048]{1,0:T(8,128)}, f32[512,2048]{1,0:T(8,128)S(1)}, u32[]{:S(2)}) copy-start(f32[512,2048]{1,0:T(8,128)S(1)} %fusion.28) | copy-start | bytes 12582916
  114.3 28.1 %copy-start.2 = (bf16[256,2048]{1,0:T(8,128)(2,1)S(1)}, bf16[256,2048]{1,0:T(8,128)(2,1)}, u32[]{:S(2)}) copy-start(bf16[256,2048]{1,0:T(8,128)(2,1)} %refs_11_.1) | copy-start | bytes 3145732
  114.9 27.5 %collective-permute-start.3 = (bf16[256,2048]{1,0:T(8,128)(2,1)}, bf16[256,2048]{1,0:T(8,128)(2,1)}, u32[]{:S(2)}, u32[]{:S(2)}) collective-permute-start(bf16[256,2048]{1,0:T(8,128)(2,1)} %collective-permute-done.1.refs_4_), channel_id=1, source_target_pairs={{0,2},{1,3},{2,6},{3,7},{4,0},{5,1},{6,4},{7,5},{8,10},{9,11},{10,... | collective-permute-start | bytes 3145736 | tf_op jit(solution)/shard_map/ppermute | solution.py:44
  121.5 20.9 %collective-permute-start = (bf16[256,2048]{1,0:T(8,128)(2,1)S(1)}, bf16[256,2048]{1,0:T(8,128)(2,1)}, u32[]{:S(2)}, u32[]{:S(2)}) collective-permute-start(bf16[256,2048]{1,0:T(8,128)(2,1)S(1)} %slice.103), channel_id=1, source_target_pairs={{0,1},{1,0},{2,3},{3,2},{4,5},{5,4},{6,7},{7,6},{8,9},{9,8},{10,11... | collective-permute-start | bytes 3145736 | tf_op jit(solution)/shard_map/ppermute | solution.py:47
  123.9 21.0 %copy-start.17 = (f32[2048]{0:T(1024)S(1)}, f32[2048]{0:T(1024)}, u32[]{:S(2)}) copy-start(f32[2048]{0:T(1024)} %param.19) | copy-start | bytes 24580
  123.9 22.2 %collective-permute-start.2 = (bf16[256,2048]{1,0:T(8,128)(2,1)}, bf16[256,2048]{1,0:T(8,128)(2,1)S(1)}, u32[]{:S(2)}, u32[]{:S(2)}) collective-permute-start(bf16[256,2048]{1,0:T(8,128)(2,1)} %collective-permute-done.1.refs_4_), channel_id=1, source_target_pairs={{0,1},{1,0},{2,3},{3,2},{4,5},{5,4},{6,7},{7,6},{8,9},{9,8},{10,11... | collective-permute-start | bytes 3145736 | tf_op jit(solution)/shard_map/ppermute | solution.py:47
  142.3 3.8 collective-permute-start.4
  146.1 1.0 copy-start.22
  146.1 1.3 copy-start.23
  147.5 150.3 %copy-start.7 = (bf16[256,2048]{1,0:T(8,128)(2,1)S(1)}, bf16[256,2048]{1,0:T(8,128)(2,1)}, u32[]{:S(2)}) copy-start(bf16[256,2048]{1,0:T(8,128)(2,1)} %refs_0_.1) | copy-start | bytes 3145732
  294.9 2.9 copy-start
  294.9 7.4 %copy-start.4 = (bf16[8,2112,256]{2,1,0:T(8,128)(2,1)S(1)}, bf16[8,2112,256]{2,1,0:T(8,128)(2,1)}, u32[]{:S(2)}) copy-start(bf16[8,2112,256]{2,1,0:T(8,128)(2,1)} %get-tuple-element.45) | copy-start | bytes 25952260
  298.5 20.9 %copy-start.13 = (bf16[256,2048]{1,0:T(8,128)(2,1)}, bf16[256,2048]{1,0:T(8,128)(2,1)S(1)}, u32[]{:S(2)}) copy-start(bf16[256,2048]{1,0:T(8,128)(2,1)S(1)} %fusion.26) | copy-start | bytes 3145732
  298.5 20.8 %collective-permute-start.9 = (bf16[256,2048]{1,0:T(8,128)(2,1)S(1)}, bf16[256,2048]{1,0:T(8,128)(2,1)S(1)}, u32[]{:S(2)}, u32[]{:S(2)}) collective-permute-start(bf16[256,2048]{1,0:T(8,128)(2,1)S(1)} %fusion.26), channel_id=1, source_target_pairs={{0,1},{1,0},{2,3},{3,2},{4,5},{5,4},{6,7},{7,6},{8,9},{9,8},{10,11... | collective-permute-start | bytes 3145736 | tf_op jit(solution)/shard_map/ppermute | solution.py:47
  302.1 38.7 %collective-permute-start.10 = (bf16[256,2048]{1,0:T(8,128)(2,1)}, bf16[256,2048]{1,0:T(8,128)(2,1)}, u32[]{:S(2)}, u32[]{:S(2)}) collective-permute-start(bf16[256,2048]{1,0:T(8,128)(2,1)} %slice_bitcast_fusion), channel_id=1, source_target_pairs={{0,2},{1,3},{2,6},{3,7},{4,0},{5,1},{6,4},{7,5},{8,10},{9,11},{10,... | collective-permute-start | bytes 3145736 | tf_op jit(solution)/shard_map/ppermute | solution.py:44
  302.3 17.0 %copy-start.26 = (bf16[1024,2048]{1,0:T(8,128)(2,1)S(1)}, bf16[1024,2048]{1,0:T(8,128)(2,1)}, u32[]{:S(2)}) copy-start(bf16[1024,2048]{1,0:T(8,128)(2,1)} %get-tuple-element.40) | copy-start | bytes 12582916
  304.1 61.5 %collective-permute-start.5 = (bf16[2112,256]{1,0:T(8,128)(2,1)}, bf16[2112,256]{1,0:T(8,128)(2,1)}, u32[]{:S(2)}, u32[]{:S(2)}) collective-permute-start(bf16[2112,256]{1,0:T(8,128)(2,1)} %get-tuple-element.96), channel_id=1, source_target_pairs={{0,8},{8,0},{16,24},{24,16},{1,9},{9,1},{17,25},{25,17},{2,10},{10... | collective-permute-start | bytes 3244040 | tf_op jit(solution)/shard_map/ppermute | solution.py:50
  305.6 60.0 %collective-permute-start.6 = (bf16[2112,256]{1,0:T(8,128)(2,1)}, bf16[2112,256]{1,0:T(8,128)(2,1)}, u32[]{:S(2)}, u32[]{:S(2)}) collective-permute-start(bf16[2112,256]{1,0:T(8,128)(2,1)} %get-tuple-element.95), channel_id=1, source_target_pairs={{0,8},{8,0},{16,24},{24,16},{1,9},{9,1},{17,25},{25,17},{2,10},{10... | collective-permute-start | bytes 3244040 | tf_op jit(solution)/shard_map/ppermute | solution.py:50
  306.1 59.4 %collective-permute-start.7 = (bf16[2112,256]{1,0:T(8,128)(2,1)}, bf16[2112,256]{1,0:T(8,128)(2,1)}, u32[]{:S(2)}, u32[]{:S(2)}) collective-permute-start(bf16[2112,256]{1,0:T(8,128)(2,1)} %get-tuple-element.94), channel_id=1, source_target_pairs={{0,16},{8,24},{16,0},{24,8},{1,17},{9,25},{17,1},{25,9},{2,18},{10... | collective-permute-start | bytes 3244040 | tf_op jit(solution)/shard_map/ppermute | solution.py:50
  319.3 3.4 copy-start.20
  319.3 47.1 %collective-permute-start.8 = (bf16[2112,256]{1,0:T(8,128)(2,1)S(1)}, bf16[2112,256]{1,0:T(8,128)(2,1)}, u32[]{:S(2)}, u32[]{:S(2)}) collective-permute-start(bf16[2112,256]{1,0:T(8,128)(2,1)S(1)} %get-tuple-element.93), channel_id=1, source_target_pairs={{0,16},{8,24},{16,0},{24,8},{1,17},{9,25},{17,1},{25,9},{2,18},{10... | collective-permute-start | bytes 3244040 | tf_op jit(solution)/shard_map/ppermute | solution.py:50
  322.7 18.0 %copy-start.6 = (bf16[4,256,2048]{2,1,0:T(8,128)(2,1)S(1)}, bf16[4,256,2048]{2,1,0:T(8,128)(2,1)}, u32[]{:S(2)}) copy-start(bf16[4,256,2048]{2,1,0:T(8,128)(2,1)} %get-tuple-element.44) | copy-start | bytes 12582916
  340.7 7.4 %copy-start.16 = (bf16[512,2048]{1,0:T(8,128)(2,1)S(1)}, bf16[512,2048]{1,0:T(8,128)(2,1)}, u32[]{:S(2)}) copy-start(bf16[512,2048]{1,0:T(8,128)(2,1)} %get-tuple-element.36) | copy-start | bytes 6291460
  340.7 7.4 %copy-start.27 = (bf16[512,1024]{1,0:T(8,128)(2,1)S(1)}, bf16[512,1024]{1,0:T(8,128)(2,1)}, u32[]{:S(2)}) copy-start(bf16[512,1024]{1,0:T(8,128)(2,1)} %get-tuple-element.52) | copy-start | bytes 3145732
  342.5 29.0 %collective-permute-start.11 = (bf16[256,2048]{1,0:T(8,128)(2,1)S(1)}, bf16[256,2048]{1,0:T(8,128)(2,1)S(1)}, u32[]{:S(2)}, u32[]{:S(2)}) collective-permute-start(bf16[256,2048]{1,0:T(8,128)(2,1)S(1)} %fusion.12), channel_id=1, source_target_pairs={{0,2},{1,3},{2,6},{3,7},{4,0},{5,1},{6,4},{7,5},{8,10},{9,11},{10,... | collective-permute-start | bytes 3145736 | tf_op jit(solution)/shard_map/ppermute | solution.py:44
  348.1 4.4 copy-start.15
  353.0 1.3 copy-start.28
  353.1 1.8 copy-start.14
  353.1 2.1 copy-start.21
  353.1 6.5 %copy-start.24 = (bf16[2048,1024]{1,0:T(8,128)(2,1)S(1)}, bf16[2048,1024]{1,0:T(8,128)(2,1)}, u32[]{:S(2)}) copy-start(bf16[2048,1024]{1,0:T(8,128)(2,1)} %get-tuple-element.37) | copy-start | bytes 12582916
  355.2 11.2 %slice-start = ((s8[8650752]{0:T(1024)(128)(4,1)}), s8[4194304]{0:T(1024)(128)(4,1)S(1)}, s32[]{:S(2)}) async-start(s8[8650752]{0:T(1024)(128)(4,1)} %bitcast.76), calls=%async_computation | async-start | bytes 8388608
  355.2 11.2 %slice-start.1 = ((s8[8650752]{0:T(1024)(128)(4,1)}), s8[4194304]{0:T(1024)(128)(4,1)S(1)}, s32[]{:S(2)}) async-start(s8[8650752]{0:T(1024)(128)(4,1)} %bitcast.76), calls=%async_computation.1 | async-start | bytes 8388608
  359.7 6.7 %slice-start.2 = ((s8[8650752]{0:T(1024)(128)(4,1)}), s8[262144]{0:T(1024)(128)(4,1)S(1)}, s32[]{:S(2)}) async-start(s8[8650752]{0:T(1024)(128)(4,1)} %bitcast.76), calls=%async_computation.2 | async-start | bytes 524288
  572.9 10.6 %copy-start.12 = (bf16[256,2048]{1,0:T(8,128)(2,1)S(1)}, bf16[256,2048]{1,0:T(8,128)(2,1)}, u32[]{:S(2)}) copy-start(bf16[256,2048]{1,0:T(8,128)(2,1)} %get-tuple-element.58) | copy-start | bytes 3145732
  585.1 3.0 copy-start.11
  589.6 3.0 copy-start.3
  589.6 3.0 copy-start.18
  592.6 5.2 copy-start.19
  592.6 6.4 %copy-start.5 = (f32[256,2048]{1,0:T(8,128)S(1)}, f32[256,2048]{1,0:T(8,128)}, u32[]{:S(2)}) copy-start(f32[256,2048]{1,0:T(8,128)} %get-tuple-element.56) | copy-start | bytes 6291460
  592.6 6.4 %copy-start.10 = (bf16[256,2048]{1,0:T(8,128)(2,1)S(1)}, bf16[256,2048]{1,0:T(8,128)(2,1)}, u32[]{:S(2)}) copy-start(bf16[256,2048]{1,0:T(8,128)(2,1)} %get-tuple-element.55) | copy-start | bytes 3145732
  594.8 4.2 copy-start.1
  594.8 4.2 copy-start.8

commit v5 on v4

--- a/solution.py
+++ b/solution.py
@@ -49,9 +49,6 @@
     def across(self, x, bit):
         return lax.ppermute(x, "dp", [(i, i ^ bit) for i in range(self.n_dp)])
 
-    def across_tensor(self, x, bit):
-        return lax.ppermute(x, "tensor", [(i, i ^ bit) for i in range(self.n_tensor)])
-
     def neighbours(self, chip):
         ahead, behind = chip * 0, chip * 0
         for i, c in enumerate(self.order):
@@ -59,94 +56,6 @@
             behind = jnp.where(chip == c, self.order[i - 1], behind)
         return ahead, behind
 
-    def orders(self, rows, unit):
-        ways = len(self.bits)
-        if ways < 2 or rows % (ways * unit):
-            return [self.bits]
-        return [self.bits[i:] + self.bits[:i] for i in range(ways)]
-
-
-def take_rows(x, index, size):
-    return lax.dynamic_slice_in_dim(x, index * size, size, 0)
-
-
-def gather_dp(links, piece, me):
-    orders = links.orders(piece.shape[0], 8)
-    part_rows = piece.shape[0] // len(orders)
-    parts = []
-    for number, bits in enumerate(orders):
-        stack = lax.slice_in_dim(piece, number * part_rows, (number + 1) * part_rows, axis=0)
-        held = [0]
-        for bit in bits:
-            stack = jnp.concatenate([stack, links.across(stack, bit)], axis=0)
-            held = held + [h ^ bit for h in held]
-        where = jnp.array([held.index(rel) for rel in range(links.n_dp)], jnp.int32)
-        parts.append((stack, where))
-    out = []
-    for j in range(links.n_dp):
-        for stack, where in parts:
-            out.append(take_rows(stack, where[me ^ j], part_rows))
-    return jnp.concatenate(out, axis=0)
-
-
-def gather_weight(links, block, me):
-    rows = block.shape[0] // links.n_dp
-    blocks = [block]
-    piece = take_rows(block, me, rows)
-    for _ in range(links.chips - 1):
-        piece = links.ring(piece)
-        blocks.append(gather_dp(links, piece, me))
-    return blocks
-
-
-def sum_dp(links, x, me):
-    orders = links.orders(x.shape[0], 8 * links.n_dp)
-    part_rows = x.shape[0] // len(orders)
-    size = part_rows // links.n_dp
-    outs = []
-    for number, bits in enumerate(orders):
-        held = lax.slice_in_dim(x, number * part_rows, (number + 1) * part_rows, axis=0)
-        pieces = [held.reshape((links.n_dp, size) + x.shape[1:])]
-        array = pieces[0]
-        axes = [links.n_dp]
-        nbits = len(links.bits)
-        array = array.reshape((2,) * nbits + (size,) + x.shape[1:])
-        left = list(reversed(links.bits))
-        for bit in bits:
-            axis = left.index(bit)
-            mine = jnp.minimum(me & bit, 1)
-            keep = lax.dynamic_index_in_dim(array, mine, axis, keepdims=False)
-            send = lax.dynamic_index_in_dim(array, 1 - mine, axis, keepdims=False)
-            got = links.across(send, bit)
-            array = (keep.astype(F32) + got.astype(F32)).astype(BF16)
-            left.remove(bit)
-        stack = array.reshape((size,) + x.shape[1:])
-        rel = [0]
-        for bit in reversed(bits):
-            stack = jnp.concatenate([stack, links.across(stack, bit)], axis=0)
-            rel = rel + [r ^ bit for r in rel]
-        where = jnp.array([rel.index(r) for r in range(links.n_dp)], jnp.int32)
-        for j in range(links.n_dp):
-            outs.append(take_rows(stack, where[me ^ j], size))
-    return jnp.concatenate(outs, axis=0).astype(F32)
-
-
-def ring_gather(links, own):
-    out = [own]
-    for _ in range(links.chips - 1):
-        out.append(links.ring(out[-1]))
-    return out
-
-
-def ring_scatter(links, terms):
-    got = None
-    for term in terms[1:] + terms[:1]:
-        total = term if got is None else term.astype(F32) + got.astype(F32)
-        if term is terms[0]:
-            return total.astype(F32)
-        got = links.ring(total.astype(BF16))
-    return got
-
 
 def both(links, own):
     return jnp.concatenate([own, links.swap(own)], axis=0)
@@ -155,16 +64,6 @@
 def pair_sum(links, part):
     rows = part.shape[0] // 2
     return part[:rows].astype(F32) + links.swap(part[rows:].astype(BF16)).astype(F32)
-
-
-def sum_all(links, x):
-    bit = 1
-    while bit < links.n_tensor:
-        x = x + links.across_tensor(x, bit)
-        bit *= 2
-    for bit in links.bits:
-        x = x + links.across(x, bit)
-    return x
 
 
 def diagonal(shape, row_axis, shift):
@@ -180,7 +79,8 @@
     return inner + 1, pl.multiple_of((block - inner) * rows, rows)
 
 
-def fwd_kernel(blocks, sp_ref, q_ref, c_ref, s_ref, k_ref, v_ref, qo_ref, ctx_ref, lse_ref):
+def fwd_kernel(blocks, sp_ref, q_ref, c_ref, s_ref, k_ref, v_ref, *refs):
+    qo_ref, ctx_ref, lse_ref = refs[-3:]
     rows = q_ref.shape[0]
     chip, two_docs, core = sp_ref[0], sp_ref[1], sp_ref[2]
     x = q_ref[...]
@@ -194,11 +94,11 @@
         def _(n=n):
             near = (n - 1) * rows
             diag = pl.ds(low + near, rows)
-            s_diag = jnp.where(mask, mm(q, k_ref[diag, :], NT) * SCALE2, MASKED)
+            s_diag = jnp.where(mask, mm(q, k_ref[diag, :], NT), MASKED)
             top = jnp.max(s_diag, axis=1, keepdims=True)
             if n > 1:
                 main = pl.ds(low, near)
-                s_main = mm(q, k_ref[main, :], NT) * SCALE2
+                s_main = mm(q, k_ref[main, :], NT)
                 top = jnp.maximum(top, jnp.max(s_main, axis=1, keepdims=True))
             p_diag = jnp.exp2(s_diag - top)
             total = jnp.sum(p_diag, axis=1, keepdims=True)
@@ -239,14 +139,14 @@
             for keys, masked in ((pl.ds(low, near), False), (pl.ds(low + near, rows), True)):
                 if not masked and n == 1:
                     continue
-                p = jnp.exp2(mm(k_ref[keys, :], q, NT) * SCALE2 - lse)
+                p = jnp.exp2(mm(k_ref[keys, :], q, NT) - lse)
                 if masked:
                     p = jnp.where(mask, p, 0.0)
                 ds = (p * (mm(v_ref[keys, :], do, NT) - dot)).astype(BF16)
                 dv_ref[keys, :] += mm(p.astype(BF16), do, NN)
                 dk_ref[keys, :] += mm(ds, q, NN)
                 dqt = dqt + mm(kt_ref[:, keys], ds, NN)
-            g = dqt.T * SCALE
+            g = dqt.T
             dq_ref[...] = (g * c_ref[...] - pltpu.roll(g, HD // 2, 1) * s_ref[...]).astype(BF16)
 
 
@@ -258,30 +158,32 @@
     return pl.BlockSpec((seq, HD), lambda *_: (0, 1))
 
 
-def attend(sp, q_lin, cosine, sine, kv_all):
+def attend(sp, q_lin, cosine, sine, kv_all, first, count, before=()):
     rows, width = q_lin.shape
     seq = kv_all.shape[0]
     heads = width // HD
-    column = pl.BlockSpec((rows, HD), lambda h, *_: (0, h))
+    column = pl.BlockSpec((rows, HD), lambda h, *_: (0, h + first))
     return pl.pallas_call(
         functools.partial(fwd_kernel, seq // rows),
         grid_spec=pltpu.PrefetchScalarGridSpec(
             num_scalar_prefetch=1,
-            grid=(heads,),
-            in_specs=[column, whole((rows, HD)), whole((rows, HD)), whole((seq, HD)), second_half(seq)],
-            out_specs=[column, column, pl.BlockSpec((1, 8, rows), lambda h, *_: (h, 0, 0))],
+            grid=(count,),
+            in_specs=[column, whole((rows, HD)), whole((rows, HD)), whole((seq, HD)), second_half(seq)]
+            + [pl.BlockSpec(memory_space=pl.ANY)] * len(before),
+            out_specs=[column, column, pl.BlockSpec((1, 8, rows), lambda h, *_: (h + first, 0, 0))],
         ),
         out_shape=[
             jax.ShapeDtypeStruct((rows, width), BF16),
             jax.ShapeDtypeStruct((rows, width), BF16),
             jax.ShapeDtypeStruct((heads, 8, rows), F32),
         ],
+        input_output_aliases={6 + i: i for i in range(len(before))},
         compiler_params=pltpu.CompilerParams(vmem_limit_bytes=VMEM_LIMIT),
         cost_estimate=pl.CostEstimate(
-            flops=8 * heads * rows * seq * HD, bytes_accessed=16 * rows * width, transcendentals=heads * rows * seq
+            flops=8 * count * rows * seq * HD, bytes_accessed=16 * rows * width, transcendentals=count * rows * seq
         ),
         name="attend",
-    )(sp, q_lin, cosine, sine, kv_all, kv_all)
+    )(sp, q_lin, cosine, sine, kv_all, kv_all, *before)
 
 
 def attend_back(sp, queries, grad_context, context, lse, cosine, sine, kv_all, key_rows_t, dk0, dv0):
@@ -471,6 +373,7 @@
                 at = (pl.ds(block * rows, rows), pl.ds(head * HD, HD))
                 second_unit(block, rows, q_two[at], g_two[at], kv, dk_ref, dv_ref, late)
                 yield
+        dk_ref[...] *= SCALE2
 
     chains = {"kv": kv_chain(), "s": second_chain(), "g": grad_chain()}
     for k in range(1, chips):
@@ -530,11 +433,13 @@
 def mlp_kernel(
     links, h_hbm, wg_hbm, wu_hbm, wd_hbm, *refs,
 ):
-    g_hbm, refs = refs[: links.n_tensor], refs[links.n_tensor :]
+    paired = 1 + min(FRONT_HOPS, links.chips - 1)
+    given = [(k, half) for k in range(links.chips) for half in ((0, 1) if k < paired else (0,))]
+    g_hbm, refs = refs[: len(given)], refs[len(given) :]
     (
     ghn_ref, mlp_hbm, grads_hbm, h_all, g_all, wg, wu, wd, act_t, gg_t, gu_t, mlp_in, stage, pair_out, pair_in, ring_out, ring_in,
     load_sem, ring_s, ring_r, swap_s, swap_r, pair_s, pair_r, rs_s, rs_r, mlp_s, mlp_r,
-    stage_sem, store_sem,
+    stage_sem, store_sem, g_s, g_r,
     ) = refs
     chips = links.chips
     own, depth = h_hbm.shape
@@ -552,7 +457,7 @@
         pltpu.make_async_copy(wu_hbm, wu, load_sem.at[2]),
         pltpu.make_async_copy(wd_hbm, wd, load_sem.at[3]),
     ] + [
-        pltpu.make_async_copy(ref, g_all.at[i // 2, i % 2], load_sem.at[4 + i]) for i, ref in enumerate(g_hbm)
+        pltpu.make_async_copy(ref, g_all.at[at], load_sem.at[4 + i]) for i, (ref, at) in enumerate(zip(g_hbm, given))
     ]
     for load in loads:
         load.start()
@@ -573,6 +478,9 @@
     def swap(k):
         return remote(h_all.at[k, 0], h_all.at[k, 1], swap_s.at[k], swap_r.at[k], sibling)
 
+    def g_swap(k):
+        return remote(g_all.at[k, 0], g_all.at[k, 1], g_s.at[k], g_r.at[k], sibling)
+
     def pair(k):
         slot = lax.rem(k, 2)
         return remote(pair_out.at[slot], pair_in.at[slot], pair_s.at[slot], pair_r.at[slot], sibling)
@@ -593,6 +501,8 @@
     swap(0).start()
     for load in loads[1:]:
         load.wait()
+    for k in range(paired, chips):
+        g_swap(k).start()
 
     def hidden_units(k, half):
         h, g = h_all[k, half], g_all[k, half]
@@ -625,6 +535,11 @@
 
         act0, gg0, gu0 = hidden_units(k, 0)
         swap(k).wait_recv()
+
+        @pl.when(k >= paired)
+        def _():
+            g_swap(k).wait_recv()
+
         act1, gg1, gu1 = hidden_units(k, 1)
 
         @pl.when(k >= 2)
@@ -712,6 +627,8 @@
         scatter(k).wait_send()
     for k in range(chips):
         swap(k).wait_send()
+    for k in range(paired, chips):
+        g_swap(k).wait_send()
     for k in range(chips - 1):
         ring(k).wait_send()
 
@@ -725,7 +642,7 @@
     dma = pltpu.SemaphoreType.DMA
     return pl.pallas_call(
         functools.partial(mlp_kernel, links),
-        in_specs=[anywhere] * (4 + links.n_tensor),
+        in_specs=[anywhere] * (4 + len(grad_chunks)),
         out_specs=[pl.BlockSpec(memory_space=pltpu.VMEM)] + [anywhere] * 2,
         out_shape=[
             jax.ShapeDtypeStruct((own, depth), F32),
@@ -747,9 +664,9 @@
             pltpu.VMEM((2, own, depth), BF16),
             pltpu.VMEM((2, own, depth), BF16),
             pltpu.VMEM((chips, own, depth), BF16),
-            dma((4 + links.n_tensor,)),
+            dma((4 + len(grad_chunks),)),
             dma((chips,)), dma((chips,)), dma((chips,)), dma((chips,)), dma((2,)), dma((2,)),
-            dma((chips,)), dma((chips,)), dma((2,)), dma((2,)), dma((1,)), dma((3, pieces)),
+            dma((chips,)), dma((chips,)), dma((2,)), dma((2,)), dma((1,)), dma((3, pieces)), dma((chips,)), dma((chips,)),
         ],
         compiler_params=pltpu.CompilerParams(
             collective_id=1, has_side_effects=True, vmem_limit_bytes=60 * 2**20
@@ -862,15 +779,15 @@
 
 def first_halving(links, parts, me):
     n = links.n_dp
-    out, names = [], []
+    stay, came, names = [], [], []
     for way, bits in enumerate((links.bits, links.bits[::-1])):
         for rel in range(n):
             if rel & bits[0] == 0:
-                mine = lax.dynamic_index_in_dim(parts, way * n + (me ^ rel), 0, keepdims=False)
+                stay.append(lax.dynamic_index_in_dim(parts, way * n + (me ^ rel), 0, keepdims=False))
                 other = lax.dynamic_index_in_dim(parts, way * n + (me ^ rel ^ bits[0]), 0, keepdims=False)
-                out.append((mine.astype(F32) + links.across(other, bits[0]).astype(F32)).astype(BF16))
+                came.append(links.across(other, bits[0]))
                 names.append((way, rel))
-    return out, names
+    return stay, came, names
 
 
 def tail_kernel(
@@ -879,8 +796,9 @@
     w_hbm, refs = refs[: len(names)], refs[len(names) :]
     (
         o_hbm, q_hbm, m_hbm, kv_keep, kv_send, gn_keep, gn_send, tokens, normed, w_kv, cosine, sine, gain_part,
-        ws_hbm, ow_hbm, qw_hbm, kvw_hbm, got_hbm, gn_ref, gains_ref,
-        o_buf, o_in, o_ring, q_buf, q_in, w_buf, w_in, c_buf, c_in, b_buf, b_in,
+        gain, grad_hidden, hidden,
+        ws_hbm, ow_hbm, qw_hbm, kvw_hbm, block_ref, grad_ref, gains_ref,
+        o_buf, o_in, o_ring, q_buf, q_in, w_buf, w_in, c_buf, c_in, b_buf, b_in, b_turned, got,
         kv_got, kv_ring, kv_in, gn_got, kvw_half, kvw_got, kvw_in, kvw_all, gains_in,
         ss, rs, o_sem, q_sem, w_sem, out_sem, w_free, o_free, b_free,
     ) = refs
@@ -969,10 +887,13 @@
         yield
         gn_swap.wait_recv()
         grad = gn_keep[...] + gn_got[...].astype(F32) + mm(kv_lin, w_kv[...], NT)
-        gn_ref[...] = grad
         x = tokens[...].astype(F32)
         factor = lax.rsqrt(jnp.mean(x * x, axis=1, keepdims=True) + EPSILON)
-        part = jnp.sum(grad * (x * factor), axis=0, keepdims=True)
+        x = x * factor
+        part = jnp.sum(grad * x, axis=0, keepdims=True)
+        scaled = grad * gain[...]
+        back = scaled - x * jnp.mean(scaled * x, axis=1, keepdims=True)
+        grad_ref[...] = (grad_hidden[...] + factor * back).astype(BF16)
         lanes = gains_ref.shape[1]
         gains_ref[...] = jnp.concatenate(
             [v[:, i * lanes : (i + 1) * lanes] for v in (part, gain_part[...]) for i in range(4)], axis=0
@@ -1062,12 +983,19 @@
     def b_chain():
         for j in range(2 * n_dp):
             b_buf[j] = q_buf[0, :, pl.ds(j * piece, piece)]
-        yield from sum_b.chain(lambda way, rel: put(b_buf.at[sum_b.at(way, rel)], columns(qw_hbm, sum_b.at(way, rel))))
+
+        def turn_over(way, rel):
+            at = sum_b.at(way, rel)
+            b_turned[at] = b_buf[at].T
+            put(b_turned.at[at], qw_hbm.at[pl.ds(pl.multiple_of(at * piece, piece), piece)])
+
+        yield from sum_b.chain(turn_over)
 
     def m_chain():
-        copy = send(m_hbm, got_hbm, right)
+        copy = send(m_hbm, got, right)
         yield
         copy.wait_recv()
+        block_ref[...] = (hidden[...] + got[...].astype(F32)).astype(BF16)
 
     chains = {
         "w": w_chain(), "o": o_chain(), "q": ring_chain("q", q_buf, q_in), "kv": kv_chain(),
@@ -1082,13 +1010,13 @@
 
 
 TAIL_ORDER = (
-    "o w kv q", "kv* kvw g kvw*", "c g* o c", "w q o c*", "o q w o", "q* b o m", "b o* b* m*", "w*",
+    "o kv w kv", "kvw kv g kvw", "q c g* o", "c w o o", "c* o q w", "q* m b b", "o o b o*", "b* w* m*",
 )
 
 
 def tail(
     links, o_parts, q_parts, m_part, w_pieces, names, kv_keep, kv_send, gn_keep, gn_send, tokens, normed, w_kv, cosine,
-    sine, gain_part,
+    sine, gain_part, gain, grad_hidden, hidden,
 ):
     chips, width, depth = q_parts.shape
     own = tokens.shape[0]
@@ -1103,12 +1031,12 @@
     count = 20 * chips + 20 * n + 16
     return pl.pallas_call(
         functools.partial(tail_kernel, links, names),
-        in_specs=[anywhere] * (3 + len(names)) + [here] * 10,
-        out_specs=[anywhere] * 5 + [here] * 2,
+        in_specs=[anywhere] * (3 + len(names)) + [here] * 13,
+        out_specs=[anywhere] * 4 + [here] * 3,
         out_shape=[
             shape((rows, depth), BF16), shape((width, depth), BF16),
-            shape((width, depth), BF16), shape((2 * HD, depth), BF16), shape((own, depth), BF16),
-            shape((own, depth), F32), shape((8, depth // 4), F32),
+            shape((depth, width), BF16), shape((2 * HD, depth), BF16), shape((own, depth), BF16),
+            shape((own, depth), BF16), shape((8, depth // 4), F32),
         ],
         scratch_shapes=[
             pltpu.VMEM((pieces, chips * width, piece), BF16), pltpu.VMEM((2, n - 1, chips * width, piece), BF16),
@@ -1117,6 +1045,7 @@
             pltpu.VMEM((pieces, rows, piece), BF16), pltpu.VMEM((2, max(1, n // 2 - 1), rows, piece), BF16),
             pltpu.VMEM((band, depth), BF16), pltpu.VMEM((n - 1, band, depth), BF16),
             pltpu.VMEM((pieces, width, piece), BF16), pltpu.VMEM((2, n - 1, width, piece), BF16),
+            pltpu.VMEM((pieces, piece, width), BF16), pltpu.VMEM((own, depth), BF16),
             pltpu.VMEM((chips, own, 2 * HD), BF16),
             pltpu.VMEM((chips - 1, own, 2 * HD), BF16), pltpu.VMEM((chips - 1, own, 2 * HD), BF16),
             pltpu.VMEM((own, depth), BF16),
@@ -1135,7 +1064,7 @@
         name="tail",
     )(
         *w_pieces, o_parts, q_parts, m_part, kv_keep, kv_send, gn_keep, gn_send, tokens, normed, w_kv, cosine, sine,
-        gain_part,
+        gain_part, gain, grad_hidden, hidden,
     )
 
 
@@ -1171,8 +1100,6 @@
     sine = jnp.concatenate([-sin, sin], axis=1)
 
     residual = tokens.astype(F32)
-    attn_scale = rms_factor(residual)
-    attn_pre = residual * attn_scale
 
     normed, wq, wo, kv_all, key_rows_t, dk2, dv2, *grad_chunks = front(
         links, doc_split, tokens, attn_gain[None], w_kv, cosine[:own], sine[:own], query_two, grad_two, w_query, w_out,
@@ -1180,23 +1107,26 @@
     )
     normed_own = normed[:own]
     grad_chunks = [out_grad] + grad_chunks
-    while len(grad_chunks) < n_tensor:
-        further = links.ring(grad_chunks[-2])
-        grad_chunks += [further, links.swap(further)]
 
     q_lin = mm(normed, wq, NN)
-    queries, context, lse = attend(sp, q_lin, cosine, sine, kv_all)
-    branch = pair_sum(links, mm(context, wo, NN))
+    some = q_lin.shape[1] // HD // 2
+    tables = (cosine * SCALE2, sine * SCALE2)
+    results = attend(sp, q_lin, *tables, kv_all, 0, some)
+    results, further = lax.optimization_barrier((results, links.ring(grad_chunks[-2])))
+    later_chunks = [further]
+    for _ in range(3 + FRONT_HOPS, chips + 1):
+        later_chunks.append(links.ring(later_chunks[-1]))
+    queries, context, lse = attend(sp, q_lin, *tables, kv_all, some, q_lin.shape[1] // HD - some, results)
+    branch, later_chunks = lax.optimization_barrier((mm(context, wo, NN), later_chunks))
+    branch = pair_sum(links, branch)
     hidden = residual + branch
     mlp_scale = rms_factor(hidden)
     mlp_pre = hidden * mlp_scale
     hidden_own = (mlp_pre * mlp_gain).astype(BF16)
 
-    grad_hn, mlp_terms, ffn_parts = feed_forward(links, hidden_own, grad_chunks, w_gate.T, w_up.T, w_down)
-    ffn_pieces, ffn_names = first_halving(links, ffn_parts, me_dp)
-    mlp_sent = mlp_terms[1]
-    for k in range(2, chips):
-        mlp_sent = (mlp_terms[k].astype(F32) + links.ring(mlp_sent).astype(F32)).astype(BF16)
+    grad_hn, mlp_terms, ffn_parts = feed_forward(links, hidden_own, grad_chunks + later_chunks, w_gate.T, w_up.T, w_down)
+    mlp_came = links.ring(mlp_terms[1])
+    ffn_stay, ffn_came, ffn_names = first_halving(links, ffn_parts, me_dp)
 
     mlp_gain_part = jnp.sum(grad_hn * mlp_pre, axis=0)
     scaled_mlp = grad_hn * mlp_gain
@@ -1207,12 +1137,17 @@
     grad_branch = both(links, grad_hidden.astype(BF16))
     grad_context = mm(grad_branch, wo, NT).astype(BF16)
     query_grad, dk, dv = attend_back(
-        sp, queries, grad_context, context, lse, cosine, sine, kv_all, key_rows_t, dk2, dv2
+        sp, queries, grad_context, context, lse, cosine * SCALE, sine * SCALE, kv_all, key_rows_t, dk2, dv2
     )
+    for k in range(2, chips - 1):
+        query_grad, mlp_came = lax.optimization_barrier((query_grad, mlp_came))
+        mlp_sent = (mlp_terms[k].astype(F32) + mlp_came.astype(F32)).astype(BF16)
+        query_grad, mlp_sent = lax.optimization_barrier((query_grad, mlp_sent))
+        mlp_came = links.ring(mlp_sent)
     out_parts = mm(context, grad_branch, TN).astype(BF16)
     query_parts = mm(query_grad, normed, TN).astype(BF16).reshape(chips, width, -1)
 
-    kv_part = jnp.concatenate([dk * SCALE, dv], axis=1).reshape(chips, 2, own, 2 * HD)
+    kv_part = jnp.concatenate([dk * (SCALE / SCALE2), dv], axis=1).reshape(chips, 2, own, 2 * HD)
     kv_part = jnp.stack(
         [
             lax.dynamic_index_in_dim(kv_part, chip ^ k, 0, keepdims=False)
@@ -1222,10 +1157,14 @@
     kv_keep = lax.dynamic_index_in_dim(kv_part, core, 1, keepdims=False)
     kv_send = lax.dynamic_index_in_dim(kv_part, 1 - core, 1, keepdims=False).astype(BF16)
     gn_part = mm(query_grad, wq, NT)
+    query_parts, ffn_came, mlp_came = lax.optimization_barrier((query_parts, ffn_came, mlp_came))
+    mlp_sent = (mlp_terms[chips - 1].astype(F32) + mlp_came.astype(F32)).astype(BF16)
+    ffn_pieces = [(a.astype(F32) + b.astype(F32)).astype(BF16) for a, b in zip(ffn_stay, ffn_came)]
     gain_part = mlp_gain_part[None]
-    ffn_w, out_w, query_w, kv_w, mlp_got, grad_normed, gains = tail(
+    ffn_w, out_w, query_w, kv_w, block_output, tokens_grad, gains = tail(
         links, out_parts, query_parts, mlp_sent, ffn_pieces, ffn_names, kv_keep, kv_send, gn_part[:own],
         gn_part[own:].astype(BF16), tokens, normed_own, w_kv, cosine[:own], sine[:own], gain_part,
+        attn_gain[None], grad_hidden, hidden + mlp_terms[0].astype(F32),
     )
     units = w_down.shape[0]
 
@@ -1233,15 +1172,10 @@
     up_w_grad = ffn_w[units : 2 * units].astype(F32).T
     down_w_grad = ffn_w[2 * units :].astype(F32)
     out_w_grad = out_w.astype(F32)
-    query_w_grad = query_w.astype(F32).T
+    query_w_grad = query_w.astype(F32)
     kv_w_grad = kv_w.astype(F32).T
     attn_gain_grad, mlp_gain_grad = gains[:4].reshape(-1), gains[4:].reshape(-1)
-    block_output = (hidden + (mlp_terms[0].astype(F32) + mlp_got.astype(F32))).astype(BF16)
-    scaled_attn = grad_normed * attn_gain
-    tokens_grad = (
-        grad_hidden
-        + attn_scale * (scaled_attn - attn_pre * jnp.mean(scaled_attn * attn_pre, axis=-1, keepdims=True))
-    ).astype(BF16)
+
     return (
         block_output,
         tokens_grad,

time: 612 us -> 599 us (0.979)
  starting transfers between devices: 30 us -> 14.9 us
  waiting for transfers between devices: 19.4 us -> 34.1 us
  Pallas kernels: 463 us -> 451 us
  other arithmetic: 43.4 us -> 35.1 us
    ppermute x4, waiting for transfers between devices: 18.6 us -> 31.5 us  [ring(): return lax.ppermute(x, 'tensor', self.ring_pairs)]
    ppermute x4, starting transfers between devices: 15.3 us -> 4.06 us  [across(): return lax.ppermute(x, 'dp', [(i, i ^ bit) for i in range(self.n_dp)])]
    pallas_call x1, Pallas kernels: 200 us -> 190 us  [tail(): pl.pallas_call(functools.partial(tail_kernel, links, names), in_specs=[an...]
    pallas_call x1 -> x2, Pallas kernels: 12 us -> 14.8 us  [attend(): pl.pallas_call(functools.partial(fwd_kernel, seq // rows), grid_spec=pltp...]
  transfers between devices with their start and end apart: 12 -> 10, of which waited for: 3 -> 4; matrix products, arithmetic and copies ran while one was open for 8% -> 8% of each run, Pallas kernels for 5% -> 5%
where the time goes in v5:
time: 599 us; the launch traced here: 589 us
  Pallas kernels  451 us (75%)
  other arithmetic  35.1 us (6%)
  waiting for transfers between devices  34.1 us (6%)
  matrix products  30.2 us (5%)
  local copies, waits for them, and re-layouts  21.3 us (4%)
  starting transfers between devices  14.9 us (2%)
    pallas_call x1, Pallas kernels, tail(): pl.pallas_call(functools.partial(tail_kernel, links, names), in_specs=[an...  190 us
    pallas_call x1, Pallas kernels, feed_forward(): pl.pallas_call(functools.partial(mlp_kernel, links), in_specs=[anywhere]...  144 us
    pallas_call x1, Pallas kernels, front(): pl.pallas_call(functools.partial(front_kernel, links), in_specs=[pl.Block...  86.5 us
    ppermute x4, waiting for transfers between devices, ring(): return lax.ppermute(x, 'tensor', self.ring_pairs)  31.5 us
    dot_general x6, matrix products, mm(): lax.dot_general(left, right, (dims, ((), ())), preferred_element_type=F32)  30.2 us
    pallas_call x1, Pallas kernels, attend_back(): pl.pallas_call(functools.partial(bwd_kernel, seq // rows), grid_spec=pltp...  16.2 us
    pallas_call x2, Pallas kernels, attend(): pl.pallas_call(functools.partial(fwd_kernel, seq // rows), grid_spec=pltp...  14.8 us
  transfers between devices with their start and end apart: 10, of which 4 were waited for; matrix products, arithmetic and copies ran while one was open for 8% of the time, Pallas kernels for 5%

profile of v5, /device:TPU:0, one launch (start us, length us, event | category | flops | bytes accessed | tf_op | source)
XLA Modules:
  0.0 588.8 jit_solution(8441056051227968208)
XLA Ops:
  1.4 1.0 multiply_sine_fusion
  2.4 0.8 fusion.9
  3.2 86.5 %front.1 = (bf16[512,2048]{1,0:T(8,128)(2,1)}, bf16[2048,1024]{1,0:T(8,128)(2,1)}, bf16[1024,2048]{1,0:T(8,128)(2,1)}, bf16[2048,256]{1,0:T(8,128)(2,1)}, bf16[1...) custom-call(s32[1]{0:T(128)S(6)} %copy.43.docs, ...), custom_call_target="tpu_custom_call" | custom-call | flops 10000000000 | bytes 67108864 | tf_op jit(solution)/shard_map/front/pallas_call | solution.py:415
  89.7 0.9 collective-permute-start
  90.6 1.2 fusion.8
  91.8 0.6 pad_add_fusion.sp_ref
  92.3 6.5 %fusion.19.q_ref = f32[512,1024]{1,0:T(8,128)} fusion(bf16[512,2048]{1,0:T(8,128)(2,1)} %get-tuple-element.56, bf16[2048,1024]{1,0:T(8,128)(2,1)} %get-tuple-element.57), kind=kOutput, calls=%fused_computation.76 | convolution fusion | flops 2147483648 | bytes 8388608 | tf_op jit(solution)/shard_map/dot_general | solution.py:22
  98.8 7.0 %attend.2 = (bf16[512,1024]{1,0:T(8,128)(2,1)}, bf16[512,1024]{1,0:T(8,128)(2,1)}, f32[8,8,512]{2,1,0:T(8,128)}) custom-call(s32[3]{0:T(128)} %pad_add_fusion.sp_ref, f32[512,1024]{1,0:T(8,128)} %fusion.19.q_ref, f32[512,128]{1,0:T(8,128)} %get-tuple-element.148.c_ref, f32[512,128]{1,0:T(8,128)} %get-tuple-element.154.s_ref, ...), custom_call_target="tpu_custom_call" | custom-call | flops 4294967296 | bytes 8388608 | tf_op jit(solution)/shard_map/attend/pallas_call | solution.py:166
  105.8 9.0 %collective-permute-done.refs_4_ = bf16[256,2048]{1,0:T(8,128)(2,1)S(1)} collective-permute-done((bf16[256,2048]{1,0:T(8,128)(2,1)}, bf16[256,2048]{1,0:T(8,128)(2,1)S(1)}, u32[]{:S(2)}, u32[]{:S(2)}) %collective-permute-start) | collective-permute-done | bytes 1048608 | tf_op jit(solution)/shard_map/ppermute | solution.py:44
  114.8 0.2 collective-permute-start.1
  115.0 7.8 %attend.3 = (bf16[512,1024]{1,0:T(8,128)(2,1)}, bf16[512,1024]{1,0:T(8,128)(2,1)}, f32[8,8,512]{2,1,0:T(8,128)}) custom-call(s32[3]{0:T(128)} %pad_add_fusion.sp_ref, f32[512,1024]{1,0:T(8,128)} %fusion.19.q_ref, f32[512,128]{1,0:T(8,128)} %get-tuple-element.148.c_ref, ...), custom_call_target="tpu_custom_call", output_to_operand_aliasing={{0}: (6, {}), {1}: (7, {}), {2}: (8, {})} | custom-call | flops 4294967296 | bytes 8388608 | tf_op jit(solution)/shard_map/attend/pallas_call | solution.py:166
  122.8 3.6 fusion.20
  126.4 12.2 %collective-permute-done.1.refs_5_ = bf16[256,2048]{1,0:T(8,128)(2,1)} collective-permute-done((bf16[256,2048]{1,0:T(8,128)(2,1)S(1)}, bf16[256,2048]{1,0:T(8,128)(2,1)}, u32[]{:S(2)}, u32[]{:S(2)}) %collective-permute-start.1) | collective-permute-done | bytes 1048608 | tf_op jit(solution)/shard_map/ppermute | solution.py:44
  138.5 0.1 slice.100
  138.7 0.0 copy-start.11
  138.7 0.1 collective-permute-start.2
  138.8 2.6 collective-permute-done.2
  141.4 0.6 multiply_reduce_fusion.2
  142.0 1.2 multiply_convert_fusion.h_hbm
  143.2 143.8 %feed_forward.1 = (f32[256,2048]{1,0:T(8,128)}, bf16[4,256,2048]{2,1,0:T(8,128)(2,1)}, bf16[8,2112,256]{2,1,0:T(8,128)(2,1)}) custom-call(bf16[256,2048]{1,0:T(8,128)(2,1)} %multiply_convert_fusion.h_hbm, bf16[704,2048]{1,0:T(8,128)(2,1)} %bitcast.83, bf16[704,2048]{1,0:T(8,128)(2,1)} %bitcast.84, bf16[704,2048]{1,0:T(8,128)(2,1)} %wd_hbm.1, ...), custom_call_target="tpu_custom_call" | custom-call | flops 53150220288 | bytes 67108864 | tf_op jit(solution)/shard_map/feed_forward/pallas_call | solution.py:643
  287.0 0.0 copy-start.9
  287.0 2.9 multiply_reduce_fusion
  289.9 2.3 fusion.18
  292.2 1.5 collective-permute-start.3
  293.6 2.4 slice.61.refs_12_
  296.0 2.3 slice_bitcast_fusion
  298.3 1.3 collective-permute-start.4
  299.6 4.1 dynamic-slice_bitcast_fusion
  303.7 1.5 collective-permute-start.8
  305.2 0.5 collective-permute-start.7
  305.8 2.0 collective-permute-start.6
  307.8 0.0 collective-permute-start.5
  307.8 5.0 convolution_convert_fusion.2.do_ref
  312.8 16.2 %attend_back.1 = (bf16[512,1024]{1,0:T(8,128)(2,1)}, f32[2048,128]{1,0:T(8,128)}, f32[2048,128]{1,0:T(8,128)}) custom-call(s32[3]{0:T(128)} %pad_add_fusion.sp_ref, bf16[512,1024]{1,0:T(8,128)(2,1)} %get-tuple-element.75.q_ref, bf16[512,1024]{1,0:T(8,128)(2,1)} %convolution_convert_fusion.2.do_ref, bf16[512,1024]{1,0:T(8,128)(2,1)} %get-tuple-element.66.ctx_ref, ...), custom_call_target="tpu_custom_call" | custom-call | flops 21474836480 | bytes 8388608 | tf_op jit(solution)/shard_map/attend_back/pallas_call | solution.py:194
  329.1 0.0 copy-start.15
  329.1 1.7 fusion.5
  330.8 4.6 fusion.21
  335.5 0.1 broadcast_multiply_fusion
  335.6 1.1 copy-done.8
  336.7 0.1 pad_maximum_fusion.1
  336.8 0.2 dynamic-slice_bitcast_fusion.8
  337.0 0.1 pad_maximum_fusion.2
  337.1 1.1 dynamic-slice_bitcast_fusion.4.refs_7_
  338.2 1.1 slice.99.refs_10_
  339.3 1.5 slice.73.refs_9_
  340.9 7.1 %collective-permute-start.9 = (bf16[256,2048]{1,0:T(8,128)(2,1)S(1)}, bf16[256,2048]{1,0:T(8,128)(2,1)S(1)}, u32[]{:S(2)}, u32[]{:S(2)}) collective-permute-start(bf16[256,2048]{1,0:T(8,128)(2,1)S(1)} %fusion.5), channel_id=1, source_target_pairs={{0,2},{1,3},{2,6},{3,7},{4,0},{5,1},{6,4},{7,5},{8,10},{9,11},{10,... | collective-permute-start | bytes 3145736 | tf_op jit(solution)/shard_map/ppermute | solution.py:44
  348.0 0.8 fusion.6.refs_8_
  348.8 6.1 %convolution_convert_fusion.refs_4_ = bf16[1024,2048]{1,0:T(8,128)(2,1)} fusion(bf16[512,1024]{1,0:T(8,128)(2,1)S(1)} %copy-done.16, bf16[256,2048]{1,0:T(8,128)(2,1)} %collective-permute-done.3, bf16[256,2048]{1,0:T(8,128)(2,1)} %get-tuple-element.124), kind=kOutput, calls=%fused_computation.2 | convolution fusion | flops 2153775104 | bytes 7340032 | tf_op jit(solution)/shard_map/dot_general | solution.py:22
  354.9 4.4 convolution_convert_fusion.1
  359.3 10.3 %collective-permute-done.9 = bf16[256,2048]{1,0:T(8,128)(2,1)S(1)} collective-permute-done((bf16[256,2048]{1,0:T(8,128)(2,1)S(1)}, bf16[256,2048]{1,0:T(8,128)(2,1)S(1)}, u32[]{:S(2)}, u32[]{:S(2)}) %collective-permute-start.9) | collective-permute-done | bytes 1048608 | tf_op jit(solution)/shard_map/ppermute | solution.py:44
  369.7 2.4 convert_add_fusion.4
  372.0 5.1 fusion
  377.1 189.8 %tail.1 = (bf16[2112,2048]{1,0:T(8,128)(2,1)}, bf16[256,2048]{1,0:T(8,128)(2,1)}, bf16[2048,256]{1,0:T(8,128)(2,1)}, bf16[256,2048]{1,0:T(8,128)(2,1)}, bf16[256...) custom-call(bf16[2112,256]{1,0:T(8,128)(2,1)} %get-tuple-element.134.refs_0_, ...), custom_call_target="tpu_custom_call" | custom-call | flops 1000000000 | bytes 67108864 | tf_op jit(solution)/shard_map/tail/pallas_call | solution.py:1032
  566.9 0.8 slice_bitcast_fusion.1
  567.7 0.6 copy.37
  568.3 0.6 copy.36
  568.9 2.7 convert_element_type.165
  571.6 0.2 convert_bitcast_fusion.2
  571.9 1.8 copy.31
  573.7 1.6 convert_element_type.166
  575.3 10.5 %slice_convert_fusion = (f32[704,2048]{1,0:T(8,128)}, f32[2048,704]{0,1:T(8,128)}, f32[2048,704]{0,1:T(8,128)}) fusion(bf16[2112,2048]{1,0:T(8,128)(2,1)} %get-tuple-element.101), kind=kLoop, calls=%fused_computation.4 | loop fusion | flops 4325376 | bytes 25952256 | tf_op jit(solution)/shard_map/convert_element_type | solution.py:1173
  585.8 1.0 copy.44
  586.8 0.6 copy-done.5
  587.4 1.0 copy.45
  (46 shorter events, 0.1 us)
Async XLA Ops:
  89.7 25.1 %collective-permute-start = (bf16[256,2048]{1,0:T(8,128)(2,1)}, bf16[256,2048]{1,0:T(8,128)(2,1)S(1)}, u32[]{:S(2)}, u32[]{:S(2)}) collective-permute-start(bf16[256,2048]{1,0:T(8,128)(2,1)} %get-tuple-element.62.refs_2_), channel_id=1, source_target_pairs={{0,2},{1,3},{2,6},{3,7},{4,0},{5,1},{6,4},{7,5},{8,10},{9,11},{10,... | collective-permute-start | bytes 3145736 | tf_op jit(solution)/shard_map/ppermute | solution.py:44
  114.8 8.0 %copy-start.12 = (bf16[256,2048]{1,0:T(8,128)(2,1)}, bf16[256,2048]{1,0:T(8,128)(2,1)S(1)}, u32[]{:S(2)}) copy-start(bf16[256,2048]{1,0:T(8,128)(2,1)S(1)} %collective-permute-done.refs_4_) | copy-start | bytes 3145732
  114.8 8.0 %copy-start.13 = (bf16[1024,2048]{1,0:T(8,128)(2,1)S(1)}, bf16[1024,2048]{1,0:T(8,128)(2,1)}, u32[]{:S(2)}) copy-start(bf16[1024,2048]{1,0:T(8,128)(2,1)} %get-tuple-element.67) | copy-start | bytes 12582916
  114.8 23.7 %collective-permute-start.1 = (bf16[256,2048]{1,0:T(8,128)(2,1)S(1)}, bf16[256,2048]{1,0:T(8,128)(2,1)}, u32[]{:S(2)}, u32[]{:S(2)}) collective-permute-start(bf16[256,2048]{1,0:T(8,128)(2,1)S(1)} %collective-permute-done.refs_4_), channel_id=1, source_target_pairs={{0,2},{1,3},{2,6},{3,7},{4,0},{5,1},{6,4},{7,5},{8,10},{9,11},{10,... | collective-permute-start | bytes 3145736 | tf_op jit(solution)/shard_map/ppermute | solution.py:44
  126.4 15.1 %copy-start.1 = (bf16[256,2048]{1,0:T(8,128)(2,1)S(1)}, bf16[256,2048]{1,0:T(8,128)(2,1)}, u32[]{:S(2)}) copy-start(bf16[256,2048]{1,0:T(8,128)(2,1)} %refs_11_.1) | copy-start | bytes 3145732
  138.7 3.3 copy-start.11
  138.7 2.7 collective-permute-start.2
  287.0 2.9 copy-start
  287.0 2.9 copy-start.9
  292.2 15.6 %collective-permute-start.3 = (bf16[256,2048]{1,0:T(8,128)(2,1)}, bf16[256,2048]{1,0:T(8,128)(2,1)}, u32[]{:S(2)}, u32[]{:S(2)}) collective-permute-start(bf16[256,2048]{1,0:T(8,128)(2,1)} %get-tuple-element.124), channel_id=1, source_target_pairs={{0,1},{1,0},{2,3},{3,2},{4,5},{5,4},{6,7},{7,6},{8,9},{9,8},{10,11... | collective-permute-start | bytes 3145736 | tf_op jit(solution)/shard_map/ppermute | solution.py:47
  298.3 30.7 %collective-permute-start.4 = (bf16[256,2048]{1,0:T(8,128)(2,1)}, bf16[256,2048]{1,0:T(8,128)(2,1)}, u32[]{:S(2)}, u32[]{:S(2)}) collective-permute-start(bf16[256,2048]{1,0:T(8,128)(2,1)} %slice_bitcast_fusion), channel_id=1, source_target_pairs={{0,2},{1,3},{2,6},{3,7},{4,0},{5,1},{6,4},{7,5},{8,10},{9,11},{10,... | collective-permute-start | bytes 3145736 | tf_op jit(solution)/shard_map/ppermute | solution.py:44
  299.6 8.2 %copy-start.14 = (bf16[1024,2048]{1,0:T(8,128)(2,1)S(1)}, bf16[1024,2048]{1,0:T(8,128)(2,1)}, u32[]{:S(2)}) copy-start(bf16[1024,2048]{1,0:T(8,128)(2,1)} %get-tuple-element.67) | copy-start | bytes 12582916
  303.7 55.6 %collective-permute-start.8 = (bf16[2112,256]{1,0:T(8,128)(2,1)}, bf16[2112,256]{1,0:T(8,128)(2,1)}, u32[]{:S(2)}, u32[]{:S(2)}) collective-permute-start(bf16[2112,256]{1,0:T(8,128)(2,1)} %get-tuple-element.135), channel_id=1, source_target_pairs={{0,16},{8,24},{16,0},{24,8},{1,17},{9,25},{17,1},{25,9},{2,18},{10... | collective-permute-start | bytes 3244040 | tf_op jit(solution)/shard_map/ppermute | solution.py:50
  305.2 54.1 %collective-permute-start.7 = (bf16[2112,256]{1,0:T(8,128)(2,1)}, bf16[2112,256]{1,0:T(8,128)(2,1)}, u32[]{:S(2)}, u32[]{:S(2)}) collective-permute-start(bf16[2112,256]{1,0:T(8,128)(2,1)} %get-tuple-element.136), channel_id=1, source_target_pairs={{0,16},{8,24},{16,0},{24,8},{1,17},{9,25},{17,1},{25,9},{2,18},{10... | collective-permute-start | bytes 3244040 | tf_op jit(solution)/shard_map/ppermute | solution.py:50
  305.8 53.5 %collective-permute-start.6 = (bf16[2112,256]{1,0:T(8,128)(2,1)}, bf16[2112,256]{1,0:T(8,128)(2,1)}, u32[]{:S(2)}, u32[]{:S(2)}) collective-permute-start(bf16[2112,256]{1,0:T(8,128)(2,1)} %get-tuple-element.137), channel_id=1, source_target_pairs={{0,8},{8,0},{16,24},{24,16},{1,9},{9,1},{17,25},{25,17},{2,10},{10... | collective-permute-start | bytes 3244040 | tf_op jit(solution)/shard_map/ppermute | solution.py:50
  307.8 51.5 %collective-permute-start.5 = (bf16[2112,256]{1,0:T(8,128)(2,1)S(1)}, bf16[2112,256]{1,0:T(8,128)(2,1)}, u32[]{:S(2)}, u32[]{:S(2)}) collective-permute-start(bf16[2112,256]{1,0:T(8,128)(2,1)S(1)} %get-tuple-element.138), channel_id=1, source_target_pairs={{0,8},{8,0},{16,24},{24,16},{1,9},{9,1},{17,25},{25,17},{2,10},{10... | collective-permute-start | bytes 3244040 | tf_op jit(solution)/shard_map/ppermute | solution.py:50
  312.8 16.3 %copy-start.2 = (bf16[4,256,2048]{2,1,0:T(8,128)(2,1)S(1)}, bf16[4,256,2048]{2,1,0:T(8,128)(2,1)}, u32[]{:S(2)}) copy-start(bf16[4,256,2048]{2,1,0:T(8,128)(2,1)} %get-tuple-element.82) | copy-start | bytes 12582916
  329.1 1.7 copy-start.15
  330.8 4.7 copy-start.7
  335.5 1.2 copy-start.8
  339.3 9.5 %copy-start.16 = (bf16[512,1024]{1,0:T(8,128)(2,1)S(1)}, bf16[512,1024]{1,0:T(8,128)(2,1)}, u32[]{:S(2)}) copy-start(bf16[512,1024]{1,0:T(8,128)(2,1)} %get-tuple-element.66.ctx_ref) | copy-start | bytes 3145732
  340.9 28.8 %collective-permute-start.9 = (bf16[256,2048]{1,0:T(8,128)(2,1)S(1)}, bf16[256,2048]{1,0:T(8,128)(2,1)S(1)}, u32[]{:S(2)}, u32[]{:S(2)}) collective-permute-start(bf16[256,2048]{1,0:T(8,128)(2,1)S(1)} %fusion.5), channel_id=1, source_target_pairs={{0,2},{1,3},{2,6},{3,7},{4,0},{5,1},{6,4},{7,5},{8,10},{9,11},{10,... | collective-permute-start | bytes 3145736 | tf_op jit(solution)/shard_map/ppermute | solution.py:44
  348.8 6.1 %copy-start.10 = (bf16[512,2048]{1,0:T(8,128)(2,1)S(1)}, bf16[512,2048]{1,0:T(8,128)(2,1)}, u32[]{:S(2)}) copy-start(bf16[512,2048]{1,0:T(8,128)(2,1)} %get-tuple-element.56) | copy-start | bytes 6291460
  354.9 17.1 %slice-start = ((s8[8650752]{0:T(1024)(128)(4,1)}), s8[4194304]{0:T(1024)(128)(4,1)S(1)}, s32[]{:S(2)}) async-start(s8[8650752]{0:T(1024)(128)(4,1)} %bitcast.74), calls=%async_computation | async-start | bytes 8388608
  354.9 17.1 %slice-start.1 = ((s8[8650752]{0:T(1024)(128)(4,1)}), s8[4194304]{0:T(1024)(128)(4,1)S(1)}, s32[]{:S(2)}) async-start(s8[8650752]{0:T(1024)(128)(4,1)} %bitcast.74), calls=%async_computation.1 | async-start | bytes 8388608
  369.7 2.4 slice-start.2
  566.9 4.7 copy-start.4
  571.9 1.8 copy-start.3
  575.3 10.6 %copy-start.6 = (bf16[256,2048]{1,0:T(8,128)(2,1)S(1)}, bf16[256,2048]{1,0:T(8,128)(2,1)}, u32[]{:S(2)}) copy-start(bf16[256,2048]{1,0:T(8,128)(2,1)} %get-tuple-element.168) | copy-start | bytes 3145732
  585.8 1.6 copy-start.5

commit v6 on v5

--- a/solution.py
+++ b/solution.py
@@ -796,9 +796,9 @@
     w_hbm, refs = refs[: len(names)], refs[len(names) :]
     (
         o_hbm, q_hbm, m_hbm, kv_keep, kv_send, gn_keep, gn_send, tokens, normed, w_kv, cosine, sine, gain_part,
-        gain, grad_hidden, hidden,
+        gain, grad_hidden, hidden, terms,
         ws_hbm, ow_hbm, qw_hbm, kvw_hbm, block_ref, grad_ref, gains_ref,
-        o_buf, o_in, o_ring, q_buf, q_in, w_buf, w_in, c_buf, c_in, b_buf, b_in, b_turned, got,
+        o_buf, o_in, o_ring, q_buf, q_in, w_buf, w_in, c_buf, c_in, b_buf, b_in, b_turned, got, mine, m_sem,
         kv_got, kv_ring, kv_in, gn_got, kvw_half, kvw_got, kvw_in, kvw_all, gains_in,
         ss, rs, o_sem, q_sem, w_sem, out_sem, w_free, o_free, b_free,
     ) = refs
@@ -993,9 +993,12 @@
 
     def m_chain():
         copy = send(m_hbm, got, right)
+        load = pltpu.make_async_copy(terms.at[0], mine, m_sem.at[0])
+        load.start()
         yield
+        load.wait()
         copy.wait_recv()
-        block_ref[...] = (hidden[...] + got[...].astype(F32)).astype(BF16)
+        block_ref[...] = (hidden[...] + mine[...].astype(F32) + got[...].astype(F32)).astype(BF16)
 
     chains = {
         "w": w_chain(), "o": o_chain(), "q": ring_chain("q", q_buf, q_in), "kv": kv_chain(),
@@ -1010,13 +1013,13 @@
 
 
 TAIL_ORDER = (
-    "o kv w kv", "kvw kv g kvw", "q c g* o", "c w o o", "c* o q w", "q* m b b", "o o b o*", "b* w* m*",
+    "o kv w kv", "kvw kvw q c", "o c w o", "c o q kv", "g o w q", "g q m g", "b o b c", "o b o b", "b w m",
 )
 
 
 def tail(
     links, o_parts, q_parts, m_part, w_pieces, names, kv_keep, kv_send, gn_keep, gn_send, tokens, normed, w_kv, cosine,
-    sine, gain_part, gain, grad_hidden, hidden,
+    sine, gain_part, gain, grad_hidden, hidden, terms,
 ):
     chips, width, depth = q_parts.shape
     own = tokens.shape[0]
@@ -1031,7 +1034,7 @@
     count = 20 * chips + 20 * n + 16
     return pl.pallas_call(
         functools.partial(tail_kernel, links, names),
-        in_specs=[anywhere] * (3 + len(names)) + [here] * 13,
+        in_specs=[anywhere] * (3 + len(names)) + [here] * 13 + [anywhere],
         out_specs=[anywhere] * 4 + [here] * 3,
         out_shape=[
             shape((rows, depth), BF16), shape((width, depth), BF16),
@@ -1046,6 +1049,7 @@
             pltpu.VMEM((band, depth), BF16), pltpu.VMEM((n - 1, band, depth), BF16),
             pltpu.VMEM((pieces, width, piece), BF16), pltpu.VMEM((2, n - 1, width, piece), BF16),
             pltpu.VMEM((pieces, piece, width), BF16), pltpu.VMEM((own, depth), BF16),
+            pltpu.VMEM((own, depth), BF16), dma((1,)),
             pltpu.VMEM((chips, own, 2 * HD), BF16),
             pltpu.VMEM((chips - 1, own, 2 * HD), BF16), pltpu.VMEM((chips - 1, own, 2 * HD), BF16),
             pltpu.VMEM((own, depth), BF16),
@@ -1064,7 +1068,7 @@
         name="tail",
     )(
         *w_pieces, o_parts, q_parts, m_part, kv_keep, kv_send, gn_keep, gn_send, tokens, normed, w_kv, cosine, sine,
-        gain_part, gain, grad_hidden, hidden,
+        gain_part, gain, grad_hidden, hidden, terms,
     )
 
 
@@ -1142,7 +1146,6 @@
     for k in range(2, chips - 1):
         query_grad, mlp_came = lax.optimization_barrier((query_grad, mlp_came))
         mlp_sent = (mlp_terms[k].astype(F32) + mlp_came.astype(F32)).astype(BF16)
-        query_grad, mlp_sent = lax.optimization_barrier((query_grad, mlp_sent))
         mlp_came = links.ring(mlp_sent)
     out_parts = mm(context, grad_branch, TN).astype(BF16)
     query_parts = mm(query_grad, normed, TN).astype(BF16).reshape(chips, width, -1)
@@ -1157,14 +1160,13 @@
     kv_keep = lax.dynamic_index_in_dim(kv_part, core, 1, keepdims=False)
     kv_send = lax.dynamic_index_in_dim(kv_part, 1 - core, 1, keepdims=False).astype(BF16)
     gn_part = mm(query_grad, wq, NT)
-    query_parts, ffn_came, mlp_came = lax.optimization_barrier((query_parts, ffn_came, mlp_came))
     mlp_sent = (mlp_terms[chips - 1].astype(F32) + mlp_came.astype(F32)).astype(BF16)
     ffn_pieces = [(a.astype(F32) + b.astype(F32)).astype(BF16) for a, b in zip(ffn_stay, ffn_came)]
     gain_part = mlp_gain_part[None]
     ffn_w, out_w, query_w, kv_w, block_output, tokens_grad, gains = tail(
         links, out_parts, query_parts, mlp_sent, ffn_pieces, ffn_names, kv_keep, kv_send, gn_part[:own],
         gn_part[own:].astype(BF16), tokens, normed_own, w_kv, cosine[:own], sine[:own], gain_part,
-        attn_gain[None], grad_hidden, hidden + mlp_terms[0].astype(F32),
+        attn_gain[None], grad_hidden, hidden, mlp_terms,
     )
     units = w_down.shape[0]
 

time: 599 us -> 585 us (0.977)
  waiting for transfers between devices: 34.1 us -> 26.1 us
    ppermute x4, waiting for transfers between devices: 31.5 us -> 23.5 us  [ring(): return lax.ppermute(x, 'tensor', self.ring_pairs)]
  transfers between devices with their start and end apart: 10 -> 10, of which waited for: 4 -> 4; matrix products, arithmetic and copies ran while one was open for 8% -> 9% of each run, Pallas kernels for 5% -> 5%
where the time goes in v6:
time: 585 us; the launch traced here: 576 us
  Pallas kernels  450 us (77%)
  other arithmetic  34.5 us (6%)
  matrix products  28.4 us (5%)
  waiting for transfers between devices  26.1 us (4%)
  local copies, waits for them, and re-layouts  20 us (3%)
  starting transfers between devices  15 us (3%)
    pallas_call x1, Pallas kernels, tail(): pl.pallas_call(functools.partial(tail_kernel, links, names), in_specs=[an...  189 us
    pallas_call x1, Pallas kernels, feed_forward(): pl.pallas_call(functools.partial(mlp_kernel, links), in_specs=[anywhere]...  144 us
    pallas_call x1, Pallas kernels, front(): pl.pallas_call(functools.partial(front_kernel, links), in_specs=[pl.Block...  86.5 us
    dot_general x6, matrix products, mm(): lax.dot_general(left, right, (dims, ((), ())), preferred_element_type=F32)  28.4 us
    ppermute x4, waiting for transfers between devices, ring(): return lax.ppermute(x, 'tensor', self.ring_pairs)  23.5 us
    pallas_call x1, Pallas kernels, attend_back(): pl.pallas_call(functools.partial(bwd_kernel, seq // rows), grid_spec=pltp...  16.3 us
    pallas_call x2, Pallas kernels, attend(): pl.pallas_call(functools.partial(fwd_kernel, seq // rows), grid_spec=pltp...  14.8 us
  transfers between devices with their start and end apart: 10, of which 4 were waited for; matrix products, arithmetic and copies ran while one was open for 9% of the time, Pallas kernels for 5%

profile of v6, /device:TPU:0, one launch (start us, length us, event | category | flops | bytes accessed | tf_op | source)
XLA Modules:
  0.0 576.0 jit_solution(15578965315809295065)
XLA Ops:
  1.4 1.0 multiply_sine_fusion
  2.4 0.8 fusion.9
  3.2 86.5 %front.1 = (bf16[512,2048]{1,0:T(8,128)(2,1)}, bf16[2048,1024]{1,0:T(8,128)(2,1)}, bf16[1024,2048]{1,0:T(8,128)(2,1)}, bf16[2048,256]{1,0:T(8,128)(2,1)}, bf16[1...) custom-call(s32[1]{0:T(128)S(6)} %copy.43.docs, ...), custom_call_target="tpu_custom_call" | custom-call | flops 10000000000 | bytes 67108864 | tf_op jit(solution)/shard_map/front/pallas_call | solution.py:415
  89.7 0.9 collective-permute-start
  90.6 1.2 fusion.8
  91.7 0.7 pad_add_fusion.sp_ref
  92.4 6.5 %fusion.19.q_ref = f32[512,1024]{1,0:T(8,128)} fusion(bf16[512,2048]{1,0:T(8,128)(2,1)} %get-tuple-element.48, bf16[2048,1024]{1,0:T(8,128)(2,1)} %get-tuple-element.49), kind=kOutput, calls=%fused_computation.75 | convolution fusion | flops 2147483648 | bytes 8388608 | tf_op jit(solution)/shard_map/dot_general | solution.py:22
  98.9 7.0 %attend.2 = (bf16[512,1024]{1,0:T(8,128)(2,1)}, bf16[512,1024]{1,0:T(8,128)(2,1)}, f32[8,8,512]{2,1,0:T(8,128)}) custom-call(s32[3]{0:T(128)} %pad_add_fusion.sp_ref, f32[512,1024]{1,0:T(8,128)} %fusion.19.q_ref, f32[512,128]{1,0:T(8,128)} %get-tuple-element.130.c_ref, f32[512,128]{1,0:T(8,128)} %get-tuple-element.136.s_ref, ...), custom_call_target="tpu_custom_call" | custom-call | flops 4294967296 | bytes 8388608 | tf_op jit(solution)/shard_map/attend/pallas_call | solution.py:166
  105.9 8.9 %collective-permute-done.refs_4_ = bf16[256,2048]{1,0:T(8,128)(2,1)S(1)} collective-permute-done((bf16[256,2048]{1,0:T(8,128)(2,1)}, bf16[256,2048]{1,0:T(8,128)(2,1)S(1)}, u32[]{:S(2)}, u32[]{:S(2)}) %collective-permute-start) | collective-permute-done | bytes 1048608 | tf_op jit(solution)/shard_map/ppermute | solution.py:44
  114.8 0.2 collective-permute-start.1
  114.9 7.8 %attend.3 = (bf16[512,1024]{1,0:T(8,128)(2,1)}, bf16[512,1024]{1,0:T(8,128)(2,1)}, f32[8,8,512]{2,1,0:T(8,128)}) custom-call(s32[3]{0:T(128)} %pad_add_fusion.sp_ref, f32[512,1024]{1,0:T(8,128)} %fusion.19.q_ref, f32[512,128]{1,0:T(8,128)} %get-tuple-element.130.c_ref, ...), custom_call_target="tpu_custom_call", output_to_operand_aliasing={{0}: (6, {}), {1}: (7, {}), {2}: (8, {})} | custom-call | flops 4294967296 | bytes 8388608 | tf_op jit(solution)/shard_map/attend/pallas_call | solution.py:166
  122.8 3.6 fusion.20
  126.3 12.0 %collective-permute-done.1.refs_5_ = bf16[256,2048]{1,0:T(8,128)(2,1)S(1)} collective-permute-done((bf16[256,2048]{1,0:T(8,128)(2,1)S(1)}, bf16[256,2048]{1,0:T(8,128)(2,1)S(1)}, u32[]{:S(2)}, u32[]{:S(2)}) %collective-permute-start.1) | collective-permute-done | bytes 1048608 | tf_op jit(solution)/shard_map/ppermute | solution.py:44
  138.4 0.1 slice.95
  138.5 0.0 copy-start.12
  138.6 0.1 collective-permute-start.2
  138.6 2.6 collective-permute-done.2
  141.3 0.6 multiply_reduce_fusion.2
  141.9 1.5 multiply_convert_fusion.h_hbm
  143.4 143.6 %feed_forward.1 = (f32[256,2048]{1,0:T(8,128)}, bf16[4,256,2048]{2,1,0:T(8,128)(2,1)}, bf16[8,2112,256]{2,1,0:T(8,128)(2,1)}) custom-call(bf16[256,2048]{1,0:T(8,128)(2,1)} %multiply_convert_fusion.h_hbm, bf16[704,2048]{1,0:T(8,128)(2,1)} %bitcast.80, bf16[704,2048]{1,0:T(8,128)(2,1)} %bitcast.81, bf16[704,2048]{1,0:T(8,128)(2,1)} %wd_hbm.1, ...), custom_call_target="tpu_custom_call" | custom-call | flops 53150220288 | bytes 67108864 | tf_op jit(solution)/shard_map/feed_forward/pallas_call | solution.py:643
  287.0 2.9 multiply_reduce_fusion
  289.9 2.3 fusion.18
  292.2 1.5 collective-permute-start.7
  293.6 2.3 slice.58.refs_12_
  295.9 2.3 slice_bitcast_fusion
  298.2 1.3 collective-permute-start.8
  299.5 3.6 dynamic-slice_bitcast_fusion
  303.2 1.5 collective-permute-start.6
  304.7 0.5 collective-permute-start.5
  305.2 2.0 collective-permute-start.4
  307.2 0.0 collective-permute-start.3
  307.2 5.0 convolution_convert_fusion.2.do_ref
  312.2 16.3 %attend_back.1 = (bf16[512,1024]{1,0:T(8,128)(2,1)}, f32[2048,128]{1,0:T(8,128)}, f32[2048,128]{1,0:T(8,128)}) custom-call(s32[3]{0:T(128)} %pad_add_fusion.sp_ref, bf16[512,1024]{1,0:T(8,128)(2,1)} %get-tuple-element.68.q_ref, bf16[512,1024]{1,0:T(8,128)(2,1)} %convolution_convert_fusion.2.do_ref, bf16[512,1024]{1,0:T(8,128)(2,1)} %get-tuple-element.58.ctx_ref, ...), custom_call_target="tpu_custom_call" | custom-call | flops 21474836480 | bytes 8388608 | tf_op jit(solution)/shard_map/attend_back/pallas_call | solution.py:194
  328.6 1.8 fusion.4
  330.4 0.1 copy-done.11
  330.4 0.3 copy-done.18
  330.7 4.4 convolution_convert_fusion
  335.2 0.1 broadcast_multiply_fusion
  335.2 7.1 %collective-permute-start.9 = (bf16[256,2048]{1,0:T(8,128)(2,1)S(1)}, bf16[256,2048]{1,0:T(8,128)(2,1)S(1)}, u32[]{:S(2)}, u32[]{:S(2)}) collective-permute-start(bf16[256,2048]{1,0:T(8,128)(2,1)S(1)} %fusion.4), channel_id=1, source_target_pairs={{0,2},{1,3},{2,6},{3,7},{4,0},{5,1},{6,4},{7,5},{8,10},{9,11},{10,... | collective-permute-start | bytes 3145736 | tf_op jit(solution)/shard_map/ppermute | solution.py:44
  342.3 0.1 pad_maximum_fusion.1
  342.5 0.2 dynamic-slice_bitcast_fusion.8
  342.6 0.1 pad_maximum_fusion.2
  342.8 1.1 dynamic-slice_bitcast_fusion.4.refs_7_
  343.9 0.1 copy-done.19
  344.0 6.5 %convolution_convert_fusion.1.refs_4_ = bf16[1024,2048]{1,0:T(8,128)(2,1)} fusion(bf16[512,1024]{1,0:T(8,128)(2,1)S(1)} %copy-done.19, bf16[256,2048]{1,0:T(8,128)(2,1)} %collective-permute-done.7, bf16[256,2048]{1,0:T(8,128)(2,1)} %get-tuple-element.108), kind=kOutput, calls=%fused_computation.3 | convolution fusion | flops 2153775104 | bytes 7340032 | tf_op jit(solution)/shard_map/dot_general | solution.py:22
  350.5 2.4 fusion.21
  352.9 0.9 fusion.6.refs_8_
  353.8 1.1 slice.94.refs_10_
  354.9 1.5 slice.69.refs_9_
  356.4 5.1 fusion
  361.5 2.5 collective-permute-done.9
  364.0 1.4 fusion.5.refs_6_
  365.4 188.9 %tail.1 = (bf16[2112,2048]{1,0:T(8,128)(2,1)}, bf16[256,2048]{1,0:T(8,128)(2,1)}, bf16[2048,256]{1,0:T(8,128)(2,1)}, bf16[256,2048]{1,0:T(8,128)(2,1)}, bf16[256...) custom-call(bf16[2112,256]{1,0:T(8,128)(2,1)} %get-tuple-element.118.refs_0_, ...), custom_call_target="tpu_custom_call" | custom-call | flops 1000000000 | bytes 67108864 | tf_op jit(solution)/shard_map/tail/pallas_call | solution.py:1035
  554.3 0.8 slice_bitcast_fusion.1
  555.1 0.6 copy.37
  555.7 0.6 copy.36
  556.3 2.7 convert_element_type.157
  559.0 0.2 convert_bitcast_fusion.2
  559.3 1.8 copy.31
  561.1 1.6 convert_element_type.158
  562.6 10.5 %slice_convert_fusion = (f32[704,2048]{1,0:T(8,128)}, f32[2048,704]{0,1:T(8,128)}, f32[2048,704]{0,1:T(8,128)}) fusion(bf16[2112,2048]{1,0:T(8,128)(2,1)} %get-tuple-element.85), kind=kLoop, calls=%fused_computation.4 | loop fusion | flops 4325376 | bytes 25952256 | tf_op jit(solution)/shard_map/convert_element_type | solution.py:1175
  573.2 1.0 copy.44
  574.2 0.6 copy-done.6
  574.8 1.0 copy.45
  (52 shorter events, 0.1 us)
Async XLA Ops:
  89.7 25.1 %collective-permute-start = (bf16[256,2048]{1,0:T(8,128)(2,1)}, bf16[256,2048]{1,0:T(8,128)(2,1)S(1)}, u32[]{:S(2)}, u32[]{:S(2)}) collective-permute-start(bf16[256,2048]{1,0:T(8,128)(2,1)} %get-tuple-element.54.refs_2_), channel_id=1, source_target_pairs={{0,2},{1,3},{2,6},{3,7},{4,0},{5,1},{6,4},{7,5},{8,10},{9,11},{10,... | collective-permute-start | bytes 3145736 | tf_op jit(solution)/shard_map/ppermute | solution.py:44
  114.8 8.0 %copy-start.13 = (bf16[256,2048]{1,0:T(8,128)(2,1)}, bf16[256,2048]{1,0:T(8,128)(2,1)S(1)}, u32[]{:S(2)}) copy-start(bf16[256,2048]{1,0:T(8,128)(2,1)S(1)} %collective-permute-done.refs_4_) | copy-start | bytes 3145732
  114.8 8.0 %copy-start.16 = (bf16[1024,2048]{1,0:T(8,128)(2,1)S(1)}, bf16[1024,2048]{1,0:T(8,128)(2,1)}, u32[]{:S(2)}) copy-start(bf16[1024,2048]{1,0:T(8,128)(2,1)} %get-tuple-element.59) | copy-start | bytes 12582916
  114.8 23.6 %collective-permute-start.1 = (bf16[256,2048]{1,0:T(8,128)(2,1)S(1)}, bf16[256,2048]{1,0:T(8,128)(2,1)S(1)}, u32[]{:S(2)}, u32[]{:S(2)}) collective-permute-start(bf16[256,2048]{1,0:T(8,128)(2,1)S(1)} %collective-permute-done.refs_4_), channel_id=1, source_target_pairs={{0,2},{1,3},{2,6},{3,7},{4,0},{5,1},{6,4},{7,5},{8,10},{9,11},{10,... | collective-permute-start | bytes 3145736 | tf_op jit(solution)/shard_map/ppermute | solution.py:44
  126.3 15.0 %copy-start.3 = (bf16[256,2048]{1,0:T(8,128)(2,1)S(1)}, bf16[256,2048]{1,0:T(8,128)(2,1)}, u32[]{:S(2)}) copy-start(bf16[256,2048]{1,0:T(8,128)(2,1)} %refs_11_.1) | copy-start | bytes 3145732
  138.4 3.5 copy-start.14
  138.5 3.4 copy-start.12
  138.6 2.7 collective-permute-start.2
  141.9 148.0 %copy-start = (f32[256,2048]{1,0:T(8,128)}, f32[256,2048]{1,0:T(8,128)S(1)}, u32[]{:S(2)}) copy-start(f32[256,2048]{1,0:T(8,128)S(1)} %get-tuple-element.111.refs_19_) | copy-start | bytes 6291460
  287.0 2.9 copy-start.2
  287.0 2.9 copy-start.10
  292.2 15.0 %collective-permute-start.7 = (bf16[256,2048]{1,0:T(8,128)(2,1)}, bf16[256,2048]{1,0:T(8,128)(2,1)}, u32[]{:S(2)}, u32[]{:S(2)}) collective-permute-start(bf16[256,2048]{1,0:T(8,128)(2,1)} %get-tuple-element.108), channel_id=1, source_target_pairs={{0,1},{1,0},{2,3},{3,2},{4,5},{5,4},{6,7},{7,6},{8,9},{9,8},{10,11... | collective-permute-start | bytes 3145736 | tf_op jit(solution)/shard_map/ppermute | solution.py:47
  298.2 30.3 %collective-permute-start.8 = (bf16[256,2048]{1,0:T(8,128)(2,1)}, bf16[256,2048]{1,0:T(8,128)(2,1)}, u32[]{:S(2)}, u32[]{:S(2)}) collective-permute-start(bf16[256,2048]{1,0:T(8,128)(2,1)} %slice_bitcast_fusion), channel_id=1, source_target_pairs={{0,2},{1,3},{2,6},{3,7},{4,0},{5,1},{6,4},{7,5},{8,10},{9,11},{10,... | collective-permute-start | bytes 3145736 | tf_op jit(solution)/shard_map/ppermute | solution.py:44
  299.5 7.7 %copy-start.17 = (bf16[1024,2048]{1,0:T(8,128)(2,1)S(1)}, bf16[1024,2048]{1,0:T(8,128)(2,1)}, u32[]{:S(2)}) copy-start(bf16[1024,2048]{1,0:T(8,128)(2,1)} %get-tuple-element.59) | copy-start | bytes 12582916
  303.2 53.2 %collective-permute-start.6 = (bf16[2112,256]{1,0:T(8,128)(2,1)}, bf16[2112,256]{1,0:T(8,128)(2,1)}, u32[]{:S(2)}, u32[]{:S(2)}) collective-permute-start(bf16[2112,256]{1,0:T(8,128)(2,1)} %get-tuple-element.119), channel_id=1, source_target_pairs={{0,16},{8,24},{16,0},{24,8},{1,17},{9,25},{17,1},{25,9},{2,18},{10... | collective-permute-start | bytes 3244040 | tf_op jit(solution)/shard_map/ppermute | solution.py:50
  304.7 51.7 %collective-permute-start.5 = (bf16[2112,256]{1,0:T(8,128)(2,1)S(1)}, bf16[2112,256]{1,0:T(8,128)(2,1)}, u32[]{:S(2)}, u32[]{:S(2)}) collective-permute-start(bf16[2112,256]{1,0:T(8,128)(2,1)S(1)} %get-tuple-element.120), channel_id=1, source_target_pairs={{0,16},{8,24},{16,0},{24,8},{1,17},{9,25},{17,1},{25,9},{2,18},{10... | collective-permute-start | bytes 3244040 | tf_op jit(solution)/shard_map/ppermute | solution.py:50
  305.2 51.2 %collective-permute-start.4 = (bf16[2112,256]{1,0:T(8,128)(2,1)S(1)}, bf16[2112,256]{1,0:T(8,128)(2,1)}, u32[]{:S(2)}, u32[]{:S(2)}) collective-permute-start(bf16[2112,256]{1,0:T(8,128)(2,1)S(1)} %get-tuple-element.121), channel_id=1, source_target_pairs={{0,8},{8,0},{16,24},{24,16},{1,9},{9,1},{17,25},{25,17},{2,10},{10... | collective-permute-start | bytes 3244040 | tf_op jit(solution)/shard_map/ppermute | solution.py:50
  307.2 49.2 %collective-permute-start.3 = (bf16[2112,256]{1,0:T(8,128)(2,1)S(1)}, bf16[2112,256]{1,0:T(8,128)(2,1)}, u32[]{:S(2)}, u32[]{:S(2)}) collective-permute-start(bf16[2112,256]{1,0:T(8,128)(2,1)S(1)} %get-tuple-element.122), channel_id=1, source_target_pairs={{0,8},{8,0},{16,24},{24,16},{1,9},{9,1},{17,25},{25,17},{2,10},{10... | collective-permute-start | bytes 3244040 | tf_op jit(solution)/shard_map/ppermute | solution.py:50
  312.2 16.3 %copy-start.1 = (bf16[4,256,2048]{2,1,0:T(8,128)(2,1)S(1)}, bf16[4,256,2048]{2,1,0:T(8,128)(2,1)}, u32[]{:S(2)}) copy-start(bf16[4,256,2048]{2,1,0:T(8,128)(2,1)} %get-tuple-element.74.refs_20_) | copy-start | bytes 12582916
  328.5 1.9 copy-start.11
  328.6 2.2 copy-start.18
  330.7 4.4 copy-start.8
  335.1 7.2 %copy-start.9 = (f32[2048,128]{1,0:T(8,128)S(1)}, f32[2048,128]{1,0:T(8,128)}, u32[]{:S(2)}) copy-start(f32[2048,128]{1,0:T(8,128)} %get-tuple-element.78) | copy-start | bytes 3145732
  335.2 28.8 %collective-permute-start.9 = (bf16[256,2048]{1,0:T(8,128)(2,1)S(1)}, bf16[256,2048]{1,0:T(8,128)(2,1)S(1)}, u32[]{:S(2)}, u32[]{:S(2)}) collective-permute-start(bf16[256,2048]{1,0:T(8,128)(2,1)S(1)} %fusion.4), channel_id=1, source_target_pairs={{0,2},{1,3},{2,6},{3,7},{4,0},{5,1},{6,4},{7,5},{8,10},{9,11},{10,... | collective-permute-start | bytes 3145736 | tf_op jit(solution)/shard_map/ppermute | solution.py:44
  342.6 1.3 copy-start.19
  342.8 7.7 %copy-start.15 = (bf16[2048,1024]{1,0:T(8,128)(2,1)S(1)}, bf16[2048,1024]{1,0:T(8,128)(2,1)}, u32[]{:S(2)}) copy-start(bf16[2048,1024]{1,0:T(8,128)(2,1)} %get-tuple-element.49) | copy-start | bytes 12582916
  344.0 12.4 %slice-start = ((s8[8650752]{0:T(1024)(128)(4,1)}), s8[4194304]{0:T(1024)(128)(4,1)S(1)}, s32[]{:S(2)}) async-start(s8[8650752]{0:T(1024)(128)(4,1)} %bitcast.71), calls=%async_computation | async-start | bytes 8388608
  344.0 12.4 %slice-start.1 = ((s8[8650752]{0:T(1024)(128)(4,1)}), s8[4194304]{0:T(1024)(128)(4,1)S(1)}, s32[]{:S(2)}) async-start(s8[8650752]{0:T(1024)(128)(4,1)} %bitcast.71), calls=%async_computation.1 | async-start | bytes 8388608
  350.5 5.9 %slice-start.2 = ((s8[8650752]{0:T(1024)(128)(4,1)}), s8[262144]{0:T(1024)(128)(4,1)S(1)}, s32[]{:S(2)}) async-start(s8[8650752]{0:T(1024)(128)(4,1)} %bitcast.71), calls=%async_computation.2 | async-start | bytes 524288
  554.3 4.7 copy-start.5
  559.3 1.8 copy-start.4
  562.6 10.6 %copy-start.7 = (bf16[256,2048]{1,0:T(8,128)(2,1)S(1)}, bf16[256,2048]{1,0:T(8,128)(2,1)}, u32[]{:S(2)}) copy-start(bf16[256,2048]{1,0:T(8,128)(2,1)} %get-tuple-element.150) | copy-start | bytes 3145732
  573.2 1.6 copy-start.6

commit v7 on v6

--- a/solution.py
+++ b/solution.py
@@ -79,13 +79,17 @@
     return inner + 1, pl.multiple_of((block - inner) * rows, rows)
 
 
+HEADS = 2
+
+
 def fwd_kernel(blocks, sp_ref, q_ref, c_ref, s_ref, k_ref, v_ref, *refs):
     qo_ref, ctx_ref, lse_ref = refs[-3:]
     rows = q_ref.shape[0]
     chip, two_docs, core = sp_ref[0], sp_ref[1], sp_ref[2]
-    x = q_ref[...]
-    q = (x * c_ref[...] + pltpu.roll(x, HD // 2, 1) * s_ref[...]).astype(BF16)
-    qo_ref[...] = q
+    heads = [slice(h * HD, (h + 1) * HD) for h in range(HEADS)]
+    for at in heads:
+        x = q_ref[:, at]
+        qo_ref[:, at] = (x * c_ref[...] + pltpu.roll(x, HD // 2, 1) * s_ref[...]).astype(BF16)
     count, low = span(chip, two_docs, rows)
     mask = diagonal((rows, rows), 0, core * (rows // 2))
     for n in range(1, blocks + 1):
@@ -93,23 +97,18 @@
         @pl.when(count == n)
         def _(n=n):
             near = (n - 1) * rows
-            diag = pl.ds(low + near, rows)
-            s_diag = jnp.where(mask, mm(q, k_ref[diag, :], NT), MASKED)
-            top = jnp.max(s_diag, axis=1, keepdims=True)
-            if n > 1:
-                main = pl.ds(low, near)
-                s_main = mm(q, k_ref[main, :], NT)
-                top = jnp.maximum(top, jnp.max(s_main, axis=1, keepdims=True))
-            p_diag = jnp.exp2(s_diag - top)
-            total = jnp.sum(p_diag, axis=1, keepdims=True)
-            out = mm(p_diag.astype(BF16), v_ref[diag, :], NN)
-            if n > 1:
-                p_main = jnp.exp2(s_main - top)
-                total = total + jnp.sum(p_main, axis=1, keepdims=True)
-                out = out + mm(p_main.astype(BF16), v_ref[main, :], NN)
-            ctx_ref[...] = (out / total).astype(BF16)
-            lse = jnp.broadcast_to(top + jnp.log2(total), (rows, HD))
-            lse_ref[0] = lse.T[:8]
+            keys = [pl.ds(low + near, rows)] + ([pl.ds(low, near)] if n > 1 else [])
+            scores = [[mm(qo_ref[:, at], k_ref[at_keys, :], NT) for at_keys in keys] for at in heads]
+            for h, at in enumerate(heads):
+                score = scores[h]
+                score[0] = jnp.where(mask, score[0], MASKED)
+                top = functools.reduce(jnp.maximum, [jnp.max(v, axis=1, keepdims=True) for v in score])
+                lifted = [jnp.exp2(v - top) for v in score]
+                total = sum(jnp.sum(p, axis=1, keepdims=True) for p in lifted)
+                out = sum(mm(p.astype(BF16), v_ref[at_keys, :], NN) for p, at_keys in zip(lifted, keys))
+                ctx_ref[:, at] = (out / total).astype(BF16)
+                lse = jnp.broadcast_to(top + jnp.log2(total), (rows, HD))
+                lse_ref[h] = lse.T[:8]
 
 
 def bwd_kernel(
@@ -124,10 +123,11 @@
         dk_ref[...] = dk0_ref[...]
         dv_ref[...] = dv0_ref[...]
 
-    q, do = q_ref[...], do_ref[...]
-    dot = jnp.sum(do.astype(F32) * ctx_ref[...].astype(F32), axis=1, keepdims=True)
-    dot = jnp.broadcast_to(dot, (rows, HD)).T[:1]
-    lse = lse_ref[0, :1]
+    heads = [slice(h * HD, (h + 1) * HD) for h in range(HEADS)]
+    dots = []
+    for at in heads:
+        dot = jnp.sum(do_ref[:, at].astype(F32) * ctx_ref[:, at].astype(F32), axis=1, keepdims=True)
+        dots.append(jnp.broadcast_to(dot, (rows, HD)).T[:1])
     count, low = span(chip, two_docs, rows)
     mask = diagonal((rows, rows), 1, core * (rows // 2))
     for n in range(1, blocks + 1):
@@ -135,19 +135,26 @@
         @pl.when(count == n)
         def _(n=n):
             near = (n - 1) * rows
-            dqt = jnp.zeros((HD, rows), F32)
+            dqt = [jnp.zeros((HD, rows), F32) for _ in heads]
             for keys, masked in ((pl.ds(low, near), False), (pl.ds(low + near, rows), True)):
                 if not masked and n == 1:
                     continue
-                p = jnp.exp2(mm(k_ref[keys, :], q, NT) - lse)
-                if masked:
-                    p = jnp.where(mask, p, 0.0)
-                ds = (p * (mm(v_ref[keys, :], do, NT) - dot)).astype(BF16)
-                dv_ref[keys, :] += mm(p.astype(BF16), do, NN)
-                dk_ref[keys, :] += mm(ds, q, NN)
-                dqt = dqt + mm(kt_ref[:, keys], ds, NN)
-            g = dqt.T
-            dq_ref[...] = (g * c_ref[...] - pltpu.roll(g, HD // 2, 1) * s_ref[...]).astype(BF16)
+                scores = [mm(k_ref[keys, :], q_ref[:, at], NT) for at in heads]
+                backs = [mm(v_ref[keys, :], do_ref[:, at], NT) for at in heads]
+                dv, dk = 0.0, 0.0
+                for h, at in enumerate(heads):
+                    p = jnp.exp2(scores[h] - lse_ref[h, :1])
+                    if masked:
+                        p = jnp.where(mask, p, 0.0)
+                    ds = (p * (backs[h] - dots[h])).astype(BF16)
+                    dv = dv + mm(p.astype(BF16), do_ref[:, at], NN)
+                    dk = dk + mm(ds, q_ref[:, at], NN)
+                    dqt[h] = dqt[h] + mm(kt_ref[:, keys], ds, NN)
+                dv_ref[keys, :] += dv
+                dk_ref[keys, :] += dk
+            for h, at in enumerate(heads):
+                g = dqt[h].T
+                dq_ref[:, at] = (g * c_ref[...] - pltpu.roll(g, HD // 2, 1) * s_ref[...]).astype(BF16)
 
 
 def whole(shape):
@@ -162,15 +169,15 @@
     rows, width = q_lin.shape
     seq = kv_all.shape[0]
     heads = width // HD
-    column = pl.BlockSpec((rows, HD), lambda h, *_: (0, h + first))
+    column = pl.BlockSpec((rows, HEADS * HD), lambda h, *_: (0, h + first // HEADS))
     return pl.pallas_call(
         functools.partial(fwd_kernel, seq // rows),
         grid_spec=pltpu.PrefetchScalarGridSpec(
             num_scalar_prefetch=1,
-            grid=(count,),
+            grid=(count // HEADS,),
             in_specs=[column, whole((rows, HD)), whole((rows, HD)), whole((seq, HD)), second_half(seq)]
             + [pl.BlockSpec(memory_space=pl.ANY)] * len(before),
-            out_specs=[column, column, pl.BlockSpec((1, 8, rows), lambda h, *_: (h + first, 0, 0))],
+            out_specs=[column, column, pl.BlockSpec((HEADS, 8, rows), lambda h, *_: (h + first // HEADS, 0, 0))],
         ),
         out_shape=[
             jax.ShapeDtypeStruct((rows, width), BF16),
@@ -190,14 +197,14 @@
     rows, width = queries.shape
     seq = kv_all.shape[0]
     heads = width // HD
-    column = pl.BlockSpec((rows, HD), lambda h, *_: (0, h))
+    column = pl.BlockSpec((rows, HEADS * HD), lambda h, *_: (0, h))
     return pl.pallas_call(
         functools.partial(bwd_kernel, seq // rows),
         grid_spec=pltpu.PrefetchScalarGridSpec(
             num_scalar_prefetch=1,
-            grid=(heads,),
+            grid=(heads // HEADS,),
             in_specs=[
-                column, column, column, pl.BlockSpec((1, 8, rows), lambda h, *_: (h, 0, 0)),
+                column, column, column, pl.BlockSpec((HEADS, 8, rows), lambda h, *_: (h, 0, 0)),
                 whole((rows, HD)), whole((rows, HD)), whole((seq, HD)), whole((HD, seq)), second_half(seq),
                 whole((seq, HD)), whole((seq, HD)),
             ],

time: 585 us -> 583 us (level)
  transfers between devices with their start and end apart: 10 -> 10, of which waited for: 4 -> 5; matrix products, arithmetic and copies ran while one was open for 9% -> 9% of each run, Pallas kernels for 5% -> 5%
where the time goes in v7:
time: 583 us; the launch traced here: 574 us
  Pallas kernels  445 us (76%)
  other arithmetic  34.5 us (6%)
  waiting for transfers between devices  28.8 us (5%)
  matrix products  28.4 us (5%)
  local copies, waits for them, and re-layouts  20 us (3%)
  starting transfers between devices  14.7 us (3%)
    pallas_call x1, Pallas kernels, tail(): pl.pallas_call(functools.partial(tail_kernel, links, names), in_specs=[an...  189 us
    pallas_call x1, Pallas kernels, feed_forward(): pl.pallas_call(functools.partial(mlp_kernel, links), in_specs=[anywhere]...  143 us
    pallas_call x1, Pallas kernels, front(): pl.pallas_call(functools.partial(front_kernel, links), in_specs=[pl.Block...  86.5 us
    dot_general x6, matrix products, mm(): lax.dot_general(left, right, (dims, ((), ())), preferred_element_type=F32)  28.4 us
    ppermute x4, waiting for transfers between devices, ring(): return lax.ppermute(x, 'tensor', self.ring_pairs)  26 us
    pallas_call x1, Pallas kernels, attend_back(): pl.pallas_call(functools.partial(bwd_kernel, seq // rows), grid_spec=pltp...  14 us
    pallas_call x2, Pallas kernels, attend(): pl.pallas_call(functools.partial(fwd_kernel, seq // rows), grid_spec=pltp...  12.2 us
  transfers between devices with their start and end apart: 10, of which 5 were waited for; matrix products, arithmetic and copies ran while one was open for 9% of the time, Pallas kernels for 5%

profile of v7, /device:TPU:0, one launch (start us, length us, event | category | flops | bytes accessed | tf_op | source)
XLA Modules:
  0.0 574.0 jit_solution(3995644765058456706)
XLA Ops:
  1.4 1.0 multiply_sine_fusion
  2.4 0.8 fusion.9
  3.2 86.5 %front.1 = (bf16[512,2048]{1,0:T(8,128)(2,1)}, bf16[2048,1024]{1,0:T(8,128)(2,1)}, bf16[1024,2048]{1,0:T(8,128)(2,1)}, bf16[2048,256]{1,0:T(8,128)(2,1)}, bf16[1...) custom-call(s32[1]{0:T(128)S(6)} %copy.43.docs, ...), custom_call_target="tpu_custom_call" | custom-call | flops 10000000000 | bytes 67108864 | tf_op jit(solution)/shard_map/front/pallas_call | solution.py:422
  89.7 0.9 collective-permute-start
  90.6 1.2 fusion.8
  91.7 0.7 pad_add_fusion.sp_ref
  92.4 6.5 %fusion.19.q_ref = f32[512,1024]{1,0:T(8,128)} fusion(bf16[512,2048]{1,0:T(8,128)(2,1)} %get-tuple-element.48, bf16[2048,1024]{1,0:T(8,128)(2,1)} %get-tuple-element.49), kind=kOutput, calls=%fused_computation.75 | convolution fusion | flops 2147483648 | bytes 8388608 | tf_op jit(solution)/shard_map/dot_general | solution.py:22
  98.9 5.7 attend.2
  104.6 10.2 %collective-permute-done.refs_4_ = bf16[256,2048]{1,0:T(8,128)(2,1)S(1)} collective-permute-done((bf16[256,2048]{1,0:T(8,128)(2,1)}, bf16[256,2048]{1,0:T(8,128)(2,1)S(1)}, u32[]{:S(2)}, u32[]{:S(2)}) %collective-permute-start) | collective-permute-done | bytes 1048608 | tf_op jit(solution)/shard_map/ppermute | solution.py:44
  114.8 0.2 collective-permute-start.1
  114.9 6.5 %attend.3 = (bf16[512,1024]{1,0:T(8,128)(2,1)}, bf16[512,1024]{1,0:T(8,128)(2,1)}, f32[8,8,512]{2,1,0:T(8,128)}) custom-call(s32[3]{0:T(128)} %pad_add_fusion.sp_ref, f32[512,1024]{1,0:T(8,128)} %fusion.19.q_ref, f32[512,128]{1,0:T(8,128)} %get-tuple-element.130.c_ref, ...), custom_call_target="tpu_custom_call", output_to_operand_aliasing={{0}: (6, {}), {1}: (7, {}), {2}: (8, {})} | custom-call | flops 4294967296 | bytes 8388608 | tf_op jit(solution)/shard_map/attend/pallas_call | solution.py:173
  121.5 3.6 fusion.20
  125.0 13.4 %collective-permute-done.1.refs_5_ = bf16[256,2048]{1,0:T(8,128)(2,1)S(1)} collective-permute-done((bf16[256,2048]{1,0:T(8,128)(2,1)S(1)}, bf16[256,2048]{1,0:T(8,128)(2,1)S(1)}, u32[]{:S(2)}, u32[]{:S(2)}) %collective-permute-start.1) | collective-permute-done | bytes 1048608 | tf_op jit(solution)/shard_map/ppermute | solution.py:44
  138.4 0.1 slice.95
  138.6 0.1 collective-permute-start.2
  138.6 2.6 collective-permute-done.2
  141.3 0.6 multiply_reduce_fusion.2
  141.9 1.5 multiply_convert_fusion.h_hbm
  143.4 143.3 %feed_forward.1 = (f32[256,2048]{1,0:T(8,128)}, bf16[4,256,2048]{2,1,0:T(8,128)(2,1)}, bf16[8,2112,256]{2,1,0:T(8,128)(2,1)}) custom-call(bf16[256,2048]{1,0:T(8,128)(2,1)} %multiply_convert_fusion.h_hbm, bf16[704,2048]{1,0:T(8,128)(2,1)} %bitcast.80, bf16[704,2048]{1,0:T(8,128)(2,1)} %bitcast.81, bf16[704,2048]{1,0:T(8,128)(2,1)} %wd_hbm.1, ...), custom_call_target="tpu_custom_call" | custom-call | flops 53150220288 | bytes 67108864 | tf_op jit(solution)/shard_map/feed_forward/pallas_call | solution.py:650
  286.7 2.9 multiply_reduce_fusion
  289.7 2.3 fusion.18
  291.9 1.5 collective-permute-start.7
  293.4 2.3 slice.58.refs_12_
  295.7 2.3 slice_bitcast_fusion
  298.0 1.3 collective-permute-start.8
  299.3 3.6 dynamic-slice_bitcast_fusion
  302.9 1.5 collective-permute-start.6
  304.4 0.5 collective-permute-start.5
  304.9 2.0 collective-permute-start.4
  306.9 0.0 collective-permute-start.3
  307.0 5.0 convolution_convert_fusion.2.do_ref
  312.0 14.0 %attend_back.1 = (bf16[512,1024]{1,0:T(8,128)(2,1)}, f32[2048,128]{1,0:T(8,128)}, f32[2048,128]{1,0:T(8,128)}) custom-call(s32[3]{0:T(128)} %pad_add_fusion.sp_ref, bf16[512,1024]{1,0:T(8,128)(2,1)} %get-tuple-element.68.q_ref, bf16[512,1024]{1,0:T(8,128)(2,1)} %convolution_convert_fusion.2.do_ref, bf16[512,1024]{1,0:T(8,128)(2,1)} %get-tuple-element.58.ctx_ref, ...), custom_call_target="tpu_custom_call" | custom-call | flops 21474836480 | bytes 8388608 | tf_op jit(solution)/shard_map/attend_back/pallas_call | solution.py:201
  326.0 1.8 fusion.4
  327.8 0.1 copy-done.11
  327.9 0.3 copy-done.18
  328.1 4.4 convolution_convert_fusion
  332.6 0.1 broadcast_multiply_fusion
  332.7 6.8 %collective-permute-start.9 = (bf16[256,2048]{1,0:T(8,128)(2,1)S(1)}, bf16[256,2048]{1,0:T(8,128)(2,1)S(1)}, u32[]{:S(2)}, u32[]{:S(2)}) collective-permute-start(bf16[256,2048]{1,0:T(8,128)(2,1)S(1)} %fusion.4), channel_id=1, source_target_pairs={{0,2},{1,3},{2,6},{3,7},{4,0},{5,1},{6,4},{7,5},{8,10},{9,11},{10,... | collective-permute-start | bytes 3145736 | tf_op jit(solution)/shard_map/ppermute | solution.py:44
  339.5 0.1 pad_maximum_fusion.1
  339.6 0.2 dynamic-slice_bitcast_fusion.8
  339.8 0.1 pad_maximum_fusion.2
  340.0 1.1 dynamic-slice_bitcast_fusion.4.refs_7_
  341.1 0.1 copy-done.19
  341.1 6.5 %convolution_convert_fusion.1.refs_4_ = bf16[1024,2048]{1,0:T(8,128)(2,1)} fusion(bf16[512,1024]{1,0:T(8,128)(2,1)S(1)} %copy-done.19, bf16[256,2048]{1,0:T(8,128)(2,1)} %collective-permute-done.7, bf16[256,2048]{1,0:T(8,128)(2,1)} %get-tuple-element.108), kind=kOutput, calls=%fused_computation.3 | convolution fusion | flops 2153775104 | bytes 7340032 | tf_op jit(solution)/shard_map/dot_general | solution.py:22
  347.7 2.4 fusion.21
  350.1 0.9 fusion.6.refs_8_
  351.0 1.1 slice.94.refs_10_
  352.1 1.5 slice.69.refs_9_
  353.5 0.1 collective-permute-done.3
  353.7 5.1 fusion
  358.8 2.5 collective-permute-done.9
  361.2 1.4 fusion.5.refs_6_
  362.6 189.5 %tail.1 = (bf16[2112,2048]{1,0:T(8,128)(2,1)}, bf16[256,2048]{1,0:T(8,128)(2,1)}, bf16[2048,256]{1,0:T(8,128)(2,1)}, bf16[256,2048]{1,0:T(8,128)(2,1)}, bf16[256...) custom-call(bf16[2112,256]{1,0:T(8,128)(2,1)} %get-tuple-element.118.refs_0_, ...), custom_call_target="tpu_custom_call" | custom-call | flops 1000000000 | bytes 67108864 | tf_op jit(solution)/shard_map/tail/pallas_call | solution.py:1042
  552.1 0.8 slice_bitcast_fusion.1
  552.9 0.6 copy.37
  553.5 0.6 copy.36
  554.1 2.7 convert_element_type.157
  556.8 0.2 convert_bitcast_fusion.2
  557.0 1.8 copy.31
  558.9 1.6 convert_element_type.158
  560.4 10.5 %slice_convert_fusion = (f32[704,2048]{1,0:T(8,128)}, f32[2048,704]{0,1:T(8,128)}, f32[2048,704]{0,1:T(8,128)}) fusion(bf16[2112,2048]{1,0:T(8,128)(2,1)} %get-tuple-element.85), kind=kLoop, calls=%fused_computation.4 | loop fusion | flops 4325376 | bytes 25952256 | tf_op jit(solution)/shard_map/convert_element_type | solution.py:1182
  571.0 1.0 copy.44
  571.9 0.6 copy-done.6
  572.6 1.0 copy.45
  (52 shorter events, 0.1 us)
Async XLA Ops:
  89.7 25.1 %collective-permute-start = (bf16[256,2048]{1,0:T(8,128)(2,1)}, bf16[256,2048]{1,0:T(8,128)(2,1)S(1)}, u32[]{:S(2)}, u32[]{:S(2)}) collective-permute-start(bf16[256,2048]{1,0:T(8,128)(2,1)} %get-tuple-element.54.refs_2_), channel_id=1, source_target_pairs={{0,2},{1,3},{2,6},{3,7},{4,0},{5,1},{6,4},{7,5},{8,10},{9,11},{10,... | collective-permute-start | bytes 3145736 | tf_op jit(solution)/shard_map/ppermute | solution.py:44
  114.8 6.7 %copy-start.13 = (bf16[256,2048]{1,0:T(8,128)(2,1)}, bf16[256,2048]{1,0:T(8,128)(2,1)S(1)}, u32[]{:S(2)}) copy-start(bf16[256,2048]{1,0:T(8,128)(2,1)S(1)} %collective-permute-done.refs_4_) | copy-start | bytes 3145732
  114.8 6.7 %copy-start.16 = (bf16[1024,2048]{1,0:T(8,128)(2,1)S(1)}, bf16[1024,2048]{1,0:T(8,128)(2,1)}, u32[]{:S(2)}) copy-start(bf16[1024,2048]{1,0:T(8,128)(2,1)} %get-tuple-element.59) | copy-start | bytes 12582916
  114.8 23.6 %collective-permute-start.1 = (bf16[256,2048]{1,0:T(8,128)(2,1)S(1)}, bf16[256,2048]{1,0:T(8,128)(2,1)S(1)}, u32[]{:S(2)}, u32[]{:S(2)}) collective-permute-start(bf16[256,2048]{1,0:T(8,128)(2,1)S(1)} %collective-permute-done.refs_4_), channel_id=1, source_target_pairs={{0,2},{1,3},{2,6},{3,7},{4,0},{5,1},{6,4},{7,5},{8,10},{9,11},{10,... | collective-permute-start | bytes 3145736 | tf_op jit(solution)/shard_map/ppermute | solution.py:44
  125.0 16.3 %copy-start.3 = (bf16[256,2048]{1,0:T(8,128)(2,1)S(1)}, bf16[256,2048]{1,0:T(8,128)(2,1)}, u32[]{:S(2)}) copy-start(bf16[256,2048]{1,0:T(8,128)(2,1)} %refs_11_.1) | copy-start | bytes 3145732
  138.4 3.5 copy-start.14
  138.5 3.4 copy-start.12
  138.6 2.7 collective-permute-start.2
  141.9 147.8 %copy-start = (f32[256,2048]{1,0:T(8,128)}, f32[256,2048]{1,0:T(8,128)S(1)}, u32[]{:S(2)}) copy-start(f32[256,2048]{1,0:T(8,128)S(1)} %get-tuple-element.111.refs_19_) | copy-start | bytes 6291460
  286.7 2.9 copy-start.2
  286.7 2.9 copy-start.10
  291.9 15.0 %collective-permute-start.7 = (bf16[256,2048]{1,0:T(8,128)(2,1)}, bf16[256,2048]{1,0:T(8,128)(2,1)}, u32[]{:S(2)}, u32[]{:S(2)}) collective-permute-start(bf16[256,2048]{1,0:T(8,128)(2,1)} %get-tuple-element.108), channel_id=1, source_target_pairs={{0,1},{1,0},{2,3},{3,2},{4,5},{5,4},{6,7},{7,6},{8,9},{9,8},{10,11... | collective-permute-start | bytes 3145736 | tf_op jit(solution)/shard_map/ppermute | solution.py:47
  298.0 28.0 %collective-permute-start.8 = (bf16[256,2048]{1,0:T(8,128)(2,1)}, bf16[256,2048]{1,0:T(8,128)(2,1)}, u32[]{:S(2)}, u32[]{:S(2)}) collective-permute-start(bf16[256,2048]{1,0:T(8,128)(2,1)} %slice_bitcast_fusion), channel_id=1, source_target_pairs={{0,2},{1,3},{2,6},{3,7},{4,0},{5,1},{6,4},{7,5},{8,10},{9,11},{10,... | collective-permute-start | bytes 3145736 | tf_op jit(solution)/shard_map/ppermute | solution.py:44
  299.3 7.7 %copy-start.17 = (bf16[1024,2048]{1,0:T(8,128)(2,1)S(1)}, bf16[1024,2048]{1,0:T(8,128)(2,1)}, u32[]{:S(2)}) copy-start(bf16[1024,2048]{1,0:T(8,128)(2,1)} %get-tuple-element.59) | copy-start | bytes 12582916
  302.9 50.6 %collective-permute-start.6 = (bf16[2112,256]{1,0:T(8,128)(2,1)}, bf16[2112,256]{1,0:T(8,128)(2,1)}, u32[]{:S(2)}, u32[]{:S(2)}) collective-permute-start(bf16[2112,256]{1,0:T(8,128)(2,1)} %get-tuple-element.119), channel_id=1, source_target_pairs={{0,16},{8,24},{16,0},{24,8},{1,17},{9,25},{17,1},{25,9},{2,18},{10... | collective-permute-start | bytes 3244040 | tf_op jit(solution)/shard_map/ppermute | solution.py:50
  304.4 49.1 %collective-permute-start.5 = (bf16[2112,256]{1,0:T(8,128)(2,1)S(1)}, bf16[2112,256]{1,0:T(8,128)(2,1)}, u32[]{:S(2)}, u32[]{:S(2)}) collective-permute-start(bf16[2112,256]{1,0:T(8,128)(2,1)S(1)} %get-tuple-element.120), channel_id=1, source_target_pairs={{0,16},{8,24},{16,0},{24,8},{1,17},{9,25},{17,1},{25,9},{2,18},{10... | collective-permute-start | bytes 3244040 | tf_op jit(solution)/shard_map/ppermute | solution.py:50
  304.9 48.6 %collective-permute-start.4 = (bf16[2112,256]{1,0:T(8,128)(2,1)S(1)}, bf16[2112,256]{1,0:T(8,128)(2,1)}, u32[]{:S(2)}, u32[]{:S(2)}) collective-permute-start(bf16[2112,256]{1,0:T(8,128)(2,1)S(1)} %get-tuple-element.121), channel_id=1, source_target_pairs={{0,8},{8,0},{16,24},{24,16},{1,9},{9,1},{17,25},{25,17},{2,10},{10... | collective-permute-start | bytes 3244040 | tf_op jit(solution)/shard_map/ppermute | solution.py:50
  306.9 46.7 %collective-permute-start.3 = (bf16[2112,256]{1,0:T(8,128)(2,1)S(1)}, bf16[2112,256]{1,0:T(8,128)(2,1)}, u32[]{:S(2)}, u32[]{:S(2)}) collective-permute-start(bf16[2112,256]{1,0:T(8,128)(2,1)S(1)} %get-tuple-element.122), channel_id=1, source_target_pairs={{0,8},{8,0},{16,24},{24,16},{1,9},{9,1},{17,25},{25,17},{2,10},{10... | collective-permute-start | bytes 3244040 | tf_op jit(solution)/shard_map/ppermute | solution.py:50
  312.0 14.0 %copy-start.1 = (bf16[4,256,2048]{2,1,0:T(8,128)(2,1)S(1)}, bf16[4,256,2048]{2,1,0:T(8,128)(2,1)}, u32[]{:S(2)}) copy-start(bf16[4,256,2048]{2,1,0:T(8,128)(2,1)} %get-tuple-element.74.refs_20_) | copy-start | bytes 12582916
  326.0 1.9 copy-start.11
  326.0 2.2 copy-start.18
  328.1 4.4 copy-start.8
  332.6 6.9 %copy-start.9 = (f32[2048,128]{1,0:T(8,128)S(1)}, f32[2048,128]{1,0:T(8,128)}, u32[]{:S(2)}) copy-start(f32[2048,128]{1,0:T(8,128)} %get-tuple-element.78) | copy-start | bytes 3145732
  332.7 28.6 %collective-permute-start.9 = (bf16[256,2048]{1,0:T(8,128)(2,1)S(1)}, bf16[256,2048]{1,0:T(8,128)(2,1)S(1)}, u32[]{:S(2)}, u32[]{:S(2)}) collective-permute-start(bf16[256,2048]{1,0:T(8,128)(2,1)S(1)} %fusion.4), channel_id=1, source_target_pairs={{0,2},{1,3},{2,6},{3,7},{4,0},{5,1},{6,4},{7,5},{8,10},{9,11},{10,... | collective-permute-start | bytes 3145736 | tf_op jit(solution)/shard_map/ppermute | solution.py:44
  339.8 1.3 copy-start.19
  340.0 7.7 %copy-start.15 = (bf16[2048,1024]{1,0:T(8,128)(2,1)S(1)}, bf16[2048,1024]{1,0:T(8,128)(2,1)}, u32[]{:S(2)}) copy-start(bf16[2048,1024]{1,0:T(8,128)(2,1)} %get-tuple-element.49) | copy-start | bytes 12582916
  341.1 12.5 %slice-start = ((s8[8650752]{0:T(1024)(128)(4,1)}), s8[4194304]{0:T(1024)(128)(4,1)S(1)}, s32[]{:S(2)}) async-start(s8[8650752]{0:T(1024)(128)(4,1)} %bitcast.71), calls=%async_computation | async-start | bytes 8388608
  341.1 12.5 %slice-start.1 = ((s8[8650752]{0:T(1024)(128)(4,1)}), s8[4194304]{0:T(1024)(128)(4,1)S(1)}, s32[]{:S(2)}) async-start(s8[8650752]{0:T(1024)(128)(4,1)} %bitcast.71), calls=%async_computation.1 | async-start | bytes 8388608
  347.7 6.0 %slice-start.2 = ((s8[8650752]{0:T(1024)(128)(4,1)}), s8[262144]{0:T(1024)(128)(4,1)S(1)}, s32[]{:S(2)}) async-start(s8[8650752]{0:T(1024)(128)(4,1)} %bitcast.71), calls=%async_computation.2 | async-start | bytes 524288
  552.0 4.7 copy-start.5
  557.0 1.8 copy-start.4
  560.4 10.6 %copy-start.7 = (bf16[256,2048]{1,0:T(8,128)(2,1)S(1)}, bf16[256,2048]{1,0:T(8,128)(2,1)}, u32[]{:S(2)}) copy-start(bf16[256,2048]{1,0:T(8,128)(2,1)} %get-tuple-element.150) | copy-start | bytes 3145732
  571.0 1.6 copy-start.6

commit v8 on v7

--- a/solution.py
+++ b/solution.py
@@ -802,10 +802,10 @@
 ):
     w_hbm, refs = refs[: len(names)], refs[len(names) :]
     (
-        o_hbm, q_hbm, m_hbm, kv_keep, kv_send, gn_keep, gn_send, tokens, normed, w_kv, cosine, sine, gain_part,
+        o_hbm, q_hbm, m_hbm, kv_keep, kv_send, gn_hbm, gn_send, tokens, normed_hbm, w_kv, cosine, sine, gain_part,
         gain, grad_hidden, hidden, terms,
         ws_hbm, ow_hbm, qw_hbm, kvw_hbm, block_ref, grad_ref, gains_ref,
-        o_buf, o_in, o_ring, q_buf, q_in, w_buf, w_in, c_buf, c_in, b_buf, b_in, b_turned, got, mine, m_sem,
+        o_buf, o_in, o_ring, q_buf, q_in, w_buf, w_in, c_buf, c_in, b_buf, b_in, b_turned, got, mine, m_sem, gn_keep, normed, own_sem,
         kv_got, kv_ring, kv_in, gn_got, kvw_half, kvw_got, kvw_in, kvw_all, gains_in,
         ss, rs, o_sem, q_sem, w_sem, out_sem, w_free, o_free, b_free,
     ) = refs
@@ -834,7 +834,12 @@
     o_loads = [
         pltpu.make_async_copy(o_hbm.at[:, pl.ds(j * piece, piece)], o_buf.at[j], o_sem.at[j]) for j in range(2 * n_dp)
     ]
-    for load in o_loads + list(loads.values()) + w_loads:
+    own_rows = pl.ds(0, gn_keep.shape[0])
+    own_loads = [
+        pltpu.make_async_copy(gn_hbm.at[own_rows], gn_keep, own_sem.at[0]),
+        pltpu.make_async_copy(normed_hbm.at[own_rows], normed, own_sem.at[1]),
+    ]
+    for load in own_loads + o_loads + list(loads.values()) + w_loads:
         load.start()
     barrier = pltpu.get_barrier_semaphore()
     peers = [right, left] + group + replicas
@@ -874,6 +879,8 @@
     held = {}
 
     def kv_chain():
+        for load in own_loads:
+            load.wait()
         kv_swap.wait_recv()
         sent = []
         for k in range(1, chips):
@@ -1041,7 +1048,10 @@
     count = 20 * chips + 20 * n + 16
     return pl.pallas_call(
         functools.partial(tail_kernel, links, names),
-        in_specs=[anywhere] * (3 + len(names)) + [here] * 13 + [anywhere],
+        in_specs=[anywhere] * (3 + len(names))
+        + [here, here, anywhere, here, here, anywhere]
+        + [here] * 7
+        + [anywhere],
         out_specs=[anywhere] * 4 + [here] * 3,
         out_shape=[
             shape((rows, depth), BF16), shape((width, depth), BF16),
@@ -1057,6 +1067,7 @@
             pltpu.VMEM((pieces, width, piece), BF16), pltpu.VMEM((2, n - 1, width, piece), BF16),
             pltpu.VMEM((pieces, piece, width), BF16), pltpu.VMEM((own, depth), BF16),
             pltpu.VMEM((own, depth), BF16), dma((1,)),
+            pltpu.VMEM((own, depth), F32), pltpu.VMEM((own, depth), BF16), dma((2,)),
             pltpu.VMEM((chips, own, 2 * HD), BF16),
             pltpu.VMEM((chips - 1, own, 2 * HD), BF16), pltpu.VMEM((chips - 1, own, 2 * HD), BF16),
             pltpu.VMEM((own, depth), BF16),
@@ -1116,7 +1127,6 @@
         links, doc_split, tokens, attn_gain[None], w_kv, cosine[:own], sine[:own], query_two, grad_two, w_query, w_out,
         out_grad,
     )
-    normed_own = normed[:own]
     grad_chunks = [out_grad] + grad_chunks
 
     q_lin = mm(normed, wq, NN)
@@ -1171,8 +1181,8 @@
     ffn_pieces = [(a.astype(F32) + b.astype(F32)).astype(BF16) for a, b in zip(ffn_stay, ffn_came)]
     gain_part = mlp_gain_part[None]
     ffn_w, out_w, query_w, kv_w, block_output, tokens_grad, gains = tail(
-        links, out_parts, query_parts, mlp_sent, ffn_pieces, ffn_names, kv_keep, kv_send, gn_part[:own],
-        gn_part[own:].astype(BF16), tokens, normed_own, w_kv, cosine[:own], sine[:own], gain_part,
+        links, out_parts, query_parts, mlp_sent, ffn_pieces, ffn_names, kv_keep, kv_send, gn_part,
+        gn_part[own:].astype(BF16), tokens, normed, w_kv, cosine[:own], sine[:own], gain_part,
         attn_gain[None], grad_hidden, hidden, mlp_terms,
     )
     units = w_down.shape[0]

time: 583 us -> 575 us (0.986)
  Pallas kernels: 445 us -> 439 us
    pallas_call x1, Pallas kernels: 189 us -> 183 us  [tail(): pl.pallas_call(functools.partial(tail_kernel, links, names), in_specs=[an...]
  transfers between devices with their start and end apart: 10 -> 10, of which waited for: 5 -> 4; matrix products, arithmetic and copies ran while one was open for 9% -> 8% of each run, Pallas kernels for 5% -> 5%
where the time goes in v8:
time: 575 us; the launch traced here: 566 us
  Pallas kernels  439 us (76%)
  other arithmetic  34.6 us (6%)
  waiting for transfers between devices  29.4 us (5%)
  matrix products  28.4 us (5%)
  local copies, waits for them, and re-layouts  17.7 us (3%)
  starting transfers between devices  14.8 us (3%)
    pallas_call x1, Pallas kernels, tail(): pl.pallas_call(functools.partial(tail_kernel, links, names), in_specs=[an...  183 us
    pallas_call x1, Pallas kernels, feed_forward(): pl.pallas_call(functools.partial(mlp_kernel, links), in_specs=[anywhere]...  143 us
    pallas_call x1, Pallas kernels, front(): pl.pallas_call(functools.partial(front_kernel, links), in_specs=[pl.Block...  86.5 us
    dot_general x6, matrix products, mm(): lax.dot_general(left, right, (dims, ((), ())), preferred_element_type=F32)  28.4 us
    ppermute x4, waiting for transfers between devices, ring(): return lax.ppermute(x, 'tensor', self.ring_pairs)  26.8 us
    pallas_call x1, Pallas kernels, attend_back(): pl.pallas_call(functools.partial(bwd_kernel, seq // rows), grid_spec=pltp...  14 us
    pallas_call x2, Pallas kernels, attend(): pl.pallas_call(functools.partial(fwd_kernel, seq // rows), grid_spec=pltp...  12.2 us
  transfers between devices with their start and end apart: 10, of which 4 were waited for; matrix products, arithmetic and copies ran while one was open for 8% of the time, Pallas kernels for 5%

profile of v8, /device:TPU:0, one launch (start us, length us, event | category | flops | bytes accessed | tf_op | source)
XLA Modules:
  0.0 566.0 jit_solution(5988888815249716030)
XLA Ops:
  1.4 1.0 multiply_sine_fusion
  2.4 0.9 fusion.9
  3.2 86.5 %front.1 = (bf16[512,2048]{1,0:T(8,128)(2,1)}, bf16[2048,1024]{1,0:T(8,128)(2,1)}, bf16[1024,2048]{1,0:T(8,128)(2,1)}, bf16[2048,256]{1,0:T(8,128)(2,1)}, bf16[1...) custom-call(s32[1]{0:T(128)S(6)} %copy.43.docs, ...), custom_call_target="tpu_custom_call" | custom-call | flops 10000000000 | bytes 67108864 | tf_op jit(solution)/shard_map/front/pallas_call | solution.py:422
  89.7 0.9 collective-permute-start
  90.6 1.1 fusion.8
  91.7 0.6 pad_add_fusion.sp_ref
  92.3 6.5 %fusion.19.q_ref = f32[512,1024]{1,0:T(8,128)} fusion(bf16[512,2048]{1,0:T(8,128)(2,1)} %get-tuple-element.48.refs_12_, bf16[2048,1024]{1,0:T(8,128)(2,1)} %get-tuple-element.49), kind=kOutput, calls=%fused_computation.75 | convolution fusion | flops 2147483648 | bytes 8388608 | tf_op jit(solution)/shard_map/dot_general | solution.py:22
  98.8 5.7 %attend.2 = (bf16[512,1024]{1,0:T(8,128)(2,1)}, bf16[512,1024]{1,0:T(8,128)(2,1)}, f32[8,8,512]{2,1,0:T(8,128)}) custom-call(s32[3]{0:T(128)} %pad_add_fusion.sp_ref, f32[512,1024]{1,0:T(8,128)} %fusion.19.q_ref, f32[512,128]{1,0:T(8,128)} %get-tuple-element.130.c_ref, f32[512,128]{1,0:T(8,128)} %get-tuple-element.136.s_ref, ...), custom_call_target="tpu_custom_call" | custom-call | flops 4294967296 | bytes 8388608 | tf_op jit(solution)/shard_map/attend/pallas_call | solution.py:173
  104.5 10.3 %collective-permute-done.refs_4_ = bf16[256,2048]{1,0:T(8,128)(2,1)S(1)} collective-permute-done((bf16[256,2048]{1,0:T(8,128)(2,1)}, bf16[256,2048]{1,0:T(8,128)(2,1)S(1)}, u32[]{:S(2)}, u32[]{:S(2)}) %collective-permute-start) | collective-permute-done | bytes 1048608 | tf_op jit(solution)/shard_map/ppermute | solution.py:44
  114.8 0.2 collective-permute-start.1
  115.0 6.5 %attend.3 = (bf16[512,1024]{1,0:T(8,128)(2,1)}, bf16[512,1024]{1,0:T(8,128)(2,1)}, f32[8,8,512]{2,1,0:T(8,128)}) custom-call(s32[3]{0:T(128)} %pad_add_fusion.sp_ref, f32[512,1024]{1,0:T(8,128)} %fusion.19.q_ref, f32[512,128]{1,0:T(8,128)} %get-tuple-element.130.c_ref, ...), custom_call_target="tpu_custom_call", output_to_operand_aliasing={{0}: (6, {}), {1}: (7, {}), {2}: (8, {})} | custom-call | flops 4294967296 | bytes 8388608 | tf_op jit(solution)/shard_map/attend/pallas_call | solution.py:173
  121.5 3.6 fusion.20
  125.0 0.0 copy-start.4
  125.0 13.4 %collective-permute-done.1.refs_5_ = bf16[256,2048]{1,0:T(8,128)(2,1)S(1)} collective-permute-done((bf16[256,2048]{1,0:T(8,128)(2,1)S(1)}, bf16[256,2048]{1,0:T(8,128)(2,1)S(1)}, u32[]{:S(2)}, u32[]{:S(2)}) %collective-permute-start.1) | collective-permute-done | bytes 1048608 | tf_op jit(solution)/shard_map/ppermute | solution.py:44
  138.4 0.1 slice.86
  138.6 0.0 copy-start.14
  138.6 0.1 collective-permute-start.2
  138.7 2.6 collective-permute-done.2
  141.3 0.6 multiply_reduce_fusion.2
  142.0 1.4 multiply_convert_fusion.h_hbm
  143.4 143.4 %feed_forward.1 = (f32[256,2048]{1,0:T(8,128)}, bf16[4,256,2048]{2,1,0:T(8,128)(2,1)}, bf16[8,2112,256]{2,1,0:T(8,128)(2,1)}) custom-call(bf16[256,2048]{1,0:T(8,128)(2,1)} %multiply_convert_fusion.h_hbm, bf16[704,2048]{1,0:T(8,128)(2,1)} %bitcast.80, bf16[704,2048]{1,0:T(8,128)(2,1)} %bitcast.81, bf16[704,2048]{1,0:T(8,128)(2,1)} %wd_hbm.1, ...), custom_call_target="tpu_custom_call" | custom-call | flops 53150220288 | bytes 67108864 | tf_op jit(solution)/shard_map/feed_forward/pallas_call | solution.py:650
  286.8 0.0 copy-start.13
  286.8 2.9 multiply_reduce_fusion
  289.7 2.3 fusion.18
  292.0 1.5 collective-permute-start.7
  293.4 1.3 slice_bitcast_fusion
  294.8 1.3 collective-permute-start.8
  296.1 4.2 dynamic-slice_bitcast_fusion
  300.3 1.5 collective-permute-start.6
  301.8 0.5 collective-permute-start.5
  302.3 2.0 collective-permute-start.4
  304.3 0.1 collective-permute-start.3
  304.4 5.0 convolution_convert_fusion.2.do_ref
  309.4 14.0 %attend_back.1 = (bf16[512,1024]{1,0:T(8,128)(2,1)}, f32[2048,128]{1,0:T(8,128)}, f32[2048,128]{1,0:T(8,128)}) custom-call(s32[3]{0:T(128)} %pad_add_fusion.sp_ref, bf16[512,1024]{1,0:T(8,128)(2,1)} %get-tuple-element.68.q_ref, bf16[512,1024]{1,0:T(8,128)(2,1)} %convolution_convert_fusion.2.do_ref, bf16[512,1024]{1,0:T(8,128)(2,1)} %get-tuple-element.58.ctx_ref, ...), custom_call_target="tpu_custom_call" | custom-call | flops 21474836480 | bytes 8388608 | tf_op jit(solution)/shard_map/attend_back/pallas_call | solution.py:201
  323.4 1.0 copy-done.6
  324.3 1.8 fusion.4
  326.1 0.1 broadcast_multiply_fusion
  326.2 6.8 %collective-permute-start.9 = (bf16[256,2048]{1,0:T(8,128)(2,1)S(1)}, bf16[256,2048]{1,0:T(8,128)(2,1)S(1)}, u32[]{:S(2)}, u32[]{:S(2)}) collective-permute-start(bf16[256,2048]{1,0:T(8,128)(2,1)S(1)} %fusion.4), channel_id=1, source_target_pairs={{0,2},{1,3},{2,6},{3,7},{4,0},{5,1},{6,4},{7,5},{8,10},{9,11},{10,... | collective-permute-start | bytes 3145736 | tf_op jit(solution)/shard_map/ppermute | solution.py:44
  333.1 4.4 convolution_convert_fusion
  337.5 0.3 pad_maximum_fusion.1
  337.7 0.2 dynamic-slice_bitcast_fusion.8
  337.9 0.1 pad_maximum_fusion.2
  338.1 1.1 dynamic-slice_bitcast_fusion.4.refs_7_
  339.2 0.0 copy-done.21
  339.2 6.6 %convolution_convert_fusion.1.refs_4_ = bf16[1024,2048]{1,0:T(8,128)(2,1)} fusion(bf16[512,1024]{1,0:T(8,128)(2,1)S(1)} %copy-done.21, bf16[256,2048]{1,0:T(8,128)(2,1)} %collective-permute-done.7, bf16[256,2048]{1,0:T(8,128)(2,1)} %get-tuple-element.108), kind=kOutput, calls=%fused_computation.3 | convolution fusion | flops 2153775104 | bytes 7340032 | tf_op jit(solution)/shard_map/dot_general | solution.py:22
  345.8 2.4 fusion.21.refs_9_
  348.2 0.9 fusion.6.refs_8_
  349.1 1.2 copy-done.3
  350.3 1.1 slice.85.refs_10_
  351.5 5.1 fusion
  356.6 3.1 collective-permute-done.9
  359.7 1.4 fusion.5.refs_6_
  361.1 182.9 %tail.1 = (bf16[2112,2048]{1,0:T(8,128)(2,1)}, bf16[256,2048]{1,0:T(8,128)(2,1)}, bf16[2048,256]{1,0:T(8,128)(2,1)}, bf16[256,2048]{1,0:T(8,128)(2,1)}, bf16[256...) custom-call(bf16[2112,256]{1,0:T(8,128)(2,1)} %get-tuple-element.118.refs_0_, ...), custom_call_target="tpu_custom_call" | custom-call | flops 1000000000 | bytes 67108864 | tf_op jit(solution)/shard_map/tail/pallas_call | solution.py:1049
  544.0 0.8 slice_bitcast_fusion.1
  544.8 0.6 copy.37
  545.5 0.6 copy.36
  546.1 2.7 convert_element_type.157
  548.8 0.2 convert_bitcast_fusion.2
  549.0 1.8 copy.31
  550.8 1.6 convert_element_type.158
  552.4 10.5 %slice_convert_fusion = (f32[704,2048]{1,0:T(8,128)}, f32[2048,704]{0,1:T(8,128)}, f32[2048,704]{0,1:T(8,128)}) fusion(bf16[2112,2048]{1,0:T(8,128)(2,1)} %get-tuple-element.85), kind=kLoop, calls=%fused_computation.4 | loop fusion | flops 4325376 | bytes 25952256 | tf_op jit(solution)/shard_map/convert_element_type | solution.py:1192
  562.9 1.0 copy.44
  563.9 0.6 copy-done.9
  564.5 1.0 copy.45
  (54 shorter events, 0.1 us)
Async XLA Ops:
  89.7 25.1 %collective-permute-start = (bf16[256,2048]{1,0:T(8,128)(2,1)}, bf16[256,2048]{1,0:T(8,128)(2,1)S(1)}, u32[]{:S(2)}, u32[]{:S(2)}) collective-permute-start(bf16[256,2048]{1,0:T(8,128)(2,1)} %get-tuple-element.54.refs_2_), channel_id=1, source_target_pairs={{0,2},{1,3},{2,6},{3,7},{4,0},{5,1},{6,4},{7,5},{8,10},{9,11},{10,... | collective-permute-start | bytes 3145736 | tf_op jit(solution)/shard_map/ppermute | solution.py:44
  114.8 6.7 %copy-start.15 = (bf16[256,2048]{1,0:T(8,128)(2,1)}, bf16[256,2048]{1,0:T(8,128)(2,1)S(1)}, u32[]{:S(2)}) copy-start(bf16[256,2048]{1,0:T(8,128)(2,1)S(1)} %collective-permute-done.refs_4_) | copy-start | bytes 3145732
  114.8 6.7 %copy-start.18 = (bf16[1024,2048]{1,0:T(8,128)(2,1)S(1)}, bf16[1024,2048]{1,0:T(8,128)(2,1)}, u32[]{:S(2)}) copy-start(bf16[1024,2048]{1,0:T(8,128)(2,1)} %get-tuple-element.59) | copy-start | bytes 12582916
  114.8 23.6 %collective-permute-start.1 = (bf16[256,2048]{1,0:T(8,128)(2,1)S(1)}, bf16[256,2048]{1,0:T(8,128)(2,1)S(1)}, u32[]{:S(2)}, u32[]{:S(2)}) collective-permute-start(bf16[256,2048]{1,0:T(8,128)(2,1)S(1)} %collective-permute-done.refs_4_), channel_id=1, source_target_pairs={{0,2},{1,3},{2,6},{3,7},{4,0},{5,1},{6,4},{7,5},{8,10},{9,11},{10,... | collective-permute-start | bytes 3145736 | tf_op jit(solution)/shard_map/ppermute | solution.py:44
  125.0 16.3 %copy-start.4 = (bf16[256,2048]{1,0:T(8,128)(2,1)S(1)}, bf16[256,2048]{1,0:T(8,128)(2,1)}, u32[]{:S(2)}) copy-start(bf16[256,2048]{1,0:T(8,128)(2,1)} %refs_11_.1) | copy-start | bytes 3145732
  138.4 3.5 copy-start.16
  138.6 3.4 copy-start.14
  138.6 2.7 collective-permute-start.2
  141.9 147.8 %copy-start = (f32[256,2048]{1,0:T(8,128)}, f32[256,2048]{1,0:T(8,128)S(1)}, u32[]{:S(2)}) copy-start(f32[256,2048]{1,0:T(8,128)S(1)} %get-tuple-element.111.refs_19_) | copy-start | bytes 6291460
  286.8 2.9 copy-start.2
  286.8 2.9 copy-start.13
  292.0 12.3 %collective-permute-start.7 = (bf16[256,2048]{1,0:T(8,128)(2,1)}, bf16[256,2048]{1,0:T(8,128)(2,1)}, u32[]{:S(2)}, u32[]{:S(2)}) collective-permute-start(bf16[256,2048]{1,0:T(8,128)(2,1)} %get-tuple-element.108), channel_id=1, source_target_pairs={{0,1},{1,0},{2,3},{3,2},{4,5},{5,4},{6,7},{7,6},{8,9},{9,8},{10,11... | collective-permute-start | bytes 3145736 | tf_op jit(solution)/shard_map/ppermute | solution.py:47
  294.8 28.6 %collective-permute-start.8 = (bf16[256,2048]{1,0:T(8,128)(2,1)S(1)}, bf16[256,2048]{1,0:T(8,128)(2,1)S(1)}, u32[]{:S(2)}, u32[]{:S(2)}) collective-permute-start(bf16[256,2048]{1,0:T(8,128)(2,1)S(1)} %slice_bitcast_fusion), channel_id=1, source_target_pairs={{0,2},{1,3},{2,6},{3,7},{4,0},{5,1},{6,4},{7,5},{8,10},{9,11},{10,... | collective-permute-start | bytes 3145736 | tf_op jit(solution)/shard_map/ppermute | solution.py:44
  296.1 8.3 %copy-start.19 = (bf16[1024,2048]{1,0:T(8,128)(2,1)S(1)}, bf16[1024,2048]{1,0:T(8,128)(2,1)}, u32[]{:S(2)}) copy-start(bf16[1024,2048]{1,0:T(8,128)(2,1)} %get-tuple-element.59) | copy-start | bytes 12582916
  300.3 51.2 %collective-permute-start.6 = (bf16[2112,256]{1,0:T(8,128)(2,1)}, bf16[2112,256]{1,0:T(8,128)(2,1)}, u32[]{:S(2)}, u32[]{:S(2)}) collective-permute-start(bf16[2112,256]{1,0:T(8,128)(2,1)} %get-tuple-element.119), channel_id=1, source_target_pairs={{0,16},{8,24},{16,0},{24,8},{1,17},{9,25},{17,1},{25,9},{2,18},{10... | collective-permute-start | bytes 3244040 | tf_op jit(solution)/shard_map/ppermute | solution.py:50
  301.8 49.7 %collective-permute-start.5 = (bf16[2112,256]{1,0:T(8,128)(2,1)}, bf16[2112,256]{1,0:T(8,128)(2,1)}, u32[]{:S(2)}, u32[]{:S(2)}) collective-permute-start(bf16[2112,256]{1,0:T(8,128)(2,1)} %get-tuple-element.120), channel_id=1, source_target_pairs={{0,16},{8,24},{16,0},{24,8},{1,17},{9,25},{17,1},{25,9},{2,18},{10... | collective-permute-start | bytes 3244040 | tf_op jit(solution)/shard_map/ppermute | solution.py:50
  302.3 49.1 %collective-permute-start.4 = (bf16[2112,256]{1,0:T(8,128)(2,1)}, bf16[2112,256]{1,0:T(8,128)(2,1)}, u32[]{:S(2)}, u32[]{:S(2)}) collective-permute-start(bf16[2112,256]{1,0:T(8,128)(2,1)} %get-tuple-element.121), channel_id=1, source_target_pairs={{0,8},{8,0},{16,24},{24,16},{1,9},{9,1},{17,25},{25,17},{2,10},{10... | collective-permute-start | bytes 3244040 | tf_op jit(solution)/shard_map/ppermute | solution.py:50
  304.3 47.2 %collective-permute-start.3 = (bf16[2112,256]{1,0:T(8,128)(2,1)S(1)}, bf16[2112,256]{1,0:T(8,128)(2,1)}, u32[]{:S(2)}, u32[]{:S(2)}) collective-permute-start(bf16[2112,256]{1,0:T(8,128)(2,1)S(1)} %get-tuple-element.122), channel_id=1, source_target_pairs={{0,8},{8,0},{16,24},{24,16},{1,9},{9,1},{17,25},{25,17},{2,10},{10... | collective-permute-start | bytes 3244040 | tf_op jit(solution)/shard_map/ppermute | solution.py:50
  309.4 15.0 %copy-start.1 = (bf16[4,256,2048]{2,1,0:T(8,128)(2,1)S(1)}, bf16[4,256,2048]{2,1,0:T(8,128)(2,1)}, u32[]{:S(2)}) copy-start(bf16[4,256,2048]{2,1,0:T(8,128)(2,1)} %get-tuple-element.74.refs_20_) | copy-start | bytes 12582916
  323.3 2.8 copy-start.11
  323.4 1.0 copy-start.6
  324.3 8.7 %copy-start.5 = (bf16[512,2048]{1,0:T(8,128)(2,1)S(1)}, bf16[512,2048]{1,0:T(8,128)(2,1)}, u32[]{:S(2)}) copy-start(bf16[512,2048]{1,0:T(8,128)(2,1)} %get-tuple-element.48.refs_12_) | copy-start | bytes 6291460
  324.3 8.7 %copy-start.20 = (bf16[512,1024]{1,0:T(8,128)(2,1)S(1)}, bf16[512,1024]{1,0:T(8,128)(2,1)}, u32[]{:S(2)}) copy-start(bf16[512,1024]{1,0:T(8,128)(2,1)} %get-tuple-element.75) | copy-start | bytes 3145732
  326.2 11.2 %copy-start.12 = (f32[2048,128]{1,0:T(8,128)S(1)}, f32[2048,128]{1,0:T(8,128)}, u32[]{:S(2)}) copy-start(f32[2048,128]{1,0:T(8,128)} %get-tuple-element.78) | copy-start | bytes 3145732
  326.2 33.5 %collective-permute-start.9 = (bf16[256,2048]{1,0:T(8,128)(2,1)S(1)}, bf16[256,2048]{1,0:T(8,128)(2,1)S(1)}, u32[]{:S(2)}, u32[]{:S(2)}) collective-permute-start(bf16[256,2048]{1,0:T(8,128)(2,1)S(1)} %fusion.4), channel_id=1, source_target_pairs={{0,2},{1,3},{2,6},{3,7},{4,0},{5,1},{6,4},{7,5},{8,10},{9,11},{10,... | collective-permute-start | bytes 3145736 | tf_op jit(solution)/shard_map/ppermute | solution.py:44
  337.9 1.3 copy-start.21
  338.1 7.7 %copy-start.17 = (bf16[2048,1024]{1,0:T(8,128)(2,1)S(1)}, bf16[2048,1024]{1,0:T(8,128)(2,1)}, u32[]{:S(2)}) copy-start(bf16[2048,1024]{1,0:T(8,128)(2,1)} %get-tuple-element.49) | copy-start | bytes 12582916
  339.2 12.3 %slice-start = ((s8[8650752]{0:T(1024)(128)(4,1)}), s8[4194304]{0:T(1024)(128)(4,1)S(1)}, s32[]{:S(2)}) async-start(s8[8650752]{0:T(1024)(128)(4,1)} %bitcast.71), calls=%async_computation | async-start | bytes 8388608
  339.2 12.3 %slice-start.1 = ((s8[8650752]{0:T(1024)(128)(4,1)}), s8[4194304]{0:T(1024)(128)(4,1)S(1)}, s32[]{:S(2)}) async-start(s8[8650752]{0:T(1024)(128)(4,1)} %bitcast.71), calls=%async_computation.1 | async-start | bytes 8388608
  345.8 5.7 %slice-start.2 = ((s8[8650752]{0:T(1024)(128)(4,1)}), s8[262144]{0:T(1024)(128)(4,1)S(1)}, s32[]{:S(2)}) async-start(s8[8650752]{0:T(1024)(128)(4,1)} %bitcast.71), calls=%async_computation.2 | async-start | bytes 524288
  348.2 2.2 copy-start.3
  544.0 4.7 copy-start.8
  549.0 1.8 copy-start.7
  552.4 10.6 %copy-start.10 = (bf16[256,2048]{1,0:T(8,128)(2,1)S(1)}, bf16[256,2048]{1,0:T(8,128)(2,1)}, u32[]{:S(2)}) copy-start(bf16[256,2048]{1,0:T(8,128)(2,1)} %get-tuple-element.150) | copy-start | bytes 3145732
  562.9 1.6 copy-start.9
